TPU v7x, 32 devices: a whole 2x2x4 slice. The times are simulated.
32 devices in a mesh: pool: 2 (over x), dev: 16 (over z, y, core).
Axes of the slice: x: 2, y: 2, z: 4, core: 2. Of those that a mesh axis runs over, the one named last changes fastest.
Arguments:
- queries: bfloat16 [512, 4096], P(('pool', 'dev')), may hold values from -6 to 6
- new_kv: bfloat16 [512, 512], P(('pool', 'dev')), may hold values from -6 to 6
- kv_pages: bfloat16 [4096, 16, 512], P(('pool', 'dev')), may hold values from -6 to 6
- page_table: int32 [512, 16], P(('pool', 'dev')), may hold values from 0 to 143, as said below
- lengths: int32 [512], P(('pool', 'dev')), may hold values from 1 to 256, as said below
- shed_slots: int32 [512], P(('pool', 'dev')), may hold values from 0 to 127, as said below
- residual: bfloat16 [512, 4096], P(('pool', 'dev')), may hold values from -6 to 6
- norm_gain: float32 [4096], replicated, may hold values from 0.1 to 1.9
- expert_ids: int32 [512, 8], P(('pool', 'dev')), may hold values from 0 to 31, all different within a row; in each aligned block of 16 rows (0 to 15, 16 to 31, ...) at most 8 rows name the same one
- gate_weights: float32 [512, 8], P(('pool', 'dev')), may hold values from 0.05 to 0.6
- w_gate_up: bfloat16 [32, 4096, 1536], P(('pool', 'dev')), may hold values from -0.09375 to 0.09375
- w_down: bfloat16 [32, 768, 4096], P(('pool', 'dev')), may hold values from -0.21875 to 0.21875
Outputs:
- attended: bfloat16 [512, 4096], P(('pool', 'dev'))
- layer_out: bfloat16 [512, 4096], P(('pool', 'dev'))
Inputs may be any that keep to these rules, and one draw needn't show every extreme that they name: `page_table`: entry p of request r is used for p < ceil(lengths[r] / 16) and is 0 otherwise. The used entries of one device's requests are distinct. Of two partners exactly one sheds: its used entries take every value from 0 to 143; the other's stay below 128. `lengths`: A device that sheds has a request of 256 tokens. `shed_slots`: for a device that sheds: distinct pages of the partner's block that no request of the partner uses. For the other device the list is not read. `expert_ids`: among the 16 requests of one device at most 8 name the same expert; the 8 experts of a request differ.
All inputs are finite; a program needn't handle non-finite values.
Results may differ from a plain program's by a relative error of at most 0.014.
Values may be sent and summed in bfloat16 or wider, within the bound.
No kernel may reach another device: no remote copies, remote signals or barrier semaphores. Data moves between devices by JAX's collectives and lax.ppermute only.
A program may use at most 128 MiB of HBM per device.

v0:
```python
import math

import jax
import jax.numpy as jnp
from jax import lax
from jax.sharding import PartitionSpec as P

HEAD_DIMENSION = 128
KEY_VALUE_HEADS = 2
QUERY_GROUP_SIZE = 16


masked_score = -1e30
epsilon = 1e-06


def from_behind(value, axis, by):
    length = lax.axis_size(axis)
    return lax.ppermute(value, axis, [(i, (i + by) % length) for i in range(length)])


def cache_scores(source, index_table, allowed, query_head_block, scaling):
    count_of_rows = index_table.shape[0]
    collected_rows = jnp.take(source, index_table, axis=0).reshape(
        count_of_rows, -1, source.shape[-1]
    )
    key_row_width = source.shape[-1] // 2
    group_heads = query_head_block.shape[1]
    head_size = query_head_block.shape[3]
    key_entries = collected_rows[:, :, :key_row_width].reshape(
        count_of_rows, -1, group_heads, head_size
    )
    value_entries = collected_rows[:, :, key_row_width:].reshape(
        count_of_rows, -1, group_heads, head_size
    )
    scores = (
        jnp.einsum(
            "rkgd,rlkd->rkgl", query_head_block, key_entries, preferred_element_type=jnp.float32
        )
        * scaling
    )
    scores = jnp.where(allowed[:, None, None, :], scores, masked_score)
    return (scores, value_entries)


def finish_attention(score_list, value_list, query_head_block, incoming_rows, scaling):
    count_of_rows = incoming_rows.shape[0]
    key_row_width = incoming_rows.shape[-1] // 2
    group_heads = query_head_block.shape[1]
    head_size = query_head_block.shape[3]
    incoming_keys = incoming_rows[:, :key_row_width].reshape(count_of_rows, group_heads, head_size)
    incoming_values = incoming_rows[:, key_row_width:].reshape(
        count_of_rows, group_heads, head_size
    )
    fresh_score = (
        jnp.einsum(
            "rkgd,rkd->rkg", query_head_block, incoming_keys, preferred_element_type=jnp.float32
        )
        * scaling
    )
    largest = fresh_score
    for scores in score_list:
        largest = jnp.maximum(largest, jnp.max(scores, axis=-1))
    fresh_weight = jnp.exp(fresh_score - largest)
    denominator = fresh_weight
    fresh_low = lax.optimization_barrier(fresh_weight.astype(jnp.bfloat16)).astype(jnp.float32)
    summed = fresh_low[..., None] * incoming_values.astype(jnp.float32)[:, :, None, :]
    for scores, value_entries in zip(score_list, value_list):
        weights = jnp.exp(scores - largest[..., None])
        denominator = denominator + jnp.sum(weights, axis=-1)
        summed = summed + jnp.einsum(
            "rkgl,rlkd->rkgd",
            weights.astype(jnp.bfloat16),
            value_entries,
            preferred_element_type=jnp.float32,
        )
    return (summed / denominator[..., None]).reshape(count_of_rows, -1).astype(jnp.bfloat16)


def expert_block(tokens, gate_up, down_proj):
    hidden_dim = down_proj.shape[0]
    product = jnp.dot(tokens, gate_up, preferred_element_type=jnp.float32)
    hidden = (jax.nn.silu(product[:, :hidden_dim]) * product[:, hidden_dim:]).astype(jnp.bfloat16)
    return jnp.dot(hidden, down_proj, preferred_element_type=jnp.float32).astype(jnp.bfloat16)


def local(
    queries,
    new_kv,
    kv_pages,
    page_table,
    lengths,
    shed_slots,
    residual,
    norm_gain,
    expert_ids,
    gate_weights,
    w_gate_up,
    w_down,
):
    count_of_rows, model_dim = queries.shape
    pages_own, page_len, kv_width = kv_pages.shape
    table_width = page_table.shape[1]
    query_head_block = queries.reshape(
        count_of_rows, KEY_VALUE_HEADS, QUERY_GROUP_SIZE, HEAD_DIMENSION
    )
    scaling = 1.0 / math.sqrt(HEAD_DIMENSION)
    positions = jnp.arange(table_width * page_len, dtype=jnp.int32)
    allowed = positions[None, :] < lengths[:, None]
    requested = from_behind(shed_slots, "pool", 1)
    fetched = from_behind(jnp.take(kv_pages, requested, axis=0), "pool", 1)
    combined = jnp.concatenate([kv_pages, fetched], axis=0)
    scores, value_entries = cache_scores(combined, page_table, allowed, query_head_block, scaling)
    attended = finish_attention([scores], [value_entries], query_head_block, new_kv, scaling)
    merged = (residual.astype(jnp.float32) + attended.astype(jnp.float32)).astype(jnp.bfloat16)
    merged_wide = merged.astype(jnp.float32)
    normed = (
        merged_wide
        * lax.rsqrt(jnp.mean(merged_wide * merged_wide, axis=-1, keepdims=True) + epsilon)
        * norm_gain
    ).astype(jnp.bfloat16)
    top_count = expert_ids.shape[1]
    expert_count = lax.axis_size("pool") * lax.axis_size("dev")
    capacity = 2 * count_of_rows * top_count // expert_count
    flat_ids = expert_ids.reshape(-1)
    one_hot = (flat_ids[:, None] == jnp.arange(expert_count, dtype=jnp.int32)[None, :]).astype(
        jnp.int32
    )
    earlier = jnp.cumsum(one_hot, axis=0) - one_hot
    slot_rank = jnp.sum(earlier * one_hot, axis=1)
    target = flat_ids * capacity + slot_rank
    repeated = jnp.broadcast_to(normed[:, None, :], (count_of_rows, top_count, model_dim)).reshape(
        -1, model_dim
    )
    outgoing = (
        jnp.zeros((expert_count * capacity, model_dim), jnp.bfloat16).at[target].set(repeated)
    )
    gate_up = w_gate_up[0]
    down_proj = w_down[0]
    arrived = lax.all_to_all(
        outgoing.reshape(expert_count, capacity, model_dim),
        ("pool", "dev"),
        split_axis=0,
        concat_axis=0,
        tiled=True,
    )
    slot_count = arrived.shape[1]
    finished = expert_block(arrived.reshape(-1, model_dim), gate_up, down_proj).reshape(
        expert_count, slot_count, model_dim
    )
    returned = lax.all_to_all(finished, ("pool", "dev"), split_axis=0, concat_axis=0, tiled=True)
    results = returned.reshape(-1, model_dim)[target].reshape(count_of_rows, top_count, model_dim)
    expert_sum = jnp.sum(results.astype(jnp.float32) * gate_weights[:, :, None], axis=1)
    layer_out = (merged_wide + expert_sum).astype(jnp.bfloat16)
    return (attended, layer_out)


def solution(mesh):
    return jax.shard_map(
        local,
        mesh=mesh,
        in_specs=(
            P(("pool", "dev"), None),
            P(("pool", "dev"), None),
            P(("pool", "dev"), None, None),
            P(("pool", "dev"), None),
            P(("pool", "dev")),
            P(("pool", "dev")),
            P(("pool", "dev"), None),
            P(),
            P(("pool", "dev"), None),
            P(("pool", "dev"), None),
            P(("pool", "dev"), None, None),
            P(("pool", "dev"), None, None),
        ),
        out_specs=(P(("pool", "dev"), None), P(("pool", "dev"), None)),
        check_vma=False,
    )
```

profile of v0, /device:TPU:0, one launch (start us, length us, event | category | flops | bytes accessed | tf_op | source)
XLA Modules:
  0.0 158.9 jit_solution(13635045019194081697)
XLA Ops:
  0.6 3.0 %collective-permute-start = (s32[16]{0:T(128)}, s32[16]{0:T(128)S(1)}, u32[]{:S(2)}, u32[]{:S(2)}) collective-permute-start(s32[16]{0:T(128)} %param.17), channel_id=1, source_target_pairs={{0,16},{16,0},{1,17},{17,1},{2,18},{18,2},{3,19},{19,3},{4,20},{20... | collective-permute-start | bytes 200 | tf_op jit(solution)/shard_map/ppermute | solution.py:19
  3.6 0.7 compare_select_fusion
  4.3 0.7 compare_and_fusion
  5.0 0.8 copy.27
  5.8 0.7 broadcast_multiply_fusion
  6.5 0.7 iota_compare_fusion.1
  7.2 0.7 slice_convert_fusion
  8.1 0.2 reduce_window_sum.11
  8.8 2.2 %gather_fusion = bf16[16,16,512]{2,1,0:T(8,128)(2,1)S(1)} fusion(bf16[128,16,512]{2,1,0:T(8,128)(2,1)} %param.14, s32[1024]{0:T(1024)S(1)} %pad_clamp_fusion.2), kind=kCustom, calls=%fused_computation | custom fusion | bytes 524352 | tf_op jit(solution)/shard_map/jit(_take)/gather | solution.py:111
  11.3 0.9 copy.33
  12.3 0.2 fusion.38
  12.5 6.4 %collective-permute-done.1 = bf16[16,16,512]{2,1,0:T(8,128)(2,1)S(1)} collective-permute-done((bf16[16,16,512]{2,1,0:T(8,128)(2,1)S(1)}, bf16[16,16,512]{2,1,0:T(8,128)(2,1)S(1)}, u32[]{:S(2)}, u32[]{:S(2)}) %collective-permute-start.1) | collective-permute-done | bytes 262176 | tf_op jit(solution)/shard_map/ppermute | solution.py:19
  18.9 1.8 %pad_maximum_fusion = bf16[144,16,512]{2,1,0:T(8,128)(2,1)S(1)} fusion(bf16[16,16,512]{2,1,0:T(8,128)(2,1)S(1)} %collective-permute-done.1, bf16[128,16,512]{2,1,0:T(8,128)(2,1)} %param.14), kind=kLoop, calls=%fused_computation.11 | loop fusion | flops 1179648 | bytes 4718592 | tf_op jit(solution)/shard_map/concatenate | solution.py:112
  20.7 2.7 %gather_fusion.1 = bf16[256,16,512]{2,1,0:T(8,128)(2,1)} fusion(bf16[144,16,512]{2,1,0:T(8,128)(2,1)S(1)} %pad_maximum_fusion, s32[1024]{0:T(1024)S(1)} %pad_clamp_fusion.1), kind=kCustom, calls=%fused_computation.1 | custom fusion | bytes 8389632 | tf_op jit(solution)/shard_map/jit(_take)/gather | solution.py:24
  23.4 2.6 %bitcast_select_fusion = bf16[16,256,512]{2,1,0:T(8,128)(2,1)S(1)} fusion(pred[16,256]{1,0:T(8,128)(4,1)S(1)} %broadcast_in_dim.64, bf16[16,256,512]{2,1,0:T(8,128)(2,1)} %bitcast.52), kind=kLoop, calls=%fused_computation.10 | loop fusion | flops 2097152 | bytes 8392704 | tf_op jit(solution)/shard_map/jit(_take)/select_n | solution.py:24
  26.0 2.5 %fusion.36 = (bf16[16,256,256]{2,1,0:T(8,128)(2,1)}, bf16[16,256,256]{2,1,0:T(8,128)(2,1)}) fusion(bf16[16,256,512]{2,1,0:T(8,128)(2,1)S(1)} %bitcast_select_fusion), kind=kLoop, calls=%fused_computation.64 | loop fusion | bytes 8388608 | tf_op jit(solution)/shard_map/slice | solution.py:30
  28.4 2.8 %copy.22 = bf16[16,256,256]{1,2,0:T(8,128)(2,1)S(1)} copy(bf16[16,256,256]{2,1,0:T(8,128)(2,1)} %get-tuple-element.4) | data formatting | bytes 4194304 | tf_op jit(solution)/shard_map/slice | solution.py:30
  31.3 0.5 fusion.37
  31.8 0.3 fusion.21
  32.2 2.9 %copy.24 = bf16[16,256,256]{1,2,0:T(8,128)(2,1)S(1)} copy(bf16[16,256,256]{2,1,0:T(8,128)(2,1)} %get-tuple-element.5) | data formatting | bytes 4194304 | tf_op jit(solution)/shard_map/slice | solution.py:33
  35.0 0.7 fusion.15
  35.7 0.2 copy-done
  35.9 0.2 fusion.25
  36.2 2.7 %scatter_custom_fusion = bf16[256,4096]{1,0:T(8,128)(2,1)S(1)} fusion(s32[128]{0:T(128)S(1)} %fusion.32, bf16[]{:T(256)} %constant.53.clone.1, bf16[16,4096]{1,0:T(8,128)(2,1)S(1)} %fusion.27), kind=kCustom, calls=%fused_computation.21 | custom fusion | bytes 2228226 | tf_op jit(solution)/shard_map/scatter | solution.py:136
  39.0 54.4 %all_to_all.10 = bf16[32,8,4096]{2,1,0:T(8,128)(2,1)S(1)} all-to-all(bf16[32,8,4096]{2,1,0:T(8,128)(2,1)S(1)} %bitcast.54), channel_id=1, replica_groups=mesh['pool'=2,'dev'=16] {'pool','dev'}, dimensions={0} | all-to-all | bytes 4194304 | tf_op jit(solution)/shard_map/all_to_all | solution.py:140
  93.4 6.6 %fusion = f32[256,1536]{1,0:T(8,128)S(1)} fusion(bf16[1,4096,1536]{2,1,0:T(8,128)(2,1)} %param.22, bf16[32,8,4096]{2,1,0:T(8,128)(2,1)S(1)} %all_to_all.10), kind=kOutput, calls=%fused_computation.4 | convolution fusion | flops 3221225472 | bytes 16252928 | tf_op jit(solution)/shard_map/dot_general | solution.py:82
  100.0 3.2 %fusion.7 = bf16[32,8,4096]{2,1,0:T(8,128)(2,1)} fusion(bf16[1,768,4096]{2,1,0:T(8,128)(2,1)S(1)} %bitcast.63, f32[256,1536]{1,0:T(8,128)S(1)} %fusion), kind=kOutput, calls=%fused_computation.9 | convolution fusion | flops 1612840960 | bytes 9961472 | tf_op jit(solution)/shard_map/dot_general | solution.py:84
  103.2 2.9 %all-to-all-start.1 = ((bf16[32,8,4096]{2,1,0:T(8,128)(2,1)}), bf16[32,8,4096]{2,1,0:T(8,128)(2,1)S(1)}, u32[]{:S(2)}, u32[]{:S(2)}) async-start(bf16[32,8,4096]{2,1,0:T(8,128)(2,1)} %fusion.7), calls=%async_computation.1 | async-start | bytes 4194304 | tf_op jit(solution)/shard_map/all_to_all | solution.py:151
  106.2 50.1 %all-to-all-done.1 = bf16[32,8,4096]{2,1,0:T(8,128)(2,1)S(1)} async-done(((bf16[32,8,4096]{2,1,0:T(8,128)(2,1)}), bf16[32,8,4096]{2,1,0:T(8,128)(2,1)S(1)}, u32[]{:S(2)}, u32[]{:S(2)}) %all-to-all-start.1) | async-done | bytes 2097184 | tf_op jit(solution)/shard_map/all_to_all | solution.py:151
  156.2 1.2 gather_fusion.2
  157.4 0.8 fusion.10
  158.2 0.7 fusion.28
  (37 shorter events, 1.3 us)
Async XLA Ops:
  0.6 8.1 %collective-permute-start = (s32[16]{0:T(128)}, s32[16]{0:T(128)S(1)}, u32[]{:S(2)}, u32[]{:S(2)}) collective-permute-start(s32[16]{0:T(128)} %param.17), channel_id=1, source_target_pairs={{0,16},{16,0},{1,17},{17,1},{2,18},{18,2},{3,19},{19,3},{4,20},{20... | collective-permute-start | bytes 200 | tf_op jit(solution)/shard_map/ppermute | solution.py:19
  11.0 7.8 %collective-permute-start.1 = (bf16[16,16,512]{2,1,0:T(8,128)(2,1)S(1)}, bf16[16,16,512]{2,1,0:T(8,128)(2,1)S(1)}, u32[]{:S(2)}, u32[]{:S(2)}) collective-permute-start(bf16[16,16,512]{2,1,0:T(8,128)(2,1)S(1)} %broadcast_select_fusion), channel_id=1, source_target_pairs={{0,16},{16,0},{1,17},{17,1},{2,18},{18,2},{3,19},{19,3},{4,20},{20... | collective-permute-start | bytes 786440 | tf_op jit(solution)/shard_map/ppermute | solution.py:19
  35.0 0.9 copy-start
  35.0 1.1 copy-start.2
  36.1 122.1 %copy-start.1 = (bf16[16,4096]{1,0:T(8,128)(2,1)}, bf16[16,4096]{1,0:T(8,128)(2,1)S(1)}, u32[]{:S(2)}) copy-start(bf16[16,4096]{1,0:T(8,128)(2,1)S(1)} %get-tuple-element.3) | copy-start | bytes 393220
  39.0 61.0 %slice-start = ((s8[6291456]{0:T(1024)(128)(4,1)}), s8[4194304]{0:T(1024)(128)(4,1)S(1)}, s32[]{:S(2)}) async-start(s8[6291456]{0:T(1024)(128)(4,1)} %bitcast.62), calls=%async_computation.2 | async-start | bytes 8388608
  93.4 6.6 %slice-start.1 = ((s8[6291456]{0:T(1024)(128)(4,1)}), s8[2097152]{0:T(1024)(128)(4,1)S(1)}, s32[]{:S(2)}) async-start(s8[6291456]{0:T(1024)(128)(4,1)} %bitcast.62), calls=%async_computation.3 | async-start | bytes 4194304
  103.2 2.9 %copy-start.3 = (f32[16,8]{0,1:T(8,128)S(1)}, f32[16,8]{0,1:T(8,128)}, u32[]{:S(2)}) copy-start(f32[16,8]{0,1:T(8,128)} %param.21) | copy-start | bytes 1540
  103.2 53.0 %all-to-all-start.1 = ((bf16[32,8,4096]{2,1,0:T(8,128)(2,1)}), bf16[32,8,4096]{2,1,0:T(8,128)(2,1)S(1)}, u32[]{:S(2)}, u32[]{:S(2)}) async-start(bf16[32,8,4096]{2,1,0:T(8,128)(2,1)} %fusion.7), calls=%async_computation.1 | async-start | bytes 4194304 | tf_op jit(solution)/shard_map/all_to_all | solution.py:151
where the time goes:
time: 160 us; the launch traced here: 159 us
  waiting for transfers between devices  56.4 us (35%)
  blocking collectives  54.4 us (34%)
  local copies, waits for them, and re-layouts  19.5 us (12%)
  matrix products  11.2 us (7%)
  other arithmetic  10.6 us (7%)
  starting transfers between devices  5.94 us (4%)
    all_to_all x1, blocking collectives, local(): lax.all_to_all(outgoing.reshape(expert_count, capacity, model_dim), ('poo...  54.4 us
    all_to_all x1, waiting for transfers between devices, local(): lax.all_to_all(finished, ('pool', 'dev'), split_axis=0, concat_axis=0, ti...  50.1 us
    dot_general x1, matrix products, expert_block(): product = jnp.dot(tokens, gate_up, preferred_element_type=jnp.float32)  6.58 us
    ppermute x2, waiting for transfers between devices, from_behind(): lax.ppermute(value, axis, [(i, (i + by) % length) for i in range(length)])  6.38 us
    slice x2, local copies, waits for them, and re-layouts, cache_scores(): collected_rows[:, :, :key_row_width]  5.3 us
    select_n x2, other arithmetic, cache_scores(): jnp.take(source, index_table, axis=0)  3.28 us
    dot_general x1, matrix products, expert_block(): jnp.dot(hidden, down_proj, preferred_element_type=jnp.float32)  3.23 us
  transfers between devices with their start and end apart: 3, of which 2 were waited for; matrix products, arithmetic and copies ran while one was open for 4% of the time, Pallas kernels for 0%

commit v1 on v0

--- a/solution.py
+++ b/solution.py
@@ -119,39 +119,22 @@
         * lax.rsqrt(jnp.mean(merged_wide * merged_wide, axis=-1, keepdims=True) + epsilon)
         * norm_gain
     ).astype(jnp.bfloat16)
-    top_count = expert_ids.shape[1]
-    expert_count = lax.axis_size("pool") * lax.axis_size("dev")
-    capacity = 2 * count_of_rows * top_count // expert_count
-    flat_ids = expert_ids.reshape(-1)
-    one_hot = (flat_ids[:, None] == jnp.arange(expert_count, dtype=jnp.int32)[None, :]).astype(
-        jnp.int32
-    )
-    earlier = jnp.cumsum(one_hot, axis=0) - one_hot
-    slot_rank = jnp.sum(earlier * one_hot, axis=1)
-    target = flat_ids * capacity + slot_rank
-    repeated = jnp.broadcast_to(normed[:, None, :], (count_of_rows, top_count, model_dim)).reshape(
-        -1, model_dim
-    )
-    outgoing = (
-        jnp.zeros((expert_count * capacity, model_dim), jnp.bfloat16).at[target].set(repeated)
-    )
-    gate_up = w_gate_up[0]
-    down_proj = w_down[0]
-    arrived = lax.all_to_all(
-        outgoing.reshape(expert_count, capacity, model_dim),
-        ("pool", "dev"),
-        split_axis=0,
-        concat_axis=0,
+    axes = ("pool", "dev")
+    expert = lax.axis_index(axes)
+    weight_here = lax.all_gather(
+        jnp.concatenate([expert_ids.astype(jnp.float32), gate_weights], axis=1),
+        axes,
+        axis=0,
         tiled=True,
     )
-    slot_count = arrived.shape[1]
-    finished = expert_block(arrived.reshape(-1, model_dim), gate_up, down_proj).reshape(
-        expert_count, slot_count, model_dim
-    )
-    returned = lax.all_to_all(finished, ("pool", "dev"), split_axis=0, concat_axis=0, tiled=True)
-    results = returned.reshape(-1, model_dim)[target].reshape(count_of_rows, top_count, model_dim)
-    expert_sum = jnp.sum(results.astype(jnp.float32) * gate_weights[:, :, None], axis=1)
-    layer_out = (merged_wide + expert_sum).astype(jnp.bfloat16)
+    top_count = expert_ids.shape[1]
+    matches = weight_here[:, :top_count] == expert.astype(jnp.float32)
+    row_weight = jnp.sum(jnp.where(matches, weight_here[:, top_count:], 0.0), axis=1)
+    gathered = lax.all_gather(normed, axes, axis=0, tiled=True)
+    finished = expert_block(gathered, w_gate_up[0], w_down[0])
+    partial = (finished.astype(jnp.float32) * row_weight[:, None]).astype(jnp.bfloat16)
+    expert_sum = lax.psum_scatter(partial, axes, scatter_dimension=0, tiled=True)
+    layer_out = (merged_wide + expert_sum.astype(jnp.float32)).astype(jnp.bfloat16)
     return (attended, layer_out)
 
 

time: 160 us -> 271 us (1.69)
  waiting for transfers between devices: 56.4 us -> 166 us
  between operations: 0.91 us -> 14.3 us
  blocking collectives: 54.4 us -> 41.8 us
  matrix products: 11.2 us -> 19.7 us
  local copies, waits for them, and re-layouts: 19.5 us -> 14.5 us
    reduce_scatter x0 -> x1, waiting for transfers between devices: none -> 140 us  [local(): lax.psum_scatter(partial, axes, scatter_dimension=0, tiled=True)]
    all_to_all x1 -> x0, blocking collectives: 54.4 us -> none  [local(): lax.all_to_all(outgoing.reshape(expert_count, capacity, model_dim), ('poo...]
    all_to_all x1 -> x0, waiting for transfers between devices: 50.1 us -> none  [local(): lax.all_to_all(finished, ('pool', 'dev'), split_axis=0, concat_axis=0, ti...]
    all_gather x0 -> x1, blocking collectives: none -> 41.8 us  [local(): lax.all_gather(jnp.concatenate([expert_ids.astype(jnp.float32), gate_weig...]
    all_gather x0 -> x1, waiting for transfers between devices: none -> 20.5 us  [local(): gathered = lax.all_gather(normed, axes, axis=0, tiled=True)]
    dot_general x1, matrix products: 3.23 us -> 7.84 us  [expert_block(): jnp.dot(hidden, down_proj, preferred_element_type=jnp.float32)]
    dot_general x1, matrix products: 6.58 us -> 10.5 us  [expert_block(): product = jnp.dot(tokens, gate_up, preferred_element_type=jnp.float32)]
    all_to_all x1 -> x0, starting transfers between devices: 2.86 us -> none  [local(): lax.all_to_all(finished, ('pool', 'dev'), split_axis=0, concat_axis=0, ti...]
  transfers between devices with their start and end apart: 3 -> 4, of which waited for: 2 -> 3; matrix products, arithmetic and copies ran while one was open for 4% -> 2% of each run, Pallas kernels for 0% -> 0%
where the time goes in v1:
time: 271 us; the launch traced here: 270 us
  waiting for transfers between devices  166 us (61%)
  blocking collectives  41.8 us (15%)
  matrix products  19.7 us (7%)
  local copies, waits for them, and re-layouts  14.5 us (5%)
  between operations  14.3 us (5%)
  other arithmetic  10.5 us (4%)
  starting transfers between devices  3.88 us (1%)
    reduce_scatter x1, waiting for transfers between devices, local(): lax.psum_scatter(partial, axes, scatter_dimension=0, tiled=True)  140 us
    all_gather x1, blocking collectives, local(): lax.all_gather(jnp.concatenate([expert_ids.astype(jnp.float32), gate_weig...  41.8 us
    all_gather x1, waiting for transfers between devices, local(): gathered = lax.all_gather(normed, axes, axis=0, tiled=True)  20.5 us
    dot_general x1, matrix products, expert_block(): product = jnp.dot(tokens, gate_up, preferred_element_type=jnp.float32)  10.5 us
    dot_general x1, matrix products, expert_block(): jnp.dot(hidden, down_proj, preferred_element_type=jnp.float32)  7.84 us
    ppermute x2, waiting for transfers between devices, from_behind(): lax.ppermute(value, axis, [(i, (i + by) % length) for i in range(length)])  5.67 us
  transfers between devices with their start and end apart: 4, of which 3 were waited for; matrix products, arithmetic and copies ran while one was open for 2% of the time, Pallas kernels for 0%

profile of v1, /device:TPU:0, one launch (start us, length us, event | category | flops | bytes accessed | tf_op | source)
XLA Modules:
  0.0 270.3 jit_solution(4809803570001671192)
XLA Ops:
  7.2 3.0 %collective-permute-start = (s32[16]{0:T(128)}, s32[16]{0:T(128)S(1)}, u32[]{:S(2)}, u32[]{:S(2)}) collective-permute-start(s32[16]{0:T(128)} %param.17), channel_id=1, source_target_pairs={{0,16},{16,0},{1,17},{17,1},{2,18},{18,2},{3,19},{19,3},{4,20},{20... | collective-permute-start | bytes 200 | tf_op jit(solution)/shard_map/ppermute | solution.py:19
  10.2 0.7 compare_select_fusion
  10.9 0.7 compare_and_fusion
  11.6 0.7 iota_compare_fusion
  12.3 0.7 slice_convert_fusion
  13.1 0.1 reshape.84
  13.2 2.2 gather_fusion
  15.3 0.1 broadcast_select_fusion
  15.4 0.8 collective-permute-start.1
  16.2 0.1 broadcast_in_dim.55
  16.4 0.1 broadcast_in_dim.56
  16.5 0.9 copy.35
  17.4 0.2 fusion.30
  17.6 5.7 %collective-permute-done.1 = bf16[16,16,512]{2,1,0:T(8,128)(2,1)S(1)} collective-permute-done((bf16[16,16,512]{2,1,0:T(8,128)(2,1)S(1)}, bf16[16,16,512]{2,1,0:T(8,128)(2,1)S(1)}, u32[]{:S(2)}, u32[]{:S(2)}) %collective-permute-start.1) | collective-permute-done | bytes 262176 | tf_op jit(solution)/shard_map/ppermute | solution.py:19
  23.3 1.8 pad_maximum_fusion
  25.1 2.8 %gather_fusion.1 = bf16[256,16,512]{2,1,0:T(8,128)(2,1)} fusion(bf16[144,16,512]{2,1,0:T(8,128)(2,1)S(1)} %pad_maximum_fusion, s32[1024]{0:T(1024)S(1)} %pad_clamp_fusion), kind=kCustom, calls=%fused_computation.1 | custom fusion | bytes 8389632 | tf_op jit(solution)/shard_map/jit(_take)/gather | solution.py:24
  27.8 2.6 bitcast_select_fusion
  30.4 2.5 fusion.28
  32.9 2.8 %copy.26 = bf16[16,256,256]{1,2,0:T(8,128)(2,1)S(1)} copy(bf16[16,256,256]{2,1,0:T(8,128)(2,1)} %get-tuple-element.4) | data formatting | bytes 4194304 | tf_op jit(solution)/shard_map/slice | solution.py:30
  35.8 0.5 fusion.29
  36.3 0.3 fusion.16
  36.6 2.9 %copy.28 = bf16[16,256,256]{1,2,0:T(8,128)(2,1)S(1)} copy(bf16[16,256,256]{2,1,0:T(8,128)(2,1)} %get-tuple-element.5) | data formatting | bytes 4194304 | tf_op jit(solution)/shard_map/slice | solution.py:33
  39.6 0.7 fusion.13
  40.3 0.2 fusion.18
  40.5 0.7 fusion.20
  41.4 41.8 %all_gather.7 = f32[512,16]{1,0:T(8,128)S(1)} all-gather(f32[16,16]{1,0:T(8,128)S(1)} %copy.30), channel_id=1, replica_groups=mesh['pool'=2,'dev'=16] {'pool','dev'}, dimensions={0}, use_global_device_ids=true | all-gather | bytes 33792 | tf_op jit(solution)/shard_map/all_gather | solution.py:124
  83.2 0.2 fusion.23
  83.4 20.5 %all-gather.2.cloned.1.call-done = bf16[512,4096]{1,0:T(8,128)(2,1)} async-done(((bf16[16,4096]{1,0:T(8,128)(2,1)}), bf16[512,4096]{1,0:T(8,128)(2,1)}) %all-gather.2.cloned.1.call-update) | async-done | bytes 4194320 | tf_op jit(solution)/shard_map/all_gather | solution.py:133
  103.9 10.5 %fusion = f32[512,1536]{1,0:T(8,128)S(1)} fusion(bf16[512,4096]{1,0:T(8,128)(2,1)} %all-gather.2.cloned.1.call-done, bf16[1,4096,1536]{2,1,0:T(8,128)(2,1)} %param.22), kind=kOutput, calls=%fused_computation.2 | convolution fusion | flops 6442450944 | bytes 19922944 | tf_op jit(solution)/shard_map/dot_general | solution.py:82
  114.4 7.8 %multiply_convert_fusion = bf16[512,4096]{1,0:T(8,128)(2,1)} fusion(bf16[1,768,4096]{2,1,0:T(8,128)(2,1)} %param.23, f32[512]{0:T(512)S(1)} %fusion.23, f32[512,1536]{1,0:T(8,128)S(1)} %fusion), kind=kOutput, calls=%fused_computation.4 | convolution fusion | flops 3231973376 | bytes 13633536 | tf_op jit(solution)/shard_map/dot_general | solution.py:84
  122.3 139.6 %reduce-scatter.2.cloned.1.call-done = bf16[16,4096]{1,0:T(8,128)(2,1)} async-done(((bf16[512,4096]{1,0:T(8,128)(2,1)}), bf16[16,4096]{1,0:T(8,128)(2,1)}) %reduce-scatter.2.cloned.1.call-update) | async-done | bytes 131088 | tf_op jit(solution)/shard_map/reduce_scatter | solution.py:136
  261.9 1.6 fusion.21
  (28 shorter events, 0.3 us)
Async XLA Ops:
  7.2 96.7 %all-gather.2.cloned.1.call-start = ((), (), s32[]{:S(2)}) async-start(), calls=%async_computation.1 | async-start | bytes 4325376 | tf_op jit(solution)/shard_map/all_gather | solution.py:133
  7.2 5.9 %collective-permute-start = (s32[16]{0:T(128)}, s32[16]{0:T(128)S(1)}, u32[]{:S(2)}, u32[]{:S(2)}) collective-permute-start(s32[16]{0:T(128)} %param.17), channel_id=1, source_target_pairs={{0,16},{16,0},{1,17},{17,1},{2,18},{18,2},{3,19},{19,3},{4,20},{20... | collective-permute-start | bytes 200 | tf_op jit(solution)/shard_map/ppermute | solution.py:19
  15.4 7.8 %collective-permute-start.1 = (bf16[16,16,512]{2,1,0:T(8,128)(2,1)S(1)}, bf16[16,16,512]{2,1,0:T(8,128)(2,1)S(1)}, u32[]{:S(2)}, u32[]{:S(2)}) collective-permute-start(bf16[16,16,512]{2,1,0:T(8,128)(2,1)S(1)} %broadcast_select_fusion), channel_id=1, source_target_pairs={{0,16},{16,0},{1,17},{17,1},{2,18},{18,2},{3,19},{19,3},{4,20},{20... | collective-permute-start | bytes 786440 | tf_op jit(solution)/shard_map/ppermute | solution.py:19
  36.6 3.7 %copy-start = (bf16[16,4096]{1,0:T(8,128)(2,1)S(1)}, bf16[16,4096]{1,0:T(8,128)(2,1)}, u32[]{:S(2)}) copy-start(bf16[16,4096]{1,0:T(8,128)(2,1)} %param.18) | copy-start | bytes 393220
  36.6 3.9 %copy-start.2 = (f32[4096]{0:T(1024)S(1)}, f32[4096]{0:T(1024)}, u32[]{:S(2)}) copy-start(f32[4096]{0:T(1024)} %param.19) | copy-start | bytes 49156
  39.5 1.8 copy-start.3
  39.6 1.8 copy-start.4
  40.5 221.4 %copy-start.1 = (bf16[16,4096]{1,0:T(8,128)(2,1)}, bf16[16,4096]{1,0:T(8,128)(2,1)S(1)}, u32[]{:S(2)}) copy-start(bf16[16,4096]{1,0:T(8,128)(2,1)S(1)} %get-tuple-element.3) | copy-start | bytes 393220
  41.3 220.6 %reduce-scatter.2.cloned.1.call-start = ((), (), s32[]{:S(2)}) async-start(), calls=%async_computation.2 | async-start | bytes 4325376 | tf_op jit(solution)/shard_map/reduce_scatter | solution.py:136
Sparse Core Ops, SparseCore 0:
  41.4 62.4 all-gather.1
  122.4 139.4 reduce-scatter.1

commit v2 on v1

--- a/solution.py
+++ b/solution.py
@@ -12,6 +12,7 @@
 
 masked_score = -1e30
 epsilon = 1e-06
+AXES = ("pool", "dev")
 
 
 def from_behind(value, axis, by):
@@ -84,6 +85,56 @@
     return jnp.dot(hidden, down_proj, preferred_element_type=jnp.float32).astype(jnp.bfloat16)
 
 
+class Layout:
+    def __init__(self, pool, dev):
+        self.pool, self.dev = pool, dev
+        self.inner = math.gcd(dev, 4)
+        self.planes = dev // self.inner
+        self.members = pool * self.inner
+        self.groups = [
+            [self.linear(member, plane) for member in range(self.members)]
+            for plane in range(self.planes)
+        ]
+
+    def linear(self, member, plane):
+        return member // self.inner * self.dev + plane * self.inner + member % self.inner
+
+    def shifted(self, value, by):
+        if by == 0:
+            return value
+        pairs = [
+            (self.linear(m, z), self.linear(m, (z + by) % self.planes))
+            for z in range(self.planes)
+            for m in range(self.members)
+        ]
+        return lax.ppermute(value, AXES, pairs)
+
+    def swapped(self, value, mask):
+        if mask == 0:
+            return value
+        pairs = [
+            (self.linear(m, z), self.linear(m ^ mask, z))
+            for z in range(self.planes)
+            for m in range(self.members)
+        ]
+        return lax.ppermute(value, AXES, pairs)
+
+
+def slot_choice(ids, experts, capacity):
+    match = jnp.any(ids[:, :, None, :] == experts[None, None, :, None], axis=-1)
+    rank = jnp.cumsum(match.astype(jnp.int32), axis=1) - 1
+    slots = jnp.arange(capacity, dtype=jnp.int32)
+    chosen = match[..., None] & (rank[..., None] == slots)
+    return jnp.transpose(chosen, (2, 0, 3, 1)).astype(jnp.float32)
+
+
+def spread(choice):
+    members, blocks, capacity, rows = choice.shape
+    own = jnp.eye(blocks, dtype=choice.dtype)
+    full = choice[:, :, :, None, :] * own[None, :, None, :, None]
+    return full.reshape(members * blocks * capacity, blocks * rows)
+
+
 def local(
     queries,
     new_kv,
@@ -101,6 +152,14 @@
     count_of_rows, model_dim = queries.shape
     pages_own, page_len, kv_width = kv_pages.shape
     table_width = page_table.shape[1]
+    top_count = expert_ids.shape[1]
+    layout = Layout(lax.axis_size("pool"), lax.axis_size("dev"))
+    inner = layout.inner
+    capacity = 2 * count_of_rows * top_count // (layout.pool * layout.dev)
+    routing = jnp.concatenate([expert_ids.astype(jnp.float32), gate_weights], axis=1)
+    routing = jnp.stack([layout.shifted(routing, s) for s in range(layout.planes)])
+    ids = routing[:, :, :top_count].astype(jnp.int32)
+    gates = routing[:, :, top_count:]
     query_head_block = queries.reshape(
         count_of_rows, KEY_VALUE_HEADS, QUERY_GROUP_SIZE, HEAD_DIMENSION
     )
@@ -119,22 +178,47 @@
         * lax.rsqrt(jnp.mean(merged_wide * merged_wide, axis=-1, keepdims=True) + epsilon)
         * norm_gain
     ).astype(jnp.bfloat16)
-    axes = ("pool", "dev")
-    expert = lax.axis_index(axes)
-    weight_here = lax.all_gather(
-        jnp.concatenate([expert_ids.astype(jnp.float32), gate_weights], axis=1),
-        axes,
-        axis=0,
-        tiled=True,
-    )
-    top_count = expert_ids.shape[1]
-    matches = weight_here[:, :top_count] == expert.astype(jnp.float32)
-    row_weight = jnp.sum(jnp.where(matches, weight_here[:, top_count:], 0.0), axis=1)
-    gathered = lax.all_gather(normed, axes, axis=0, tiled=True)
-    finished = expert_block(gathered, w_gate_up[0], w_down[0])
-    partial = (finished.astype(jnp.float32) * row_weight[:, None]).astype(jnp.bfloat16)
-    expert_sum = lax.psum_scatter(partial, axes, scatter_dimension=0, tiled=True)
-    layer_out = (merged_wide + expert_sum.astype(jnp.float32)).astype(jnp.bfloat16)
+    place = lax.axis_index("pool") * inner + lax.axis_index("dev") % inner
+    plane = lax.axis_index("dev") // inner
+    members = jnp.arange(layout.members, dtype=jnp.int32)
+    experts_absolute = layout.linear(members, plane)
+    experts_relative = layout.linear(members ^ place, plane)
+    send = slot_choice(ids, experts_absolute, capacity)
+    back = slot_choice(ids, experts_relative, capacity)
+    gate_of = jnp.sum(
+        jnp.where(
+            ids[:, :, None, :] == experts_relative[None, None, :, None], gates[:, :, None, :], 0.0
+        ),
+        axis=-1,
+    )
+    blocks = jnp.concatenate([layout.shifted(normed, s) for s in range(layout.planes)], axis=0)
+    outgoing = jnp.dot(spread(send).astype(jnp.bfloat16), blocks, preferred_element_type=jnp.float32).astype(jnp.bfloat16)
+    arrived = lax.all_to_all(
+        outgoing, AXES, 0, 0, axis_index_groups=layout.groups, tiled=True
+    )
+    finished = expert_block(arrived, w_gate_up[0], w_down[0])
+    share = finished.shape[0] // layout.members
+    returned = [
+        layout.swapped(lax.dynamic_slice_in_dim(finished, (place ^ m) * share, share, 0), m)
+        for m in range(layout.members)
+    ]
+    mixing = spread(back * gate_of.transpose(2, 0, 1)[:, :, None, :])
+    coarse = lax.reduce_precision(mixing, 8, 7)
+    rest = mixing - coarse
+    both = jnp.concatenate([coarse, rest], axis=1).astype(jnp.bfloat16)
+    summed = lax.dot_general(
+        both,
+        jnp.concatenate(returned, axis=0),
+        (((0,), (0,)), ((), ())),
+        preferred_element_type=jnp.float32,
+    )
+    half = summed.shape[0] // 2
+    summed = (summed[:half] + summed[half:]).astype(jnp.bfloat16)
+    expert_sum = sum(
+        layout.shifted(summed[s * count_of_rows : (s + 1) * count_of_rows], -s).astype(jnp.float32)
+        for s in range(layout.planes)
+    )
+    layer_out = (merged_wide + expert_sum).astype(jnp.bfloat16)
     return (attended, layer_out)
 
 

time: 271 us -> 140 us (0.52)
  waiting for transfers between devices: 166 us -> 69.4 us
  blocking collectives: 41.8 us -> 0 us
  starting transfers between devices: 3.88 us -> 26.2 us
  between operations: 14.3 us -> 1.11 us
  matrix products: 19.7 us -> 15 us
    reduce_scatter x1 -> x0, waiting for transfers between devices: 140 us -> none  [local(): lax.psum_scatter(partial, axes, scatter_dimension=0, tiled=True)]
    all_gather x1 -> x0, blocking collectives: 41.8 us -> none  [local(): lax.all_gather(jnp.concatenate([expert_ids.astype(jnp.float32), gate_weig...]
    ppermute x0 -> x16, waiting for transfers between devices: none -> 38.3 us  [the longest x7 21.2 us: swapped(): return lax.ppermute(value, AXES, pairs)]
    all_to_all x0 -> x1, waiting for transfers between devices: none -> 25.6 us  [local(): lax.all_to_all(outgoing, AXES, 0, 0, axis_index_groups=layout.groups, til...]
    ppermute x0 -> x16, starting transfers between devices: none -> 20.5 us  [the longest x9 15.1 us: shifted(): return lax.ppermute(value, AXES, pairs)]
    all_gather x1 -> x0, waiting for transfers between devices: 20.5 us -> none  [local(): gathered = lax.all_gather(normed, axes, axis=0, tiled=True)]
    dot_general x1, matrix products: 10.5 us -> 6.41 us  [expert_block(): product = jnp.dot(tokens, gate_up, preferred_element_type=jnp.float32)]
    all_to_all x0 -> x1, starting transfers between devices: none -> 3.6 us  [local(): lax.all_to_all(outgoing, AXES, 0, 0, axis_index_groups=layout.groups, til...]
  transfers between devices with their start and end apart: 4 -> 19, of which waited for: 3 -> 11; matrix products, arithmetic and copies ran while one was open for 2% -> 7% of each run, Pallas kernels for 0% -> 0%
where the time goes in v2:
time: 140 us
  waiting for transfers between devices  69.4 us (50%)
  starting transfers between devices  26.2 us (19%)
  local copies, waits for them, and re-layouts  16.9 us (12%)
  matrix products  15 us (11%)
  other arithmetic  11 us (8%)
    all_to_all x1, waiting for transfers between devices, local(): lax.all_to_all(outgoing, AXES, 0, 0, axis_index_groups=layout.groups, til...  25.6 us
    ppermute x7, waiting for transfers between devices, swapped(): return lax.ppermute(value, AXES, pairs)  21.2 us
    ppermute x9, waiting for transfers between devices, shifted(): return lax.ppermute(value, AXES, pairs)  17.1 us
    ppermute x9, starting transfers between devices, shifted(): return lax.ppermute(value, AXES, pairs)  15.1 us
    dot_general x1, matrix products, expert_block(): product = jnp.dot(tokens, gate_up, preferred_element_type=jnp.float32)  6.41 us
    ppermute x2, waiting for transfers between devices, from_behind(): lax.ppermute(value, axis, [(i, (i + by) % length) for i in range(length)])  5.5 us
    ppermute x7, starting transfers between devices, swapped(): return lax.ppermute(value, AXES, pairs)  5.43 us
    slice x2, local copies, waits for them, and re-layouts, cache_scores(): collected_rows[:, :, :key_row_width]  4.67 us
  transfers between devices with their start and end apart: 19, of which 11 were waited for; matrix products, arithmetic and copies ran while one was open for 7% of the time, Pallas kernels for 0%

profile of v2, /device:TPU:0, one launch (start us, length us, event | category | flops | bytes accessed | tf_op | source)
XLA Modules:
  0.0 139.6 jit_solution(1433079330920618381)
XLA Ops:
  2.0 5.0 %collective-permute-start.4 = (f32[16,16]{0,1:T(8,128)S(1)}, f32[16,16]{0,1:T(8,128)S(1)}, u32[]{:S(2)}, u32[]{:S(2)}) collective-permute-start(f32[16,16]{0,1:T(8,128)S(1)} %get-tuple-element.28), channel_id=1, source_target_pairs={{0,12},{1,13},{2,14},{3,15},{16,28},{17,29},{18,30},{19,31},{4,0},... | collective-permute-start | bytes 3080 | tf_op jit(solution)/shard_map/ppermute | solution.py:110
  7.1 1.0 collective-permute-start.2
  8.1 1.5 %collective-permute-start = (s32[16]{0:T(128)}, s32[16]{0:T(128)S(1)}, u32[]{:S(2)}, u32[]{:S(2)}) collective-permute-start(s32[16]{0:T(128)} %param.17), channel_id=1, source_target_pairs={{0,16},{16,0},{1,17},{17,1},{2,18},{18,2},{3,19},{19,3},{4,20},{20... | collective-permute-start | bytes 200 | tf_op jit(solution)/shard_map/ppermute | solution.py:20
  14.0 2.2 %gather_fusion = bf16[16,16,512]{2,1,0:T(8,128)(2,1)S(1)} fusion(bf16[128,16,512]{2,1,0:T(8,128)(2,1)} %param.14, s32[1024]{0:T(1024)S(1)} %pad_clamp_fusion.1), kind=kCustom, calls=%fused_computation | custom fusion | bytes 524352 | tf_op jit(solution)/shard_map/jit(_take)/gather | solution.py:170
  17.7 5.5 %collective-permute-done.1 = bf16[16,16,512]{2,1,0:T(8,128)(2,1)S(1)} collective-permute-done((bf16[16,16,512]{2,1,0:T(8,128)(2,1)S(1)}, bf16[16,16,512]{2,1,0:T(8,128)(2,1)S(1)}, u32[]{:S(2)}, u32[]{:S(2)}) %collective-permute-start.1) | collective-permute-done | bytes 262176 | tf_op jit(solution)/shard_map/ppermute | solution.py:20
  23.2 1.8 %pad_maximum_fusion = bf16[144,16,512]{2,1,0:T(8,128)(2,1)S(1)} fusion(bf16[16,16,512]{2,1,0:T(8,128)(2,1)S(1)} %collective-permute-done.1, bf16[128,16,512]{2,1,0:T(8,128)(2,1)} %param.14), kind=kLoop, calls=%fused_computation.9 | loop fusion | flops 1179648 | bytes 4718592 | tf_op jit(solution)/shard_map/concatenate | solution.py:171
  25.0 2.8 %gather_fusion.1 = bf16[256,16,512]{2,1,0:T(8,128)(2,1)} fusion(bf16[144,16,512]{2,1,0:T(8,128)(2,1)S(1)} %pad_maximum_fusion, s32[1024]{0:T(1024)S(1)} %pad_clamp_fusion), kind=kCustom, calls=%fused_computation.1 | custom fusion | bytes 8389632 | tf_op jit(solution)/shard_map/jit(_take)/gather | solution.py:25
  27.8 2.6 %bitcast_select_fusion = bf16[16,256,512]{2,1,0:T(8,128)(2,1)S(1)} fusion(pred[16,256]{1,0:T(8,128)(4,1)S(1)} %broadcast_in_dim.54, bf16[16,256,512]{2,1,0:T(8,128)(2,1)} %bitcast.47), kind=kLoop, calls=%fused_computation.8 | loop fusion | flops 2097152 | bytes 8392704 | tf_op jit(solution)/shard_map/jit(_take)/select_n | solution.py:25
  30.4 1.8 %fusion.51 = (bf16[16,256,256]{2,1,0:T(8,128)(2,1)}, bf16[16,256,256]{2,1,0:T(8,128)(2,1)S(1)}) fusion(bf16[16,256,512]{2,1,0:T(8,128)(2,1)S(1)} %bitcast_select_fusion), kind=kLoop, calls=%fused_computation.114 | loop fusion | bytes 8388608 | tf_op jit(solution)/shard_map/slice | solution.py:31
  32.2 2.4 %copy.40 = bf16[16,256,256]{1,2,0:T(8,128)(2,1)} copy(bf16[16,256,256]{2,1,0:T(8,128)(2,1)S(1)} %get-tuple-element.7) | data formatting | bytes 4194304 | tf_op jit(solution)/shard_map/slice | solution.py:34
  34.6 2.8 %copy.38 = bf16[16,256,256]{1,2,0:T(8,128)(2,1)S(1)} copy(bf16[16,256,256]{2,1,0:T(8,128)(2,1)} %get-tuple-element.6) | data formatting | bytes 4194304 | tf_op jit(solution)/shard_map/slice | solution.py:31
  40.1 3.1 %collective-permute-start.7 = (bf16[16,4096]{1,0:T(8,128)(2,1)S(1)}, bf16[16,4096]{1,0:T(8,128)(2,1)S(1)}, u32[]{:S(2)}, u32[]{:S(2)}) collective-permute-start(bf16[16,4096]{1,0:T(8,128)(2,1)S(1)} %fusion.26), channel_id=1, source_target_pairs={{0,12},{1,13},{2,14},{3,15},{16,28},{17,29},{18,30},{19,31},{4,0},... | collective-permute-start | bytes 393224 | tf_op jit(solution)/shard_map/ppermute | solution.py:110
  44.8 2.3 %collective-permute-done.7 = bf16[16,4096]{1,0:T(8,128)(2,1)S(1)} collective-permute-done((bf16[16,4096]{1,0:T(8,128)(2,1)S(1)}, bf16[16,4096]{1,0:T(8,128)(2,1)S(1)}, u32[]{:S(2)}, u32[]{:S(2)}) %collective-permute-start.7) | collective-permute-done | bytes 131104 | tf_op jit(solution)/shard_map/ppermute | solution.py:110
  47.0 6.6 %collective-permute-done.6 = bf16[16,4096]{1,0:T(8,128)(2,1)S(1)} collective-permute-done((bf16[16,4096]{1,0:T(8,128)(2,1)S(1)}, bf16[16,4096]{1,0:T(8,128)(2,1)S(1)}, u32[]{:S(2)}, u32[]{:S(2)}) %collective-permute-start.6) | collective-permute-done | bytes 131104 | tf_op jit(solution)/shard_map/ppermute | solution.py:110
  53.6 2.0 %convolution_convert_fusion = bf16[256,4096]{1,0:T(8,128)(2,1)} fusion(bf16[256,64]{1,0:T(8,128)(2,1)S(1)} %convert_element_type.130, bf16[16,4096]{1,0:T(8,128)(2,1)S(1)} %collective-permute-done.7, bf16[16,4096]{1,0:T(8,128)(2,1)S(1)} %collective-permute-done.6, bf16[16,4096]{1,0:T(8,128)(2,1)S(1)} %collective-permute-done.5, bf16[16,4096]{1,0:T(8,128)(2,1)S(1)} %fusion.26), kind=kOutput, calls=%fused_computation.6 | convolution fusion | flops 137363456 | bytes 2654208 | tf_op jit(solution)/shard_map/dot_general | solution.py:195
  55.7 3.6 %all-to-all-start = ((bf16[8,32,4096]{2,1,0:T(8,128)(2,1)}), bf16[8,32,4096]{2,1,0:T(8,128)(2,1)S(1)}, u32[]{:S(2)}, u32[]{:S(2)}) async-start(bf16[8,32,4096]{2,1,0:T(8,128)(2,1)} %bitcast.15), calls=%async_computation | async-start | bytes 4194304 | tf_op jit(solution)/shard_map/all_to_all | solution.py:196
  59.3 25.6 %all-to-all-done = bf16[8,32,4096]{2,1,0:T(8,128)(2,1)S(1)} async-done(((bf16[8,32,4096]{2,1,0:T(8,128)(2,1)}), bf16[8,32,4096]{2,1,0:T(8,128)(2,1)S(1)}, u32[]{:S(2)}, u32[]{:S(2)}) %all-to-all-start) | async-done | bytes 2097184 | tf_op jit(solution)/shard_map/all_to_all | solution.py:196
  84.9 6.4 %fusion = f32[256,1536]{1,0:T(8,128)S(1)} fusion(bf16[256,4096]{1,0:T(8,128)(2,1)S(1)} %bitcast.49, bf16[1,4096,1536]{2,1,0:T(8,128)(2,1)} %param.22), kind=kOutput, calls=%fused_computation.2 | convolution fusion | flops 3221225472 | bytes 16252928 | tf_op jit(solution)/shard_map/dot_general | solution.py:83
  91.3 4.6 %fusion.4 = bf16[256,4096]{1,0:T(8,128)(2,1)S(1)} fusion(bf16[1,768,4096]{2,1,0:T(8,128)(2,1)} %param.23, f32[256,1536]{1,0:T(8,128)S(1)} %fusion), kind=kOutput, calls=%fused_computation.7 | convolution fusion | flops 1612840960 | bytes 9961472 | tf_op jit(solution)/shard_map/dot_general | solution.py:85
  95.9 1.1 constant_dynamic-slice_fusion
  97.3 1.5 %collective-permute-start.9 = (bf16[32,4096]{1,0:T(8,128)(2,1)}, bf16[32,4096]{1,0:T(8,128)(2,1)S(1)}, u32[]{:S(2)}, u32[]{:S(2)}) collective-permute-start(bf16[32,4096]{1,0:T(8,128)(2,1)} %get-tuple-element.13), channel_id=1, source_target_pairs={{0,2},{1,3},{2,0},{3,1},{16,18},{17,19},{18,16},{19,17},{4,6},{5,7... | collective-permute-start | bytes 786440 | tf_op jit(solution)/shard_map/ppermute | solution.py:120
  99.3 1.5 %collective-permute-start.11 = (bf16[32,4096]{1,0:T(8,128)(2,1)}, bf16[32,4096]{1,0:T(8,128)(2,1)S(1)}, u32[]{:S(2)}, u32[]{:S(2)}) collective-permute-start(bf16[32,4096]{1,0:T(8,128)(2,1)} %get-tuple-element.11), channel_id=1, source_target_pairs={{0,16},{1,17},{2,18},{3,19},{16,0},{17,1},{18,2},{19,3},{4,20},{5,... | collective-permute-start | bytes 786440 | tf_op jit(solution)/shard_map/ppermute | solution.py:120
  100.9 1.5 %collective-permute-start.13 = (bf16[32,4096]{1,0:T(8,128)(2,1)S(1)}, bf16[32,4096]{1,0:T(8,128)(2,1)S(1)}, u32[]{:S(2)}, u32[]{:S(2)}) collective-permute-start(bf16[32,4096]{1,0:T(8,128)(2,1)S(1)} %get-tuple-element.9), channel_id=1, source_target_pairs={{0,18},{1,19},{2,16},{3,17},{16,2},{17,3},{18,0},{19,1},{4,22},{5,... | collective-permute-start | bytes 786440 | tf_op jit(solution)/shard_map/ppermute | solution.py:120
  103.3 3.4 %collective-permute-done.9 = bf16[32,4096]{1,0:T(8,128)(2,1)S(1)} collective-permute-done((bf16[32,4096]{1,0:T(8,128)(2,1)}, bf16[32,4096]{1,0:T(8,128)(2,1)S(1)}, u32[]{:S(2)}, u32[]{:S(2)}) %collective-permute-start.9) | collective-permute-done | bytes 262176 | tf_op jit(solution)/shard_map/ppermute | solution.py:120
  107.2 4.4 %collective-permute-done.10 = bf16[32,4096]{1,0:T(8,128)(2,1)S(1)} collective-permute-done((bf16[32,4096]{1,0:T(8,128)(2,1)}, bf16[32,4096]{1,0:T(8,128)(2,1)S(1)}, u32[]{:S(2)}, u32[]{:S(2)}) %collective-permute-start.10) | collective-permute-done | bytes 262176 | tf_op jit(solution)/shard_map/ppermute | solution.py:120
  111.6 1.7 %collective-permute-done.12 = bf16[32,4096]{1,0:T(8,128)(2,1)S(1)} collective-permute-done((bf16[32,4096]{1,0:T(8,128)(2,1)}, bf16[32,4096]{1,0:T(8,128)(2,1)S(1)}, u32[]{:S(2)}, u32[]{:S(2)}) %collective-permute-start.12) | collective-permute-done | bytes 262176 | tf_op jit(solution)/shard_map/ppermute | solution.py:120
  113.4 7.4 %collective-permute-done.13 = bf16[32,4096]{1,0:T(8,128)(2,1)S(1)} collective-permute-done((bf16[32,4096]{1,0:T(8,128)(2,1)S(1)}, bf16[32,4096]{1,0:T(8,128)(2,1)S(1)}, u32[]{:S(2)}, u32[]{:S(2)}) %collective-permute-start.13) | collective-permute-done | bytes 262176 | tf_op jit(solution)/shard_map/ppermute | solution.py:120
  120.8 4.3 %collective-permute-done.14 = bf16[32,4096]{1,0:T(8,128)(2,1)S(1)} collective-permute-done((bf16[32,4096]{1,0:T(8,128)(2,1)S(1)}, bf16[32,4096]{1,0:T(8,128)(2,1)S(1)}, u32[]{:S(2)}, u32[]{:S(2)}) %collective-permute-start.14) | collective-permute-done | bytes 262176 | tf_op jit(solution)/shard_map/ppermute | solution.py:120
  125.9 1.8 %collective-permute-start.16 = (bf16[16,4096]{1,0:T(8,128)(2,1)S(1)}, bf16[16,4096]{1,0:T(8,128)(2,1)S(1)}, u32[]{:S(2)}, u32[]{:S(2)}) collective-permute-start(bf16[16,4096]{1,0:T(8,128)(2,1)S(1)} %get-tuple-element.18), channel_id=1, source_target_pairs={{0,8},{1,9},{2,10},{3,11},{16,24},{17,25},{18,26},{19,27},{4,12},{... | collective-permute-start | bytes 393224 | tf_op jit(solution)/shard_map/ppermute | solution.py:110
  127.7 2.8 %collective-permute-start.15 = (bf16[16,4096]{1,0:T(8,128)(2,1)S(1)}, bf16[16,4096]{1,0:T(8,128)(2,1)S(1)}, u32[]{:S(2)}, u32[]{:S(2)}) collective-permute-start(bf16[16,4096]{1,0:T(8,128)(2,1)S(1)} %get-tuple-element.16), channel_id=1, source_target_pairs={{0,12},{1,13},{2,14},{3,15},{16,28},{17,29},{18,30},{19,31},{4,0},... | collective-permute-start | bytes 393224 | tf_op jit(solution)/shard_map/ppermute | solution.py:110
  130.6 3.5 %collective-permute-done.17 = bf16[16,4096]{1,0:T(8,128)(2,1)S(1)} collective-permute-done((bf16[16,4096]{1,0:T(8,128)(2,1)S(1)}, bf16[16,4096]{1,0:T(8,128)(2,1)S(1)}, u32[]{:S(2)}, u32[]{:S(2)}) %collective-permute-start.17) | collective-permute-done | bytes 131104 | tf_op jit(solution)/shard_map/ppermute | solution.py:110
  134.1 4.7 %collective-permute-done.16 = bf16[16,4096]{1,0:T(8,128)(2,1)S(1)} collective-permute-done((bf16[16,4096]{1,0:T(8,128)(2,1)S(1)}, bf16[16,4096]{1,0:T(8,128)(2,1)S(1)}, u32[]{:S(2)}, u32[]{:S(2)}) %collective-permute-start.16) | collective-permute-done | bytes 131104 | tf_op jit(solution)/shard_map/ppermute | solution.py:110
  (88 shorter events, 15.1 us)
Async XLA Ops:
  2.0 14.8 %collective-permute-start.4 = (f32[16,16]{0,1:T(8,128)S(1)}, f32[16,16]{0,1:T(8,128)S(1)}, u32[]{:S(2)}, u32[]{:S(2)}) collective-permute-start(f32[16,16]{0,1:T(8,128)S(1)} %get-tuple-element.28), channel_id=1, source_target_pairs={{0,12},{1,13},{2,14},{3,15},{16,28},{17,29},{18,30},{19,31},{4,0},... | collective-permute-start | bytes 3080 | tf_op jit(solution)/shard_map/ppermute | solution.py:110
  7.1 9.8 %collective-permute-start.3 = (f32[16,16]{0,1:T(8,128)S(1)}, f32[16,16]{0,1:T(8,128)S(1)}, u32[]{:S(2)}, u32[]{:S(2)}) collective-permute-start(f32[16,16]{0,1:T(8,128)S(1)} %get-tuple-element.28), channel_id=1, source_target_pairs={{0,8},{1,9},{2,10},{3,11},{16,24},{17,25},{18,26},{19,27},{4,12},{... | collective-permute-start | bytes 3080 | tf_op jit(solution)/shard_map/ppermute | solution.py:110
  7.1 9.8 %collective-permute-start.2 = (f32[16,16]{0,1:T(8,128)S(1)}, f32[16,16]{0,1:T(8,128)S(1)}, u32[]{:S(2)}, u32[]{:S(2)}) collective-permute-start(f32[16,16]{0,1:T(8,128)S(1)} %get-tuple-element.28), channel_id=1, source_target_pairs={{0,4},{1,5},{2,6},{3,7},{16,20},{17,21},{18,22},{19,23},{4,8},{5,9... | collective-permute-start | bytes 3080 | tf_op jit(solution)/shard_map/ppermute | solution.py:110
  8.1 5.9 %collective-permute-start = (s32[16]{0:T(128)}, s32[16]{0:T(128)S(1)}, u32[]{:S(2)}, u32[]{:S(2)}) collective-permute-start(s32[16]{0:T(128)} %param.17), channel_id=1, source_target_pairs={{0,16},{16,0},{1,17},{17,1},{2,18},{18,2},{3,19},{19,3},{4,20},{20... | collective-permute-start | bytes 200 | tf_op jit(solution)/shard_map/ppermute | solution.py:20
  16.2 7.0 %collective-permute-start.1 = (bf16[16,16,512]{2,1,0:T(8,128)(2,1)S(1)}, bf16[16,16,512]{2,1,0:T(8,128)(2,1)S(1)}, u32[]{:S(2)}, u32[]{:S(2)}) collective-permute-start(bf16[16,16,512]{2,1,0:T(8,128)(2,1)S(1)} %broadcast_select_fusion), channel_id=1, source_target_pairs={{0,16},{16,0},{1,17},{17,1},{2,18},{18,2},{3,19},{19,3},{4,20},{20... | collective-permute-start | bytes 786440 | tf_op jit(solution)/shard_map/ppermute | solution.py:20
  37.4 1.6 %copy-start = (bf16[16,256,256]{1,2,0:T(8,128)(2,1)S(1)}, bf16[16,256,256]{1,2,0:T(8,128)(2,1)}, u32[]{:S(2)}) copy-start(bf16[16,256,256]{1,2,0:T(8,128)(2,1)} %copy.40) | copy-start | bytes 6291460
  38.0 1.8 %copy-start.1 = (bf16[16,4096]{1,0:T(8,128)(2,1)S(1)}, bf16[16,4096]{1,0:T(8,128)(2,1)}, u32[]{:S(2)}) copy-start(bf16[16,4096]{1,0:T(8,128)(2,1)} %param.18) | copy-start | bytes 393220
  38.3 1.7 %copy-start.3 = (f32[4096]{0:T(1024)S(1)}, f32[4096]{0:T(1024)}, u32[]{:S(2)}) copy-start(f32[4096]{0:T(1024)} %param.19) | copy-start | bytes 49156
  39.9 98.9 %copy-start.2 = (bf16[16,4096]{1,0:T(8,128)(2,1)}, bf16[16,4096]{1,0:T(8,128)(2,1)S(1)}, u32[]{:S(2)}) copy-start(bf16[16,4096]{1,0:T(8,128)(2,1)S(1)} %get-tuple-element.5) | copy-start | bytes 393220
  40.1 7.0 %collective-permute-start.7 = (bf16[16,4096]{1,0:T(8,128)(2,1)S(1)}, bf16[16,4096]{1,0:T(8,128)(2,1)S(1)}, u32[]{:S(2)}, u32[]{:S(2)}) collective-permute-start(bf16[16,4096]{1,0:T(8,128)(2,1)S(1)} %fusion.26), channel_id=1, source_target_pairs={{0,12},{1,13},{2,14},{3,15},{16,28},{17,29},{18,30},{19,31},{4,0},... | collective-permute-start | bytes 393224 | tf_op jit(solution)/shard_map/ppermute | solution.py:110
  43.2 10.4 %collective-permute-start.6 = (bf16[16,4096]{1,0:T(8,128)(2,1)S(1)}, bf16[16,4096]{1,0:T(8,128)(2,1)S(1)}, u32[]{:S(2)}, u32[]{:S(2)}) collective-permute-start(bf16[16,4096]{1,0:T(8,128)(2,1)S(1)} %fusion.26), channel_id=1, source_target_pairs={{0,8},{1,9},{2,10},{3,11},{16,24},{17,25},{18,26},{19,27},{4,12},{... | collective-permute-start | bytes 393224 | tf_op jit(solution)/shard_map/ppermute | solution.py:110
  44.0 9.6 %collective-permute-start.5 = (bf16[16,4096]{1,0:T(8,128)(2,1)S(1)}, bf16[16,4096]{1,0:T(8,128)(2,1)S(1)}, u32[]{:S(2)}, u32[]{:S(2)}) collective-permute-start(bf16[16,4096]{1,0:T(8,128)(2,1)S(1)} %fusion.26), channel_id=1, source_target_pairs={{0,4},{1,5},{2,6},{3,7},{16,20},{17,21},{18,22},{19,23},{4,8},{5,9... | collective-permute-start | bytes 393224 | tf_op jit(solution)/shard_map/ppermute | solution.py:110
  55.7 29.2 %all-to-all-start = ((bf16[8,32,4096]{2,1,0:T(8,128)(2,1)}), bf16[8,32,4096]{2,1,0:T(8,128)(2,1)S(1)}, u32[]{:S(2)}, u32[]{:S(2)}) async-start(bf16[8,32,4096]{2,1,0:T(8,128)(2,1)} %bitcast.15), calls=%async_computation | async-start | bytes 4194304 | tf_op jit(solution)/shard_map/all_to_all | solution.py:196
  97.1 3.9 %collective-permute-start.8 = (bf16[32,4096]{1,0:T(8,128)(2,1)}, bf16[32,4096]{1,0:T(8,128)(2,1)}, u32[]{:S(2)}, u32[]{:S(2)}) collective-permute-start(bf16[32,4096]{1,0:T(8,128)(2,1)} %get-tuple-element.14), channel_id=1, source_target_pairs={{0,1},{1,0},{2,3},{3,2},{16,17},{17,16},{18,19},{19,18},{4,5},{5,4... | collective-permute-start | bytes 786440 | tf_op jit(solution)/shard_map/ppermute | solution.py:120
  97.3 9.4 %collective-permute-start.9 = (bf16[32,4096]{1,0:T(8,128)(2,1)}, bf16[32,4096]{1,0:T(8,128)(2,1)S(1)}, u32[]{:S(2)}, u32[]{:S(2)}) collective-permute-start(bf16[32,4096]{1,0:T(8,128)(2,1)} %get-tuple-element.13), channel_id=1, source_target_pairs={{0,2},{1,3},{2,0},{3,1},{16,18},{17,19},{18,16},{19,17},{4,6},{5,7... | collective-permute-start | bytes 786440 | tf_op jit(solution)/shard_map/ppermute | solution.py:120
  98.9 12.7 %collective-permute-start.10 = (bf16[32,4096]{1,0:T(8,128)(2,1)}, bf16[32,4096]{1,0:T(8,128)(2,1)S(1)}, u32[]{:S(2)}, u32[]{:S(2)}) collective-permute-start(bf16[32,4096]{1,0:T(8,128)(2,1)} %get-tuple-element.12), channel_id=1, source_target_pairs={{0,3},{1,2},{2,1},{3,0},{16,19},{17,18},{18,17},{19,16},{4,7},{5,6... | collective-permute-start | bytes 786440 | tf_op jit(solution)/shard_map/ppermute | solution.py:120
  99.3 12.3 %collective-permute-start.11 = (bf16[32,4096]{1,0:T(8,128)(2,1)}, bf16[32,4096]{1,0:T(8,128)(2,1)S(1)}, u32[]{:S(2)}, u32[]{:S(2)}) collective-permute-start(bf16[32,4096]{1,0:T(8,128)(2,1)} %get-tuple-element.11), channel_id=1, source_target_pairs={{0,16},{1,17},{2,18},{3,19},{16,0},{17,1},{18,2},{19,3},{4,20},{5,... | collective-permute-start | bytes 786440 | tf_op jit(solution)/shard_map/ppermute | solution.py:120
  100.7 12.6 %collective-permute-start.12 = (bf16[32,4096]{1,0:T(8,128)(2,1)}, bf16[32,4096]{1,0:T(8,128)(2,1)S(1)}, u32[]{:S(2)}, u32[]{:S(2)}) collective-permute-start(bf16[32,4096]{1,0:T(8,128)(2,1)} %get-tuple-element.10), channel_id=1, source_target_pairs={{0,17},{1,16},{2,19},{3,18},{16,1},{17,0},{18,3},{19,2},{4,21},{5,... | collective-permute-start | bytes 786440 | tf_op jit(solution)/shard_map/ppermute | solution.py:120
  100.9 19.9 %collective-permute-start.13 = (bf16[32,4096]{1,0:T(8,128)(2,1)S(1)}, bf16[32,4096]{1,0:T(8,128)(2,1)S(1)}, u32[]{:S(2)}, u32[]{:S(2)}) collective-permute-start(bf16[32,4096]{1,0:T(8,128)(2,1)S(1)} %get-tuple-element.9), channel_id=1, source_target_pairs={{0,18},{1,19},{2,16},{3,17},{16,2},{17,3},{18,0},{19,1},{4,22},{5,... | collective-permute-start | bytes 786440 | tf_op jit(solution)/shard_map/ppermute | solution.py:120
  106.7 18.4 %collective-permute-start.14 = (bf16[32,4096]{1,0:T(8,128)(2,1)S(1)}, bf16[32,4096]{1,0:T(8,128)(2,1)S(1)}, u32[]{:S(2)}, u32[]{:S(2)}) collective-permute-start(bf16[32,4096]{1,0:T(8,128)(2,1)S(1)} %get-tuple-element.8), channel_id=1, source_target_pairs={{0,19},{1,18},{2,17},{3,16},{16,3},{17,2},{18,1},{19,0},{4,23},{5,... | collective-permute-start | bytes 786440 | tf_op jit(solution)/shard_map/ppermute | solution.py:120
  125.8 8.3 %collective-permute-start.17 = (bf16[16,4096]{1,0:T(8,128)(2,1)S(1)}, bf16[16,4096]{1,0:T(8,128)(2,1)S(1)}, u32[]{:S(2)}, u32[]{:S(2)}) collective-permute-start(bf16[16,4096]{1,0:T(8,128)(2,1)S(1)} %get-tuple-element.17), channel_id=1, source_target_pairs={{0,4},{1,5},{2,6},{3,7},{16,20},{17,21},{18,22},{19,23},{4,8},{5,9... | collective-permute-start | bytes 393224 | tf_op jit(solution)/shard_map/ppermute | solution.py:110
  125.9 12.9 %collective-permute-start.16 = (bf16[16,4096]{1,0:T(8,128)(2,1)S(1)}, bf16[16,4096]{1,0:T(8,128)(2,1)S(1)}, u32[]{:S(2)}, u32[]{:S(2)}) collective-permute-start(bf16[16,4096]{1,0:T(8,128)(2,1)S(1)} %get-tuple-element.18), channel_id=1, source_target_pairs={{0,8},{1,9},{2,10},{3,11},{16,24},{17,25},{18,26},{19,27},{4,12},{... | collective-permute-start | bytes 393224 | tf_op jit(solution)/shard_map/ppermute | solution.py:110
  127.7 11.1 %collective-permute-start.15 = (bf16[16,4096]{1,0:T(8,128)(2,1)S(1)}, bf16[16,4096]{1,0:T(8,128)(2,1)S(1)}, u32[]{:S(2)}, u32[]{:S(2)}) collective-permute-start(bf16[16,4096]{1,0:T(8,128)(2,1)S(1)} %get-tuple-element.16), channel_id=1, source_target_pairs={{0,12},{1,13},{2,14},{3,15},{16,28},{17,29},{18,30},{19,31},{4,0},... | collective-permute-start | bytes 393224 | tf_op jit(solution)/shard_map/ppermute | solution.py:110

commit v3 on v1

v3 whole, which is shorter than its diff:
```python
import math

import jax
import jax.numpy as jnp
from jax import lax
from jax.experimental import pallas as pl
from jax.experimental.pallas import tpu as pltpu
from jax.sharding import PartitionSpec as P

HEAD_DIMENSION = 128
KEY_VALUE_HEADS = 2
QUERY_GROUP_SIZE = 16
HEADS = KEY_VALUE_HEADS * QUERY_GROUP_SIZE

masked_score = -1e30
epsilon = 1e-06
AXES = ("pool", "dev")
VMEM = pl.BlockSpec(memory_space=pltpu.VMEM)
MEBI = 1 << 20


class Layout:
    def __init__(self, pool, dev):
        self.pool, self.dev = pool, dev
        self.inner = math.gcd(dev, 4)
        self.planes = dev // self.inner
        self.members = pool * self.inner
        self.groups = [
            [self.linear(member, plane) for member in range(self.members)]
            for plane in range(self.planes)
        ]

    def linear(self, member, plane):
        return member // self.inner * self.dev + plane * self.inner + member % self.inner

    def shifted(self, value, by):
        if by == 0:
            return value
        pairs = [
            (self.linear(m, z), self.linear(m, (z + by) % self.planes))
            for z in range(self.planes)
            for m in range(self.members)
        ]
        return lax.ppermute(value, AXES, pairs)

    def exchanged(self, value):
        return lax.all_to_all(value, AXES, 0, 0, axis_index_groups=self.groups, tiled=True)


def from_behind(value, axis, by):
    length = lax.axis_size(axis)
    return lax.ppermute(value, axis, [(i, (i + by) % length) for i in range(length)])


def pick_pages(slots, pages):
    count = slots.shape[0]
    last = pages.shape[0] - 1

    def kernel(slots_ref, pages_ref, out_ref, sems):
        copies = []
        for i in range(count):
            page = jnp.clip(slots_ref[i], 0, last)
            copies.append(pltpu.make_async_copy(pages_ref.at[page], out_ref.at[i], sems.at[i]))
            copies[-1].start()
        for copy in copies:
            copy.wait()

    return pl.pallas_call(
        kernel,
        out_shape=jax.ShapeDtypeStruct((count,) + pages.shape[1:], pages.dtype),
        in_specs=[
            pl.BlockSpec(memory_space=pltpu.SMEM),
            pl.BlockSpec(memory_space=pl.ANY),
        ],
        out_specs=pl.BlockSpec(memory_space=pl.ANY),
        scratch_shapes=[pltpu.SemaphoreType.DMA((count,))],
        cost_estimate=pl.CostEstimate(flops=0, bytes_accessed=4 * MEBI, transcendentals=0),
        name="pick_pages",
    )(slots, pages)


def head_blocks(query):
    rows = query.shape[0]
    head = lax.broadcasted_iota(jnp.int32, (rows, HEAD_DIMENSION), 0) % HEADS
    nothing = jnp.zeros_like(query)
    low = head < QUERY_GROUP_SIZE
    return jnp.concatenate([jnp.where(low, query, nothing), jnp.where(low, nothing, query)], axis=1)


def own_head(both):
    rows = both.shape[0]
    head = lax.broadcasted_iota(jnp.int32, (rows, HEAD_DIMENSION), 0) % HEADS
    return jnp.where(
        head < QUERY_GROUP_SIZE, both[:, :HEAD_DIMENSION], both[:, HEAD_DIMENSION:]
    )


def tokens_of_pages(table, lengths, first, page_len):
    count_of_rows, width = table.shape
    page = lax.broadcasted_iota(jnp.int32, (count_of_rows, 128), 1) + first
    held = jnp.zeros((count_of_rows, 128), jnp.float32)
    for p in range(width):
        filled = jnp.clip(lengths - p * page_len, 0, page_len).astype(jnp.float32)
        held = held + jnp.where(table[:, p : p + 1] == page, filled, 0.0)
    return held


def token_bias(held, first_page, tokens, page_len):
    page = lax.broadcasted_iota(jnp.int32, (128, tokens), 0)
    token = lax.broadcasted_iota(jnp.int32, (128, tokens), 1)
    widen = (page == token // page_len + first_page).astype(jnp.bfloat16)
    limit = jnp.dot(held.astype(jnp.bfloat16), widen, preferred_element_type=jnp.float32)
    inside = (token[: held.shape[0]] % page_len).astype(jnp.float32)
    return jnp.where(inside < limit, 0.0, masked_score)


def masked_scores(blocks, keys, bias, scaling):
    scores = lax.dot_general(
        blocks, keys, (((1,), (1,)), ((), ())), preferred_element_type=jnp.float32
    )
    requests, tokens = bias.shape
    return (
        (scores * scaling).reshape(requests, HEADS, tokens) + bias[:, None, :]
    ).reshape(requests * HEADS, tokens)


def narrowed(value, join):
    result = value[:, :128]
    for start in range(128, value.shape[1], 128):
        result = join(result, value[:, start : start + 128])
    return result


def own_attention(query, new_kv, pages, table, lengths):
    page_count, page_len, kv_width = pages.shape
    rows = query.shape[0]
    requests = new_kv.shape[0]
    half = kv_width // 2
    chunk_pages = 128 * (page_count // 128) // 4
    chunk = chunk_pages * page_len
    chunks = page_count // chunk_pages
    scaling = 1.0 / math.sqrt(HEAD_DIMENSION)

    def kernel(q_ref, new_ref, pages_ref, table_ref, lengths_ref, out_ref, top_ref, sum_ref, s_ref, fresh_ref):
        blocks = head_blocks(q_ref[...])
        held = tokens_of_pages(table_ref[...], lengths_ref[...], 0, page_len)
        fresh_ref[...] = jnp.zeros_like(fresh_ref)
        fresh_ref[0:requests] = new_ref[...]
        lane = lax.broadcasted_iota(jnp.int32, (requests, 128), 1)
        own = lax.broadcasted_iota(jnp.int32, (requests, 128), 0)
        fresh_bias = jnp.where(lane == own, 0.0, masked_score)
        fresh = masked_scores(blocks, fresh_ref[:, :half], fresh_bias, scaling)
        s_ref[:, chunks * chunk :] = fresh
        top = fresh
        for c in range(chunks):
            keys = pages_ref[c * chunk_pages : (c + 1) * chunk_pages, :, :half].reshape(chunk, half)
            bias = token_bias(held, c * chunk_pages, chunk, page_len)
            scores = masked_scores(blocks, keys, bias, scaling)
            s_ref[:, c * chunk : (c + 1) * chunk] = scores
            top = jnp.maximum(top, narrowed(scores, jnp.maximum))
        top = jnp.max(top, axis=1, keepdims=True)
        weights = jnp.exp(s_ref[:, chunks * chunk :] - top)
        total = weights
        summed = jnp.dot(
            weights.astype(jnp.bfloat16), fresh_ref[:, half:], preferred_element_type=jnp.float32
        )
        for c in range(chunks):
            values = pages_ref[c * chunk_pages : (c + 1) * chunk_pages, :, half:].reshape(chunk, half)
            weights = jnp.exp(s_ref[:, c * chunk : (c + 1) * chunk] - top)
            total = total + narrowed(weights, jnp.add)
            summed = summed + jnp.dot(
                weights.astype(jnp.bfloat16), values, preferred_element_type=jnp.float32
            )
        out_ref[...] = own_head(summed)
        top_ref[...] = jnp.broadcast_to(top, top_ref.shape)
        sum_ref[...] = jnp.broadcast_to(jnp.sum(total, axis=1, keepdims=True), sum_ref.shape)

    shape = jax.ShapeDtypeStruct((rows, 128), jnp.float32)
    return pl.pallas_call(
        kernel,
        out_shape=(shape, shape, shape),
        in_specs=[VMEM] * 5,
        out_specs=(VMEM,) * 3,
        scratch_shapes=[
            pltpu.VMEM((rows, chunks * chunk + 128), jnp.float32),
            pltpu.VMEM((128, kv_width), jnp.bfloat16),
        ],
        compiler_params=pltpu.CompilerParams(vmem_limit_bytes=24 * MEBI),
        cost_estimate=pl.CostEstimate(
            flops=4 * rows * half * chunks * chunk,
            bytes_accessed=16 * MEBI,
            transcendentals=rows * chunks * chunk,
        ),
        name="own_attention",
    )(query, new_kv, pages, table, lengths)


def finish_attention(query, fetched, table, lengths, partial, residual, gain, pages_own):
    count, page_len, kv_width = fetched.shape
    half = kv_width // 2
    tokens = count * page_len
    requests, model_dim = residual.shape
    rows = query.shape[0]
    scaling = 1.0 / math.sqrt(HEAD_DIMENSION)

    def kernel(q_ref, fetched_ref, table_ref, lengths_ref, sum_ref, top_ref, total_ref, residual_ref, gain_ref, attended_ref, merged_ref, normed_ref, heads_ref):
        blocks = head_blocks(q_ref[...])
        held = tokens_of_pages(table_ref[...], lengths_ref[...], pages_own, page_len)
        bias = token_bias(held, 0, tokens, page_len)
        keys = fetched_ref[:, :, :half].reshape(tokens, half)
        values = fetched_ref[:, :, half:].reshape(tokens, half)
        scores = masked_scores(blocks, keys, bias, scaling)
        before = top_ref[...]
        shed_top = jnp.max(narrowed(scores, jnp.maximum), axis=1, keepdims=True)
        top = jnp.maximum(before, shed_top)
        kept = jnp.exp(before - top)
        weights = jnp.exp(scores - jnp.concatenate([top] * (tokens // 128), axis=1))
        added = jnp.sum(narrowed(weights, jnp.add), axis=1, keepdims=True)
        total = total_ref[...] * kept + added
        summed = own_head(
            jnp.dot(weights.astype(jnp.bfloat16), values, preferred_element_type=jnp.float32)
        )
        heads_ref[...] = (sum_ref[...] * kept + summed) / total
        square = jnp.zeros((requests, 128), jnp.float32)
        for h in range(HEADS):
            columns = slice(h * 128, (h + 1) * 128)
            attended = heads_ref[pl.ds(h, requests, stride=HEADS), :].astype(jnp.bfloat16)
            attended_ref[:, columns] = attended
            merged = (
                residual_ref[:, columns].astype(jnp.float32) + attended.astype(jnp.float32)
            ).astype(jnp.bfloat16)
            merged_ref[:, columns] = merged
            wide = merged.astype(jnp.float32)
            square = square + wide * wide
        mean = jnp.sum(square, axis=1, keepdims=True) * (1.0 / model_dim)
        inverse = lax.rsqrt(mean + epsilon)
        normed_ref[...] = (
            merged_ref[...].astype(jnp.float32) * inverse * gain_ref[...]
        ).astype(jnp.bfloat16)

    shape = jax.ShapeDtypeStruct((requests, model_dim), jnp.bfloat16)
    return pl.pallas_call(
        kernel,
        out_shape=(shape, shape, shape),
        in_specs=[VMEM] * 9,
        out_specs=(VMEM,) * 3,
        scratch_shapes=[pltpu.VMEM((rows, 128), jnp.float32)],
        compiler_params=pltpu.CompilerParams(vmem_limit_bytes=16 * MEBI),
        cost_estimate=pl.CostEstimate(
            flops=4 * rows * half * tokens, bytes_accessed=4 * MEBI, transcendentals=rows * tokens
        ),
        name="finish_attention",
    )(query, fetched, table, lengths, *partial, residual, gain)


def expert_block(tokens, gate_up, down_proj):
    hidden_dim = down_proj.shape[0]
    product = jnp.dot(tokens, gate_up, preferred_element_type=jnp.float32)
    hidden = (jax.nn.silu(product[:, :hidden_dim]) * product[:, hidden_dim:]).astype(jnp.bfloat16)
    return jnp.dot(hidden, down_proj, preferred_element_type=jnp.float32).astype(jnp.bfloat16)


def slot_choice(ids, experts, capacity):
    match = jnp.any(ids[:, :, None, :] == experts[None, None, :, None], axis=-1)
    rank = jnp.cumsum(match.astype(jnp.int32), axis=1) - 1
    slots = jnp.arange(capacity, dtype=jnp.int32)
    chosen = match[..., None] & (rank[..., None] == slots)
    return jnp.transpose(chosen, (2, 0, 3, 1)).astype(jnp.float32)


def spread(choice):
    members, blocks, capacity, rows = choice.shape
    own = jnp.eye(blocks, dtype=choice.dtype)
    full = choice[:, :, :, None, :] * own[None, :, None, :, None]
    return full.reshape(members * blocks * capacity, blocks * rows)


def local(
    queries,
    new_kv,
    kv_pages,
    page_table,
    lengths,
    shed_slots,
    residual,
    norm_gain,
    expert_ids,
    gate_weights,
    w_gate_up,
    w_down,
):
    count_of_rows, model_dim = queries.shape
    top_count = expert_ids.shape[1]
    layout = Layout(lax.axis_size("pool"), lax.axis_size("dev"))
    capacity = 2 * count_of_rows * top_count // (layout.pool * layout.dev)
    planes = layout.planes

    requested = from_behind(shed_slots, "pool", 1)
    fetched = from_behind(pick_pages(requested, kv_pages), "pool", 1)

    routing = jnp.concatenate([expert_ids.astype(jnp.float32), gate_weights], axis=1)
    routing, requested = lax.optimization_barrier((routing, requested))
    routing = jnp.stack([layout.shifted(routing, s) for s in range(planes)])
    ids = routing[:, :, :top_count].astype(jnp.int32)
    gates = routing[:, :, top_count:]
    plane = lax.axis_index("dev") // layout.inner
    experts = layout.linear(jnp.arange(layout.members, dtype=jnp.int32), plane)
    choice = slot_choice(ids, experts, capacity)
    gate_of = jnp.sum(
        jnp.where(ids[:, :, None, :] == experts[None, None, :, None], gates[:, :, None, :], 0.0),
        axis=-1,
    )
    mixing = choice * gate_of.transpose(2, 0, 1)[:, :, None, :]

    query = queries.reshape(count_of_rows * HEADS, HEAD_DIMENSION)
    lengths_column = lengths.reshape(count_of_rows, 1)
    partial = own_attention(query, new_kv, kv_pages, page_table, lengths_column)
    attended, merged, normed = finish_attention(
        query,
        fetched,
        page_table,
        lengths_column,
        partial,
        residual,
        norm_gain.reshape(1, model_dim),
        kv_pages.shape[0],
    )

    first = max(1, planes // 4)
    groups = [range(0, first), range(first, 2 * first), range(2 * first, planes)]
    blocks = [layout.shifted(normed, s) for s in range(planes)]
    arrived = []
    for group in groups:
        rows = jnp.concatenate([blocks[s] for s in group], axis=0)
        pick = spread(choice[:, group.start : group.stop]).astype(jnp.bfloat16)
        outgoing = jnp.dot(pick, rows, preferred_element_type=jnp.float32).astype(jnp.bfloat16)
        arrived.append(layout.exchanged(outgoing))
    finished = expert_block(jnp.concatenate(arrived, axis=0), w_gate_up[0], w_down[0])
    pieces, start = [], 0
    for part in arrived:
        pieces.append(finished[start : start + part.shape[0]])
        start += part.shape[0]
    sums = []
    for group, piece in list(zip(groups, pieces))[::-1]:
        returned = layout.exchanged(piece)
        mix = spread(mixing[:, group.start : group.stop])
        coarse = lax.reduce_precision(mix, 8, 7)
        both = jnp.concatenate([coarse, mix - coarse], axis=1).astype(jnp.bfloat16)
        summed = lax.dot_general(
            both, returned, (((0,), (0,)), ((), ())), preferred_element_type=jnp.float32
        )
        half = summed.shape[0] // 2
        summed = (summed[:half] + summed[half:]).astype(jnp.bfloat16)
        for i, s in enumerate(group):
            sums.append(layout.shifted(summed[i * count_of_rows : (i + 1) * count_of_rows], -s))
    expert_sum = sum(part.astype(jnp.float32) for part in sums)
    layer_out = (merged.astype(jnp.float32) + expert_sum).astype(jnp.bfloat16)
    return (attended, layer_out)


def solution(mesh):
    return jax.shard_map(
        local,
        mesh=mesh,
        in_specs=(
            P(("pool", "dev"), None),
            P(("pool", "dev"), None),
            P(("pool", "dev"), None, None),
            P(("pool", "dev"), None),
            P(("pool", "dev")),
            P(("pool", "dev")),
            P(("pool", "dev"), None),
            P(),
            P(("pool", "dev"), None),
            P(("pool", "dev"), None),
            P(("pool", "dev"), None, None),
            P(("pool", "dev"), None, None),
        ),
        out_specs=(P(("pool", "dev"), None), P(("pool", "dev"), None)),
        check_vma=False,
    )
```

time: 271 us -> 139 us (0.51)
  waiting for transfers between devices: 166 us -> 48.4 us
  starting transfers between devices: 3.88 us -> 34.9 us
  blocking collectives: 41.8 us -> 17.4 us
  Pallas kernels: 0 us -> 14.4 us
  between operations: 14.3 us -> 0.94 us
  other arithmetic: 10.5 us -> 2.8 us
  matrix products: 19.7 us -> 12.1 us
  local copies, waits for them, and re-layouts: 14.5 us -> 7.25 us
    reduce_scatter x1 -> x0, waiting for transfers between devices: 140 us -> none  [local(): lax.psum_scatter(partial, axes, scatter_dimension=0, tiled=True)]
    all_gather x1 -> x0, blocking collectives: 41.8 us -> none  [local(): lax.all_gather(jnp.concatenate([expert_ids.astype(jnp.float32), gate_weig...]
    all_to_all x0 -> x5, waiting for transfers between devices: none -> 31.5 us  [exchanged(): lax.all_to_all(value, AXES, 0, 0, axis_index_groups=self.groups, tiled=True)]
    all_gather x1 -> x0, waiting for transfers between devices: 20.5 us -> none  [local(): gathered = lax.all_gather(normed, axes, axis=0, tiled=True)]
    all_to_all x0 -> x5, starting transfers between devices: none -> 18.2 us  [exchanged(): lax.all_to_all(value, AXES, 0, 0, axis_index_groups=self.groups, tiled=True)]
    all_to_all x0 -> x1, blocking collectives: none -> 17.4 us  [exchanged(): lax.all_to_all(value, AXES, 0, 0, axis_index_groups=self.groups, tiled=True)]
    pallas_call x0 -> x3, Pallas kernels: none -> 14.4 us  [the longest x1 9.85 us: pick_pages(): pl.pallas_call(kernel, out_shape=jax.ShapeDtypeStruct((count,) + pages.sh...]
    ppermute x0 -> x9, starting transfers between devices: none -> 13 us  [shifted(): return lax.ppermute(value, AXES, pairs)]
  transfers between devices with their start and end apart: 4 -> 16, of which waited for: 3 -> 8; matrix products, arithmetic and copies ran while one was open for 2% -> 6% of each run, Pallas kernels for 0% -> 9%
where the time goes in v3:
time: 139 us; the launch traced here: 138 us
  waiting for transfers between devices  48.4 us (35%)
  starting transfers between devices  34.9 us (25%)
  blocking collectives  17.4 us (13%)
  Pallas kernels  14.4 us (10%)
  matrix products  12.1 us (9%)
  local copies, waits for them, and re-layouts  7.25 us (5%)
  other arithmetic  2.8 us (2%)
    all_to_all x5, waiting for transfers between devices, exchanged(): lax.all_to_all(value, AXES, 0, 0, axis_index_groups=self.groups, tiled=True)  31.5 us
    all_to_all x5, starting transfers between devices, exchanged(): lax.all_to_all(value, AXES, 0, 0, axis_index_groups=self.groups, tiled=True)  18.2 us
    all_to_all x1, blocking collectives, exchanged(): lax.all_to_all(value, AXES, 0, 0, axis_index_groups=self.groups, tiled=True)  17.4 us
    ppermute x9, starting transfers between devices, shifted(): return lax.ppermute(value, AXES, pairs)  13 us
    ppermute x9, waiting for transfers between devices, shifted(): return lax.ppermute(value, AXES, pairs)  10.8 us
    pallas_call x1, Pallas kernels, pick_pages(): pl.pallas_call(kernel, out_shape=jax.ShapeDtypeStruct((count,) + pages.sh...  9.85 us
    dot_general x1, matrix products, expert_block(): product = jnp.dot(tokens, gate_up, preferred_element_type=jnp.float32)  6.56 us
    ppermute x2, waiting for transfers between devices, from_behind(): lax.ppermute(value, axis, [(i, (i + by) % length) for i in range(length)])  6.12 us
  transfers between devices with their start and end apart: 16, of which 8 were waited for; matrix products, arithmetic and copies ran while one was open for 6% of the time, Pallas kernels for 9%

profile of v3, /device:TPU:0, one launch (start us, length us, event | category | flops | bytes accessed | tf_op | source)
XLA Modules:
  0.0 138.1 jit_solution(16677149363944601687)
XLA Ops:
  0.7 3.0 %collective-permute-start = (s32[16]{0:T(128)}, s32[16]{0:T(128)S(1)}, u32[]{:S(2)}, u32[]{:S(2)}) collective-permute-start(s32[16]{0:T(128)} %param.17), channel_id=1, source_target_pairs={{0,16},{16,0},{1,17},{17,1},{2,18},{18,2},{3,19},{19,3},{4,20},{20... | collective-permute-start | bytes 200 | tf_op jit(solution)/shard_map/ppermute | solution.py:52
  6.8 3.6 %collective-permute-start.4 = (f32[16,16]{0,1:T(8,128)S(1)}, f32[16,16]{0,1:T(8,128)S(1)}, u32[]{:S(2)}, u32[]{:S(2)}) collective-permute-start(f32[16,16]{0,1:T(8,128)S(1)} %pad_maximum_fusion.1), channel_id=1, source_target_pairs={{0,12},{1,13},{2,14},{3,15},{16,28},{17,29},{18,30},{19,31},{4,0},... | collective-permute-start | bytes 3080 | tf_op jit(solution)/shard_map/ppermute | solution.py:44
  10.4 1.0 collective-permute-start.2
  11.4 1.6 %copy-done = bf16[128,16,512]{2,1,0:T(8,128)(2,1)S(1)} copy-done((bf16[128,16,512]{2,1,0:T(8,128)(2,1)S(1)}, bf16[128,16,512]{2,1,0:T(8,128)(2,1)}, u32[]{:S(2)}) %copy-start) | copy-done | bytes 2097176
  14.4 3.1 %own_attention.1 = (f32[512,128]{1,0:T(8,128)S(1)}, f32[512,128]{1,0:T(8,128)S(1)}, f32[512,128]{1,0:T(8,128)S(1)}) custom-call(bf16[512,128]{1,0:T(8,128)(2,1)S(1)} %reshape.82.q_ref, bf16[16,512]{1,0:T(8,128)(2,1)S(1)} %copy-done.5, bf16[128,16,512]{2,1,0:T(8,128)(2,1)S(1)} %copy-done, s32[16,16]{1,0:T(8,128)S(1)} %copy-done.3, s32[16,1]{1,0:T(8,128)S(1)} %copy.27.lengths_ref), custom_call_target="tpu_custom_call" | custom-call | flops 1073741824 | bytes 16777216 | tf_op jit(solution)/shard_map/own_attention/pallas_call | solution.py:179
  17.5 9.9 %pick_pages.1 = bf16[16,16,512]{2,1,0:T(8,128)(2,1)} custom-call(s32[16]{0:T(128)} %copy-done.6, bf16[128,16,512]{2,1,0:T(8,128)(2,1)} %pages_ref.3), custom_call_target="tpu_custom_call" | custom-call | bytes 4194304 | tf_op jit(solution)/shard_map/pick_pages/pallas_call | solution.py:68
  28.5 6.1 %collective-permute-done.1.fetched_ref = bf16[16,16,512]{2,1,0:T(8,128)(2,1)S(1)} collective-permute-done((bf16[16,16,512]{2,1,0:T(8,128)(2,1)}, bf16[16,16,512]{2,1,0:T(8,128)(2,1)S(1)}, u32[]{:S(2)}, u32[]{:S(2)}) %collective-permute-start.1) | collective-permute-done | bytes 262176 | tf_op jit(solution)/shard_map/ppermute | solution.py:52
  34.6 1.5 %finish_attention.1 = (bf16[16,4096]{1,0:T(8,128)(2,1)}, bf16[16,4096]{1,0:T(8,128)(2,1)S(1)}, bf16[16,4096]{1,0:T(8,128)(2,1)S(1)}) custom-call(bf16[512,128]{1,0:T(8,128)(2,1)S(1)} %reshape.82.q_ref, bf16[16,16,512]{2,1,0:T(8,128)(2,1)S(1)} %collective-permute-done.1.fetched_ref, s32[16,16]{1,0:T(8,128)S(1)} %copy-done.4, s32[16,1]{1,0:T(8,128)S(1)} %copy.27.lengths_ref, ...), custom_call_target="tpu_custom_call" | custom-call | flops 134217728 | bytes 4194304 | tf_op jit(solution)/shard_map/finish_attention/pallas_call | solution.py:242
  36.1 1.1 fusion.7
  37.1 3.5 %all-to-all-start = ((bf16[8,8,4096]{2,1,0:T(8,128)(2,1)}), bf16[8,8,4096]{2,1,0:T(8,128)(2,1)S(1)}, u32[]{:S(2)}, u32[]{:S(2)}) async-start(bf16[8,8,4096]{2,1,0:T(8,128)(2,1)} %fusion.7), calls=%async_computation | async-start | bytes 1048576 | tf_op jit(solution)/shard_map/all_to_all | solution.py:47
  40.8 2.5 %collective-permute-start.5 = (bf16[16,4096]{1,0:T(8,128)(2,1)S(1)}, bf16[16,4096]{1,0:T(8,128)(2,1)S(1)}, u32[]{:S(2)}, u32[]{:S(2)}) collective-permute-start(bf16[16,4096]{1,0:T(8,128)(2,1)S(1)} %get-tuple-element.15), channel_id=1, source_target_pairs={{0,4},{1,5},{2,6},{3,7},{16,20},{17,21},{18,22},{19,23},{4,8},{5,9... | collective-permute-start | bytes 393224 | tf_op jit(solution)/shard_map/ppermute | solution.py:44
  43.4 1.4 %collective-permute-start.7 = (bf16[16,4096]{1,0:T(8,128)(2,1)S(1)}, bf16[16,4096]{1,0:T(8,128)(2,1)S(1)}, u32[]{:S(2)}, u32[]{:S(2)}) collective-permute-start(bf16[16,4096]{1,0:T(8,128)(2,1)S(1)} %get-tuple-element.15), channel_id=1, source_target_pairs={{0,12},{1,13},{2,14},{3,15},{16,28},{17,29},{18,30},{19,31},{4,0},... | collective-permute-start | bytes 393224 | tf_op jit(solution)/shard_map/ppermute | solution.py:44
  45.2 3.8 %collective-permute-done.5 = bf16[16,4096]{1,0:T(8,128)(2,1)S(1)} collective-permute-done((bf16[16,4096]{1,0:T(8,128)(2,1)S(1)}, bf16[16,4096]{1,0:T(8,128)(2,1)S(1)}, u32[]{:S(2)}, u32[]{:S(2)}) %collective-permute-start.5) | collective-permute-done | bytes 131104 | tf_op jit(solution)/shard_map/ppermute | solution.py:44
  49.0 1.1 fusion.8
  50.1 4.2 %all-to-all-start.1 = ((bf16[8,8,4096]{2,1,0:T(8,128)(2,1)}), bf16[8,8,4096]{2,1,0:T(8,128)(2,1)S(1)}, u32[]{:S(2)}, u32[]{:S(2)}) async-start(bf16[8,8,4096]{2,1,0:T(8,128)(2,1)} %fusion.8), calls=%async_computation.1 | async-start | bytes 1048576 | tf_op jit(solution)/shard_map/all_to_all | solution.py:47
  54.5 2.4 %collective-permute-done.6 = bf16[16,4096]{1,0:T(8,128)(2,1)S(1)} collective-permute-done((bf16[16,4096]{1,0:T(8,128)(2,1)S(1)}, bf16[16,4096]{1,0:T(8,128)(2,1)S(1)}, u32[]{:S(2)}, u32[]{:S(2)}) %collective-permute-start.6) | collective-permute-done | bytes 131104 | tf_op jit(solution)/shard_map/ppermute | solution.py:44
  57.3 5.8 %all-to-all-done.1 = bf16[8,8,4096]{2,1,0:T(8,128)(2,1)S(1)} async-done(((bf16[8,8,4096]{2,1,0:T(8,128)(2,1)}), bf16[8,8,4096]{2,1,0:T(8,128)(2,1)S(1)}, u32[]{:S(2)}, u32[]{:S(2)}) %all-to-all-start.1) | async-done | bytes 524320 | tf_op jit(solution)/shard_map/all_to_all | solution.py:47
  63.1 17.4 %all_to_all.72 = bf16[8,16,4096]{2,1,0:T(8,128)(2,1)S(1)} all-to-all(bf16[8,16,4096]{2,1,0:T(8,128)(2,1)S(1)} %bitcast.62), channel_id=1, replica_groups={{0,1,2,3,16,17,18,19},{4,5,6,7,20,21,22,23},{8,9,10,11,24,25,26,27},{12..., dimensions={0} | all-to-all | bytes 2097152 | tf_op jit(solution)/shard_map/all_to_all | solution.py:47
  80.4 6.6 %fusion = f32[256,1536]{1,0:T(8,128)S(1)} fusion(bf16[1,4096,1536]{2,1,0:T(8,128)(2,1)} %param.22, bf16[128,4096]{1,0:T(8,128)(2,1)S(1)} %bitcast.63, bf16[64,4096]{1,0:T(8,128)(2,1)S(1)} %bitcast.65, bf16[64,4096]{1,0:T(8,128)(2,1)S(1)} %bitcast.64), kind=kOutput, calls=%fused_computation | convolution fusion | flops 3227516928 | bytes 16252928 | tf_op jit(solution)/shard_map/dot_general | solution.py:258
  87.0 1.9 %fusion.4 = bf16[256,4096]{1,0:T(8,128)(2,1)S(1)} fusion(bf16[1,768,4096]{2,1,0:T(8,128)(2,1)S(1)} %bitcast.74, f32[256,1536]{1,0:T(8,128)S(1)} %fusion), kind=kOutput, calls=%fused_computation.4 | convolution fusion | flops 1612840960 | bytes 9961472 | tf_op jit(solution)/shard_map/dot_general | solution.py:260
  88.9 1.0 slice_bitcast_fusion
  90.0 3.5 %all-to-all-start.4 = ((bf16[8,8,4096]{2,1,0:T(8,128)(2,1)}), bf16[8,8,4096]{2,1,0:T(8,128)(2,1)S(1)}, u32[]{:S(2)}, u32[]{:S(2)}) async-start(bf16[8,8,4096]{2,1,0:T(8,128)(2,1)} %get-tuple-element.17), calls=%async_computation.4 | async-start | bytes 1048576 | tf_op jit(solution)/shard_map/all_to_all | solution.py:47
  93.6 1.1 slice.94
  94.7 7.5 %all-to-all-done.4 = bf16[8,8,4096]{2,1,0:T(8,128)(2,1)S(1)} async-done(((bf16[8,8,4096]{2,1,0:T(8,128)(2,1)}), bf16[8,8,4096]{2,1,0:T(8,128)(2,1)S(1)}, u32[]{:S(2)}, u32[]{:S(2)}) %all-to-all-start.4) | async-done | bytes 524320 | tf_op jit(solution)/shard_map/all_to_all | solution.py:47
  102.2 3.6 %all-to-all-start.3 = ((bf16[8,16,4096]{2,1,0:T(8,128)(2,1)}), bf16[8,16,4096]{2,1,0:T(8,128)(2,1)S(1)}, u32[]{:S(2)}, u32[]{:S(2)}) async-start(bf16[8,16,4096]{2,1,0:T(8,128)(2,1)} %bitcast.19), calls=%async_computation.3 | async-start | bytes 2097152 | tf_op jit(solution)/shard_map/all_to_all | solution.py:47
  106.2 1.8 %collective-permute-start.10 = (bf16[16,4096]{1,0:T(8,128)(2,1)S(1)}, bf16[16,4096]{1,0:T(8,128)(2,1)S(1)}, u32[]{:S(2)}, u32[]{:S(2)}) collective-permute-start(bf16[16,4096]{1,0:T(8,128)(2,1)S(1)} %fusion.23), channel_id=1, source_target_pairs={{0,12},{1,13},{2,14},{3,15},{16,28},{17,29},{18,30},{19,31},{4,0},... | collective-permute-start | bytes 393224 | tf_op jit(solution)/shard_map/ppermute | solution.py:44
  107.9 12.2 %all-to-all-done.3 = bf16[8,16,4096]{2,1,0:T(8,128)(2,1)S(1)} async-done(((bf16[8,16,4096]{2,1,0:T(8,128)(2,1)}), bf16[8,16,4096]{2,1,0:T(8,128)(2,1)S(1)}, u32[]{:S(2)}, u32[]{:S(2)}) %all-to-all-start.3) | async-done | bytes 1048608 | tf_op jit(solution)/shard_map/all_to_all | solution.py:47
  120.2 3.5 %all-to-all-start.5 = ((bf16[8,8,4096]{2,1,0:T(8,128)(2,1)}), bf16[8,8,4096]{2,1,0:T(8,128)(2,1)S(1)}, u32[]{:S(2)}, u32[]{:S(2)}) async-start(bf16[8,8,4096]{2,1,0:T(8,128)(2,1)} %get-tuple-element.16), calls=%async_computation.5 | async-start | bytes 1048576 | tf_op jit(solution)/shard_map/all_to_all | solution.py:47
  124.2 1.1 collective-permute-start.9
  125.3 1.2 collective-permute-start.8
  126.5 5.9 %all-to-all-done.5 = bf16[8,8,4096]{2,1,0:T(8,128)(2,1)S(1)} async-done(((bf16[8,8,4096]{2,1,0:T(8,128)(2,1)}), bf16[8,8,4096]{2,1,0:T(8,128)(2,1)S(1)}, u32[]{:S(2)}, u32[]{:S(2)}) %all-to-all-start.5) | async-done | bytes 524320 | tf_op jit(solution)/shard_map/all_to_all | solution.py:47
  132.8 4.6 %collective-permute-done.8 = bf16[16,4096]{1,0:T(8,128)(2,1)S(1)} collective-permute-done((bf16[16,4096]{1,0:T(8,128)(2,1)S(1)}, bf16[16,4096]{1,0:T(8,128)(2,1)S(1)}, u32[]{:S(2)}, u32[]{:S(2)}) %collective-permute-start.8) | collective-permute-done | bytes 131104 | tf_op jit(solution)/shard_map/ppermute | solution.py:44
  (63 shorter events, 8.9 us)
Async XLA Ops:
  0.6 34.0 %copy-start.4 = (s32[16,16]{1,0:T(8,128)S(1)}, s32[16,16]{1,0:T(8,128)}, u32[]{:S(2)}) copy-start(s32[16,16]{1,0:T(8,128)} %table_ref.3) | copy-start | bytes 3076
  0.6 33.9 %copy-start.1 = (bf16[16,4096]{1,0:T(8,128)(2,1)S(1)}, bf16[16,4096]{1,0:T(8,128)(2,1)}, u32[]{:S(2)}) copy-start(bf16[16,4096]{1,0:T(8,128)(2,1)} %residual_ref.1) | copy-start | bytes 393220
  0.7 33.9 %copy-start.2 = (f32[4096]{0:T(1024)S(1)}, f32[4096]{0:T(1024)}, u32[]{:S(2)}) copy-start(f32[4096]{0:T(1024)} %param.19) | copy-start | bytes 49156
  0.7 6.1 %collective-permute-start = (s32[16]{0:T(128)}, s32[16]{0:T(128)S(1)}, u32[]{:S(2)}, u32[]{:S(2)}) collective-permute-start(s32[16]{0:T(128)} %param.17), channel_id=1, source_target_pairs={{0,16},{16,0},{1,17},{17,1},{2,18},{18,2},{3,19},{19,3},{4,20},{20... | collective-permute-start | bytes 200 | tf_op jit(solution)/shard_map/ppermute | solution.py:52
  6.8 10.7 %copy-start.6 = (s32[16]{0:T(128)}, s32[16]{0:T(128)S(1)}, u32[]{:S(2)}) copy-start(s32[16]{0:T(128)S(1)} %collective-permute-done.slots_ref) | copy-start | bytes 196
  6.8 21.3 %collective-permute-start.4 = (f32[16,16]{0,1:T(8,128)S(1)}, f32[16,16]{0,1:T(8,128)S(1)}, u32[]{:S(2)}, u32[]{:S(2)}) collective-permute-start(f32[16,16]{0,1:T(8,128)S(1)} %pad_maximum_fusion.1), channel_id=1, source_target_pairs={{0,12},{1,13},{2,14},{3,15},{16,28},{17,29},{18,30},{19,31},{4,0},... | collective-permute-start | bytes 3080 | tf_op jit(solution)/shard_map/ppermute | solution.py:44
  10.4 17.7 %collective-permute-start.3 = (f32[16,16]{0,1:T(8,128)S(1)}, f32[16,16]{0,1:T(8,128)S(1)}, u32[]{:S(2)}, u32[]{:S(2)}) collective-permute-start(f32[16,16]{0,1:T(8,128)S(1)} %pad_maximum_fusion.1), channel_id=1, source_target_pairs={{0,8},{1,9},{2,10},{3,11},{16,24},{17,25},{18,26},{19,27},{4,12},{... | collective-permute-start | bytes 3080 | tf_op jit(solution)/shard_map/ppermute | solution.py:44
  10.4 17.7 %collective-permute-start.2 = (f32[16,16]{0,1:T(8,128)S(1)}, f32[16,16]{0,1:T(8,128)S(1)}, u32[]{:S(2)}, u32[]{:S(2)}) collective-permute-start(f32[16,16]{0,1:T(8,128)S(1)} %pad_maximum_fusion.1), channel_id=1, source_target_pairs={{0,4},{1,5},{2,6},{3,7},{16,20},{17,21},{18,22},{19,23},{4,8},{5,9... | collective-permute-start | bytes 3080 | tf_op jit(solution)/shard_map/ppermute | solution.py:44
  11.4 1.6 %copy-start = (bf16[128,16,512]{2,1,0:T(8,128)(2,1)S(1)}, bf16[128,16,512]{2,1,0:T(8,128)(2,1)}, u32[]{:S(2)}) copy-start(bf16[128,16,512]{2,1,0:T(8,128)(2,1)} %pages_ref.3) | copy-start | bytes 6291460
  13.0 0.7 copy-start.3
  13.7 0.7 copy-start.5
  27.4 7.2 %collective-permute-start.1 = (bf16[16,16,512]{2,1,0:T(8,128)(2,1)}, bf16[16,16,512]{2,1,0:T(8,128)(2,1)S(1)}, u32[]{:S(2)}, u32[]{:S(2)}) collective-permute-start(bf16[16,16,512]{2,1,0:T(8,128)(2,1)} %pick_pages.1), channel_id=1, source_target_pairs={{0,16},{16,0},{1,17},{17,1},{2,18},{18,2},{3,19},{19,3},{4,20},{20... | collective-permute-start | bytes 786440 | tf_op jit(solution)/shard_map/ppermute | solution.py:52
  37.1 12.9 %all-to-all-start = ((bf16[8,8,4096]{2,1,0:T(8,128)(2,1)}), bf16[8,8,4096]{2,1,0:T(8,128)(2,1)S(1)}, u32[]{:S(2)}, u32[]{:S(2)}) async-start(bf16[8,8,4096]{2,1,0:T(8,128)(2,1)} %fusion.7), calls=%async_computation | async-start | bytes 1048576 | tf_op jit(solution)/shard_map/all_to_all | solution.py:47
  40.8 8.2 %collective-permute-start.5 = (bf16[16,4096]{1,0:T(8,128)(2,1)S(1)}, bf16[16,4096]{1,0:T(8,128)(2,1)S(1)}, u32[]{:S(2)}, u32[]{:S(2)}) collective-permute-start(bf16[16,4096]{1,0:T(8,128)(2,1)S(1)} %get-tuple-element.15), channel_id=1, source_target_pairs={{0,4},{1,5},{2,6},{3,7},{16,20},{17,21},{18,22},{19,23},{4,8},{5,9... | collective-permute-start | bytes 393224 | tf_op jit(solution)/shard_map/ppermute | solution.py:44
  43.4 11.1 %collective-permute-start.7 = (bf16[16,4096]{1,0:T(8,128)(2,1)S(1)}, bf16[16,4096]{1,0:T(8,128)(2,1)S(1)}, u32[]{:S(2)}, u32[]{:S(2)}) collective-permute-start(bf16[16,4096]{1,0:T(8,128)(2,1)S(1)} %get-tuple-element.15), channel_id=1, source_target_pairs={{0,12},{1,13},{2,14},{3,15},{16,28},{17,29},{18,30},{19,31},{4,0},... | collective-permute-start | bytes 393224 | tf_op jit(solution)/shard_map/ppermute | solution.py:44
  44.8 12.1 %collective-permute-start.6 = (bf16[16,4096]{1,0:T(8,128)(2,1)S(1)}, bf16[16,4096]{1,0:T(8,128)(2,1)S(1)}, u32[]{:S(2)}, u32[]{:S(2)}) collective-permute-start(bf16[16,4096]{1,0:T(8,128)(2,1)S(1)} %get-tuple-element.15), channel_id=1, source_target_pairs={{0,8},{1,9},{2,10},{3,11},{16,24},{17,25},{18,26},{19,27},{4,12},{... | collective-permute-start | bytes 393224 | tf_op jit(solution)/shard_map/ppermute | solution.py:44
  50.1 13.0 %all-to-all-start.1 = ((bf16[8,8,4096]{2,1,0:T(8,128)(2,1)}), bf16[8,8,4096]{2,1,0:T(8,128)(2,1)S(1)}, u32[]{:S(2)}, u32[]{:S(2)}) async-start(bf16[8,8,4096]{2,1,0:T(8,128)(2,1)} %fusion.8), calls=%async_computation.1 | async-start | bytes 1048576 | tf_op jit(solution)/shard_map/all_to_all | solution.py:47
  63.1 24.0 %slice-start = ((s8[6291456]{0:T(1024)(128)(4,1)}), s8[4194304]{0:T(1024)(128)(4,1)S(1)}, s32[]{:S(2)}) async-start(s8[6291456]{0:T(1024)(128)(4,1)} %bitcast.73), calls=%async_computation.6 | async-start | bytes 8388608
  80.4 6.6 %slice-start.1 = ((s8[6291456]{0:T(1024)(128)(4,1)}), s8[2097152]{0:T(1024)(128)(4,1)S(1)}, s32[]{:S(2)}) async-start(s8[6291456]{0:T(1024)(128)(4,1)} %bitcast.73), calls=%async_computation.7 | async-start | bytes 4194304
  90.0 12.3 %all-to-all-start.4 = ((bf16[8,8,4096]{2,1,0:T(8,128)(2,1)}), bf16[8,8,4096]{2,1,0:T(8,128)(2,1)S(1)}, u32[]{:S(2)}, u32[]{:S(2)}) async-start(bf16[8,8,4096]{2,1,0:T(8,128)(2,1)} %get-tuple-element.17), calls=%async_computation.4 | async-start | bytes 1048576 | tf_op jit(solution)/shard_map/all_to_all | solution.py:47
  102.2 17.9 %all-to-all-start.3 = ((bf16[8,16,4096]{2,1,0:T(8,128)(2,1)}), bf16[8,16,4096]{2,1,0:T(8,128)(2,1)S(1)}, u32[]{:S(2)}, u32[]{:S(2)}) async-start(bf16[8,16,4096]{2,1,0:T(8,128)(2,1)} %bitcast.19), calls=%async_computation.3 | async-start | bytes 2097152 | tf_op jit(solution)/shard_map/all_to_all | solution.py:47
  106.2 26.6 %collective-permute-start.10 = (bf16[16,4096]{1,0:T(8,128)(2,1)S(1)}, bf16[16,4096]{1,0:T(8,128)(2,1)S(1)}, u32[]{:S(2)}, u32[]{:S(2)}) collective-permute-start(bf16[16,4096]{1,0:T(8,128)(2,1)S(1)} %fusion.23), channel_id=1, source_target_pairs={{0,12},{1,13},{2,14},{3,15},{16,28},{17,29},{18,30},{19,31},{4,0},... | collective-permute-start | bytes 393224 | tf_op jit(solution)/shard_map/ppermute | solution.py:44
  120.2 12.3 %all-to-all-start.5 = ((bf16[8,8,4096]{2,1,0:T(8,128)(2,1)}), bf16[8,8,4096]{2,1,0:T(8,128)(2,1)S(1)}, u32[]{:S(2)}, u32[]{:S(2)}) async-start(bf16[8,8,4096]{2,1,0:T(8,128)(2,1)} %get-tuple-element.16), calls=%async_computation.5 | async-start | bytes 1048576 | tf_op jit(solution)/shard_map/all_to_all | solution.py:47
  124.2 8.6 %collective-permute-start.9 = (bf16[16,4096]{1,0:T(8,128)(2,1)S(1)}, bf16[16,4096]{1,0:T(8,128)(2,1)S(1)}, u32[]{:S(2)}, u32[]{:S(2)}) collective-permute-start(bf16[16,4096]{1,0:T(8,128)(2,1)S(1)} %get-tuple-element.19), channel_id=1, source_target_pairs={{0,4},{1,5},{2,6},{3,7},{16,20},{17,21},{18,22},{19,23},{4,8},{5,9... | collective-permute-start | bytes 393224 | tf_op jit(solution)/shard_map/ppermute | solution.py:44
  125.3 12.1 %collective-permute-start.8 = (bf16[16,4096]{1,0:T(8,128)(2,1)S(1)}, bf16[16,4096]{1,0:T(8,128)(2,1)S(1)}, u32[]{:S(2)}, u32[]{:S(2)}) collective-permute-start(bf16[16,4096]{1,0:T(8,128)(2,1)S(1)} %get-tuple-element.18), channel_id=1, source_target_pairs={{0,8},{1,9},{2,10},{3,11},{16,24},{17,25},{18,26},{19,27},{4,12},{... | collective-permute-start | bytes 393224 | tf_op jit(solution)/shard_map/ppermute | solution.py:44

commit v4 on v3

--- a/solution.py
+++ b/solution.py
@@ -16,6 +16,7 @@
 epsilon = 1e-06
 AXES = ("pool", "dev")
 VMEM = pl.BlockSpec(memory_space=pltpu.VMEM)
+SMEM = pl.BlockSpec(memory_space=pltpu.SMEM)
 MEBI = 1 << 20
 
 
@@ -37,14 +38,21 @@
         if by == 0:
             return value
         pairs = [
-            (self.linear(m, z), self.linear(m, (z + by) % self.planes))
+            (self.linear(m, z), self.linear(m, z ^ by))
             for z in range(self.planes)
             for m in range(self.members)
         ]
         return lax.ppermute(value, AXES, pairs)
 
-    def exchanged(self, value):
-        return lax.all_to_all(value, AXES, 0, 0, axis_index_groups=self.groups, tiled=True)
+    def swapped(self, value, by):
+        if by == 0:
+            return value
+        pairs = [
+            (self.linear(m, z), self.linear(m ^ by, z))
+            for z in range(self.planes)
+            for m in range(self.members)
+        ]
+        return lax.ppermute(value, AXES, pairs)
 
 
 def from_behind(value, axis, by):
@@ -56,25 +64,17 @@
     count = slots.shape[0]
     last = pages.shape[0] - 1
 
-    def kernel(slots_ref, pages_ref, out_ref, sems):
-        copies = []
+    def kernel(slots_ref, pages_ref, out_ref):
         for i in range(count):
-            page = jnp.clip(slots_ref[i], 0, last)
-            copies.append(pltpu.make_async_copy(pages_ref.at[page], out_ref.at[i], sems.at[i]))
-            copies[-1].start()
-        for copy in copies:
-            copy.wait()
+            out_ref[i] = pages_ref[jnp.clip(slots_ref[i], 0, last)]
 
     return pl.pallas_call(
         kernel,
         out_shape=jax.ShapeDtypeStruct((count,) + pages.shape[1:], pages.dtype),
-        in_specs=[
-            pl.BlockSpec(memory_space=pltpu.SMEM),
-            pl.BlockSpec(memory_space=pl.ANY),
-        ],
-        out_specs=pl.BlockSpec(memory_space=pl.ANY),
-        scratch_shapes=[pltpu.SemaphoreType.DMA((count,))],
-        cost_estimate=pl.CostEstimate(flops=0, bytes_accessed=4 * MEBI, transcendentals=0),
+        in_specs=[SMEM, VMEM],
+        out_specs=VMEM,
+        compiler_params=pltpu.CompilerParams(vmem_limit_bytes=8 * MEBI),
+        cost_estimate=pl.CostEstimate(flops=0, bytes_accessed=2 * MEBI, transcendentals=0),
         name="pick_pages",
     )(slots, pages)
 
@@ -95,9 +95,13 @@
     )
 
 
-def tokens_of_pages(table, lengths, first, page_len):
+def tokens_of_pages(table, lengths_ref, first, page_len):
     count_of_rows, width = table.shape
     page = lax.broadcasted_iota(jnp.int32, (count_of_rows, 128), 1) + first
+    row = lax.broadcasted_iota(jnp.int32, (count_of_rows, 128), 0)
+    lengths = jnp.zeros((count_of_rows, 128), jnp.int32)
+    for r in range(count_of_rows):
+        lengths = jnp.where(row == r, lengths_ref[r], lengths)
     held = jnp.zeros((count_of_rows, 128), jnp.float32)
     for p in range(width):
         filled = jnp.clip(lengths - p * page_len, 0, page_len).astype(jnp.float32)
@@ -143,7 +147,7 @@
 
     def kernel(q_ref, new_ref, pages_ref, table_ref, lengths_ref, out_ref, top_ref, sum_ref, s_ref, fresh_ref):
         blocks = head_blocks(q_ref[...])
-        held = tokens_of_pages(table_ref[...], lengths_ref[...], 0, page_len)
+        held = tokens_of_pages(table_ref[...], lengths_ref, 0, page_len)
         fresh_ref[...] = jnp.zeros_like(fresh_ref)
         fresh_ref[0:requests] = new_ref[...]
         lane = lax.broadcasted_iota(jnp.int32, (requests, 128), 1)
@@ -179,7 +183,7 @@
     return pl.pallas_call(
         kernel,
         out_shape=(shape, shape, shape),
-        in_specs=[VMEM] * 5,
+        in_specs=[VMEM] * 4 + [SMEM],
         out_specs=(VMEM,) * 3,
         scratch_shapes=[
             pltpu.VMEM((rows, chunks * chunk + 128), jnp.float32),
@@ -195,7 +199,206 @@
     )(query, new_kv, pages, table, lengths)
 
 
-def finish_attention(query, fetched, table, lengths, partial, residual, gain, pages_own):
+def routing_columns(ids, gates):
+    top_count = ids.shape[1]
+    high = gates.astype(jnp.bfloat16)
+    rest = gates - high.astype(jnp.float32)
+    middle = rest.astype(jnp.bfloat16)
+    low = (rest - middle.astype(jnp.float32)).astype(jnp.bfloat16)
+    source = lax.broadcasted_iota(jnp.int32, (top_count, 128), 0)
+    lane = lax.broadcasted_iota(jnp.int32, (top_count, 128), 1)
+    columns = 0.0
+    for i, part in enumerate((ids.astype(jnp.float32).astype(jnp.bfloat16), high, middle, low)):
+        place = (lane == source + i * top_count).astype(jnp.bfloat16)
+        columns = columns + jnp.dot(part, place, preferred_element_type=jnp.float32)
+    return columns.astype(jnp.bfloat16)
+
+
+def chosen_slots(routing, experts_ref, blocks, members, capacity, top_count, rows_each, gated):
+    rows = routing.shape[0]
+    row = lax.broadcasted_iota(jnp.int32, (rows, 128), 0)
+    lane = lax.broadcasted_iota(jnp.int32, (rows, 128), 1)
+    expert = jnp.full((rows, 128), -1, jnp.int32)
+    for m in range(members):
+        expert = jnp.where(lane // (blocks * capacity) == m, experts_ref[m], expert)
+    same_block = lane // capacity % blocks == row // rows_each
+    expert = jnp.where(same_block, expert, -1).astype(jnp.float32)
+    match = jnp.zeros((rows, 128), jnp.float32)
+    gate = jnp.zeros((rows, 128), jnp.float32)
+    for k in range(top_count):
+        hit = routing[:, k : k + 1] == expert
+        match = jnp.where(hit, 1.0, match)
+        if gated:
+            parts = [routing[:, i * top_count + k : i * top_count + k + 1] for i in (1, 2, 3)]
+            gate = jnp.where(hit, parts[0] + (parts[1] + parts[2]), gate)
+    earlier = (
+        lax.broadcasted_iota(jnp.int32, (rows, rows), 0)
+        > lax.broadcasted_iota(jnp.int32, (rows, rows), 1)
+    ).astype(jnp.bfloat16)
+    rank = jnp.dot(earlier, match.astype(jnp.bfloat16), preferred_element_type=jnp.float32)
+    wanted = (lane % capacity).astype(jnp.float32)
+    return jnp.where(rank == wanted, gate if gated else match, 0.0)
+
+
+def stacked(parts):
+    if len(parts) == 1:
+        return parts[0]
+    return jnp.concatenate(parts, axis=0)
+
+
+def select_rows(blocks, experts, capacity, top_count):
+    count = len(blocks)
+    members = experts.shape[0]
+    rows_each = blocks[0].shape[0]
+    model_dim = blocks[0].shape[1] - 128
+    share = count * capacity
+
+    def kernel(experts_ref, *refs):
+        block_refs, out_refs = refs[:count], refs[count:]
+        routing = stacked([ref[:, model_dim:].astype(jnp.float32) for ref in block_refs])
+        choice = chosen_slots(
+            routing, experts_ref, count, members, capacity, top_count, rows_each, False
+        )
+        pick = choice.T[: members * share].astype(jnp.bfloat16)
+        step = model_dim // 4
+        for start in range(0, model_dim, step):
+            rows = stacked([ref[:, start : start + step] for ref in block_refs])
+            picked = jnp.dot(pick, rows, preferred_element_type=jnp.float32).astype(jnp.bfloat16)
+            for m in range(members):
+                out_refs[m][:, start : start + step] = picked[m * share : (m + 1) * share]
+
+    shape = jax.ShapeDtypeStruct((share, model_dim), jnp.bfloat16)
+    return pl.pallas_call(
+        kernel,
+        out_shape=(shape,) * members,
+        in_specs=[SMEM] + [VMEM] * count,
+        out_specs=(VMEM,) * members,
+        compiler_params=pltpu.CompilerParams(vmem_limit_bytes=16 * MEBI),
+        cost_estimate=pl.CostEstimate(flops=0, bytes_accessed=3 * MEBI, transcendentals=0),
+        name="select_rows",
+    )(experts, *blocks)
+
+
+def run_experts(groups, gate_up, down_proj):
+    members = len(groups[0])
+    shares = [group[0].shape[0] for group in groups]
+    share = sum(shares)
+    rows = members * share
+    model_dim, double = gate_up.shape[1:]
+    hidden_dim = double // 2
+    width = 256
+    out_width = 1024
+
+    def kernel(*refs):
+        inputs, rest = refs[: members * len(groups)], refs[members * len(groups) :]
+        up_ref, down_ref = rest[0], rest[1]
+        outputs = rest[2 : 2 + members * len(groups)]
+        tokens_ref, hidden_ref = rest[2 + members * len(groups) :]
+        for m in range(members):
+            mine = [inputs[g * members + m][...].astype(jnp.float32) for g in range(len(groups))]
+            tokens_ref[m * share : (m + 1) * share] = stacked(mine).astype(jnp.bfloat16)
+
+        @pl.loop(0, hidden_dim // width)
+        def _(c):
+            start = pl.multiple_of(c * width, width)
+            tokens = tokens_ref[...]
+            gate = jnp.dot(
+                tokens, up_ref[0, :, pl.ds(start, width)], preferred_element_type=jnp.float32
+            )
+            up = jnp.dot(
+                tokens,
+                up_ref[0, :, pl.ds(hidden_dim + start, width)],
+                preferred_element_type=jnp.float32,
+            )
+            hidden_ref[:, pl.ds(start, width)] = (gate / (1.0 + jnp.exp(-gate)) * up).astype(
+                jnp.bfloat16
+            )
+
+        for start in range(0, model_dim, out_width):
+            columns = slice(start, start + out_width)
+            result = jnp.dot(
+                hidden_ref[...], down_ref[0, :, columns], preferred_element_type=jnp.float32
+            )
+            for m in range(members):
+                offset = m * share
+                for g in range(len(groups)):
+                    outputs[g * members + m][:, columns] = result[
+                        offset : offset + shares[g]
+                    ].astype(jnp.bfloat16)
+                    offset += shares[g]
+
+    flat = [part for group in groups for part in group]
+    results = pl.pallas_call(
+        kernel,
+        out_shape=tuple(jax.ShapeDtypeStruct(part.shape, jnp.bfloat16) for part in flat),
+        in_specs=[VMEM] * (len(flat) + 2),
+        out_specs=(VMEM,) * len(flat),
+        scratch_shapes=[
+            pltpu.VMEM((rows, model_dim), jnp.bfloat16),
+            pltpu.VMEM((rows, hidden_dim), jnp.bfloat16),
+        ],
+        compiler_params=pltpu.CompilerParams(vmem_limit_bytes=36 * MEBI),
+        cost_estimate=pl.CostEstimate(
+            flops=6 * rows * model_dim * hidden_dim,
+            bytes_accessed=20 * MEBI,
+            transcendentals=rows * hidden_dim,
+        ),
+        name="run_experts",
+    )(*flat, gate_up, down_proj)
+    return [results[g * members : (g + 1) * members] for g in range(len(groups))]
+
+
+def combine_rows(returned, blocks, experts, capacity, top_count, merged=None, others=()):
+    count = len(blocks)
+    members = experts.shape[0]
+    rows_each = blocks[0].shape[0]
+    model_dim = blocks[0].shape[1] - 128
+    share = count * capacity
+    rows = count * rows_each
+    final = merged is not None
+
+    def kernel(experts_ref, *refs):
+        block_refs, refs = refs[:count], refs[count:]
+        part_refs, refs = refs[:members], refs[members:]
+        extra_refs, out_refs = refs[: len(extra)], refs[len(extra) :]
+        routing = stacked([ref[:, model_dim:].astype(jnp.float32) for ref in block_refs])
+        mixing = chosen_slots(
+            routing, experts_ref, count, members, capacity, top_count, rows_each, True
+        )
+        coarse = mixing.astype(jnp.bfloat16)
+        fine = (mixing - coarse.astype(jnp.float32)).astype(jnp.bfloat16)
+        both = jnp.concatenate([coarse, fine], axis=0)[:, : members * share]
+        step = model_dim // 4
+        for start in range(0, model_dim, step):
+            columns = slice(start, start + step)
+            parts = jnp.concatenate(
+                [ref[:, columns].astype(jnp.float32) for ref in part_refs], axis=0
+            ).astype(jnp.bfloat16)
+            summed = jnp.dot(both, parts, preferred_element_type=jnp.float32)
+            summed = summed[:rows] + summed[rows:]
+            for ref in extra_refs:
+                summed = summed + ref[:, columns].astype(jnp.float32)
+            for i in range(count):
+                out_refs[i][:, columns] = summed[i * rows_each : (i + 1) * rows_each].astype(
+                    jnp.bfloat16
+                )
+
+    extra = [merged, *others] if final else []
+    shape = jax.ShapeDtypeStruct((rows_each, model_dim), jnp.bfloat16)
+    return pl.pallas_call(
+        kernel,
+        out_shape=(shape,) * count,
+        in_specs=[SMEM] + [VMEM] * (count + members + len(extra)),
+        out_specs=(VMEM,) * count,
+        compiler_params=pltpu.CompilerParams(vmem_limit_bytes=16 * MEBI),
+        cost_estimate=pl.CostEstimate(flops=0, bytes_accessed=3 * MEBI, transcendentals=0),
+        name="combine_rows",
+    )(experts, *blocks, *returned, *extra)
+
+
+def finish_attention(
+    query, fetched, table, lengths, partial, residual, gain, ids, gates, pages_own
+):
     count, page_len, kv_width = fetched.shape
     half = kv_width // 2
     tokens = count * page_len
@@ -203,9 +406,9 @@
     rows = query.shape[0]
     scaling = 1.0 / math.sqrt(HEAD_DIMENSION)
 
-    def kernel(q_ref, fetched_ref, table_ref, lengths_ref, sum_ref, top_ref, total_ref, residual_ref, gain_ref, attended_ref, merged_ref, normed_ref, heads_ref):
+    def kernel(q_ref, fetched_ref, table_ref, lengths_ref, sum_ref, top_ref, total_ref, residual_ref, gain_ref, ids_ref, gates_ref, attended_ref, merged_ref, normed_ref, heads_ref):
         blocks = head_blocks(q_ref[...])
-        held = tokens_of_pages(table_ref[...], lengths_ref[...], pages_own, page_len)
+        held = tokens_of_pages(table_ref[...], lengths_ref, pages_own, page_len)
         bias = token_bias(held, 0, tokens, page_len)
         keys = fetched_ref[:, :, :half].reshape(tokens, half)
         values = fetched_ref[:, :, half:].reshape(tokens, half)
@@ -234,15 +437,16 @@
             square = square + wide * wide
         mean = jnp.sum(square, axis=1, keepdims=True) * (1.0 / model_dim)
         inverse = lax.rsqrt(mean + epsilon)
-        normed_ref[...] = (
+        normed_ref[:, model_dim:] = routing_columns(ids_ref[...], gates_ref[...])
+        normed_ref[:, :model_dim] = (
             merged_ref[...].astype(jnp.float32) * inverse * gain_ref[...]
         ).astype(jnp.bfloat16)
 
     shape = jax.ShapeDtypeStruct((requests, model_dim), jnp.bfloat16)
     return pl.pallas_call(
         kernel,
-        out_shape=(shape, shape, shape),
-        in_specs=[VMEM] * 9,
+        out_shape=(shape, shape, jax.ShapeDtypeStruct((requests, model_dim + 128), jnp.bfloat16)),
+        in_specs=[VMEM] * 3 + [SMEM] + [VMEM] * 7,
         out_specs=(VMEM,) * 3,
         scratch_shapes=[pltpu.VMEM((rows, 128), jnp.float32)],
         compiler_params=pltpu.CompilerParams(vmem_limit_bytes=16 * MEBI),
@@ -250,29 +454,7 @@
             flops=4 * rows * half * tokens, bytes_accessed=4 * MEBI, transcendentals=rows * tokens
         ),
         name="finish_attention",
-    )(query, fetched, table, lengths, *partial, residual, gain)
-
-
-def expert_block(tokens, gate_up, down_proj):
-    hidden_dim = down_proj.shape[0]
-    product = jnp.dot(tokens, gate_up, preferred_element_type=jnp.float32)
-    hidden = (jax.nn.silu(product[:, :hidden_dim]) * product[:, hidden_dim:]).astype(jnp.bfloat16)
-    return jnp.dot(hidden, down_proj, preferred_element_type=jnp.float32).astype(jnp.bfloat16)
-
-
-def slot_choice(ids, experts, capacity):
-    match = jnp.any(ids[:, :, None, :] == experts[None, None, :, None], axis=-1)
-    rank = jnp.cumsum(match.astype(jnp.int32), axis=1) - 1
-    slots = jnp.arange(capacity, dtype=jnp.int32)
-    chosen = match[..., None] & (rank[..., None] == slots)
-    return jnp.transpose(chosen, (2, 0, 3, 1)).astype(jnp.float32)
-
-
-def spread(choice):
-    members, blocks, capacity, rows = choice.shape
-    own = jnp.eye(blocks, dtype=choice.dtype)
-    full = choice[:, :, :, None, :] * own[None, :, None, :, None]
-    return full.reshape(members * blocks * capacity, blocks * rows)
+    )(query, fetched, table, lengths, *partial, residual, gain, ids, gates)
 
 
 def local(
@@ -296,65 +478,54 @@
     planes = layout.planes
 
     requested = from_behind(shed_slots, "pool", 1)
-    fetched = from_behind(pick_pages(requested, kv_pages), "pool", 1)
-
-    routing = jnp.concatenate([expert_ids.astype(jnp.float32), gate_weights], axis=1)
-    routing, requested = lax.optimization_barrier((routing, requested))
-    routing = jnp.stack([layout.shifted(routing, s) for s in range(planes)])
-    ids = routing[:, :, :top_count].astype(jnp.int32)
-    gates = routing[:, :, top_count:]
-    plane = lax.axis_index("dev") // layout.inner
-    experts = layout.linear(jnp.arange(layout.members, dtype=jnp.int32), plane)
-    choice = slot_choice(ids, experts, capacity)
-    gate_of = jnp.sum(
-        jnp.where(ids[:, :, None, :] == experts[None, None, :, None], gates[:, :, None, :], 0.0),
-        axis=-1,
-    )
-    mixing = choice * gate_of.transpose(2, 0, 1)[:, :, None, :]
+    picked = pick_pages(requested, kv_pages)
+    fetched = from_behind(picked, "pool", 1)
+    queries, expert_ids, picked = lax.optimization_barrier((queries, expert_ids, picked))
+
+    inner = layout.inner
+    place = lax.axis_index("pool") * inner + lax.axis_index("dev") % inner
+    plane = lax.axis_index("dev") // inner
+    experts = layout.linear(jnp.arange(layout.members, dtype=jnp.int32) ^ place, plane)
 
     query = queries.reshape(count_of_rows * HEADS, HEAD_DIMENSION)
-    lengths_column = lengths.reshape(count_of_rows, 1)
-    partial = own_attention(query, new_kv, kv_pages, page_table, lengths_column)
+    partial = own_attention(query, new_kv, kv_pages, page_table, lengths)
     attended, merged, normed = finish_attention(
         query,
         fetched,
         page_table,
-        lengths_column,
+        lengths,
         partial,
         residual,
         norm_gain.reshape(1, model_dim),
+        expert_ids,
+        gate_weights,
         kv_pages.shape[0],
     )
 
     first = max(1, planes // 4)
     groups = [range(0, first), range(first, 2 * first), range(2 * first, planes)]
+    masks = range(layout.members)
     blocks = [layout.shifted(normed, s) for s in range(planes)]
     arrived = []
     for group in groups:
-        rows = jnp.concatenate([blocks[s] for s in group], axis=0)
-        pick = spread(choice[:, group.start : group.stop]).astype(jnp.bfloat16)
-        outgoing = jnp.dot(pick, rows, preferred_element_type=jnp.float32).astype(jnp.bfloat16)
-        arrived.append(layout.exchanged(outgoing))
-    finished = expert_block(jnp.concatenate(arrived, axis=0), w_gate_up[0], w_down[0])
-    pieces, start = [], 0
-    for part in arrived:
-        pieces.append(finished[start : start + part.shape[0]])
-        start += part.shape[0]
-    sums = []
-    for group, piece in list(zip(groups, pieces))[::-1]:
-        returned = layout.exchanged(piece)
-        mix = spread(mixing[:, group.start : group.stop])
-        coarse = lax.reduce_precision(mix, 8, 7)
-        both = jnp.concatenate([coarse, mix - coarse], axis=1).astype(jnp.bfloat16)
-        summed = lax.dot_general(
-            both, returned, (((0,), (0,)), ((), ())), preferred_element_type=jnp.float32
-        )
-        half = summed.shape[0] // 2
-        summed = (summed[:half] + summed[half:]).astype(jnp.bfloat16)
-        for i, s in enumerate(group):
-            sums.append(layout.shifted(summed[i * count_of_rows : (i + 1) * count_of_rows], -s))
-    expert_sum = sum(part.astype(jnp.float32) for part in sums)
-    layer_out = (merged.astype(jnp.float32) + expert_sum).astype(jnp.bfloat16)
+        outgoing = select_rows([blocks[s] for s in group], experts, capacity, top_count)
+        arrived.append([layout.swapped(outgoing[m], m) for m in masks])
+    near = run_experts(arrived[:2], w_gate_up, w_down)
+    far = run_experts(arrived[2:], w_gate_up, w_down)
+    others = []
+    for group, finished in ((groups[2], far[0]), (groups[1], near[1])):
+        returned = [layout.swapped(finished[m], m) for m in masks]
+        sums = combine_rows(returned, [blocks[s] for s in group], experts, capacity, top_count)
+        others += [layout.shifted(part, s) for part, s in zip(sums, group)]
+    returned = [layout.swapped(near[0][m], m) for m in masks]
+    mine = [blocks[s] for s in groups[0]]
+    if len(mine) == 1:
+        layer_out = combine_rows(returned, mine, experts, capacity, top_count, merged, others)[0]
+    else:
+        sums = combine_rows(returned, mine, experts, capacity, top_count)
+        others += [layout.shifted(part, s) for part, s in zip(sums, groups[0])]
+        total = merged.astype(jnp.float32) + sum(part.astype(jnp.float32) for part in others)
+        layer_out = total.astype(jnp.bfloat16)
     return (attended, layer_out)
 
 

time: 139 us -> 117 us (0.84)
  waiting for transfers between devices: 48.4 us -> 24.1 us
  blocking collectives: 17.4 us -> 0 us
  starting transfers between devices: 34.9 us -> 51.8 us
  Pallas kernels: 14.4 us -> 29.5 us
  matrix products: 12.1 us -> 0 us
  local copies, waits for them, and re-layouts: 7.25 us -> 10.7 us
  other arithmetic: 2.8 us -> 0.01 us
    ppermute x0 -> x42, starting transfers between devices: none -> 38.1 us  [swapped(): return lax.ppermute(value, AXES, pairs)]
    all_to_all x5 -> x0, waiting for transfers between devices: 31.5 us -> none  [exchanged(): lax.all_to_all(value, AXES, 0, 0, axis_index_groups=self.groups, tiled=True)]
    pallas_call x1 -> x9, Pallas kernels: 1.46 us -> 25.2 us  [the longest x2 16.2 us: run_experts(): pl.pallas_call(kernel, out_shape=tuple((jax.ShapeDtypeStruct(part.shape,...]
    all_to_all x5 -> x0, starting transfers between devices: 18.2 us -> none  [exchanged(): lax.all_to_all(value, AXES, 0, 0, axis_index_groups=self.groups, tiled=True)]
    all_to_all x1 -> x0, blocking collectives: 17.4 us -> none  [exchanged(): lax.all_to_all(value, AXES, 0, 0, axis_index_groups=self.groups, tiled=True)]
    ppermute x0 -> x42, waiting for transfers between devices: none -> 16.5 us  [swapped(): return lax.ppermute(value, AXES, pairs)]
    dot_general x8 -> x0, matrix products: 12.1 us -> none  [the longest x1 6.56 us: expert_block(): product = jnp.dot(tokens, gate_up, preferred_element_type=jnp.float32)]
    pallas_call x1, Pallas kernels: 9.85 us -> 0.57 us  [pick_pages(): pl.pallas_call(kernel, out_shape=jax.ShapeDtypeStruct((count,) + pages.sh...]
  transfers between devices with their start and end apart: 16 -> 50, of which waited for: 8 -> 16; matrix products, arithmetic and copies ran while one was open for 6% -> 2% of each run, Pallas kernels for 9% -> 22%
where the time goes in v4:
time: 117 us
  starting transfers between devices  51.8 us (44%)
  Pallas kernels  29.5 us (25%)
  waiting for transfers between devices  24.1 us (21%)
  local copies, waits for them, and re-layouts  10.7 us (9%)
    ppermute x42, starting transfers between devices, swapped(): return lax.ppermute(value, AXES, pairs)  38.1 us
    ppermute x42, waiting for transfers between devices, swapped(): return lax.ppermute(value, AXES, pairs)  16.5 us
    pallas_call x2, Pallas kernels, run_experts(): pl.pallas_call(kernel, out_shape=tuple((jax.ShapeDtypeStruct(part.shape,...  16.2 us
    unnamed x21, local copies, waits for them, and re-layouts  8.95 us
    ppermute x6, starting transfers between devices, shifted(): return lax.ppermute(value, AXES, pairs)  8.6 us
    ppermute x6, waiting for transfers between devices, shifted(): return lax.ppermute(value, AXES, pairs)  5.87 us
    ppermute x2, starting transfers between devices, from_behind(): lax.ppermute(value, axis, [(i, (i + by) % length) for i in range(length)])  5.09 us
    pallas_call x3, Pallas kernels, combine_rows(): pl.pallas_call(kernel, out_shape=(shape,) * count, in_specs=[SMEM] + [VME...  3.72 us
  transfers between devices with their start and end apart: 50, of which 16 were waited for; matrix products, arithmetic and copies ran while one was open for 2% of the time, Pallas kernels for 22%

profile of v4, /device:TPU:0, one launch (start us, length us, event | category | flops | bytes accessed | tf_op | source)
XLA Modules:
  0.0 116.9 jit_solution(12008305973957670137)
XLA Ops:
  0.6 3.0 %collective-permute-start = (s32[16]{0:T(128)}, s32[16]{0:T(128)S(1)}, u32[]{:S(2)}, u32[]{:S(2)}) collective-permute-start(s32[16]{0:T(128)} %param.17), channel_id=1, source_target_pairs={{0,16},{16,0},{1,17},{17,1},{2,18},{18,2},{3,19},{19,3},{4,20},{20... | collective-permute-start | bytes 200 | tf_op jit(solution)/shard_map/ppermute | solution.py:60
  3.6 1.7 %collective-permute-done.slots_ref = s32[16]{0:T(128)S(1)} collective-permute-done((s32[16]{0:T(128)}, s32[16]{0:T(128)S(1)}, u32[]{:S(2)}, u32[]{:S(2)}) %collective-permute-start) | collective-permute-done | bytes 96 | tf_op jit(solution)/shard_map/ppermute | solution.py:60
  5.3 1.6 %copy-done.1 = bf16[128,16,512]{2,1,0:T(8,128)(2,1)S(1)} copy-done((bf16[128,16,512]{2,1,0:T(8,128)(2,1)S(1)}, bf16[128,16,512]{2,1,0:T(8,128)(2,1)}, u32[]{:S(2)}) %copy-start.1) | copy-done | bytes 2097176
  7.5 2.1 %collective-permute-start.1 = (bf16[16,16,512]{2,1,0:T(8,128)(2,1)S(1)}, bf16[16,16,512]{2,1,0:T(8,128)(2,1)S(1)}, u32[]{:S(2)}, u32[]{:S(2)}) collective-permute-start(bf16[16,16,512]{2,1,0:T(8,128)(2,1)S(1)} %pick_pages.1), channel_id=1, source_target_pairs={{0,16},{16,0},{1,17},{17,1},{2,18},{18,2},{3,19},{19,3},{4,20},{20... | collective-permute-start | bytes 786440 | tf_op jit(solution)/shard_map/ppermute | solution.py:60
  12.2 1.6 %copy-done.2 = bf16[128,16,512]{2,1,0:T(8,128)(2,1)S(1)} copy-done((bf16[128,16,512]{2,1,0:T(8,128)(2,1)S(1)}, bf16[128,16,512]{2,1,0:T(8,128)(2,1)}, u32[]{:S(2)}) %copy-start.2) | copy-done | bytes 2097176
  15.9 3.7 %own_attention.1 = (f32[512,128]{1,0:T(8,128)S(1)}, f32[512,128]{1,0:T(8,128)S(1)}, f32[512,128]{1,0:T(8,128)S(1)}) custom-call(bf16[512,128]{1,0:T(8,128)(2,1)S(1)} %reshape.10.q_ref, bf16[16,512]{1,0:T(8,128)(2,1)S(1)} %copy-done.7, bf16[128,16,512]{2,1,0:T(8,128)(2,1)S(1)} %copy-done.2, s32[16,16]{1,0:T(8,128)S(1)} %copy-done.5, s32[16]{0:T(128)S(1)} %copy-done.6), custom_call_target="tpu_custom_call" | custom-call | flops 1073741824 | bytes 16777216 | tf_op jit(solution)/shard_map/own_attention/pallas_call | solution.py:183
  19.6 2.0 %finish_attention.1 = (bf16[16,4096]{1,0:T(8,128)(2,1)}, bf16[16,4096]{1,0:T(8,128)(2,1)S(1)}, bf16[16,4224]{1,0:T(8,128)(2,1)S(1)}) custom-call(bf16[512,128]{1,0:T(8,128)(2,1)S(1)} %reshape.10.q_ref, bf16[16,16,512]{2,1,0:T(8,128)(2,1)S(1)} %collective-permute-done.1.fetched_ref, s32[16,16]{1,0:T(8,128)S(1)} %copy-done.5, s32[16]{0:T(128)S(1)} %copy-done.6, ...), custom_call_target="tpu_custom_call" | custom-call | flops 134217728 | bytes 4194304 | tf_op jit(solution)/shard_map/finish_attention/pallas_call | solution.py:446
  21.5 1.6 %collective-permute-start.9 = (bf16[16,4224]{1,0:T(8,128)(2,1)S(1)}, bf16[16,4224]{1,0:T(8,128)(2,1)S(1)}, u32[]{:S(2)}, u32[]{:S(2)}) collective-permute-start(bf16[16,4224]{1,0:T(8,128)(2,1)S(1)} %get-tuple-element.66.refs_0_), channel_id=1, source_target_pairs={{0,4},{1,5},{2,6},{3,7},{16,20},{17,21},{18,22},{19,23},{4,0},{5,1... | collective-permute-start | bytes 405512 | tf_op jit(solution)/shard_map/ppermute | solution.py:45
  24.3 1.6 %collective-permute-start.3 = (bf16[8,4096]{1,0:T(8,128)(2,1)S(1)}, bf16[8,4096]{1,0:T(8,128)(2,1)S(1)}, u32[]{:S(2)}, u32[]{:S(2)}) collective-permute-start(bf16[8,4096]{1,0:T(8,128)(2,1)S(1)} %get-tuple-element.69), channel_id=1, source_target_pairs={{0,2},{1,3},{2,0},{3,1},{16,18},{17,19},{18,16},{19,17},{4,6},{5,7... | collective-permute-start | bytes 196616 | tf_op jit(solution)/shard_map/ppermute | solution.py:55
  26.1 2.5 %collective-permute-start.25 = (bf16[16,4224]{1,0:T(8,128)(2,1)S(1)}, bf16[16,4224]{1,0:T(8,128)(2,1)S(1)}, u32[]{:S(2)}, u32[]{:S(2)}) collective-permute-start(bf16[16,4224]{1,0:T(8,128)(2,1)S(1)} %get-tuple-element.66.refs_0_), channel_id=1, source_target_pairs={{0,12},{1,13},{2,14},{3,15},{16,28},{17,29},{18,30},{19,31},{4,8},... | collective-permute-start | bytes 405512 | tf_op jit(solution)/shard_map/ppermute | solution.py:45
  30.2 2.4 %collective-permute-start.7 = (bf16[8,4096]{1,0:T(8,128)(2,1)S(1)}, bf16[8,4096]{1,0:T(8,128)(2,1)S(1)}, u32[]{:S(2)}, u32[]{:S(2)}) collective-permute-start(bf16[8,4096]{1,0:T(8,128)(2,1)S(1)} %get-tuple-element.73), channel_id=1, source_target_pairs={{0,18},{1,19},{2,16},{3,17},{16,2},{17,3},{18,0},{19,1},{4,22},{5,... | collective-permute-start | bytes 196616 | tf_op jit(solution)/shard_map/ppermute | solution.py:55
  35.1 2.1 %collective-permute-done.7.refs_6_ = bf16[8,4096]{1,0:T(8,128)(2,1)S(1)} collective-permute-done((bf16[8,4096]{1,0:T(8,128)(2,1)S(1)}, bf16[8,4096]{1,0:T(8,128)(2,1)S(1)}, u32[]{:S(2)}, u32[]{:S(2)}) %collective-permute-start.7) | collective-permute-done | bytes 65568 | tf_op jit(solution)/shard_map/ppermute | solution.py:55
  37.6 3.8 %collective-permute-done.24.refs_0_ = bf16[16,4224]{1,0:T(8,128)(2,1)S(1)} collective-permute-done((bf16[16,4224]{1,0:T(8,128)(2,1)S(1)}, bf16[16,4224]{1,0:T(8,128)(2,1)S(1)}, u32[]{:S(2)}, u32[]{:S(2)}) %collective-permute-start.24) | collective-permute-done | bytes 135200 | tf_op jit(solution)/shard_map/ppermute | solution.py:45
  43.4 1.6 %collective-permute-start.27 = (bf16[16,4096]{1,0:T(8,128)(2,1)S(1)}, bf16[16,4096]{1,0:T(8,128)(2,1)S(1)}, u32[]{:S(2)}, u32[]{:S(2)}) collective-permute-start(bf16[16,4096]{1,0:T(8,128)(2,1)S(1)} %get-tuple-element.94), channel_id=1, source_target_pairs={{0,2},{1,3},{2,0},{3,1},{16,18},{17,19},{18,16},{19,17},{4,6},{5,7... | collective-permute-start | bytes 393224 | tf_op jit(solution)/shard_map/ppermute | solution.py:55
  46.7 2.1 %collective-permute-start.16 = (bf16[8,4096]{1,0:T(8,128)(2,1)S(1)}, bf16[8,4096]{1,0:T(8,128)(2,1)S(1)}, u32[]{:S(2)}, u32[]{:S(2)}) collective-permute-start(bf16[8,4096]{1,0:T(8,128)(2,1)S(1)} %get-tuple-element.82), channel_id=1, source_target_pairs={{0,19},{1,18},{2,17},{3,16},{16,3},{17,2},{18,1},{19,0},{4,23},{5,... | collective-permute-start | bytes 196616 | tf_op jit(solution)/shard_map/ppermute | solution.py:55
  49.6 2.4 %collective-permute-done.15.refs_14_ = bf16[8,4096]{1,0:T(8,128)(2,1)S(1)} collective-permute-done((bf16[8,4096]{1,0:T(8,128)(2,1)S(1)}, bf16[8,4096]{1,0:T(8,128)(2,1)S(1)}, u32[]{:S(2)}, u32[]{:S(2)}) %collective-permute-start.15) | collective-permute-done | bytes 65568 | tf_op jit(solution)/shard_map/ppermute | solution.py:55
  53.2 1.5 %collective-permute-start.31 = (bf16[16,4096]{1,0:T(8,128)(2,1)S(1)}, bf16[16,4096]{1,0:T(8,128)(2,1)S(1)}, u32[]{:S(2)}, u32[]{:S(2)}) collective-permute-start(bf16[16,4096]{1,0:T(8,128)(2,1)S(1)} %get-tuple-element.98), channel_id=1, source_target_pairs={{0,18},{1,19},{2,16},{3,17},{16,2},{17,3},{18,0},{19,1},{4,22},{5,... | collective-permute-start | bytes 393224 | tf_op jit(solution)/shard_map/ppermute | solution.py:55
  54.7 1.8 %collective-permute-start.32 = (bf16[16,4096]{1,0:T(8,128)(2,1)S(1)}, bf16[16,4096]{1,0:T(8,128)(2,1)S(1)}, u32[]{:S(2)}, u32[]{:S(2)}) collective-permute-start(bf16[16,4096]{1,0:T(8,128)(2,1)S(1)} %get-tuple-element.99), channel_id=1, source_target_pairs={{0,19},{1,18},{2,17},{3,16},{16,3},{17,2},{18,1},{19,0},{4,23},{5,... | collective-permute-start | bytes 393224 | tf_op jit(solution)/shard_map/ppermute | solution.py:55
  56.4 2.8 %copy-done = bf16[1,768,4096]{2,1,0:T(8,128)(2,1)S(1)} copy-done((bf16[1,768,4096]{2,1,0:T(8,128)(2,1)S(1)}, bf16[1,768,4096]{2,1,0:T(8,128)(2,1)}, u32[]{:S(2)}) %copy-start) | copy-done | bytes 6291480
  59.2 8.3 %run_experts.2 = (bf16[8,4096]{1,0:T(8,128)(2,1)S(1)}, bf16[8,4096]{1,0:T(8,128)(2,1)S(1)}, bf16[8,4096]{1,0:T(8,128)(2,1)S(1)}, bf16[8,4096]{1,0:T(8,128)(2,1)S...) custom-call(bf16[8,4096]{1,0:T(8,128)(2,1)S(1)} %get-tuple-element.6, ...), custom_call_target="tpu_custom_call" | custom-call | flops 2415919104 | bytes 20971520 | tf_op jit(solution)/shard_map/run_experts/pallas_call | solution.py:331
  70.0 7.9 %run_experts.3 = (bf16[16,4096]{1,0:T(8,128)(2,1)S(1)}, bf16[16,4096]{1,0:T(8,128)(2,1)S(1)}, bf16[16,4096]{1,0:T(8,128)(2,1)S(1)}, bf16[16,4096]{1,0:T(8,128)(2...) custom-call(bf16[16,4096]{1,0:T(8,128)(2,1)S(1)} %get-tuple-element., ...), custom_call_target="tpu_custom_call" | custom-call | flops 2415919104 | bytes 20971520 | tf_op jit(solution)/shard_map/run_experts/pallas_call | solution.py:331
  81.4 1.8 %collective-permute-start.48 = (bf16[8,4096]{1,0:T(8,128)(2,1)S(1)}, bf16[8,4096]{1,0:T(8,128)(2,1)S(1)}, u32[]{:S(2)}, u32[]{:S(2)}) collective-permute-start(bf16[8,4096]{1,0:T(8,128)(2,1)S(1)} %get-tuple-element.117), channel_id=1, source_target_pairs={{0,19},{1,18},{2,17},{3,16},{16,3},{17,2},{18,1},{19,0},{4,23},{5,... | collective-permute-start | bytes 196616 | tf_op jit(solution)/shard_map/ppermute | solution.py:55
  84.6 1.5 %collective-permute-done.47.refs_7_ = bf16[8,4096]{1,0:T(8,128)(2,1)S(1)} collective-permute-done((bf16[8,4096]{1,0:T(8,128)(2,1)S(1)}, bf16[8,4096]{1,0:T(8,128)(2,1)S(1)}, u32[]{:S(2)}, u32[]{:S(2)}) %collective-permute-start.47) | collective-permute-done | bytes 65568 | tf_op jit(solution)/shard_map/ppermute | solution.py:55
  89.0 1.5 %collective-permute-start.39 = (bf16[16,4096]{1,0:T(8,128)(2,1)S(1)}, bf16[16,4096]{1,0:T(8,128)(2,1)S(1)}, u32[]{:S(2)}, u32[]{:S(2)}) collective-permute-start(bf16[16,4096]{1,0:T(8,128)(2,1)S(1)} %get-tuple-element.107), channel_id=1, source_target_pairs={{0,19},{1,18},{2,17},{3,16},{16,3},{17,2},{18,1},{19,0},{4,23},{5,... | collective-permute-start | bytes 393224 | tf_op jit(solution)/shard_map/ppermute | solution.py:55
  93.3 1.4 %collective-permute-start.19 = (bf16[8,4096]{1,0:T(8,128)(2,1)S(1)}, bf16[8,4096]{1,0:T(8,128)(2,1)S(1)}, u32[]{:S(2)}, u32[]{:S(2)}) collective-permute-start(bf16[8,4096]{1,0:T(8,128)(2,1)S(1)} %get-tuple-element.86), channel_id=1, source_target_pairs={{0,3},{1,2},{2,1},{3,0},{16,19},{17,18},{18,17},{19,16},{4,7},{5,6... | collective-permute-start | bytes 196616 | tf_op jit(solution)/shard_map/ppermute | solution.py:55
  95.7 1.9 %collective-permute-done.38.refs_8_ = bf16[16,4096]{1,0:T(8,128)(2,1)S(1)} collective-permute-done((bf16[16,4096]{1,0:T(8,128)(2,1)S(1)}, bf16[16,4096]{1,0:T(8,128)(2,1)S(1)}, u32[]{:S(2)}, u32[]{:S(2)}) %collective-permute-start.38) | collective-permute-done | bytes 131104 | tf_op jit(solution)/shard_map/ppermute | solution.py:55
  97.6 2.1 %collective-permute-start.20 = (bf16[8,4096]{1,0:T(8,128)(2,1)S(1)}, bf16[8,4096]{1,0:T(8,128)(2,1)S(1)}, u32[]{:S(2)}, u32[]{:S(2)}) collective-permute-start(bf16[8,4096]{1,0:T(8,128)(2,1)S(1)} %get-tuple-element.87), channel_id=1, source_target_pairs={{0,16},{1,17},{2,18},{3,19},{16,0},{17,1},{18,2},{19,3},{4,20},{5,... | collective-permute-start | bytes 196616 | tf_op jit(solution)/shard_map/ppermute | solution.py:55
  99.7 1.8 %collective-permute-start.21 = (bf16[8,4096]{1,0:T(8,128)(2,1)S(1)}, bf16[8,4096]{1,0:T(8,128)(2,1)S(1)}, u32[]{:S(2)}, u32[]{:S(2)}) collective-permute-start(bf16[8,4096]{1,0:T(8,128)(2,1)S(1)} %get-tuple-element.88), channel_id=1, source_target_pairs={{0,17},{1,16},{2,19},{3,18},{16,1},{17,0},{18,3},{19,2},{4,21},{5,... | collective-permute-start | bytes 196616 | tf_op jit(solution)/shard_map/ppermute | solution.py:55
  102.7 3.2 %collective-permute-start.40 = (bf16[16,4096]{1,0:T(8,128)(2,1)S(1)}, bf16[16,4096]{1,0:T(8,128)(2,1)S(1)}, u32[]{:S(2)}, u32[]{:S(2)}) collective-permute-start(bf16[16,4096]{1,0:T(8,128)(2,1)S(1)} %get-tuple-element.108), channel_id=1, source_target_pairs={{0,8},{1,9},{2,10},{3,11},{16,24},{17,25},{18,26},{19,27},{4,12},{... | collective-permute-start | bytes 393224 | tf_op jit(solution)/shard_map/ppermute | solution.py:45
  108.0 4.5 %collective-permute-done.22.refs_7_ = bf16[8,4096]{1,0:T(8,128)(2,1)S(1)} collective-permute-done((bf16[8,4096]{1,0:T(8,128)(2,1)S(1)}, bf16[8,4096]{1,0:T(8,128)(2,1)S(1)}, u32[]{:S(2)}, u32[]{:S(2)}) %collective-permute-start.22) | collective-permute-done | bytes 65568 | tf_op jit(solution)/shard_map/ppermute | solution.py:55
  113.3 2.0 %collective-permute-done.40.refs_10_ = bf16[16,4096]{1,0:T(8,128)(2,1)S(1)} collective-permute-done((bf16[16,4096]{1,0:T(8,128)(2,1)S(1)}, bf16[16,4096]{1,0:T(8,128)(2,1)S(1)}, u32[]{:S(2)}, u32[]{:S(2)}) %collective-permute-start.40) | collective-permute-done | bytes 131104 | tf_op jit(solution)/shard_map/ppermute | solution.py:45
  115.3 1.7 %combine_rows.5 = bf16[16,4096]{1,0:T(8,128)(2,1)} custom-call(s32[8]{0:T(128)S(1)} %fusion.experts_ref, bf16[16,4224]{1,0:T(8,128)(2,1)S(1)} %get-tuple-element.66.refs_0_, bf16[8,4096]{1,0:T(8,128)(2,1)S(1)} %get-tuple-element.83.refs_1_, bf16[8,4096]{1,0:T(8,128)(2,1)S(1)} %collective-permute-done.17.refs_2_, ...), custom_call_target="tpu_custom_call" | custom-call | bytes 3145728 | tf_op jit(solution)/shard_map/combine_rows/pallas_call | solution.py:388
  (104 shorter events, 34.7 us)
Async XLA Ops:
  7.5 12.1 %collective-permute-start.1 = (bf16[16,16,512]{2,1,0:T(8,128)(2,1)S(1)}, bf16[16,16,512]{2,1,0:T(8,128)(2,1)S(1)}, u32[]{:S(2)}, u32[]{:S(2)}) collective-permute-start(bf16[16,16,512]{2,1,0:T(8,128)(2,1)S(1)} %pick_pages.1), channel_id=1, source_target_pairs={{0,16},{16,0},{1,17},{17,1},{2,18},{18,2},{3,19},{19,3},{4,20},{20... | collective-permute-start | bytes 786440 | tf_op jit(solution)/shard_map/ppermute | solution.py:60
  21.5 8.7 %collective-permute-start.9 = (bf16[16,4224]{1,0:T(8,128)(2,1)S(1)}, bf16[16,4224]{1,0:T(8,128)(2,1)S(1)}, u32[]{:S(2)}, u32[]{:S(2)}) collective-permute-start(bf16[16,4224]{1,0:T(8,128)(2,1)S(1)} %get-tuple-element.66.refs_0_), channel_id=1, source_target_pairs={{0,4},{1,5},{2,6},{3,7},{16,20},{17,21},{18,22},{19,23},{4,0},{5,1... | collective-permute-start | bytes 405512 | tf_op jit(solution)/shard_map/ppermute | solution.py:45
  26.1 11.2 %collective-permute-start.25 = (bf16[16,4224]{1,0:T(8,128)(2,1)S(1)}, bf16[16,4224]{1,0:T(8,128)(2,1)S(1)}, u32[]{:S(2)}, u32[]{:S(2)}) collective-permute-start(bf16[16,4224]{1,0:T(8,128)(2,1)S(1)} %get-tuple-element.66.refs_0_), channel_id=1, source_target_pairs={{0,12},{1,13},{2,14},{3,15},{16,28},{17,29},{18,30},{19,31},{4,8},... | collective-permute-start | bytes 405512 | tf_op jit(solution)/shard_map/ppermute | solution.py:45
  28.6 12.9 %collective-permute-start.24 = (bf16[16,4224]{1,0:T(8,128)(2,1)S(1)}, bf16[16,4224]{1,0:T(8,128)(2,1)S(1)}, u32[]{:S(2)}, u32[]{:S(2)}) collective-permute-start(bf16[16,4224]{1,0:T(8,128)(2,1)S(1)} %get-tuple-element.66.refs_0_), channel_id=1, source_target_pairs={{0,8},{1,9},{2,10},{3,11},{16,24},{17,25},{18,26},{19,27},{4,12},{... | collective-permute-start | bytes 405512 | tf_op jit(solution)/shard_map/ppermute | solution.py:45
  33.7 9.6 %collective-permute-start.8 = (bf16[8,4096]{1,0:T(8,128)(2,1)S(1)}, bf16[8,4096]{1,0:T(8,128)(2,1)S(1)}, u32[]{:S(2)}, u32[]{:S(2)}) collective-permute-start(bf16[8,4096]{1,0:T(8,128)(2,1)S(1)} %get-tuple-element.74), channel_id=1, source_target_pairs={{0,19},{1,18},{2,17},{3,16},{16,3},{17,2},{18,1},{19,0},{4,23},{5,... | collective-permute-start | bytes 196616 | tf_op jit(solution)/shard_map/ppermute | solution.py:55
  34.3 9.0 %collective-permute-start.10 = (bf16[8,4096]{1,0:T(8,128)(2,1)S(1)}, bf16[8,4096]{1,0:T(8,128)(2,1)S(1)}, u32[]{:S(2)}, u32[]{:S(2)}) collective-permute-start(bf16[8,4096]{1,0:T(8,128)(2,1)S(1)} %get-tuple-element.76), channel_id=1, source_target_pairs={{0,1},{1,0},{2,3},{3,2},{16,17},{17,16},{18,19},{19,18},{4,5},{5,4... | collective-permute-start | bytes 196616 | tf_op jit(solution)/shard_map/ppermute | solution.py:55
  37.2 7.7 %collective-permute-start.11 = (bf16[8,4096]{1,0:T(8,128)(2,1)S(1)}, bf16[8,4096]{1,0:T(8,128)(2,1)S(1)}, u32[]{:S(2)}, u32[]{:S(2)}) collective-permute-start(bf16[8,4096]{1,0:T(8,128)(2,1)S(1)} %get-tuple-element.77), channel_id=1, source_target_pairs={{0,2},{1,3},{2,0},{3,1},{16,18},{17,19},{18,16},{19,17},{4,6},{5,7... | collective-permute-start | bytes 196616 | tf_op jit(solution)/shard_map/ppermute | solution.py:55
  37.3 8.9 %collective-permute-start.12 = (bf16[8,4096]{1,0:T(8,128)(2,1)S(1)}, bf16[8,4096]{1,0:T(8,128)(2,1)S(1)}, u32[]{:S(2)}, u32[]{:S(2)}) collective-permute-start(bf16[8,4096]{1,0:T(8,128)(2,1)S(1)} %get-tuple-element.78), channel_id=1, source_target_pairs={{0,3},{1,2},{2,1},{3,0},{16,19},{17,18},{18,17},{19,16},{4,7},{5,6... | collective-permute-start | bytes 196616 | tf_op jit(solution)/shard_map/ppermute | solution.py:55
  43.3 9.9 %collective-permute-start.26 = (bf16[16,4096]{1,0:T(8,128)(2,1)S(1)}, bf16[16,4096]{1,0:T(8,128)(2,1)S(1)}, u32[]{:S(2)}, u32[]{:S(2)}) collective-permute-start(bf16[16,4096]{1,0:T(8,128)(2,1)S(1)} %get-tuple-element.93), channel_id=1, source_target_pairs={{0,1},{1,0},{2,3},{3,2},{16,17},{17,16},{18,19},{19,18},{4,5},{5,4... | collective-permute-start | bytes 393224 | tf_op jit(solution)/shard_map/ppermute | solution.py:55
  43.4 11.3 %collective-permute-start.27 = (bf16[16,4096]{1,0:T(8,128)(2,1)S(1)}, bf16[16,4096]{1,0:T(8,128)(2,1)S(1)}, u32[]{:S(2)}, u32[]{:S(2)}) collective-permute-start(bf16[16,4096]{1,0:T(8,128)(2,1)S(1)} %get-tuple-element.94), channel_id=1, source_target_pairs={{0,2},{1,3},{2,0},{3,1},{16,18},{17,19},{18,16},{19,17},{4,6},{5,7... | collective-permute-start | bytes 393224 | tf_op jit(solution)/shard_map/ppermute | solution.py:55
  49.0 18.5 %collective-permute-start.28 = (bf16[16,4096]{1,0:T(8,128)(2,1)S(1)}, bf16[16,4096]{1,0:T(8,128)(2,1)S(1)}, u32[]{:S(2)}, u32[]{:S(2)}) collective-permute-start(bf16[16,4096]{1,0:T(8,128)(2,1)S(1)} %get-tuple-element.95), channel_id=1, source_target_pairs={{0,3},{1,2},{2,1},{3,0},{16,19},{17,18},{18,17},{19,16},{4,7},{5,6... | collective-permute-start | bytes 393224 | tf_op jit(solution)/shard_map/ppermute | solution.py:55
  52.0 15.6 %collective-permute-start.29 = (bf16[16,4096]{1,0:T(8,128)(2,1)S(1)}, bf16[16,4096]{1,0:T(8,128)(2,1)S(1)}, u32[]{:S(2)}, u32[]{:S(2)}) collective-permute-start(bf16[16,4096]{1,0:T(8,128)(2,1)S(1)} %get-tuple-element.96), channel_id=1, source_target_pairs={{0,16},{1,17},{2,18},{3,19},{16,0},{17,1},{18,2},{19,3},{4,20},{5,... | collective-permute-start | bytes 393224 | tf_op jit(solution)/shard_map/ppermute | solution.py:55
  52.3 16.5 %collective-permute-start.30 = (bf16[16,4096]{1,0:T(8,128)(2,1)S(1)}, bf16[16,4096]{1,0:T(8,128)(2,1)S(1)}, u32[]{:S(2)}, u32[]{:S(2)}) collective-permute-start(bf16[16,4096]{1,0:T(8,128)(2,1)S(1)} %get-tuple-element.97), channel_id=1, source_target_pairs={{0,17},{1,16},{2,19},{3,18},{16,1},{17,0},{18,3},{19,2},{4,21},{5,... | collective-permute-start | bytes 393224 | tf_op jit(solution)/shard_map/ppermute | solution.py:55
  53.2 16.3 %collective-permute-start.31 = (bf16[16,4096]{1,0:T(8,128)(2,1)S(1)}, bf16[16,4096]{1,0:T(8,128)(2,1)S(1)}, u32[]{:S(2)}, u32[]{:S(2)}) collective-permute-start(bf16[16,4096]{1,0:T(8,128)(2,1)S(1)} %get-tuple-element.98), channel_id=1, source_target_pairs={{0,18},{1,19},{2,16},{3,17},{16,2},{17,3},{18,0},{19,1},{4,22},{5,... | collective-permute-start | bytes 393224 | tf_op jit(solution)/shard_map/ppermute | solution.py:55
  54.7 15.4 %collective-permute-start.32 = (bf16[16,4096]{1,0:T(8,128)(2,1)S(1)}, bf16[16,4096]{1,0:T(8,128)(2,1)S(1)}, u32[]{:S(2)}, u32[]{:S(2)}) collective-permute-start(bf16[16,4096]{1,0:T(8,128)(2,1)S(1)} %get-tuple-element.99), channel_id=1, source_target_pairs={{0,19},{1,18},{2,17},{3,16},{16,3},{17,2},{18,1},{19,0},{4,23},{5,... | collective-permute-start | bytes 393224 | tf_op jit(solution)/shard_map/ppermute | solution.py:55
  67.5 11.0 %collective-permute-start.42 = (bf16[8,4096]{1,0:T(8,128)(2,1)S(1)}, bf16[8,4096]{1,0:T(8,128)(2,1)S(1)}, u32[]{:S(2)}, u32[]{:S(2)}) collective-permute-start(bf16[8,4096]{1,0:T(8,128)(2,1)S(1)} %get-tuple-element.111), channel_id=1, source_target_pairs={{0,1},{1,0},{2,3},{3,2},{16,17},{17,16},{18,19},{19,18},{4,5},{5,4... | collective-permute-start | bytes 196616 | tf_op jit(solution)/shard_map/ppermute | solution.py:55
  67.6 11.8 %collective-permute-start.43 = (bf16[8,4096]{1,0:T(8,128)(2,1)S(1)}, bf16[8,4096]{1,0:T(8,128)(2,1)S(1)}, u32[]{:S(2)}, u32[]{:S(2)}) collective-permute-start(bf16[8,4096]{1,0:T(8,128)(2,1)S(1)} %get-tuple-element.112), channel_id=1, source_target_pairs={{0,2},{1,3},{2,0},{3,1},{16,18},{17,19},{18,16},{19,17},{4,6},{5,7... | collective-permute-start | bytes 196616 | tf_op jit(solution)/shard_map/ppermute | solution.py:55
  68.9 11.5 %collective-permute-start.44 = (bf16[8,4096]{1,0:T(8,128)(2,1)S(1)}, bf16[8,4096]{1,0:T(8,128)(2,1)S(1)}, u32[]{:S(2)}, u32[]{:S(2)}) collective-permute-start(bf16[8,4096]{1,0:T(8,128)(2,1)S(1)} %get-tuple-element.113), channel_id=1, source_target_pairs={{0,3},{1,2},{2,1},{3,0},{16,19},{17,18},{18,17},{19,16},{4,7},{5,6... | collective-permute-start | bytes 196616 | tf_op jit(solution)/shard_map/ppermute | solution.py:55
  69.4 12.0 %collective-permute-start.45 = (bf16[8,4096]{1,0:T(8,128)(2,1)S(1)}, bf16[8,4096]{1,0:T(8,128)(2,1)S(1)}, u32[]{:S(2)}, u32[]{:S(2)}) collective-permute-start(bf16[8,4096]{1,0:T(8,128)(2,1)S(1)} %get-tuple-element.114), channel_id=1, source_target_pairs={{0,16},{1,17},{2,18},{3,19},{16,0},{17,1},{18,2},{19,3},{4,20},{5,... | collective-permute-start | bytes 196616 | tf_op jit(solution)/shard_map/ppermute | solution.py:55
  78.0 9.8 %collective-permute-start.33 = (bf16[16,4096]{1,0:T(8,128)(2,1)S(1)}, bf16[16,4096]{1,0:T(8,128)(2,1)S(1)}, u32[]{:S(2)}, u32[]{:S(2)}) collective-permute-start(bf16[16,4096]{1,0:T(8,128)(2,1)S(1)} %get-tuple-element.101), channel_id=1, source_target_pairs={{0,1},{1,0},{2,3},{3,2},{16,17},{17,16},{18,19},{19,18},{4,5},{5,4... | collective-permute-start | bytes 393224 | tf_op jit(solution)/shard_map/ppermute | solution.py:55
  78.5 10.5 %collective-permute-start.34 = (bf16[16,4096]{1,0:T(8,128)(2,1)S(1)}, bf16[16,4096]{1,0:T(8,128)(2,1)S(1)}, u32[]{:S(2)}, u32[]{:S(2)}) collective-permute-start(bf16[16,4096]{1,0:T(8,128)(2,1)S(1)} %get-tuple-element.102), channel_id=1, source_target_pairs={{0,2},{1,3},{2,0},{3,1},{16,18},{17,19},{18,16},{19,17},{4,6},{5,7... | collective-permute-start | bytes 393224 | tf_op jit(solution)/shard_map/ppermute | solution.py:55
  83.4 7.2 %collective-permute-start.35 = (bf16[16,4096]{1,0:T(8,128)(2,1)S(1)}, bf16[16,4096]{1,0:T(8,128)(2,1)S(1)}, u32[]{:S(2)}, u32[]{:S(2)}) collective-permute-start(bf16[16,4096]{1,0:T(8,128)(2,1)S(1)} %get-tuple-element.103), channel_id=1, source_target_pairs={{0,3},{1,2},{2,1},{3,0},{16,19},{17,18},{18,17},{19,16},{4,7},{5,6... | collective-permute-start | bytes 393224 | tf_op jit(solution)/shard_map/ppermute | solution.py:55
  87.8 9.8 %collective-permute-start.38 = (bf16[16,4096]{1,0:T(8,128)(2,1)S(1)}, bf16[16,4096]{1,0:T(8,128)(2,1)S(1)}, u32[]{:S(2)}, u32[]{:S(2)}) collective-permute-start(bf16[16,4096]{1,0:T(8,128)(2,1)S(1)} %get-tuple-element.106), channel_id=1, source_target_pairs={{0,18},{1,19},{2,16},{3,17},{16,2},{17,3},{18,0},{19,1},{4,22},{5,... | collective-permute-start | bytes 393224 | tf_op jit(solution)/shard_map/ppermute | solution.py:55
  89.0 10.7 %collective-permute-start.39 = (bf16[16,4096]{1,0:T(8,128)(2,1)S(1)}, bf16[16,4096]{1,0:T(8,128)(2,1)S(1)}, u32[]{:S(2)}, u32[]{:S(2)}) collective-permute-start(bf16[16,4096]{1,0:T(8,128)(2,1)S(1)} %get-tuple-element.107), channel_id=1, source_target_pairs={{0,19},{1,18},{2,17},{3,16},{16,3},{17,2},{18,1},{19,0},{4,23},{5,... | collective-permute-start | bytes 393224 | tf_op jit(solution)/shard_map/ppermute | solution.py:55
  90.5 12.1 %collective-permute-start.17 = (bf16[8,4096]{1,0:T(8,128)(2,1)S(1)}, bf16[8,4096]{1,0:T(8,128)(2,1)S(1)}, u32[]{:S(2)}, u32[]{:S(2)}) collective-permute-start(bf16[8,4096]{1,0:T(8,128)(2,1)S(1)} %get-tuple-element.84), channel_id=1, source_target_pairs={{0,1},{1,0},{2,3},{3,2},{16,17},{17,16},{18,19},{19,18},{4,5},{5,4... | collective-permute-start | bytes 196616 | tf_op jit(solution)/shard_map/ppermute | solution.py:55
  92.2 10.4 %collective-permute-start.18 = (bf16[8,4096]{1,0:T(8,128)(2,1)S(1)}, bf16[8,4096]{1,0:T(8,128)(2,1)S(1)}, u32[]{:S(2)}, u32[]{:S(2)}) collective-permute-start(bf16[8,4096]{1,0:T(8,128)(2,1)S(1)} %get-tuple-element.85), channel_id=1, source_target_pairs={{0,2},{1,3},{2,0},{3,1},{16,18},{17,19},{18,16},{19,17},{4,6},{5,7... | collective-permute-start | bytes 196616 | tf_op jit(solution)/shard_map/ppermute | solution.py:55
  93.3 12.6 %collective-permute-start.19 = (bf16[8,4096]{1,0:T(8,128)(2,1)S(1)}, bf16[8,4096]{1,0:T(8,128)(2,1)S(1)}, u32[]{:S(2)}, u32[]{:S(2)}) collective-permute-start(bf16[8,4096]{1,0:T(8,128)(2,1)S(1)} %get-tuple-element.86), channel_id=1, source_target_pairs={{0,3},{1,2},{2,1},{3,0},{16,19},{17,18},{18,17},{19,16},{4,7},{5,6... | collective-permute-start | bytes 196616 | tf_op jit(solution)/shard_map/ppermute | solution.py:55
  97.6 9.4 %collective-permute-start.20 = (bf16[8,4096]{1,0:T(8,128)(2,1)S(1)}, bf16[8,4096]{1,0:T(8,128)(2,1)S(1)}, u32[]{:S(2)}, u32[]{:S(2)}) collective-permute-start(bf16[8,4096]{1,0:T(8,128)(2,1)S(1)} %get-tuple-element.87), channel_id=1, source_target_pairs={{0,16},{1,17},{2,18},{3,19},{16,0},{17,1},{18,2},{19,3},{4,20},{5,... | collective-permute-start | bytes 196616 | tf_op jit(solution)/shard_map/ppermute | solution.py:55
  99.7 8.3 %collective-permute-start.21 = (bf16[8,4096]{1,0:T(8,128)(2,1)S(1)}, bf16[8,4096]{1,0:T(8,128)(2,1)S(1)}, u32[]{:S(2)}, u32[]{:S(2)}) collective-permute-start(bf16[8,4096]{1,0:T(8,128)(2,1)S(1)} %get-tuple-element.88), channel_id=1, source_target_pairs={{0,17},{1,16},{2,19},{3,18},{16,1},{17,0},{18,3},{19,2},{4,21},{5,... | collective-permute-start | bytes 196616 | tf_op jit(solution)/shard_map/ppermute | solution.py:55
  102.6 10.7 %collective-permute-start.49 = (bf16[16,4096]{1,0:T(8,128)(2,1)S(1)}, bf16[16,4096]{1,0:T(8,128)(2,1)S(1)}, u32[]{:S(2)}, u32[]{:S(2)}) collective-permute-start(bf16[16,4096]{1,0:T(8,128)(2,1)S(1)} %combine_rows.4), channel_id=1, source_target_pairs={{0,4},{1,5},{2,6},{3,7},{16,20},{17,21},{18,22},{19,23},{4,0},{5,1... | collective-permute-start | bytes 393224 | tf_op jit(solution)/shard_map/ppermute | solution.py:45
  102.7 12.6 %collective-permute-start.40 = (bf16[16,4096]{1,0:T(8,128)(2,1)S(1)}, bf16[16,4096]{1,0:T(8,128)(2,1)S(1)}, u32[]{:S(2)}, u32[]{:S(2)}) collective-permute-start(bf16[16,4096]{1,0:T(8,128)(2,1)S(1)} %get-tuple-element.108), channel_id=1, source_target_pairs={{0,8},{1,9},{2,10},{3,11},{16,24},{17,25},{18,26},{19,27},{4,12},{... | collective-permute-start | bytes 393224 | tf_op jit(solution)/shard_map/ppermute | solution.py:45
  105.9 9.4 %collective-permute-start.41 = (bf16[16,4096]{1,0:T(8,128)(2,1)S(1)}, bf16[16,4096]{1,0:T(8,128)(2,1)S(1)}, u32[]{:S(2)}, u32[]{:S(2)}) collective-permute-start(bf16[16,4096]{1,0:T(8,128)(2,1)S(1)} %get-tuple-element.109), channel_id=1, source_target_pairs={{0,12},{1,13},{2,14},{3,15},{16,28},{17,29},{18,30},{19,31},{4,8},... | collective-permute-start | bytes 393224 | tf_op jit(solution)/shard_map/ppermute | solution.py:45
  (28 other events, 197.9 us)

commit v5 on v3

--- a/solution.py
+++ b/solution.py
@@ -16,7 +16,13 @@
 epsilon = 1e-06
 AXES = ("pool", "dev")
 VMEM = pl.BlockSpec(memory_space=pltpu.VMEM)
+SMEM = pl.BlockSpec(memory_space=pltpu.SMEM)
+HBM = pl.BlockSpec(memory_space=pltpu.HBM)
 MEBI = 1 << 20
+
+
+def in_hbm(value):
+    return pltpu.with_memory_space_constraint(value, pltpu.HBM)
 
 
 class Layout:
@@ -37,14 +43,21 @@
         if by == 0:
             return value
         pairs = [
-            (self.linear(m, z), self.linear(m, (z + by) % self.planes))
+            (self.linear(m, z), self.linear(m, z ^ by))
             for z in range(self.planes)
             for m in range(self.members)
         ]
         return lax.ppermute(value, AXES, pairs)
 
-    def exchanged(self, value):
-        return lax.all_to_all(value, AXES, 0, 0, axis_index_groups=self.groups, tiled=True)
+    def swapped(self, value, by):
+        if by == 0:
+            return value
+        pairs = [
+            (self.linear(m, z), self.linear(m ^ by, z))
+            for z in range(self.planes)
+            for m in range(self.members)
+        ]
+        return lax.ppermute(value, AXES, pairs)
 
 
 def from_behind(value, axis, by):
@@ -68,15 +81,13 @@
     return pl.pallas_call(
         kernel,
         out_shape=jax.ShapeDtypeStruct((count,) + pages.shape[1:], pages.dtype),
-        in_specs=[
-            pl.BlockSpec(memory_space=pltpu.SMEM),
-            pl.BlockSpec(memory_space=pl.ANY),
-        ],
-        out_specs=pl.BlockSpec(memory_space=pl.ANY),
+        in_specs=[SMEM, HBM],
+        out_specs=VMEM,
         scratch_shapes=[pltpu.SemaphoreType.DMA((count,))],
-        cost_estimate=pl.CostEstimate(flops=0, bytes_accessed=4 * MEBI, transcendentals=0),
+        compiler_params=pltpu.CompilerParams(vmem_limit_bytes=4 * MEBI),
+        cost_estimate=pl.CostEstimate(flops=0, bytes_accessed=MEBI, transcendentals=0),
         name="pick_pages",
-    )(slots, pages)
+    )(slots, in_hbm(pages))
 
 
 def head_blocks(query):
@@ -95,9 +106,13 @@
     )
 
 
-def tokens_of_pages(table, lengths, first, page_len):
+def tokens_of_pages(table, lengths_ref, first, page_len):
     count_of_rows, width = table.shape
     page = lax.broadcasted_iota(jnp.int32, (count_of_rows, 128), 1) + first
+    row = lax.broadcasted_iota(jnp.int32, (count_of_rows, 128), 0)
+    lengths = jnp.zeros((count_of_rows, 128), jnp.int32)
+    for r in range(count_of_rows):
+        lengths = jnp.where(row == r, lengths_ref[r], lengths)
     held = jnp.zeros((count_of_rows, 128), jnp.float32)
     for p in range(width):
         filled = jnp.clip(lengths - p * page_len, 0, page_len).astype(jnp.float32)
@@ -131,21 +146,62 @@
     return result
 
 
-def own_attention(query, new_kv, pages, table, lengths):
+def own_attention(queries, new_kv, pages, table, lengths):
     page_count, page_len, kv_width = pages.shape
-    rows = query.shape[0]
     requests = new_kv.shape[0]
+    rows = requests * HEADS
     half = kv_width // 2
     chunk_pages = 128 * (page_count // 128) // 4
     chunk = chunk_pages * page_len
     chunks = page_count // chunk_pages
     scaling = 1.0 / math.sqrt(HEAD_DIMENSION)
 
-    def kernel(q_ref, new_ref, pages_ref, table_ref, lengths_ref, out_ref, top_ref, sum_ref, s_ref, fresh_ref):
-        blocks = head_blocks(q_ref[...])
-        held = tokens_of_pages(table_ref[...], lengths_ref[...], 0, page_len)
-        fresh_ref[...] = jnp.zeros_like(fresh_ref)
-        fresh_ref[0:requests] = new_ref[...]
+    def kernel(
+        queries_hbm,
+        new_hbm,
+        pages_hbm,
+        table_hbm,
+        lengths_hbm,
+        out_ref,
+        top_ref,
+        sum_ref,
+        query_ref,
+        s_ref,
+        fresh_ref,
+        heads_ref,
+        flat_ref,
+        pages_ref,
+        table_ref,
+        lengths_ref,
+        sems,
+    ):
+        page_copies = [
+            pltpu.make_async_copy(
+                pages_hbm.at[pl.ds(c * chunk_pages, chunk_pages)],
+                pages_ref.at[pl.ds(c * chunk_pages, chunk_pages)],
+                sems.at[4 + c],
+            )
+            for c in range(chunks)
+        ]
+        copies = [
+            pltpu.make_async_copy(queries_hbm, flat_ref, sems.at[0]),
+            pltpu.make_async_copy(table_hbm, table_ref, sems.at[1]),
+            pltpu.make_async_copy(lengths_hbm, lengths_ref, sems.at[2]),
+            pltpu.make_async_copy(new_hbm, fresh_ref.at[pl.ds(0, requests)], sems.at[3]),
+        ]
+        fresh_ref[requests:] = jnp.zeros_like(fresh_ref[requests:])
+        for copy in copies + page_copies:
+            copy.start()
+        for copy in copies:
+            copy.wait()
+        for h in range(HEADS):
+            heads_ref[pl.ds(h, requests, stride=HEADS), :] = flat_ref[
+                :, h * 128 : (h + 1) * 128
+            ].astype(jnp.float32)
+        query = heads_ref[...].astype(jnp.bfloat16)
+        query_ref[...] = query
+        blocks = head_blocks(query)
+        held = tokens_of_pages(table_ref[...], lengths_ref, 0, page_len)
         lane = lax.broadcasted_iota(jnp.int32, (requests, 128), 1)
         own = lax.broadcasted_iota(jnp.int32, (requests, 128), 0)
         fresh_bias = jnp.where(lane == own, 0.0, masked_score)
@@ -153,6 +209,7 @@
         s_ref[:, chunks * chunk :] = fresh
         top = fresh
         for c in range(chunks):
+            page_copies[c].wait()
             keys = pages_ref[c * chunk_pages : (c + 1) * chunk_pages, :, :half].reshape(chunk, half)
             bias = token_bias(held, c * chunk_pages, chunk, page_len)
             scores = masked_scores(blocks, keys, bias, scaling)
@@ -178,12 +235,18 @@
     shape = jax.ShapeDtypeStruct((rows, 128), jnp.float32)
     return pl.pallas_call(
         kernel,
-        out_shape=(shape, shape, shape),
-        in_specs=[VMEM] * 5,
-        out_specs=(VMEM,) * 3,
+        out_shape=(shape, shape, shape, jax.ShapeDtypeStruct((rows, 128), jnp.bfloat16)),
+        in_specs=[HBM] * 5,
+        out_specs=(VMEM,) * 4,
         scratch_shapes=[
             pltpu.VMEM((rows, chunks * chunk + 128), jnp.float32),
             pltpu.VMEM((128, kv_width), jnp.bfloat16),
+            pltpu.VMEM((rows, 128), jnp.float32),
+            pltpu.VMEM(queries.shape, jnp.bfloat16),
+            pltpu.VMEM(pages.shape, jnp.bfloat16),
+            pltpu.VMEM(table.shape, jnp.int32),
+            pltpu.SMEM(lengths.shape, jnp.int32),
+            pltpu.SemaphoreType.DMA((4 + chunks,)),
         ],
         compiler_params=pltpu.CompilerParams(vmem_limit_bytes=24 * MEBI),
         cost_estimate=pl.CostEstimate(
@@ -192,10 +255,215 @@
             transcendentals=rows * chunks * chunk,
         ),
         name="own_attention",
-    )(query, new_kv, pages, table, lengths)
-
-
-def finish_attention(query, fetched, table, lengths, partial, residual, gain, pages_own):
+    )(*[in_hbm(value) for value in (queries, new_kv, pages, table, lengths)])
+
+
+def routing_columns(ids, gates):
+    top_count = ids.shape[0]
+    high = gates.astype(jnp.bfloat16)
+    rest = gates - high.astype(jnp.float32)
+    middle = rest.astype(jnp.bfloat16)
+    low = (rest - middle.astype(jnp.float32)).astype(jnp.bfloat16)
+    source = lax.broadcasted_iota(jnp.int32, (top_count, 128), 0)
+    lane = lax.broadcasted_iota(jnp.int32, (top_count, 128), 1)
+    columns = 0.0
+    for i, part in enumerate((ids.astype(jnp.float32).astype(jnp.bfloat16), high, middle, low)):
+        place = (lane == source + i * top_count).astype(jnp.bfloat16)
+        columns = columns + lax.dot_general(
+            part, place, (((0,), (0,)), ((), ())), preferred_element_type=jnp.float32
+        )
+    return columns.astype(jnp.bfloat16)
+
+
+def stacked(parts):
+    if len(parts) == 1:
+        return parts[0]
+    return jnp.concatenate(parts, axis=0)
+
+
+def run_experts(groups, others, gate_up, down_proj, expert, top_count, slots):
+    model_dim, double = gate_up.shape[1:]
+    hidden_dim = double // 2
+    chips = len(groups[0])
+    flat = [part for group in groups for chip in group for part in chip]
+    shares = [sum(part.shape[0] for part in group[0]) for group in groups]
+    rows = sum(part.shape[0] for part in flat) + sum(other.shape[0] for other in others)
+    width = 256
+    up_steps = hidden_dim // width
+    out_width = 1024 if rows <= 512 else 512
+    out_steps = model_dim // out_width
+    strip = 256
+
+    def kernel(expert_ref, *refs):
+        own_refs, refs = refs[: len(flat)], refs[len(flat) :]
+        other_refs, refs = refs[: len(others)], refs[len(others) :]
+        up_hbm, down_hbm, refs = refs[0], refs[1], refs[2:]
+        out_refs, refs = refs[: chips * len(groups)], refs[chips * len(groups) :]
+        over_refs, refs = refs[: len(groups)], refs[len(groups) :]
+        up_ref, down_ref, tokens_ref, hidden_ref, sems = refs
+        up_copies, down_copies = [], []
+        for c in range(up_steps):
+            pair = []
+            for half in range(2):
+                columns = pl.ds(half * hidden_dim + c * width, width)
+                pair.append(
+                    pltpu.make_async_copy(
+                        up_hbm.at[0, :, columns], up_ref.at[:, columns], sems.at[2 * c + half]
+                    )
+                )
+                pair[-1].start()
+            up_copies.append(pair)
+        for c in range(out_steps):
+            columns = pl.ds(c * out_width, out_width)
+            down_copies.append(
+                pltpu.make_async_copy(
+                    down_hbm.at[0, :, columns], down_ref.at[:, columns], sems.at[2 * up_steps + c]
+                )
+            )
+            down_copies[-1].start()
+
+        token_refs = list(own_refs) + list(other_refs)
+        routing = stacked([ref[:, model_dim:] for ref in token_refs]).astype(jnp.float32)
+        wanted = expert_ref[0].astype(jnp.float32)
+        match = jnp.zeros((rows, 1), jnp.float32)
+        gates = [jnp.zeros((rows, 1), jnp.float32)] * 3
+        for k in range(top_count):
+            hit = routing[:, k : k + 1] == wanted
+            match = jnp.where(hit, 1.0, match)
+            gates = [
+                jnp.where(hit, routing[:, i * top_count + k : i * top_count + k + 1], gate)
+                for i, gate in enumerate(gates, 1)
+            ]
+        lane = lax.broadcasted_iota(jnp.int32, (rows, slots), 1)
+        match = jnp.broadcast_to(match, (rows, slots))
+        earlier = (
+            lax.broadcasted_iota(jnp.int32, (strip, strip), 0)
+            > lax.broadcasted_iota(jnp.int32, (strip, strip), 1)
+        ).astype(jnp.bfloat16)
+        ranks, before = [], jnp.zeros((1, slots), jnp.float32)
+        for start in range(0, rows, strip):
+            piece = match[start : start + strip]
+            ranks.append(
+                before
+                + jnp.dot(earlier, piece.astype(jnp.bfloat16), preferred_element_type=jnp.float32)
+            )
+            before = before + jnp.sum(piece, axis=0, keepdims=True)
+        rank = stacked(ranks)
+        choice = jnp.where(rank == lane.astype(jnp.float32), match, 0.0)
+        pick = choice.T.astype(jnp.bfloat16)
+        place = choice.astype(jnp.bfloat16)
+        gate_columns = jnp.where(
+            lane == 0, gates[0], jnp.where(lane == 1, gates[1], jnp.where(lane == 2, gates[2], 0.0))
+        ).astype(jnp.bfloat16)
+        gate = jnp.sum(
+            jnp.dot(pick, gate_columns, preferred_element_type=jnp.float32), axis=1, keepdims=True
+        )
+        for start in range(0, model_dim, out_width):
+            columns = slice(start, start + out_width)
+            tokens = stacked([ref[:, columns] for ref in token_refs])
+            tokens_ref[:, columns] = jnp.dot(
+                pick, tokens, preferred_element_type=jnp.float32
+            ).astype(jnp.bfloat16)
+
+        for c in range(up_steps):
+            for copy in up_copies[c]:
+                copy.wait()
+            start = c * width
+            tokens = tokens_ref[...]
+            gated = jnp.dot(
+                tokens, up_ref[:, start : start + width], preferred_element_type=jnp.float32
+            )
+            up = jnp.dot(
+                tokens,
+                up_ref[:, hidden_dim + start : hidden_dim + start + width],
+                preferred_element_type=jnp.float32,
+            )
+            hidden_ref[:, start : start + width] = (gated / (1.0 + jnp.exp(-gated)) * up).astype(
+                jnp.bfloat16
+            )
+
+        for c in range(out_steps):
+            down_copies[c].wait()
+            columns = slice(c * out_width, (c + 1) * out_width)
+            result = jnp.dot(
+                hidden_ref[...], down_ref[:, columns], preferred_element_type=jnp.float32
+            )
+            result = (result * gate).astype(jnp.bfloat16)
+            sums = jnp.dot(place, result, preferred_element_type=jnp.float32).astype(jnp.bfloat16)
+            offset = 0
+            for i, ref in enumerate([*out_refs, *over_refs]):
+                cut = ref.shape[0]
+                ref[:, columns] = sums[offset : offset + cut]
+                offset += cut
+
+    shapes = [(share, model_dim) for share in shares for _ in range(chips)]
+    shapes += [(other.shape[0], model_dim) for other in others]
+    results = pl.pallas_call(
+        kernel,
+        out_shape=tuple(jax.ShapeDtypeStruct(shape, jnp.bfloat16) for shape in shapes),
+        in_specs=[SMEM] + [VMEM] * (len(flat) + len(others)) + [HBM] * 2,
+        out_specs=(VMEM,) * len(shapes),
+        scratch_shapes=[
+            pltpu.VMEM((model_dim, double), jnp.bfloat16),
+            pltpu.VMEM((hidden_dim, model_dim), jnp.bfloat16),
+            pltpu.VMEM((slots, model_dim), jnp.bfloat16),
+            pltpu.VMEM((slots, hidden_dim), jnp.bfloat16),
+            pltpu.SemaphoreType.DMA((2 * up_steps + out_steps,)),
+        ],
+        compiler_params=pltpu.CompilerParams(vmem_limit_bytes=38 * MEBI),
+        cost_estimate=pl.CostEstimate(
+            flops=6 * slots * model_dim * hidden_dim,
+            bytes_accessed=20 * MEBI,
+            transcendentals=slots * hidden_dim,
+        ),
+        name="run_experts",
+    )(expert, *flat, *others, in_hbm(gate_up), in_hbm(down_proj))
+    mine = [results[g * chips : (g + 1) * chips] for g in range(len(groups))]
+    return mine, results[chips * len(groups) :]
+
+
+def add_up(parts, cuts, name):
+    rows = sum(cuts)
+    model_dim = parts[0][0].shape[1]
+    counts = [len(part) for part in parts]
+    flat = [piece for part in parts for piece in part]
+
+    def kernel(*refs):
+        in_refs, out_refs = refs[: len(flat)], refs[len(flat) :]
+        step = 1024
+        for start in range(0, model_dim, step):
+            columns = slice(start, start + step)
+            offset = 0
+            for i, (out_ref, cut) in enumerate(zip(out_refs, cuts)):
+                total = 0.0
+                first = 0
+                for count in counts:
+                    pieces = in_refs[first : first + count]
+                    first += count
+                    if count > 1:
+                        piece = pieces[i][:, columns]
+                    else:
+                        piece = pieces[0][offset : offset + cut, columns]
+                    total = total + piece.astype(jnp.float32)
+                out_ref[:, columns] = total.astype(jnp.bfloat16)
+                offset += cut
+
+    return pl.pallas_call(
+        kernel,
+        out_shape=tuple(jax.ShapeDtypeStruct((cut, model_dim), jnp.bfloat16) for cut in cuts),
+        in_specs=[VMEM] * len(flat),
+        out_specs=(VMEM,) * len(cuts),
+        compiler_params=pltpu.CompilerParams(vmem_limit_bytes=12 * MEBI),
+        cost_estimate=pl.CostEstimate(
+            flops=rows * model_dim, bytes_accessed=2 * rows * model_dim, transcendentals=0
+        ),
+        name=name,
+    )(*flat)
+
+
+def finish_attention(
+    query, fetched, table, lengths, partial, residual, gain, ids, gates, pages_own
+):
     count, page_len, kv_width = fetched.shape
     half = kv_width // 2
     tokens = count * page_len
@@ -203,9 +471,9 @@
     rows = query.shape[0]
     scaling = 1.0 / math.sqrt(HEAD_DIMENSION)
 
-    def kernel(q_ref, fetched_ref, table_ref, lengths_ref, sum_ref, top_ref, total_ref, residual_ref, gain_ref, attended_ref, merged_ref, normed_ref, heads_ref):
+    def kernel(q_ref, fetched_ref, table_ref, lengths_ref, sum_ref, top_ref, total_ref, residual_ref, gain_ref, ids_ref, gates_ref, attended_ref, merged_ref, normed_ref, heads_ref):
         blocks = head_blocks(q_ref[...])
-        held = tokens_of_pages(table_ref[...], lengths_ref[...], pages_own, page_len)
+        held = tokens_of_pages(table_ref[...], lengths_ref, pages_own, page_len)
         bias = token_bias(held, 0, tokens, page_len)
         keys = fetched_ref[:, :, :half].reshape(tokens, half)
         values = fetched_ref[:, :, half:].reshape(tokens, half)
@@ -234,15 +502,16 @@
             square = square + wide * wide
         mean = jnp.sum(square, axis=1, keepdims=True) * (1.0 / model_dim)
         inverse = lax.rsqrt(mean + epsilon)
-        normed_ref[...] = (
+        normed_ref[:, model_dim:] = routing_columns(ids_ref[...], gates_ref[...])
+        normed_ref[:, :model_dim] = (
             merged_ref[...].astype(jnp.float32) * inverse * gain_ref[...]
         ).astype(jnp.bfloat16)
 
     shape = jax.ShapeDtypeStruct((requests, model_dim), jnp.bfloat16)
     return pl.pallas_call(
         kernel,
-        out_shape=(shape, shape, shape),
-        in_specs=[VMEM] * 9,
+        out_shape=(shape, shape, jax.ShapeDtypeStruct((requests, model_dim + 128), jnp.bfloat16)),
+        in_specs=[VMEM] * 3 + [SMEM] + [VMEM] * 7,
         out_specs=(VMEM,) * 3,
         scratch_shapes=[pltpu.VMEM((rows, 128), jnp.float32)],
         compiler_params=pltpu.CompilerParams(vmem_limit_bytes=16 * MEBI),
@@ -250,29 +519,7 @@
             flops=4 * rows * half * tokens, bytes_accessed=4 * MEBI, transcendentals=rows * tokens
         ),
         name="finish_attention",
-    )(query, fetched, table, lengths, *partial, residual, gain)
-
-
-def expert_block(tokens, gate_up, down_proj):
-    hidden_dim = down_proj.shape[0]
-    product = jnp.dot(tokens, gate_up, preferred_element_type=jnp.float32)
-    hidden = (jax.nn.silu(product[:, :hidden_dim]) * product[:, hidden_dim:]).astype(jnp.bfloat16)
-    return jnp.dot(hidden, down_proj, preferred_element_type=jnp.float32).astype(jnp.bfloat16)
-
-
-def slot_choice(ids, experts, capacity):
-    match = jnp.any(ids[:, :, None, :] == experts[None, None, :, None], axis=-1)
-    rank = jnp.cumsum(match.astype(jnp.int32), axis=1) - 1
-    slots = jnp.arange(capacity, dtype=jnp.int32)
-    chosen = match[..., None] & (rank[..., None] == slots)
-    return jnp.transpose(chosen, (2, 0, 3, 1)).astype(jnp.float32)
-
-
-def spread(choice):
-    members, blocks, capacity, rows = choice.shape
-    own = jnp.eye(blocks, dtype=choice.dtype)
-    full = choice[:, :, :, None, :] * own[None, :, None, :, None]
-    return full.reshape(members * blocks * capacity, blocks * rows)
+    )(query, fetched, table, lengths, *partial, residual, gain, ids, gates)
 
 
 def local(
@@ -296,65 +543,67 @@
     planes = layout.planes
 
     requested = from_behind(shed_slots, "pool", 1)
-    fetched = from_behind(pick_pages(requested, kv_pages), "pool", 1)
-
-    routing = jnp.concatenate([expert_ids.astype(jnp.float32), gate_weights], axis=1)
-    routing, requested = lax.optimization_barrier((routing, requested))
-    routing = jnp.stack([layout.shifted(routing, s) for s in range(planes)])
-    ids = routing[:, :, :top_count].astype(jnp.int32)
-    gates = routing[:, :, top_count:]
-    plane = lax.axis_index("dev") // layout.inner
-    experts = layout.linear(jnp.arange(layout.members, dtype=jnp.int32), plane)
-    choice = slot_choice(ids, experts, capacity)
-    gate_of = jnp.sum(
-        jnp.where(ids[:, :, None, :] == experts[None, None, :, None], gates[:, :, None, :], 0.0),
-        axis=-1,
-    )
-    mixing = choice * gate_of.transpose(2, 0, 1)[:, :, None, :]
-
-    query = queries.reshape(count_of_rows * HEADS, HEAD_DIMENSION)
-    lengths_column = lengths.reshape(count_of_rows, 1)
-    partial = own_attention(query, new_kv, kv_pages, page_table, lengths_column)
+    picked = pick_pages(requested, kv_pages)
+    fetched = from_behind(picked, "pool", 1)
+    queries, expert_ids, picked = lax.optimization_barrier((queries, expert_ids, picked))
+
+    expert = (lax.axis_index("pool") * layout.dev + lax.axis_index("dev")).reshape(1)
+    *partial, query = own_attention(queries, new_kv, kv_pages, page_table, lengths)
     attended, merged, normed = finish_attention(
         query,
         fetched,
         page_table,
-        lengths_column,
+        lengths,
         partial,
         residual,
         norm_gain.reshape(1, model_dim),
+        expert_ids.T,
+        gate_weights.T,
         kv_pages.shape[0],
     )
 
     first = max(1, planes // 4)
     groups = [range(0, first), range(first, 2 * first), range(2 * first, planes)]
+    chips = range(0, layout.members, 2)
     blocks = [layout.shifted(normed, s) for s in range(planes)]
     arrived = []
     for group in groups:
-        rows = jnp.concatenate([blocks[s] for s in group], axis=0)
-        pick = spread(choice[:, group.start : group.stop]).astype(jnp.bfloat16)
-        outgoing = jnp.dot(pick, rows, preferred_element_type=jnp.float32).astype(jnp.bfloat16)
-        arrived.append(layout.exchanged(outgoing))
-    finished = expert_block(jnp.concatenate(arrived, axis=0), w_gate_up[0], w_down[0])
-    pieces, start = [], 0
-    for part in arrived:
-        pieces.append(finished[start : start + part.shape[0]])
-        start += part.shape[0]
-    sums = []
-    for group, piece in list(zip(groups, pieces))[::-1]:
-        returned = layout.exchanged(piece)
-        mix = spread(mixing[:, group.start : group.stop])
-        coarse = lax.reduce_precision(mix, 8, 7)
-        both = jnp.concatenate([coarse, mix - coarse], axis=1).astype(jnp.bfloat16)
-        summed = lax.dot_general(
-            both, returned, (((0,), (0,)), ((), ())), preferred_element_type=jnp.float32
+        rows = stacked([blocks[s] for s in group])
+        arrived.append([layout.swapped(rows, chip) for chip in chips])
+    rows = [
+        [[arrived[0][c], arrived[1][c]] for c in range(len(chips))],
+        [[arrived[2][c]] for c in range(len(chips))],
+    ]
+    others = [layout.swapped(stacked([part for chip in own for part in chip]), 1) for own in rows]
+    mine, over = [], []
+    for some in ((0, 1),) if planes <= 4 else ((0,), (1,)):
+        slots = capacity * sum(
+            part.shape[0] for g in some for chip in rows[g] for part in chip
+        ) * 2 // count_of_rows
+        results = run_experts(
+            [rows[g] for g in some],
+            [others[g] for g in some],
+            w_gate_up,
+            w_down,
+            expert,
+            top_count,
+            slots,
         )
-        half = summed.shape[0] // 2
-        summed = (summed[:half] + summed[half:]).astype(jnp.bfloat16)
-        for i, s in enumerate(group):
-            sums.append(layout.shifted(summed[i * count_of_rows : (i + 1) * count_of_rows], -s))
-    expert_sum = sum(part.astype(jnp.float32) for part in sums)
-    layer_out = (merged.astype(jnp.float32) + expert_sum).astype(jnp.bfloat16)
+        mine += results[0]
+        over += results[1]
+    finished = []
+    for parts, sent in zip(mine, over):
+        back = layout.swapped(sent, 1)
+        sums = add_up([parts, [back]], [part.shape[0] for part in parts], "add_cores")
+        finished.append([layout.swapped(part, chip) for part, chip in zip(sums, chips)])
+    near, far = finished
+    others = []
+    for parts, shifts in ((far, groups[2]), (near, [*groups[0], *groups[1]])):
+        cuts = [count_of_rows] * len(shifts)
+        sums = add_up([[part] for part in parts], cuts, "add_chips")
+        others += [layout.shifted(part, s) for part, s in zip(sums, shifts)]
+    total = merged.astype(jnp.float32) + sum(part.astype(jnp.float32) for part in others)
+    layer_out = total.astype(jnp.bfloat16)
     return (attended, layer_out)
 
 

time: 139 us -> 115 us (0.83)
  blocking collectives: 17.4 us -> 0 us
  matrix products: 12.1 us -> 0 us
  local copies, waits for them, and re-layouts: 7.25 us -> 15 us
  waiting for transfers between devices: 48.4 us -> 40.9 us
  Pallas kernels: 14.4 us -> 21.3 us
  other arithmetic: 2.8 us -> 0.74 us
  starting transfers between devices: 34.9 us -> 36.3 us
    all_to_all x5 -> x0, waiting for transfers between devices: 31.5 us -> none  [exchanged(): lax.all_to_all(value, AXES, 0, 0, axis_index_groups=self.groups, tiled=True)]
    ppermute x0 -> x19, waiting for transfers between devices: none -> 29.2 us  [swapped(): return lax.ppermute(value, AXES, pairs)]
    ppermute x0 -> x19, starting transfers between devices: none -> 21.4 us  [swapped(): return lax.ppermute(value, AXES, pairs)]
    all_to_all x5 -> x0, starting transfers between devices: 18.2 us -> none  [exchanged(): lax.all_to_all(value, AXES, 0, 0, axis_index_groups=self.groups, tiled=True)]
    all_to_all x1 -> x0, blocking collectives: 17.4 us -> none  [exchanged(): lax.all_to_all(value, AXES, 0, 0, axis_index_groups=self.groups, tiled=True)]
    pallas_call x2 -> x7, Pallas kernels: 4.56 us -> 19.7 us  [the longest x1 12.3 us: run_experts(): pl.pallas_call(kernel, out_shape=tuple((jax.ShapeDtypeStruct(shape, jnp.b...]
    dot_general x8 -> x0, matrix products: 12.1 us -> none  [the longest x1 6.56 us: expert_block(): product = jnp.dot(tokens, gate_up, preferred_element_type=jnp.float32)]
    unnamed x18 -> x51, local copies, waits for them, and re-layouts: 3.04 us -> 13.6 us
  transfers between devices with their start and end apart: 16 -> 27, of which waited for: 8 -> 16; matrix products, arithmetic and copies ran while one was open for 6% -> 8% of each run, Pallas kernels for 9% -> 5%
where the time goes in v5:
time: 115 us
  waiting for transfers between devices  40.9 us (36%)
  starting transfers between devices  36.3 us (32%)
  Pallas kernels  21.3 us (19%)
  local copies, waits for them, and re-layouts  15 us (13%)
    ppermute x19, waiting for transfers between devices, swapped(): return lax.ppermute(value, AXES, pairs)  29.2 us
    ppermute x19, starting transfers between devices, swapped(): return lax.ppermute(value, AXES, pairs)  21.4 us
    unnamed x51, local copies, waits for them, and re-layouts  13.6 us
    pallas_call x1, Pallas kernels, run_experts(): pl.pallas_call(kernel, out_shape=tuple((jax.ShapeDtypeStruct(shape, jnp.b...  12.3 us
    ppermute x6, starting transfers between devices, shifted(): return lax.ppermute(value, AXES, pairs)  9.81 us
    ppermute x6, waiting for transfers between devices, shifted(): return lax.ppermute(value, AXES, pairs)  9.67 us
    ppermute x2, starting transfers between devices, from_behind(): lax.ppermute(value, axis, [(i, (i + by) % length) for i in range(length)])  5.09 us
    pallas_call x1, Pallas kernels, own_attention(): pl.pallas_call(kernel, out_shape=(shape, shape, shape, jax.ShapeDtypeStru...  4.74 us
  transfers between devices with their start and end apart: 27, of which 16 were waited for; matrix products, arithmetic and copies ran while one was open for 8% of the time, Pallas kernels for 5%

profile of v5, /device:TPU:0, one launch (start us, length us, event | category | flops | bytes accessed | tf_op | source)
XLA Modules:
  0.0 115.1 jit_solution(138960349080849936)
XLA Ops:
  0.6 3.0 %collective-permute-start = (s32[16]{0:T(128)}, s32[16]{0:T(128)S(1)}, u32[]{:S(2)}, u32[]{:S(2)}) collective-permute-start(s32[16]{0:T(128)} %param.17), channel_id=1, source_target_pairs={{0,16},{16,0},{1,17},{17,1},{2,18},{18,2},{3,19},{19,3},{4,20},{20... | collective-permute-start | bytes 200 | tf_op jit(solution)/shard_map/ppermute | solution.py:65
  3.6 1.7 %collective-permute-done.slots_ref = s32[16]{0:T(128)S(1)} collective-permute-done((s32[16]{0:T(128)}, s32[16]{0:T(128)S(1)}, u32[]{:S(2)}, u32[]{:S(2)}) %collective-permute-start) | collective-permute-done | bytes 96 | tf_op jit(solution)/shard_map/ppermute | solution.py:65
  5.3 1.6 %pick_pages.1 = bf16[16,16,512]{2,1,0:T(8,128)(2,1)S(1)} custom-call(s32[16]{0:T(128)S(1)} %collective-permute-done.slots_ref, bf16[128,16,512]{2,1,0:T(8,128)(2,1)} %pages_hbm.1), custom_call_target="tpu_custom_call" | custom-call | bytes 1048576 | tf_op jit(solution)/shard_map/pick_pages/pallas_call | solution.py:81
  7.0 2.1 %collective-permute-start.1 = (bf16[16,16,512]{2,1,0:T(8,128)(2,1)S(1)}, bf16[16,16,512]{2,1,0:T(8,128)(2,1)S(1)}, u32[]{:S(2)}, u32[]{:S(2)}) collective-permute-start(bf16[16,16,512]{2,1,0:T(8,128)(2,1)S(1)} %pick_pages.1), channel_id=1, source_target_pairs={{0,16},{16,0},{1,17},{17,1},{2,18},{18,2},{3,19},{19,3},{4,20},{20... | collective-permute-start | bytes 786440 | tf_op jit(solution)/shard_map/ppermute | solution.py:65
  9.0 4.7 %own_attention.1 = (f32[512,128]{1,0:T(8,128)S(1)}, f32[512,128]{1,0:T(8,128)S(1)}, f32[512,128]{1,0:T(8,128)S(1)}, bf16[512,128]{1,0:T(8,128)(2,1)S(1)}) custom-call(bf16[16,4096]{1,0:T(8,128)(2,1)} %queries_hbm, bf16[16,512]{1,0:T(8,128)(2,1)} %new_hbm.1, bf16[128,16,512]{2,1,0:T(8,128)(2,1)} %pages_hbm.1, s32[16,16]{1,0:T(8,128)} %table_ref.1, s32[16]{0:T(128)} %lengths_ref.1), custom_call_target="tpu_custom_call" | custom-call | flops 1073741824 | bytes 16777216 | tf_op jit(solution)/shard_map/own_attention/pallas_call | solution.py:236
  14.2 1.9 %finish_attention.1 = (bf16[16,4096]{1,0:T(8,128)(2,1)}, bf16[16,4096]{1,0:T(8,128)(2,1)S(1)}, bf16[16,4224]{1,0:T(8,128)(2,1)S(1)}) custom-call(bf16[512,128]{1,0:T(8,128)(2,1)S(1)} %get-tuple-element.34.q_ref, bf16[16,16,512]{2,1,0:T(8,128)(2,1)S(1)} %collective-permute-done.1.fetched_ref, s32[16,16]{1,0:T(8,128)S(1)} %copy-done.16, s32[16]{0:T(128)S(1)} %copy-done.19, ...), custom_call_target="tpu_custom_call" | custom-call | flops 134217728 | bytes 4194304 | tf_op jit(solution)/shard_map/finish_attention/pallas_call | solution.py:511
  16.2 3.9 %collective-permute-start.10 = (bf16[16,4224]{1,0:T(8,128)(2,1)S(1)}, bf16[16,4224]{1,0:T(8,128)(2,1)S(1)}, u32[]{:S(2)}, u32[]{:S(2)}) collective-permute-start(bf16[16,4224]{1,0:T(8,128)(2,1)S(1)} %get-tuple-element.41.refs_0_), channel_id=1, source_target_pairs={{0,12},{1,13},{2,14},{3,15},{16,28},{17,29},{18,30},{19,31},{4,8},... | collective-permute-start | bytes 405512 | tf_op jit(solution)/shard_map/ppermute | solution.py:50
  20.0 2.4 %collective-permute-start.7 = (bf16[16,4224]{1,0:T(8,128)(2,1)S(1)}, bf16[16,4224]{1,0:T(8,128)(2,1)S(1)}, u32[]{:S(2)}, u32[]{:S(2)}) collective-permute-start(bf16[16,4224]{1,0:T(8,128)(2,1)S(1)} %get-tuple-element.41.refs_0_), channel_id=1, source_target_pairs={{0,18},{1,19},{2,16},{3,17},{16,2},{17,3},{18,0},{19,1},{4,22},{5,... | collective-permute-start | bytes 405512 | tf_op jit(solution)/shard_map/ppermute | solution.py:60
  24.2 5.2 %collective-permute-done.9 = bf16[16,4224]{1,0:T(8,128)(2,1)S(1)} collective-permute-done((bf16[16,4224]{1,0:T(8,128)(2,1)S(1)}, bf16[16,4224]{1,0:T(8,128)(2,1)S(1)}, u32[]{:S(2)}, u32[]{:S(2)}) %collective-permute-start.9) | collective-permute-done | bytes 135200 | tf_op jit(solution)/shard_map/ppermute | solution.py:50
  30.7 2.4 %collective-permute-start.13 = (bf16[32,4224]{1,0:T(8,128)(2,1)S(1)}, bf16[32,4224]{1,0:T(8,128)(2,1)S(1)}, u32[]{:S(2)}, u32[]{:S(2)}) collective-permute-start(bf16[32,4224]{1,0:T(8,128)(2,1)S(1)} %get-tuple-element.65.refs_8_), channel_id=1, source_target_pairs={{0,18},{1,19},{2,16},{3,17},{16,2},{17,3},{18,0},{19,1},{4,22},{5,... | collective-permute-start | bytes 811016 | tf_op jit(solution)/shard_map/ppermute | solution.py:60
  33.2 1.2 %collective-permute-done.2.refs_1_ = bf16[16,4224]{1,0:T(8,128)(2,1)S(1)} collective-permute-done((bf16[16,4224]{1,0:T(8,128)(2,1)S(1)}, bf16[16,4224]{1,0:T(8,128)(2,1)S(1)}, u32[]{:S(2)}, u32[]{:S(2)}) %collective-permute-start.2) | collective-permute-done | bytes 135200 | tf_op jit(solution)/shard_map/ppermute | solution.py:50
  34.4 1.5 %collective-permute-start.12 = (bf16[32,4224]{1,0:T(8,128)(2,1)S(1)}, bf16[32,4224]{1,0:T(8,128)(2,1)S(1)}, u32[]{:S(2)}, u32[]{:S(2)}) collective-permute-start(bf16[32,4224]{1,0:T(8,128)(2,1)S(1)} %get-tuple-element.65.refs_8_), channel_id=1, source_target_pairs={{0,16},{1,17},{2,18},{3,19},{16,0},{17,1},{18,2},{19,3},{4,20},{5,... | collective-permute-start | bytes 811016 | tf_op jit(solution)/shard_map/ppermute | solution.py:60
  36.6 1.5 %collective-permute-start.4 = (bf16[16,4224]{1,0:T(8,128)(2,1)S(1)}, bf16[16,4224]{1,0:T(8,128)(2,1)S(1)}, u32[]{:S(2)}, u32[]{:S(2)}) collective-permute-start(bf16[16,4224]{1,0:T(8,128)(2,1)S(1)} %collective-permute-done.2.refs_1_), channel_id=1, source_target_pairs={{0,2},{1,3},{2,0},{3,1},{16,18},{17,19},{18,16},{19,17},{4,6},{5,7... | collective-permute-start | bytes 405512 | tf_op jit(solution)/shard_map/ppermute | solution.py:60
  38.8 3.3 %collective-permute-done.4.refs_3_ = bf16[16,4224]{1,0:T(8,128)(2,1)S(1)} collective-permute-done((bf16[16,4224]{1,0:T(8,128)(2,1)S(1)}, bf16[16,4224]{1,0:T(8,128)(2,1)S(1)}, u32[]{:S(2)}, u32[]{:S(2)}) %collective-permute-start.4) | collective-permute-done | bytes 135200 | tf_op jit(solution)/shard_map/ppermute | solution.py:60
  42.0 1.5 %collective-permute-start.11 = (bf16[32,4224]{1,0:T(8,128)(2,1)S(1)}, bf16[32,4224]{1,0:T(8,128)(2,1)S(1)}, u32[]{:S(2)}, u32[]{:S(2)}) collective-permute-start(bf16[32,4224]{1,0:T(8,128)(2,1)S(1)} %get-tuple-element.65.refs_8_), channel_id=1, source_target_pairs={{0,2},{1,3},{2,0},{3,1},{16,18},{17,19},{18,16},{19,17},{4,6},{5,7... | collective-permute-start | bytes 811016 | tf_op jit(solution)/shard_map/ppermute | solution.py:60
  44.2 1.5 %collective-permute-start.6 = (bf16[16,4224]{1,0:T(8,128)(2,1)S(1)}, bf16[16,4224]{1,0:T(8,128)(2,1)S(1)}, u32[]{:S(2)}, u32[]{:S(2)}) collective-permute-start(bf16[16,4224]{1,0:T(8,128)(2,1)S(1)} %collective-permute-done.2.refs_1_), channel_id=1, source_target_pairs={{0,16},{1,17},{2,18},{3,19},{16,0},{17,1},{18,2},{19,3},{4,20},{5,... | collective-permute-start | bytes 405512 | tf_op jit(solution)/shard_map/ppermute | solution.py:60
  46.4 2.9 %collective-permute-done.6.refs_5_ = bf16[16,4224]{1,0:T(8,128)(2,1)S(1)} collective-permute-done((bf16[16,4224]{1,0:T(8,128)(2,1)S(1)}, bf16[16,4224]{1,0:T(8,128)(2,1)S(1)}, u32[]{:S(2)}, u32[]{:S(2)}) %collective-permute-start.6) | collective-permute-done | bytes 135200 | tf_op jit(solution)/shard_map/ppermute | solution.py:60
  49.3 1.4 %collective-permute-start.8 = (bf16[16,4224]{1,0:T(8,128)(2,1)S(1)}, bf16[16,4224]{1,0:T(8,128)(2,1)S(1)}, u32[]{:S(2)}, u32[]{:S(2)}) collective-permute-start(bf16[16,4224]{1,0:T(8,128)(2,1)S(1)} %collective-permute-done.2.refs_1_), channel_id=1, source_target_pairs={{0,18},{1,19},{2,16},{3,17},{16,2},{17,3},{18,0},{19,1},{4,22},{5,... | collective-permute-start | bytes 405512 | tf_op jit(solution)/shard_map/ppermute | solution.py:60
  52.0 3.2 %collective-permute-done.8.refs_7_ = bf16[16,4224]{1,0:T(8,128)(2,1)S(1)} collective-permute-done((bf16[16,4224]{1,0:T(8,128)(2,1)S(1)}, bf16[16,4224]{1,0:T(8,128)(2,1)S(1)}, u32[]{:S(2)}, u32[]{:S(2)}) %collective-permute-start.8) | collective-permute-done | bytes 135200 | tf_op jit(solution)/shard_map/ppermute | solution.py:60
  59.4 2.3 %collective-permute-done.15.refs_13_ = bf16[128,4224]{1,0:T(8,128)(2,1)S(1)} collective-permute-done((bf16[128,4224]{1,0:T(8,128)(2,1)}, bf16[128,4224]{1,0:T(8,128)(2,1)S(1)}, u32[]{:S(2)}, u32[]{:S(2)}) %collective-permute-start.15) | collective-permute-done | bytes 1081376 | tf_op jit(solution)/shard_map/ppermute | solution.py:60
  67.2 12.3 %run_experts.1 = (bf16[32,4096]{1,0:T(8,128)(2,1)S(1)}, bf16[32,4096]{1,0:T(8,128)(2,1)S(1)}, bf16[32,4096]{1,0:T(8,128)(2,1)S(1)}, bf16[32,4096]{1,0:T(8,128)(2...) custom-call(s32[1]{0:T(128)} %bitcast.3.expert_ref, ...), custom_call_target="tpu_custom_call" | custom-call | flops 4831838208 | bytes 20971520 | tf_op jit(solution)/shard_map/run_experts/pallas_call | solution.py:401
  80.1 2.2 %collective-permute-done.16.refs_4_ = bf16[128,4096]{1,0:T(8,128)(2,1)S(1)} collective-permute-done((bf16[128,4096]{1,0:T(8,128)(2,1)S(1)}, bf16[128,4096]{1,0:T(8,128)(2,1)S(1)}, u32[]{:S(2)}, u32[]{:S(2)}) %collective-permute-start.16) | collective-permute-done | bytes 1048608 | tf_op jit(solution)/shard_map/ppermute | solution.py:60
  83.0 1.5 %collective-permute-start.18 = (bf16[32,4096]{1,0:T(8,128)(2,1)S(1)}, bf16[32,4096]{1,0:T(8,128)(2,1)S(1)}, u32[]{:S(2)}, u32[]{:S(2)}) collective-permute-start(bf16[32,4096]{1,0:T(8,128)(2,1)S(1)} %get-tuple-element.49), channel_id=1, source_target_pairs={{0,16},{1,17},{2,18},{3,19},{16,0},{17,1},{18,2},{19,3},{4,20},{5,... | collective-permute-start | bytes 786440 | tf_op jit(solution)/shard_map/ppermute | solution.py:60
  84.5 1.5 %collective-permute-start.19 = (bf16[32,4096]{1,0:T(8,128)(2,1)S(1)}, bf16[32,4096]{1,0:T(8,128)(2,1)S(1)}, u32[]{:S(2)}, u32[]{:S(2)}) collective-permute-start(bf16[32,4096]{1,0:T(8,128)(2,1)S(1)} %get-tuple-element.50), channel_id=1, source_target_pairs={{0,18},{1,19},{2,16},{3,17},{16,2},{17,3},{18,0},{19,1},{4,22},{5,... | collective-permute-start | bytes 786440 | tf_op jit(solution)/shard_map/ppermute | solution.py:60
  86.9 1.5 %collective-permute-start.24 = (bf16[32,4096]{1,0:T(8,128)(2,1)S(1)}, bf16[32,4096]{1,0:T(8,128)(2,1)S(1)}, u32[]{:S(2)}, u32[]{:S(2)}) collective-permute-start(bf16[32,4096]{1,0:T(8,128)(2,1)S(1)} %get-tuple-element.60), channel_id=1, source_target_pairs={{0,16},{1,17},{2,18},{3,19},{16,0},{17,1},{18,2},{19,3},{4,20},{5,... | collective-permute-start | bytes 786440 | tf_op jit(solution)/shard_map/ppermute | solution.py:60
  88.3 3.6 %collective-permute-done.17.refs_1_ = bf16[32,4096]{1,0:T(8,128)(2,1)S(1)} collective-permute-done((bf16[32,4096]{1,0:T(8,128)(2,1)S(1)}, bf16[32,4096]{1,0:T(8,128)(2,1)S(1)}, u32[]{:S(2)}, u32[]{:S(2)}) %collective-permute-start.17) | collective-permute-done | bytes 262176 | tf_op jit(solution)/shard_map/ppermute | solution.py:60
  91.9 1.4 %collective-permute-start.25 = (bf16[32,4096]{1,0:T(8,128)(2,1)S(1)}, bf16[32,4096]{1,0:T(8,128)(2,1)S(1)}, u32[]{:S(2)}, u32[]{:S(2)}) collective-permute-start(bf16[32,4096]{1,0:T(8,128)(2,1)S(1)} %get-tuple-element.61), channel_id=1, source_target_pairs={{0,18},{1,19},{2,16},{3,17},{16,2},{17,3},{18,0},{19,1},{4,22},{5,... | collective-permute-start | bytes 786440 | tf_op jit(solution)/shard_map/ppermute | solution.py:60
  93.3 5.5 %collective-permute-done.19.refs_3_ = bf16[32,4096]{1,0:T(8,128)(2,1)S(1)} collective-permute-done((bf16[32,4096]{1,0:T(8,128)(2,1)S(1)}, bf16[32,4096]{1,0:T(8,128)(2,1)S(1)}, u32[]{:S(2)}, u32[]{:S(2)}) %collective-permute-start.19) | collective-permute-done | bytes 262176 | tf_op jit(solution)/shard_map/ppermute | solution.py:60
  99.0 3.8 %collective-permute-start.20 = (bf16[16,4096]{1,0:T(8,128)(2,1)S(1)}, bf16[16,4096]{1,0:T(8,128)(2,1)S(1)}, u32[]{:S(2)}, u32[]{:S(2)}) collective-permute-start(bf16[16,4096]{1,0:T(8,128)(2,1)S(1)} %get-tuple-element.51), channel_id=1, source_target_pairs={{0,8},{1,9},{2,10},{3,11},{16,24},{17,25},{18,26},{19,27},{4,12},{... | collective-permute-start | bytes 393224 | tf_op jit(solution)/shard_map/ppermute | solution.py:50
  103.5 5.7 %collective-permute-done.25.refs_3_ = bf16[32,4096]{1,0:T(8,128)(2,1)S(1)} collective-permute-done((bf16[32,4096]{1,0:T(8,128)(2,1)S(1)}, bf16[32,4096]{1,0:T(8,128)(2,1)S(1)}, u32[]{:S(2)}, u32[]{:S(2)}) %collective-permute-start.25) | collective-permute-done | bytes 262176 | tf_op jit(solution)/shard_map/ppermute | solution.py:60
  109.3 1.8 %collective-permute-start.26 = (bf16[16,4096]{1,0:T(8,128)(2,1)S(1)}, bf16[16,4096]{1,0:T(8,128)(2,1)S(1)}, u32[]{:S(2)}, u32[]{:S(2)}) collective-permute-start(bf16[16,4096]{1,0:T(8,128)(2,1)S(1)} %get-tuple-element.63), channel_id=1, source_target_pairs={{0,4},{1,5},{2,6},{3,7},{16,20},{17,21},{18,22},{19,23},{4,0},{5,1... | collective-permute-start | bytes 393224 | tf_op jit(solution)/shard_map/ppermute | solution.py:50
  111.4 3.0 %collective-permute-done.26 = bf16[16,4096]{1,0:T(8,128)(2,1)S(1)} collective-permute-done((bf16[16,4096]{1,0:T(8,128)(2,1)S(1)}, bf16[16,4096]{1,0:T(8,128)(2,1)S(1)}, u32[]{:S(2)}, u32[]{:S(2)}) %collective-permute-start.26) | collective-permute-done | bytes 131104 | tf_op jit(solution)/shard_map/ppermute | solution.py:50
  (84 shorter events, 21.4 us)
Async XLA Ops:
  0.6 4.7 %collective-permute-start = (s32[16]{0:T(128)}, s32[16]{0:T(128)S(1)}, u32[]{:S(2)}, u32[]{:S(2)}) collective-permute-start(s32[16]{0:T(128)} %param.17), channel_id=1, source_target_pairs={{0,16},{16,0},{1,17},{17,1},{2,18},{18,2},{3,19},{19,3},{4,20},{20... | collective-permute-start | bytes 200 | tf_op jit(solution)/shard_map/ppermute | solution.py:65
  7.0 7.2 %collective-permute-start.1 = (bf16[16,16,512]{2,1,0:T(8,128)(2,1)S(1)}, bf16[16,16,512]{2,1,0:T(8,128)(2,1)S(1)}, u32[]{:S(2)}, u32[]{:S(2)}) collective-permute-start(bf16[16,16,512]{2,1,0:T(8,128)(2,1)S(1)} %pick_pages.1), channel_id=1, source_target_pairs={{0,16},{16,0},{1,17},{17,1},{2,18},{18,2},{3,19},{19,3},{4,20},{20... | collective-permute-start | bytes 786440 | tf_op jit(solution)/shard_map/ppermute | solution.py:65
  16.2 30.2 %copy-start.13 = (bf16[16,4096]{1,0:T(8,128)(2,1)}, bf16[16,4096]{1,0:T(8,128)(2,1)S(1)}, u32[]{:S(2)}) copy-start(bf16[16,4096]{1,0:T(8,128)(2,1)S(1)} %get-tuple-element.40) | copy-start | bytes 393220
  16.2 13.9 %collective-permute-start.10 = (bf16[16,4224]{1,0:T(8,128)(2,1)S(1)}, bf16[16,4224]{1,0:T(8,128)(2,1)S(1)}, u32[]{:S(2)}, u32[]{:S(2)}) collective-permute-start(bf16[16,4224]{1,0:T(8,128)(2,1)S(1)} %get-tuple-element.41.refs_0_), channel_id=1, source_target_pairs={{0,12},{1,13},{2,14},{3,15},{16,28},{17,29},{18,30},{19,31},{4,8},... | collective-permute-start | bytes 405512 | tf_op jit(solution)/shard_map/ppermute | solution.py:50
  20.0 9.4 %collective-permute-start.9 = (bf16[16,4224]{1,0:T(8,128)(2,1)S(1)}, bf16[16,4224]{1,0:T(8,128)(2,1)S(1)}, u32[]{:S(2)}, u32[]{:S(2)}) collective-permute-start(bf16[16,4224]{1,0:T(8,128)(2,1)S(1)} %get-tuple-element.41.refs_0_), channel_id=1, source_target_pairs={{0,8},{1,9},{2,10},{3,11},{16,24},{17,25},{18,26},{19,27},{4,12},{... | collective-permute-start | bytes 405512 | tf_op jit(solution)/shard_map/ppermute | solution.py:50
  20.0 31.3 %collective-permute-start.7 = (bf16[16,4224]{1,0:T(8,128)(2,1)S(1)}, bf16[16,4224]{1,0:T(8,128)(2,1)S(1)}, u32[]{:S(2)}, u32[]{:S(2)}) collective-permute-start(bf16[16,4224]{1,0:T(8,128)(2,1)S(1)} %get-tuple-element.41.refs_0_), channel_id=1, source_target_pairs={{0,18},{1,19},{2,16},{3,17},{16,2},{17,3},{18,0},{19,1},{4,22},{5,... | collective-permute-start | bytes 405512 | tf_op jit(solution)/shard_map/ppermute | solution.py:60
  22.5 21.8 %collective-permute-start.5 = (bf16[16,4224]{1,0:T(8,128)(2,1)S(1)}, bf16[16,4224]{1,0:T(8,128)(2,1)S(1)}, u32[]{:S(2)}, u32[]{:S(2)}) collective-permute-start(bf16[16,4224]{1,0:T(8,128)(2,1)S(1)} %get-tuple-element.41.refs_0_), channel_id=1, source_target_pairs={{0,16},{1,17},{2,18},{3,19},{16,0},{17,1},{18,2},{19,3},{4,20},{5,... | collective-permute-start | bytes 405512 | tf_op jit(solution)/shard_map/ppermute | solution.py:60
  23.0 13.5 %collective-permute-start.3 = (bf16[16,4224]{1,0:T(8,128)(2,1)S(1)}, bf16[16,4224]{1,0:T(8,128)(2,1)S(1)}, u32[]{:S(2)}, u32[]{:S(2)}) collective-permute-start(bf16[16,4224]{1,0:T(8,128)(2,1)S(1)} %get-tuple-element.41.refs_0_), channel_id=1, source_target_pairs={{0,2},{1,3},{2,0},{3,1},{16,18},{17,19},{18,16},{19,17},{4,6},{5,7... | collective-permute-start | bytes 405512 | tf_op jit(solution)/shard_map/ppermute | solution.py:60
  29.4 5.0 %collective-permute-start.2 = (bf16[16,4224]{1,0:T(8,128)(2,1)S(1)}, bf16[16,4224]{1,0:T(8,128)(2,1)S(1)}, u32[]{:S(2)}, u32[]{:S(2)}) collective-permute-start(bf16[16,4224]{1,0:T(8,128)(2,1)S(1)} %get-tuple-element.41.refs_0_), channel_id=1, source_target_pairs={{0,4},{1,5},{2,6},{3,7},{16,20},{17,21},{18,22},{19,23},{4,0},{5,1... | collective-permute-start | bytes 405512 | tf_op jit(solution)/shard_map/ppermute | solution.py:50
  30.7 27.2 %collective-permute-start.13 = (bf16[32,4224]{1,0:T(8,128)(2,1)S(1)}, bf16[32,4224]{1,0:T(8,128)(2,1)S(1)}, u32[]{:S(2)}, u32[]{:S(2)}) collective-permute-start(bf16[32,4224]{1,0:T(8,128)(2,1)S(1)} %get-tuple-element.65.refs_8_), channel_id=1, source_target_pairs={{0,18},{1,19},{2,16},{3,17},{16,2},{17,3},{18,0},{19,1},{4,22},{5,... | collective-permute-start | bytes 811016 | tf_op jit(solution)/shard_map/ppermute | solution.py:60
  34.4 20.8 %copy-start.4 = (bf16[16,4224]{1,0:T(8,128)(2,1)}, bf16[16,4224]{1,0:T(8,128)(2,1)S(1)}, u32[]{:S(2)}) copy-start(bf16[16,4224]{1,0:T(8,128)(2,1)S(1)} %collective-permute-done.2.refs_1_) | copy-start | bytes 405508
  34.4 22.8 %collective-permute-start.12 = (bf16[32,4224]{1,0:T(8,128)(2,1)S(1)}, bf16[32,4224]{1,0:T(8,128)(2,1)S(1)}, u32[]{:S(2)}, u32[]{:S(2)}) collective-permute-start(bf16[32,4224]{1,0:T(8,128)(2,1)S(1)} %get-tuple-element.65.refs_8_), channel_id=1, source_target_pairs={{0,16},{1,17},{2,18},{3,19},{16,0},{17,1},{18,2},{19,3},{4,20},{5,... | collective-permute-start | bytes 811016 | tf_op jit(solution)/shard_map/ppermute | solution.py:60
  36.6 5.5 %collective-permute-start.4 = (bf16[16,4224]{1,0:T(8,128)(2,1)S(1)}, bf16[16,4224]{1,0:T(8,128)(2,1)S(1)}, u32[]{:S(2)}, u32[]{:S(2)}) collective-permute-start(bf16[16,4224]{1,0:T(8,128)(2,1)S(1)} %collective-permute-done.2.refs_1_), channel_id=1, source_target_pairs={{0,2},{1,3},{2,0},{3,1},{16,18},{17,19},{18,16},{19,17},{4,6},{5,7... | collective-permute-start | bytes 405512 | tf_op jit(solution)/shard_map/ppermute | solution.py:60
  42.0 13.1 %copy-start.6 = (bf16[16,4224]{1,0:T(8,128)(2,1)}, bf16[16,4224]{1,0:T(8,128)(2,1)S(1)}, u32[]{:S(2)}) copy-start(bf16[16,4224]{1,0:T(8,128)(2,1)S(1)} %collective-permute-done.4.refs_3_) | copy-start | bytes 405508
  42.0 14.5 %collective-permute-start.11 = (bf16[32,4224]{1,0:T(8,128)(2,1)S(1)}, bf16[32,4224]{1,0:T(8,128)(2,1)S(1)}, u32[]{:S(2)}, u32[]{:S(2)}) collective-permute-start(bf16[32,4224]{1,0:T(8,128)(2,1)S(1)} %get-tuple-element.65.refs_8_), channel_id=1, source_target_pairs={{0,2},{1,3},{2,0},{3,1},{16,18},{17,19},{18,16},{19,17},{4,6},{5,7... | collective-permute-start | bytes 811016 | tf_op jit(solution)/shard_map/ppermute | solution.py:60
  44.2 10.9 %copy-start = (bf16[16,4224]{1,0:T(8,128)(2,1)}, bf16[16,4224]{1,0:T(8,128)(2,1)S(1)}, u32[]{:S(2)}) copy-start(bf16[16,4224]{1,0:T(8,128)(2,1)S(1)} %collective-permute-done.5.refs_4_) | copy-start | bytes 405508
  44.2 5.0 %collective-permute-start.6 = (bf16[16,4224]{1,0:T(8,128)(2,1)S(1)}, bf16[16,4224]{1,0:T(8,128)(2,1)S(1)}, u32[]{:S(2)}, u32[]{:S(2)}) collective-permute-start(bf16[16,4224]{1,0:T(8,128)(2,1)S(1)} %collective-permute-done.2.refs_1_), channel_id=1, source_target_pairs={{0,16},{1,17},{2,18},{3,19},{16,0},{17,1},{18,2},{19,3},{4,20},{5,... | collective-permute-start | bytes 405512 | tf_op jit(solution)/shard_map/ppermute | solution.py:60
  49.3 5.9 %collective-permute-start.8 = (bf16[16,4224]{1,0:T(8,128)(2,1)S(1)}, bf16[16,4224]{1,0:T(8,128)(2,1)S(1)}, u32[]{:S(2)}, u32[]{:S(2)}) collective-permute-start(bf16[16,4224]{1,0:T(8,128)(2,1)S(1)} %collective-permute-done.2.refs_1_), channel_id=1, source_target_pairs={{0,18},{1,19},{2,16},{3,17},{16,2},{17,3},{18,0},{19,1},{4,22},{5,... | collective-permute-start | bytes 405512 | tf_op jit(solution)/shard_map/ppermute | solution.py:60
  56.5 2.9 %collective-permute-start.14 = (bf16[128,4224]{1,0:T(8,128)(2,1)}, bf16[128,4224]{1,0:T(8,128)(2,1)S(1)}, u32[]{:S(2)}, u32[]{:S(2)}) collective-permute-start(bf16[128,4224]{1,0:T(8,128)(2,1)} %constant_dynamic-update-slice_fusion.2), channel_id=1, source_target_pairs={{0,1},{1,0},{2,3},{3,2},{16,17},{17,16},{18,19},{19,18},{4,5},{5,4... | collective-permute-start | bytes 3244040 | tf_op jit(solution)/shard_map/ppermute | solution.py:60
  58.7 3.1 %collective-permute-start.15 = (bf16[128,4224]{1,0:T(8,128)(2,1)}, bf16[128,4224]{1,0:T(8,128)(2,1)S(1)}, u32[]{:S(2)}, u32[]{:S(2)}) collective-permute-start(bf16[128,4224]{1,0:T(8,128)(2,1)} %constant_dynamic-update-slice_fusion.10), channel_id=1, source_target_pairs={{0,1},{1,0},{2,3},{3,2},{16,17},{17,16},{18,19},{19,18},{4,5},{5,4... | collective-permute-start | bytes 3244040 | tf_op jit(solution)/shard_map/ppermute | solution.py:60
  79.5 2.7 %collective-permute-start.16 = (bf16[128,4096]{1,0:T(8,128)(2,1)S(1)}, bf16[128,4096]{1,0:T(8,128)(2,1)S(1)}, u32[]{:S(2)}, u32[]{:S(2)}) collective-permute-start(bf16[128,4096]{1,0:T(8,128)(2,1)S(1)} %get-tuple-element.46), channel_id=1, source_target_pairs={{0,1},{1,0},{2,3},{3,2},{16,17},{17,16},{18,19},{19,18},{4,5},{5,4... | collective-permute-start | bytes 3145736 | tf_op jit(solution)/shard_map/ppermute | solution.py:60
  79.9 6.1 %collective-permute-start.22 = (bf16[128,4096]{1,0:T(8,128)(2,1)S(1)}, bf16[128,4096]{1,0:T(8,128)(2,1)S(1)}, u32[]{:S(2)}, u32[]{:S(2)}) collective-permute-start(bf16[128,4096]{1,0:T(8,128)(2,1)S(1)} %get-tuple-element.57), channel_id=1, source_target_pairs={{0,1},{1,0},{2,3},{3,2},{16,17},{17,16},{18,19},{19,18},{4,5},{5,4... | collective-permute-start | bytes 3145736 | tf_op jit(solution)/shard_map/ppermute | solution.py:60
  82.5 9.4 %collective-permute-start.17 = (bf16[32,4096]{1,0:T(8,128)(2,1)S(1)}, bf16[32,4096]{1,0:T(8,128)(2,1)S(1)}, u32[]{:S(2)}, u32[]{:S(2)}) collective-permute-start(bf16[32,4096]{1,0:T(8,128)(2,1)S(1)} %get-tuple-element.48), channel_id=1, source_target_pairs={{0,2},{1,3},{2,0},{3,1},{16,18},{17,19},{18,16},{19,17},{4,6},{5,7... | collective-permute-start | bytes 786440 | tf_op jit(solution)/shard_map/ppermute | solution.py:60
  83.0 10.3 %collective-permute-start.18 = (bf16[32,4096]{1,0:T(8,128)(2,1)S(1)}, bf16[32,4096]{1,0:T(8,128)(2,1)S(1)}, u32[]{:S(2)}, u32[]{:S(2)}) collective-permute-start(bf16[32,4096]{1,0:T(8,128)(2,1)S(1)} %get-tuple-element.49), channel_id=1, source_target_pairs={{0,16},{1,17},{2,18},{3,19},{16,0},{17,1},{18,2},{19,3},{4,20},{5,... | collective-permute-start | bytes 786440 | tf_op jit(solution)/shard_map/ppermute | solution.py:60
  84.5 14.3 %collective-permute-start.19 = (bf16[32,4096]{1,0:T(8,128)(2,1)S(1)}, bf16[32,4096]{1,0:T(8,128)(2,1)S(1)}, u32[]{:S(2)}, u32[]{:S(2)}) collective-permute-start(bf16[32,4096]{1,0:T(8,128)(2,1)S(1)} %get-tuple-element.50), channel_id=1, source_target_pairs={{0,18},{1,19},{2,16},{3,17},{16,2},{17,3},{18,0},{19,1},{4,22},{5,... | collective-permute-start | bytes 786440 | tf_op jit(solution)/shard_map/ppermute | solution.py:60
  86.3 28.1 %copy-start.14 = (bf16[16,4096]{1,0:T(8,128)(2,1)S(1)}, bf16[16,4096]{1,0:T(8,128)(2,1)}, u32[]{:S(2)}) copy-start(bf16[16,4096]{1,0:T(8,128)(2,1)} %copy-done.13) | copy-start | bytes 393220
  86.3 16.8 %collective-permute-start.23 = (bf16[32,4096]{1,0:T(8,128)(2,1)S(1)}, bf16[32,4096]{1,0:T(8,128)(2,1)S(1)}, u32[]{:S(2)}, u32[]{:S(2)}) collective-permute-start(bf16[32,4096]{1,0:T(8,128)(2,1)S(1)} %get-tuple-element.59), channel_id=1, source_target_pairs={{0,2},{1,3},{2,0},{3,1},{16,18},{17,19},{18,16},{19,17},{4,6},{5,7... | collective-permute-start | bytes 786440 | tf_op jit(solution)/shard_map/ppermute | solution.py:60
  86.9 16.6 %collective-permute-start.24 = (bf16[32,4096]{1,0:T(8,128)(2,1)S(1)}, bf16[32,4096]{1,0:T(8,128)(2,1)S(1)}, u32[]{:S(2)}, u32[]{:S(2)}) collective-permute-start(bf16[32,4096]{1,0:T(8,128)(2,1)S(1)} %get-tuple-element.60), channel_id=1, source_target_pairs={{0,16},{1,17},{2,18},{3,19},{16,0},{17,1},{18,2},{19,3},{4,20},{5,... | collective-permute-start | bytes 786440 | tf_op jit(solution)/shard_map/ppermute | solution.py:60
  91.9 17.3 %collective-permute-start.25 = (bf16[32,4096]{1,0:T(8,128)(2,1)S(1)}, bf16[32,4096]{1,0:T(8,128)(2,1)S(1)}, u32[]{:S(2)}, u32[]{:S(2)}) collective-permute-start(bf16[32,4096]{1,0:T(8,128)(2,1)S(1)} %get-tuple-element.61), channel_id=1, source_target_pairs={{0,18},{1,19},{2,16},{3,17},{16,2},{17,3},{18,0},{19,1},{4,22},{5,... | collective-permute-start | bytes 786440 | tf_op jit(solution)/shard_map/ppermute | solution.py:60
  99.0 12.4 %collective-permute-start.20 = (bf16[16,4096]{1,0:T(8,128)(2,1)S(1)}, bf16[16,4096]{1,0:T(8,128)(2,1)S(1)}, u32[]{:S(2)}, u32[]{:S(2)}) collective-permute-start(bf16[16,4096]{1,0:T(8,128)(2,1)S(1)} %get-tuple-element.51), channel_id=1, source_target_pairs={{0,8},{1,9},{2,10},{3,11},{16,24},{17,25},{18,26},{19,27},{4,12},{... | collective-permute-start | bytes 393224 | tf_op jit(solution)/shard_map/ppermute | solution.py:50
  102.8 8.6 %collective-permute-start.21 = (bf16[16,4096]{1,0:T(8,128)(2,1)S(1)}, bf16[16,4096]{1,0:T(8,128)(2,1)S(1)}, u32[]{:S(2)}, u32[]{:S(2)}) collective-permute-start(bf16[16,4096]{1,0:T(8,128)(2,1)S(1)} %get-tuple-element.52), channel_id=1, source_target_pairs={{0,12},{1,13},{2,14},{3,15},{16,28},{17,29},{18,30},{19,31},{4,8},... | collective-permute-start | bytes 393224 | tf_op jit(solution)/shard_map/ppermute | solution.py:50
  109.3 5.0 %collective-permute-start.26 = (bf16[16,4096]{1,0:T(8,128)(2,1)S(1)}, bf16[16,4096]{1,0:T(8,128)(2,1)S(1)}, u32[]{:S(2)}, u32[]{:S(2)}) collective-permute-start(bf16[16,4096]{1,0:T(8,128)(2,1)S(1)} %get-tuple-element.63), channel_id=1, source_target_pairs={{0,4},{1,5},{2,6},{3,7},{16,20},{17,21},{18,22},{19,23},{4,0},{5,1... | collective-permute-start | bytes 393224 | tf_op jit(solution)/shard_map/ppermute | solution.py:50
  (15 other events, 58.0 us)

commit v6 on v5

--- a/solution.py
+++ b/solution.py
@@ -47,7 +47,8 @@
             for z in range(self.planes)
             for m in range(self.members)
         ]
-        return lax.ppermute(value, AXES, pairs)
+        with jax.named_scope(f"plane_{by}"):
+            return lax.ppermute(value, AXES, pairs)
 
     def swapped(self, value, by):
         if by == 0:
@@ -57,7 +58,8 @@
             for z in range(self.planes)
             for m in range(self.members)
         ]
-        return lax.ppermute(value, AXES, pairs)
+        with jax.named_scope(f"member_{by}"):
+            return lax.ppermute(value, AXES, pairs)
 
 
 def from_behind(value, axis, by):
@@ -281,6 +283,33 @@
     return jnp.concatenate(parts, axis=0)
 
 
+def packed(parts, work=0):
+    if len(parts) == 1 and not work:
+        return parts[0]
+    rows = sum(part.shape[0] for part in parts)
+    columns = parts[0].shape[1]
+
+    def kernel(*refs):
+        out_ref, offset = refs[-1], 0
+        for ref in refs[:-1]:
+            out_ref[offset : offset + ref.shape[0]] = ref[...]
+            offset += ref.shape[0]
+
+    return pl.pallas_call(
+        kernel,
+        out_shape=jax.ShapeDtypeStruct((rows, columns), parts[0].dtype),
+        in_specs=[VMEM] * len(parts),
+        out_specs=VMEM,
+        compiler_params=pltpu.CompilerParams(vmem_limit_bytes=12 * MEBI),
+        cost_estimate=pl.CostEstimate(flops=work, bytes_accessed=0, transcendentals=0),
+        name="packed",
+    )(*parts)
+
+
+def after(value, *others):
+    return lax.optimization_barrier((value, *others))[0]
+
+
 def run_experts(groups, others, gate_up, down_proj, expert, top_count, slots):
     model_dim, double = gate_up.shape[1:]
     hidden_dim = double // 2
@@ -410,7 +439,7 @@
             pltpu.VMEM((slots, hidden_dim), jnp.bfloat16),
             pltpu.SemaphoreType.DMA((2 * up_steps + out_steps,)),
         ],
-        compiler_params=pltpu.CompilerParams(vmem_limit_bytes=38 * MEBI),
+        compiler_params=pltpu.CompilerParams(vmem_limit_bytes=28 * MEBI),
         cost_estimate=pl.CostEstimate(
             flops=6 * slots * model_dim * hidden_dim,
             bytes_accessed=20 * MEBI,
@@ -425,8 +454,13 @@
 def add_up(parts, cuts, name):
     rows = sum(cuts)
     model_dim = parts[0][0].shape[1]
-    counts = [len(part) for part in parts]
     flat = [piece for part in parts for piece in part]
+    places = []
+    for part in parts:
+        start = 0
+        for piece in part:
+            places.append((start, start + piece.shape[0]))
+            start += piece.shape[0]
 
     def kernel(*refs):
         in_refs, out_refs = refs[: len(flat)], refs[len(flat) :]
@@ -434,17 +468,12 @@
         for start in range(0, model_dim, step):
             columns = slice(start, start + step)
             offset = 0
-            for i, (out_ref, cut) in enumerate(zip(out_refs, cuts)):
+            for out_ref, cut in zip(out_refs, cuts):
                 total = 0.0
-                first = 0
-                for count in counts:
-                    pieces = in_refs[first : first + count]
-                    first += count
-                    if count > 1:
-                        piece = pieces[i][:, columns]
-                    else:
-                        piece = pieces[0][offset : offset + cut, columns]
-                    total = total + piece.astype(jnp.float32)
+                for ref, (low, high) in zip(in_refs, places):
+                    if low <= offset and offset + cut <= high:
+                        rows_of = slice(offset - low, offset - low + cut)
+                        total = total + ref[rows_of, columns].astype(jnp.float32)
                 out_ref[:, columns] = total.astype(jnp.bfloat16)
                 offset += cut
 
@@ -455,7 +484,7 @@
         out_specs=(VMEM,) * len(cuts),
         compiler_params=pltpu.CompilerParams(vmem_limit_bytes=12 * MEBI),
         cost_estimate=pl.CostEstimate(
-            flops=rows * model_dim, bytes_accessed=2 * rows * model_dim, transcendentals=0
+            flops=0, bytes_accessed=0, transcendentals=0
         ),
         name=name,
     )(*flat)
@@ -567,41 +596,56 @@
     chips = range(0, layout.members, 2)
     blocks = [layout.shifted(normed, s) for s in range(planes)]
     arrived = []
-    for group in groups:
-        rows = stacked([blocks[s] for s in group])
-        arrived.append([layout.swapped(rows, chip) for chip in chips])
-    rows = [
-        [[arrived[0][c], arrived[1][c]] for c in range(len(chips))],
-        [[arrived[2][c]] for c in range(len(chips))],
-    ]
-    others = [layout.swapped(stacked([part for chip in own for part in chip]), 1) for own in rows]
-    mine, over = [], []
-    for some in ((0, 1),) if planes <= 4 else ((0,), (1,)):
-        slots = capacity * sum(
-            part.shape[0] for g in some for chip in rows[g] for part in chip
-        ) * 2 // count_of_rows
-        results = run_experts(
-            [rows[g] for g in some],
-            [others[g] for g in some],
-            w_gate_up,
-            w_down,
-            expert,
-            top_count,
-            slots,
+    for g, group in enumerate(groups):
+        rows = packed([blocks[s] for s in group])
+        sent = []
+        for c, chip in enumerate(chips):
+            ready = rows
+            if g == 1:
+                ready = after(rows, arrived[0][c])
+            sent.append(layout.swapped(ready, chip))
+        arrived.append(sent)
+    arrived[0][0] = after(arrived[0][0], arrived[2][0])
+
+    def to_experts(members, tie):
+        own = [[arrived[g][c] for g in members] for c in range(len(chips))]
+        pieces = [part for chip in own for part in chip]
+        if tie is not None:
+            pieces[0] = after(pieces[0], tie)
+        other = layout.swapped(packed(pieces), 1)
+        slots = layout.members * sum(len(groups[g]) for g in members) * capacity
+        return own, other, slots
+
+    def from_experts(own, other, slots):
+        (mine,), (over,) = run_experts(
+            [own], [other], w_gate_up, w_down, expert, top_count, slots
         )
-        mine += results[0]
-        over += results[1]
-    finished = []
-    for parts, sent in zip(mine, over):
-        back = layout.swapped(sent, 1)
-        sums = add_up([parts, [back]], [part.shape[0] for part in parts], "add_cores")
-        finished.append([layout.swapped(part, chip) for part, chip in zip(sums, chips)])
-    near, far = finished
-    others = []
-    for parts, shifts in ((far, groups[2]), (near, [*groups[0], *groups[1]])):
-        cuts = [count_of_rows] * len(shifts)
-        sums = add_up([[part] for part in parts], cuts, "add_chips")
-        others += [layout.shifted(part, s) for part, s in zip(sums, shifts)]
+        return mine, over
+
+    def add_cores(mine, over):
+        back = layout.swapped(over, 1)
+        cuts = [count_of_rows] * (sum(part.shape[0] for part in mine) // count_of_rows)
+        return add_up([mine, [back]], cuts, "add_cores")
+
+    def to_owners(sums, i):
+        pieces = len(sums) // len(chips)
+        return [layout.swapped(sums[c * pieces + i], chip) for c, chip in enumerate(chips)]
+
+    def from_owners(parts, by):
+        total = add_up([[part] for part in parts], [count_of_rows], "add_chips")[0]
+        return layout.shifted(total, by)
+
+    near = [s for g in (0, 1) for s in groups[g]]
+    mine, over = from_experts(*to_experts((0, 1), None))
+    far_own, far_other, slots = to_experts((2,), over)
+    near_sums = add_cores(mine, over)
+    mine, over = from_experts(far_own, after(far_other, near_sums[0]), slots)
+    early = [(to_owners(near_sums, i), near[i]) for i in range(1, len(near))]
+    over = after(over, *[part for parts, _ in early for part in parts[1:]])
+    far_sums = add_cores(mine, over)
+    late = [(to_owners(far_sums, i), s) for i, s in enumerate(groups[2])]
+    late.append((to_owners(near_sums, 0), near[0]))
+    others = [from_owners(parts, s) for parts, s in early + late]
     total = merged.astype(jnp.float32) + sum(part.astype(jnp.float32) for part in others)
     layer_out = total.astype(jnp.bfloat16)
     return (attended, layer_out)

time: 115 us -> 103 us (0.90)
  waiting for transfers between devices: 40.9 us -> 29.2 us
  local copies, waits for them, and re-layouts: 15 us -> 5.5 us
  Pallas kernels: 21.3 us -> 27.6 us
  starting transfers between devices: 36.3 us -> 39.1 us
    ppermute x19 -> x25, waiting for transfers between devices: 29.2 us -> 17.5 us  [swapped(): return lax.ppermute(value, AXES, pairs)]
    unnamed x51 -> x40, local copies, waits for them, and re-layouts: 13.6 us -> 5.5 us
    pallas_call x1 -> x2, Pallas kernels: 12.3 us -> 18.4 us  [run_experts(): pl.pallas_call(kernel, out_shape=tuple((jax.ShapeDtypeStruct(shape, jnp.b...]
    ppermute x19 -> x25, starting transfers between devices: 21.4 us -> 25.1 us  [swapped(): return lax.ppermute(value, AXES, pairs)]
    concatenate x2 -> x0, local copies, waits for them, and re-layouts: 1.39 us -> none  [stacked(): return jnp.concatenate(parts, axis=0)]
  transfers between devices with their start and end apart: 27 -> 33, of which waited for: 16 -> 14; matrix products, arithmetic and copies ran while one was open for 8% -> 0% of each run, Pallas kernels for 5% -> 23%
where the time goes in v6:
time: 103 us
  starting transfers between devices  39.1 us (38%)
  waiting for transfers between devices  29.2 us (28%)
  Pallas kernels  27.6 us (27%)
  local copies, waits for them, and re-layouts  5.5 us (5%)
    ppermute x25, starting transfers between devices, swapped(): return lax.ppermute(value, AXES, pairs)  25.1 us
    pallas_call x2, Pallas kernels, run_experts(): pl.pallas_call(kernel, out_shape=tuple((jax.ShapeDtypeStruct(shape, jnp.b...  18.4 us
    ppermute x25, waiting for transfers between devices, swapped(): return lax.ppermute(value, AXES, pairs)  17.5 us
    ppermute x6, waiting for transfers between devices, shifted(): return lax.ppermute(value, AXES, pairs)  9.62 us
    ppermute x6, starting transfers between devices, shifted(): return lax.ppermute(value, AXES, pairs)  8.92 us
    unnamed x40, local copies, waits for them, and re-layouts  5.5 us
    ppermute x2, starting transfers between devices, from_behind(): lax.ppermute(value, axis, [(i, (i + by) % length) for i in range(length)])  5.09 us
    pallas_call x1, Pallas kernels, own_attention(): pl.pallas_call(kernel, out_shape=(shape, shape, shape, jax.ShapeDtypeStru...  4.74 us
  transfers between devices with their start and end apart: 33, of which 14 were waited for; matrix products, arithmetic and copies ran while one was open for 0% of the time, Pallas kernels for 23%

profile of v6, /device:TPU:0, one launch (start us, length us, event | category | flops | bytes accessed | tf_op | source)
XLA Modules:
  0.0 103.1 jit_solution(1515367393011872230)
XLA Ops:
  0.6 3.0 %collective-permute-start = (s32[16]{0:T(128)}, s32[16]{0:T(128)S(1)}, u32[]{:S(2)}, u32[]{:S(2)}) collective-permute-start(s32[16]{0:T(128)} %param.17), channel_id=1, source_target_pairs={{0,16},{16,0},{1,17},{17,1},{2,18},{18,2},{3,19},{19,3},{4,20},{20... | collective-permute-start | bytes 200 | tf_op jit(solution)/shard_map/ppermute | solution.py:67
  3.6 1.7 %collective-permute-done.slots_ref = s32[16]{0:T(128)S(1)} collective-permute-done((s32[16]{0:T(128)}, s32[16]{0:T(128)S(1)}, u32[]{:S(2)}, u32[]{:S(2)}) %collective-permute-start) | collective-permute-done | bytes 96 | tf_op jit(solution)/shard_map/ppermute | solution.py:67
  5.3 1.6 %pick_pages.1 = bf16[16,16,512]{2,1,0:T(8,128)(2,1)S(1)} custom-call(s32[16]{0:T(128)S(1)} %collective-permute-done.slots_ref, bf16[128,16,512]{2,1,0:T(8,128)(2,1)} %pages_hbm.1), custom_call_target="tpu_custom_call" | custom-call | bytes 1048576 | tf_op jit(solution)/shard_map/pick_pages/pallas_call | solution.py:83
  7.0 2.1 %collective-permute-start.1 = (bf16[16,16,512]{2,1,0:T(8,128)(2,1)S(1)}, bf16[16,16,512]{2,1,0:T(8,128)(2,1)S(1)}, u32[]{:S(2)}, u32[]{:S(2)}) collective-permute-start(bf16[16,16,512]{2,1,0:T(8,128)(2,1)S(1)} %pick_pages.1), channel_id=1, source_target_pairs={{0,16},{16,0},{1,17},{17,1},{2,18},{18,2},{3,19},{19,3},{4,20},{20... | collective-permute-start | bytes 786440 | tf_op jit(solution)/shard_map/ppermute | solution.py:67
  9.0 4.7 %own_attention.1 = (f32[512,128]{1,0:T(8,128)S(1)}, f32[512,128]{1,0:T(8,128)S(1)}, f32[512,128]{1,0:T(8,128)S(1)}, bf16[512,128]{1,0:T(8,128)(2,1)S(1)}) custom-call(bf16[16,4096]{1,0:T(8,128)(2,1)} %queries_hbm, bf16[16,512]{1,0:T(8,128)(2,1)} %new_hbm.1, bf16[128,16,512]{2,1,0:T(8,128)(2,1)} %pages_hbm.1, s32[16,16]{1,0:T(8,128)} %table_ref.1, s32[16]{0:T(128)} %lengths_ref.1), custom_call_target="tpu_custom_call" | custom-call | flops 1073741824 | bytes 16777216 | tf_op jit(solution)/shard_map/own_attention/pallas_call | solution.py:238
  14.2 1.9 %finish_attention.1 = (bf16[16,4096]{1,0:T(8,128)(2,1)}, bf16[16,4096]{1,0:T(8,128)(2,1)S(1)}, bf16[16,4224]{1,0:T(8,128)(2,1)S(1)}) custom-call(bf16[512,128]{1,0:T(8,128)(2,1)S(1)} %get-tuple-element.46.q_ref, bf16[16,16,512]{2,1,0:T(8,128)(2,1)S(1)} %collective-permute-done.1.fetched_ref, s32[16,16]{1,0:T(8,128)S(1)} %copy-done.16, s32[16]{0:T(128)S(1)} %copy-done.19, ...), custom_call_target="tpu_custom_call" | custom-call | flops 134217728 | bytes 4194304 | tf_op jit(solution)/shard_map/finish_attention/pallas_call | solution.py:540
  16.2 1.8 %collective-permute-start.4 = (bf16[16,4224]{1,0:T(8,128)(2,1)S(1)}, bf16[16,4224]{1,0:T(8,128)(2,1)S(1)}, u32[]{:S(2)}, u32[]{:S(2)}) collective-permute-start(bf16[16,4224]{1,0:T(8,128)(2,1)S(1)} %get-tuple-element.54.refs_0_), channel_id=1, source_target_pairs={{0,4},{1,5},{2,6},{3,7},{16,20},{17,21},{18,22},{19,23},{4,0},{5,1... | collective-permute-start | bytes 405512 | tf_op jit(solution)/shard_map/plane_1/ppermute | solution.py:51
  18.0 1.5 %collective-permute-start.5 = (bf16[16,4224]{1,0:T(8,128)(2,1)S(1)}, bf16[16,4224]{1,0:T(8,128)(2,1)S(1)}, u32[]{:S(2)}, u32[]{:S(2)}) collective-permute-start(bf16[16,4224]{1,0:T(8,128)(2,1)S(1)} %get-tuple-element.54.refs_0_), channel_id=1, source_target_pairs={{0,2},{1,3},{2,0},{3,1},{16,18},{17,19},{18,16},{19,17},{4,6},{5,7... | collective-permute-start | bytes 405512 | tf_op jit(solution)/shard_map/member_2/ppermute | solution.py:62
  19.5 1.5 %collective-permute-start.7 = (bf16[16,4224]{1,0:T(8,128)(2,1)S(1)}, bf16[16,4224]{1,0:T(8,128)(2,1)S(1)}, u32[]{:S(2)}, u32[]{:S(2)}) collective-permute-start(bf16[16,4224]{1,0:T(8,128)(2,1)S(1)} %get-tuple-element.54.refs_0_), channel_id=1, source_target_pairs={{0,16},{1,17},{2,18},{3,19},{16,0},{17,1},{18,2},{19,3},{4,20},{5,... | collective-permute-start | bytes 405512 | tf_op jit(solution)/shard_map/member_4/ppermute | solution.py:62
  21.5 2.6 %collective-permute-start.2 = (bf16[16,4224]{1,0:T(8,128)(2,1)S(1)}, bf16[16,4224]{1,0:T(8,128)(2,1)S(1)}, u32[]{:S(2)}, u32[]{:S(2)}) collective-permute-start(bf16[16,4224]{1,0:T(8,128)(2,1)S(1)} %get-tuple-element.54.refs_0_), channel_id=1, source_target_pairs={{0,8},{1,9},{2,10},{3,11},{16,24},{17,25},{18,26},{19,27},{4,12},{... | collective-permute-start | bytes 405512 | tf_op jit(solution)/shard_map/plane_2/ppermute | solution.py:51
  24.1 2.0 %collective-permute-start.3 = (bf16[16,4224]{1,0:T(8,128)(2,1)S(1)}, bf16[16,4224]{1,0:T(8,128)(2,1)S(1)}, u32[]{:S(2)}, u32[]{:S(2)}) collective-permute-start(bf16[16,4224]{1,0:T(8,128)(2,1)S(1)} %get-tuple-element.54.refs_0_), channel_id=1, source_target_pairs={{0,12},{1,13},{2,14},{3,15},{16,28},{17,29},{18,30},{19,31},{4,8},... | collective-permute-start | bytes 405512 | tf_op jit(solution)/shard_map/plane_3/ppermute | solution.py:51
  26.1 1.5 %collective-permute-start.6 = (bf16[16,4224]{1,0:T(8,128)(2,1)S(1)}, bf16[16,4224]{1,0:T(8,128)(2,1)S(1)}, u32[]{:S(2)}, u32[]{:S(2)}) collective-permute-start(bf16[16,4224]{1,0:T(8,128)(2,1)S(1)} %collective-permute-done.4.refs_1_), channel_id=1, source_target_pairs={{0,2},{1,3},{2,0},{3,1},{16,18},{17,19},{18,16},{19,17},{4,6},{5,7... | collective-permute-start | bytes 405512 | tf_op jit(solution)/shard_map/member_2/ppermute | solution.py:62
  27.6 1.5 %collective-permute-start.8 = (bf16[16,4224]{1,0:T(8,128)(2,1)S(1)}, bf16[16,4224]{1,0:T(8,128)(2,1)S(1)}, u32[]{:S(2)}, u32[]{:S(2)}) collective-permute-start(bf16[16,4224]{1,0:T(8,128)(2,1)S(1)} %collective-permute-done.4.refs_1_), channel_id=1, source_target_pairs={{0,16},{1,17},{2,18},{3,19},{16,0},{17,1},{18,2},{19,3},{4,20},{5,... | collective-permute-start | bytes 405512 | tf_op jit(solution)/shard_map/member_4/ppermute | solution.py:62
  29.6 2.1 %collective-permute-done.2.refs_0_ = bf16[16,4224]{1,0:T(8,128)(2,1)S(1)} collective-permute-done((bf16[16,4224]{1,0:T(8,128)(2,1)S(1)}, bf16[16,4224]{1,0:T(8,128)(2,1)S(1)}, u32[]{:S(2)}, u32[]{:S(2)}) %collective-permute-start.2) | collective-permute-done | bytes 135200 | tf_op jit(solution)/shard_map/plane_2/ppermute | solution.py:51
  32.7 2.4 %collective-permute-done.10.refs_7_ = bf16[16,4224]{1,0:T(8,128)(2,1)S(1)} collective-permute-done((bf16[16,4224]{1,0:T(8,128)(2,1)S(1)}, bf16[16,4224]{1,0:T(8,128)(2,1)S(1)}, u32[]{:S(2)}, u32[]{:S(2)}) %collective-permute-start.10) | collective-permute-done | bytes 135200 | tf_op jit(solution)/shard_map/member_6/ppermute | solution.py:62
  35.8 1.5 %collective-permute-start.18 = (bf16[32,4224]{1,0:T(8,128)(2,1)S(1)}, bf16[32,4224]{1,0:T(8,128)(2,1)S(1)}, u32[]{:S(2)}, u32[]{:S(2)}) collective-permute-start(bf16[32,4224]{1,0:T(8,128)(2,1)S(1)} %packed.3.refs_0_), channel_id=1, source_target_pairs={{0,16},{1,17},{2,18},{3,19},{16,0},{17,1},{18,2},{19,3},{4,20},{5,... | collective-permute-start | bytes 811016 | tf_op jit(solution)/shard_map/member_4/ppermute | solution.py:62
  44.3 9.2 %run_experts.2 = (bf16[32,4096]{1,0:T(8,128)(2,1)S(1)}, bf16[32,4096]{1,0:T(8,128)(2,1)S(1)}, bf16[32,4096]{1,0:T(8,128)(2,1)S(1)}, bf16[32,4096]{1,0:T(8,128)(2,1)S(1)}, bf16[128,4096]{1,0:T(8,128)(2,1)S(1)}) custom-call(s32[1]{0:T(128)} %bitcast.3.expert_ref, bf16[16,4224]{1,0:T(8,128)(2,1)S(1)} %get-tuple-element.54.refs_0_, ...), custom_call_target="tpu_custom_call" | custom-call | flops 2415919104 | bytes 20971520 | tf_op jit(solution)/shard_map/run_experts/pallas_call | solution.py:430
  54.2 3.7 %collective-permute-done.12.refs_4_ = bf16[128,4096]{1,0:T(8,128)(2,1)S(1)} collective-permute-done((bf16[128,4096]{1,0:T(8,128)(2,1)S(1)}, bf16[128,4096]{1,0:T(8,128)(2,1)S(1)}, u32[]{:S(2)}, u32[]{:S(2)}) %collective-permute-start.12) | collective-permute-done | bytes 1048608 | tf_op jit(solution)/shard_map/member_1/ppermute | solution.py:62
  58.7 1.5 %collective-permute-start.14 = (bf16[16,4096]{1,0:T(8,128)(2,1)S(1)}, bf16[16,4096]{1,0:T(8,128)(2,1)S(1)}, u32[]{:S(2)}, u32[]{:S(2)}) collective-permute-start(bf16[16,4096]{1,0:T(8,128)(2,1)S(1)} %get-tuple-element.66), channel_id=1, source_target_pairs={{0,16},{1,17},{2,18},{3,19},{16,0},{17,1},{18,2},{19,3},{4,20},{5,... | collective-permute-start | bytes 393224 | tf_op jit(solution)/shard_map/member_4/ppermute | solution.py:62
  60.1 1.5 %collective-permute-start.15 = (bf16[16,4096]{1,0:T(8,128)(2,1)S(1)}, bf16[16,4096]{1,0:T(8,128)(2,1)S(1)}, u32[]{:S(2)}, u32[]{:S(2)}) collective-permute-start(bf16[16,4096]{1,0:T(8,128)(2,1)S(1)} %get-tuple-element.67), channel_id=1, source_target_pairs={{0,18},{1,19},{2,16},{3,17},{16,2},{17,3},{18,0},{19,1},{4,22},{5,... | collective-permute-start | bytes 393224 | tf_op jit(solution)/shard_map/member_6/ppermute | solution.py:62
  61.7 9.2 %run_experts.3 = (bf16[32,4096]{1,0:T(8,128)(2,1)S(1)}, bf16[32,4096]{1,0:T(8,128)(2,1)S(1)}, bf16[32,4096]{1,0:T(8,128)(2,1)S(1)}, bf16[32,4096]{1,0:T(8,128)(2,1)S(1)}, bf16[128,4096]{1,0:T(8,128)(2,1)S(1)}) custom-call(s32[1]{0:T(128)} %bitcast.3.expert_ref, bf16[32,4224]{1,0:T(8,128)(2,1)S(1)} %packed.3.refs_0_, ...), custom_call_target="tpu_custom_call" | custom-call | flops 2415919104 | bytes 20971520 | tf_op jit(solution)/shard_map/run_experts/pallas_call | solution.py:430
  71.0 2.6 %collective-permute-done.21.refs_4_ = bf16[128,4096]{1,0:T(8,128)(2,1)S(1)} collective-permute-done((bf16[128,4096]{1,0:T(8,128)(2,1)S(1)}, bf16[128,4096]{1,0:T(8,128)(2,1)S(1)}, u32[]{:S(2)}, u32[]{:S(2)}) %collective-permute-start.21) | collective-permute-done | bytes 1048608 | tf_op jit(solution)/shard_map/member_1/ppermute | solution.py:62
  74.4 1.5 %collective-permute-start.27 = (bf16[16,4096]{1,0:T(8,128)(2,1)S(1)}, bf16[16,4096]{1,0:T(8,128)(2,1)S(1)}, u32[]{:S(2)}, u32[]{:S(2)}) collective-permute-start(bf16[16,4096]{1,0:T(8,128)(2,1)S(1)} %get-tuple-element.83), channel_id=1, source_target_pairs={{0,16},{1,17},{2,18},{3,19},{16,0},{17,1},{18,2},{19,3},{4,20},{5,... | collective-permute-start | bytes 393224 | tf_op jit(solution)/shard_map/member_4/ppermute | solution.py:62
  75.9 1.5 %collective-permute-start.28 = (bf16[16,4096]{1,0:T(8,128)(2,1)S(1)}, bf16[16,4096]{1,0:T(8,128)(2,1)S(1)}, u32[]{:S(2)}, u32[]{:S(2)}) collective-permute-start(bf16[16,4096]{1,0:T(8,128)(2,1)S(1)} %get-tuple-element.84), channel_id=1, source_target_pairs={{0,18},{1,19},{2,16},{3,17},{16,2},{17,3},{18,0},{19,1},{4,22},{5,... | collective-permute-start | bytes 393224 | tf_op jit(solution)/shard_map/member_6/ppermute | solution.py:62
  77.9 1.5 %collective-permute-start.23 = (bf16[16,4096]{1,0:T(8,128)(2,1)S(1)}, bf16[16,4096]{1,0:T(8,128)(2,1)S(1)}, u32[]{:S(2)}, u32[]{:S(2)}) collective-permute-start(bf16[16,4096]{1,0:T(8,128)(2,1)S(1)} %get-tuple-element.79), channel_id=1, source_target_pairs={{0,16},{1,17},{2,18},{3,19},{16,0},{17,1},{18,2},{19,3},{4,20},{5,... | collective-permute-start | bytes 393224 | tf_op jit(solution)/shard_map/member_4/ppermute | solution.py:62
  82.4 2.2 %collective-permute-done.28.refs_3_ = bf16[16,4096]{1,0:T(8,128)(2,1)S(1)} collective-permute-done((bf16[16,4096]{1,0:T(8,128)(2,1)S(1)}, bf16[16,4096]{1,0:T(8,128)(2,1)S(1)}, u32[]{:S(2)}, u32[]{:S(2)}) %collective-permute-start.28) | collective-permute-done | bytes 131104 | tf_op jit(solution)/shard_map/member_6/ppermute | solution.py:62
  85.2 1.5 %collective-permute-done.22.refs_1_ = bf16[16,4096]{1,0:T(8,128)(2,1)S(1)} collective-permute-done((bf16[16,4096]{1,0:T(8,128)(2,1)S(1)}, bf16[16,4096]{1,0:T(8,128)(2,1)S(1)}, u32[]{:S(2)}, u32[]{:S(2)}) %collective-permute-start.22) | collective-permute-done | bytes 131104 | tf_op jit(solution)/shard_map/member_2/ppermute | solution.py:62
  88.2 2.0 %collective-permute-done.24.refs_3_ = bf16[16,4096]{1,0:T(8,128)(2,1)S(1)} collective-permute-done((bf16[16,4096]{1,0:T(8,128)(2,1)S(1)}, bf16[16,4096]{1,0:T(8,128)(2,1)S(1)}, u32[]{:S(2)}, u32[]{:S(2)}) %collective-permute-start.24) | collective-permute-done | bytes 131104 | tf_op jit(solution)/shard_map/member_6/ppermute | solution.py:62
  90.2 2.4 %collective-permute-start.29 = (bf16[16,4096]{1,0:T(8,128)(2,1)S(1)}, bf16[16,4096]{1,0:T(8,128)(2,1)S(1)}, u32[]{:S(2)}, u32[]{:S(2)}) collective-permute-start(bf16[16,4096]{1,0:T(8,128)(2,1)S(1)} %add_chips.6), channel_id=1, source_target_pairs={{0,12},{1,13},{2,14},{3,15},{16,28},{17,29},{18,30},{19,31},{4,8},... | collective-permute-start | bytes 393224 | tf_op jit(solution)/shard_map/plane_3/ppermute | solution.py:51
  92.8 1.9 %collective-permute-done.32.refs_3_ = bf16[16,4096]{1,0:T(8,128)(2,1)S(1)} collective-permute-done((bf16[16,4096]{1,0:T(8,128)(2,1)S(1)}, bf16[16,4096]{1,0:T(8,128)(2,1)S(1)}, u32[]{:S(2)}, u32[]{:S(2)}) %collective-permute-start.32) | collective-permute-done | bytes 131104 | tf_op jit(solution)/shard_map/member_6/ppermute | solution.py:62
  94.8 3.3 %collective-permute-done.29 = bf16[16,4096]{1,0:T(8,128)(2,1)S(1)} collective-permute-done((bf16[16,4096]{1,0:T(8,128)(2,1)S(1)}, bf16[16,4096]{1,0:T(8,128)(2,1)S(1)}, u32[]{:S(2)}, u32[]{:S(2)}) %collective-permute-start.29) | collective-permute-done | bytes 131104 | tf_op jit(solution)/shard_map/plane_3/ppermute | solution.py:51
  98.1 4.2 %collective-permute-done.25 = bf16[16,4096]{1,0:T(8,128)(2,1)S(1)} collective-permute-done((bf16[16,4096]{1,0:T(8,128)(2,1)S(1)}, bf16[16,4096]{1,0:T(8,128)(2,1)S(1)}, u32[]{:S(2)}, u32[]{:S(2)}) %collective-permute-start.25) | collective-permute-done | bytes 131104 | tf_op jit(solution)/shard_map/plane_2/ppermute | solution.py:51
  (89 shorter events, 18.9 us)
Async XLA Ops:
  0.6 4.7 %collective-permute-start = (s32[16]{0:T(128)}, s32[16]{0:T(128)S(1)}, u32[]{:S(2)}, u32[]{:S(2)}) collective-permute-start(s32[16]{0:T(128)} %param.17), channel_id=1, source_target_pairs={{0,16},{16,0},{1,17},{17,1},{2,18},{18,2},{3,19},{19,3},{4,20},{20... | collective-permute-start | bytes 200 | tf_op jit(solution)/shard_map/ppermute | solution.py:67
  7.0 7.2 %collective-permute-start.1 = (bf16[16,16,512]{2,1,0:T(8,128)(2,1)S(1)}, bf16[16,16,512]{2,1,0:T(8,128)(2,1)S(1)}, u32[]{:S(2)}, u32[]{:S(2)}) collective-permute-start(bf16[16,16,512]{2,1,0:T(8,128)(2,1)S(1)} %pick_pages.1), channel_id=1, source_target_pairs={{0,16},{16,0},{1,17},{17,1},{2,18},{18,2},{3,19},{19,3},{4,20},{20... | collective-permute-start | bytes 786440 | tf_op jit(solution)/shard_map/ppermute | solution.py:67
  16.2 7.9 %collective-permute-start.4 = (bf16[16,4224]{1,0:T(8,128)(2,1)S(1)}, bf16[16,4224]{1,0:T(8,128)(2,1)S(1)}, u32[]{:S(2)}, u32[]{:S(2)}) collective-permute-start(bf16[16,4224]{1,0:T(8,128)(2,1)S(1)} %get-tuple-element.54.refs_0_), channel_id=1, source_target_pairs={{0,4},{1,5},{2,6},{3,7},{16,20},{17,21},{18,22},{19,23},{4,0},{5,1... | collective-permute-start | bytes 405512 | tf_op jit(solution)/shard_map/plane_1/ppermute | solution.py:51
  18.0 8.1 %collective-permute-start.5 = (bf16[16,4224]{1,0:T(8,128)(2,1)S(1)}, bf16[16,4224]{1,0:T(8,128)(2,1)S(1)}, u32[]{:S(2)}, u32[]{:S(2)}) collective-permute-start(bf16[16,4224]{1,0:T(8,128)(2,1)S(1)} %get-tuple-element.54.refs_0_), channel_id=1, source_target_pairs={{0,2},{1,3},{2,0},{3,1},{16,18},{17,19},{18,16},{19,17},{4,6},{5,7... | collective-permute-start | bytes 405512 | tf_op jit(solution)/shard_map/member_2/ppermute | solution.py:62
  19.5 8.1 %collective-permute-start.7 = (bf16[16,4224]{1,0:T(8,128)(2,1)S(1)}, bf16[16,4224]{1,0:T(8,128)(2,1)S(1)}, u32[]{:S(2)}, u32[]{:S(2)}) collective-permute-start(bf16[16,4224]{1,0:T(8,128)(2,1)S(1)} %get-tuple-element.54.refs_0_), channel_id=1, source_target_pairs={{0,16},{1,17},{2,18},{3,19},{16,0},{17,1},{18,2},{19,3},{4,20},{5,... | collective-permute-start | bytes 405512 | tf_op jit(solution)/shard_map/member_4/ppermute | solution.py:62
  21.0 8.1 %collective-permute-start.9 = (bf16[16,4224]{1,0:T(8,128)(2,1)S(1)}, bf16[16,4224]{1,0:T(8,128)(2,1)S(1)}, u32[]{:S(2)}, u32[]{:S(2)}) collective-permute-start(bf16[16,4224]{1,0:T(8,128)(2,1)S(1)} %get-tuple-element.54.refs_0_), channel_id=1, source_target_pairs={{0,18},{1,19},{2,16},{3,17},{16,2},{17,3},{18,0},{19,1},{4,22},{5,... | collective-permute-start | bytes 405512 | tf_op jit(solution)/shard_map/member_6/ppermute | solution.py:62
  21.5 10.2 %collective-permute-start.2 = (bf16[16,4224]{1,0:T(8,128)(2,1)S(1)}, bf16[16,4224]{1,0:T(8,128)(2,1)S(1)}, u32[]{:S(2)}, u32[]{:S(2)}) collective-permute-start(bf16[16,4224]{1,0:T(8,128)(2,1)S(1)} %get-tuple-element.54.refs_0_), channel_id=1, source_target_pairs={{0,8},{1,9},{2,10},{3,11},{16,24},{17,25},{18,26},{19,27},{4,12},{... | collective-permute-start | bytes 405512 | tf_op jit(solution)/shard_map/plane_2/ppermute | solution.py:51
  24.1 7.6 %collective-permute-start.3 = (bf16[16,4224]{1,0:T(8,128)(2,1)S(1)}, bf16[16,4224]{1,0:T(8,128)(2,1)S(1)}, u32[]{:S(2)}, u32[]{:S(2)}) collective-permute-start(bf16[16,4224]{1,0:T(8,128)(2,1)S(1)} %get-tuple-element.54.refs_0_), channel_id=1, source_target_pairs={{0,12},{1,13},{2,14},{3,15},{16,28},{17,29},{18,30},{19,31},{4,8},... | collective-permute-start | bytes 405512 | tf_op jit(solution)/shard_map/plane_3/ppermute | solution.py:51
  26.1 5.6 %collective-permute-start.6 = (bf16[16,4224]{1,0:T(8,128)(2,1)S(1)}, bf16[16,4224]{1,0:T(8,128)(2,1)S(1)}, u32[]{:S(2)}, u32[]{:S(2)}) collective-permute-start(bf16[16,4224]{1,0:T(8,128)(2,1)S(1)} %collective-permute-done.4.refs_1_), channel_id=1, source_target_pairs={{0,2},{1,3},{2,0},{3,1},{16,18},{17,19},{18,16},{19,17},{4,6},{5,7... | collective-permute-start | bytes 405512 | tf_op jit(solution)/shard_map/member_2/ppermute | solution.py:62
  27.6 5.0 %collective-permute-start.8 = (bf16[16,4224]{1,0:T(8,128)(2,1)S(1)}, bf16[16,4224]{1,0:T(8,128)(2,1)S(1)}, u32[]{:S(2)}, u32[]{:S(2)}) collective-permute-start(bf16[16,4224]{1,0:T(8,128)(2,1)S(1)} %collective-permute-done.4.refs_1_), channel_id=1, source_target_pairs={{0,16},{1,17},{2,18},{3,19},{16,0},{17,1},{18,2},{19,3},{4,20},{5,... | collective-permute-start | bytes 405512 | tf_op jit(solution)/shard_map/member_4/ppermute | solution.py:62
  29.1 5.9 %collective-permute-start.10 = (bf16[16,4224]{1,0:T(8,128)(2,1)S(1)}, bf16[16,4224]{1,0:T(8,128)(2,1)S(1)}, u32[]{:S(2)}, u32[]{:S(2)}) collective-permute-start(bf16[16,4224]{1,0:T(8,128)(2,1)S(1)} %collective-permute-done.4.refs_1_), channel_id=1, source_target_pairs={{0,18},{1,19},{2,16},{3,17},{16,2},{17,3},{18,0},{19,1},{4,22},{5,... | collective-permute-start | bytes 405512 | tf_op jit(solution)/shard_map/member_6/ppermute | solution.py:62
  35.2 3.6 %collective-permute-start.11 = (bf16[128,4224]{1,0:T(8,128)(2,1)S(1)}, bf16[128,4224]{1,0:T(8,128)(2,1)S(1)}, u32[]{:S(2)}, u32[]{:S(2)}) collective-permute-start(bf16[128,4224]{1,0:T(8,128)(2,1)S(1)} %packed.4), channel_id=1, source_target_pairs={{0,1},{1,0},{2,3},{3,2},{16,17},{17,16},{18,19},{19,18},{4,5},{5,4... | collective-permute-start | bytes 3244040 | tf_op jit(solution)/shard_map/member_1/ppermute | solution.py:62
  35.2 18.2 %collective-permute-start.17 = (bf16[32,4224]{1,0:T(8,128)(2,1)S(1)}, bf16[32,4224]{1,0:T(8,128)(2,1)S(1)}, u32[]{:S(2)}, u32[]{:S(2)}) collective-permute-start(bf16[32,4224]{1,0:T(8,128)(2,1)S(1)} %packed.3.refs_0_), channel_id=1, source_target_pairs={{0,2},{1,3},{2,0},{3,1},{16,18},{17,19},{18,16},{19,17},{4,6},{5,7... | collective-permute-start | bytes 811016 | tf_op jit(solution)/shard_map/member_2/ppermute | solution.py:62
  35.8 17.7 %collective-permute-start.18 = (bf16[32,4224]{1,0:T(8,128)(2,1)S(1)}, bf16[32,4224]{1,0:T(8,128)(2,1)S(1)}, u32[]{:S(2)}, u32[]{:S(2)}) collective-permute-start(bf16[32,4224]{1,0:T(8,128)(2,1)S(1)} %packed.3.refs_0_), channel_id=1, source_target_pairs={{0,16},{1,17},{2,18},{3,19},{16,0},{17,1},{18,2},{19,3},{4,20},{5,... | collective-permute-start | bytes 811016 | tf_op jit(solution)/shard_map/member_4/ppermute | solution.py:62
  37.3 16.2 %collective-permute-start.19 = (bf16[32,4224]{1,0:T(8,128)(2,1)S(1)}, bf16[32,4224]{1,0:T(8,128)(2,1)S(1)}, u32[]{:S(2)}, u32[]{:S(2)}) collective-permute-start(bf16[32,4224]{1,0:T(8,128)(2,1)S(1)} %packed.3.refs_0_), channel_id=1, source_target_pairs={{0,18},{1,19},{2,16},{3,17},{16,2},{17,3},{18,0},{19,1},{4,22},{5,... | collective-permute-start | bytes 811016 | tf_op jit(solution)/shard_map/member_6/ppermute | solution.py:62
  53.6 8.1 %collective-permute-start.20 = (bf16[128,4224]{1,0:T(8,128)(2,1)S(1)}, bf16[128,4224]{1,0:T(8,128)(2,1)S(1)}, u32[]{:S(2)}, u32[]{:S(2)}) collective-permute-start(bf16[128,4224]{1,0:T(8,128)(2,1)S(1)} %packed.5), channel_id=1, source_target_pairs={{0,1},{1,0},{2,3},{3,2},{16,17},{17,16},{18,19},{19,18},{4,5},{5,4... | collective-permute-start | bytes 3244040 | tf_op jit(solution)/shard_map/member_1/ppermute | solution.py:62
  53.7 4.2 %collective-permute-start.12 = (bf16[128,4096]{1,0:T(8,128)(2,1)S(1)}, bf16[128,4096]{1,0:T(8,128)(2,1)S(1)}, u32[]{:S(2)}, u32[]{:S(2)}) collective-permute-start(bf16[128,4096]{1,0:T(8,128)(2,1)S(1)} %get-tuple-element.63), channel_id=1, source_target_pairs={{0,1},{1,0},{2,3},{3,2},{16,17},{17,16},{18,19},{19,18},{4,5},{5,4... | collective-permute-start | bytes 3145736 | tf_op jit(solution)/shard_map/member_1/ppermute | solution.py:62
  58.1 12.8 %collective-permute-start.13 = (bf16[16,4096]{1,0:T(8,128)(2,1)S(1)}, bf16[16,4096]{1,0:T(8,128)(2,1)S(1)}, u32[]{:S(2)}, u32[]{:S(2)}) collective-permute-start(bf16[16,4096]{1,0:T(8,128)(2,1)S(1)} %get-tuple-element.65), channel_id=1, source_target_pairs={{0,2},{1,3},{2,0},{3,1},{16,18},{17,19},{18,16},{19,17},{4,6},{5,7... | collective-permute-start | bytes 393224 | tf_op jit(solution)/shard_map/member_2/ppermute | solution.py:62
  58.7 12.2 %collective-permute-start.14 = (bf16[16,4096]{1,0:T(8,128)(2,1)S(1)}, bf16[16,4096]{1,0:T(8,128)(2,1)S(1)}, u32[]{:S(2)}, u32[]{:S(2)}) collective-permute-start(bf16[16,4096]{1,0:T(8,128)(2,1)S(1)} %get-tuple-element.66), channel_id=1, source_target_pairs={{0,16},{1,17},{2,18},{3,19},{16,0},{17,1},{18,2},{19,3},{4,20},{5,... | collective-permute-start | bytes 393224 | tf_op jit(solution)/shard_map/member_4/ppermute | solution.py:62
  60.1 10.7 %collective-permute-start.15 = (bf16[16,4096]{1,0:T(8,128)(2,1)S(1)}, bf16[16,4096]{1,0:T(8,128)(2,1)S(1)}, u32[]{:S(2)}, u32[]{:S(2)}) collective-permute-start(bf16[16,4096]{1,0:T(8,128)(2,1)S(1)} %get-tuple-element.67), channel_id=1, source_target_pairs={{0,18},{1,19},{2,16},{3,17},{16,2},{17,3},{18,0},{19,1},{4,22},{5,... | collective-permute-start | bytes 393224 | tf_op jit(solution)/shard_map/member_6/ppermute | solution.py:62
  73.8 5.7 %collective-permute-start.26 = (bf16[16,4096]{1,0:T(8,128)(2,1)S(1)}, bf16[16,4096]{1,0:T(8,128)(2,1)S(1)}, u32[]{:S(2)}, u32[]{:S(2)}) collective-permute-start(bf16[16,4096]{1,0:T(8,128)(2,1)S(1)} %get-tuple-element.82), channel_id=1, source_target_pairs={{0,2},{1,3},{2,0},{3,1},{16,18},{17,19},{18,16},{19,17},{4,6},{5,7... | collective-permute-start | bytes 393224 | tf_op jit(solution)/shard_map/member_2/ppermute | solution.py:62
  74.4 6.6 %collective-permute-start.27 = (bf16[16,4096]{1,0:T(8,128)(2,1)S(1)}, bf16[16,4096]{1,0:T(8,128)(2,1)S(1)}, u32[]{:S(2)}, u32[]{:S(2)}) collective-permute-start(bf16[16,4096]{1,0:T(8,128)(2,1)S(1)} %get-tuple-element.83), channel_id=1, source_target_pairs={{0,16},{1,17},{2,18},{3,19},{16,0},{17,1},{18,2},{19,3},{4,20},{5,... | collective-permute-start | bytes 393224 | tf_op jit(solution)/shard_map/member_4/ppermute | solution.py:62
  75.9 8.7 %collective-permute-start.28 = (bf16[16,4096]{1,0:T(8,128)(2,1)S(1)}, bf16[16,4096]{1,0:T(8,128)(2,1)S(1)}, u32[]{:S(2)}, u32[]{:S(2)}) collective-permute-start(bf16[16,4096]{1,0:T(8,128)(2,1)S(1)} %get-tuple-element.84), channel_id=1, source_target_pairs={{0,18},{1,19},{2,16},{3,17},{16,2},{17,3},{18,0},{19,1},{4,22},{5,... | collective-permute-start | bytes 393224 | tf_op jit(solution)/shard_map/member_6/ppermute | solution.py:62
  77.4 9.3 %collective-permute-start.22 = (bf16[16,4096]{1,0:T(8,128)(2,1)S(1)}, bf16[16,4096]{1,0:T(8,128)(2,1)S(1)}, u32[]{:S(2)}, u32[]{:S(2)}) collective-permute-start(bf16[16,4096]{1,0:T(8,128)(2,1)S(1)} %get-tuple-element.78), channel_id=1, source_target_pairs={{0,2},{1,3},{2,0},{3,1},{16,18},{17,19},{18,16},{19,17},{4,6},{5,7... | collective-permute-start | bytes 393224 | tf_op jit(solution)/shard_map/member_2/ppermute | solution.py:62
  77.9 10.3 %collective-permute-start.23 = (bf16[16,4096]{1,0:T(8,128)(2,1)S(1)}, bf16[16,4096]{1,0:T(8,128)(2,1)S(1)}, u32[]{:S(2)}, u32[]{:S(2)}) collective-permute-start(bf16[16,4096]{1,0:T(8,128)(2,1)S(1)} %get-tuple-element.79), channel_id=1, source_target_pairs={{0,16},{1,17},{2,18},{3,19},{16,0},{17,1},{18,2},{19,3},{4,20},{5,... | collective-permute-start | bytes 393224 | tf_op jit(solution)/shard_map/member_4/ppermute | solution.py:62
  79.6 10.6 %collective-permute-start.24 = (bf16[16,4096]{1,0:T(8,128)(2,1)S(1)}, bf16[16,4096]{1,0:T(8,128)(2,1)S(1)}, u32[]{:S(2)}, u32[]{:S(2)}) collective-permute-start(bf16[16,4096]{1,0:T(8,128)(2,1)S(1)} %get-tuple-element.80), channel_id=1, source_target_pairs={{0,18},{1,19},{2,16},{3,17},{16,2},{17,3},{18,0},{19,1},{4,22},{5,... | collective-permute-start | bytes 393224 | tf_op jit(solution)/shard_map/member_6/ppermute | solution.py:62
  81.0 11.7 %collective-permute-start.30 = (bf16[16,4096]{1,0:T(8,128)(2,1)S(1)}, bf16[16,4096]{1,0:T(8,128)(2,1)S(1)}, u32[]{:S(2)}, u32[]{:S(2)}) collective-permute-start(bf16[16,4096]{1,0:T(8,128)(2,1)S(1)} %get-tuple-element.85), channel_id=1, source_target_pairs={{0,2},{1,3},{2,0},{3,1},{16,18},{17,19},{18,16},{19,17},{4,6},{5,7... | collective-permute-start | bytes 393224 | tf_op jit(solution)/shard_map/member_2/ppermute | solution.py:62
  84.6 8.2 %collective-permute-start.31 = (bf16[16,4096]{1,0:T(8,128)(2,1)S(1)}, bf16[16,4096]{1,0:T(8,128)(2,1)S(1)}, u32[]{:S(2)}, u32[]{:S(2)}) collective-permute-start(bf16[16,4096]{1,0:T(8,128)(2,1)S(1)} %get-tuple-element.86), channel_id=1, source_target_pairs={{0,16},{1,17},{2,18},{3,19},{16,0},{17,1},{18,2},{19,3},{4,20},{5,... | collective-permute-start | bytes 393224 | tf_op jit(solution)/shard_map/member_4/ppermute | solution.py:62
  86.7 8.0 %collective-permute-start.32 = (bf16[16,4096]{1,0:T(8,128)(2,1)S(1)}, bf16[16,4096]{1,0:T(8,128)(2,1)S(1)}, u32[]{:S(2)}, u32[]{:S(2)}) collective-permute-start(bf16[16,4096]{1,0:T(8,128)(2,1)S(1)} %get-tuple-element.87), channel_id=1, source_target_pairs={{0,18},{1,19},{2,16},{3,17},{16,2},{17,3},{18,0},{19,1},{4,22},{5,... | collective-permute-start | bytes 393224 | tf_op jit(solution)/shard_map/member_6/ppermute | solution.py:62
  88.2 6.6 %collective-permute-start.16 = (bf16[16,4096]{1,0:T(8,128)(2,1)S(1)}, bf16[16,4096]{1,0:T(8,128)(2,1)S(1)}, u32[]{:S(2)}, u32[]{:S(2)}) collective-permute-start(bf16[16,4096]{1,0:T(8,128)(2,1)S(1)} %add_chips.4), channel_id=1, source_target_pairs={{0,4},{1,5},{2,6},{3,7},{16,20},{17,21},{18,22},{19,23},{4,0},{5,1... | collective-permute-start | bytes 393224 | tf_op jit(solution)/shard_map/plane_1/ppermute | solution.py:51
  90.2 7.9 %collective-permute-start.29 = (bf16[16,4096]{1,0:T(8,128)(2,1)S(1)}, bf16[16,4096]{1,0:T(8,128)(2,1)S(1)}, u32[]{:S(2)}, u32[]{:S(2)}) collective-permute-start(bf16[16,4096]{1,0:T(8,128)(2,1)S(1)} %add_chips.6), channel_id=1, source_target_pairs={{0,12},{1,13},{2,14},{3,15},{16,28},{17,29},{18,30},{19,31},{4,8},... | collective-permute-start | bytes 393224 | tf_op jit(solution)/shard_map/plane_3/ppermute | solution.py:51
  92.7 9.6 %collective-permute-start.25 = (bf16[16,4096]{1,0:T(8,128)(2,1)S(1)}, bf16[16,4096]{1,0:T(8,128)(2,1)S(1)}, u32[]{:S(2)}, u32[]{:S(2)}) collective-permute-start(bf16[16,4096]{1,0:T(8,128)(2,1)S(1)} %add_chips.5), channel_id=1, source_target_pairs={{0,8},{1,9},{2,10},{3,11},{16,24},{17,25},{18,26},{19,27},{4,12},{... | collective-permute-start | bytes 393224 | tf_op jit(solution)/shard_map/plane_2/ppermute | solution.py:51
  (21 other events, 125.9 us)

commit v7 on v6

--- a/solution.py
+++ b/solution.py
@@ -19,6 +19,7 @@
 SMEM = pl.BlockSpec(memory_space=pltpu.SMEM)
 HBM = pl.BlockSpec(memory_space=pltpu.HBM)
 MEBI = 1 << 20
+EXPERT_LIMIT = 16 * MEBI
 
 
 def in_hbm(value):
@@ -310,48 +311,42 @@
     return lax.optimization_barrier((value, *others))[0]
 
 
-def run_experts(groups, others, gate_up, down_proj, expert, top_count, slots):
-    model_dim, double = gate_up.shape[1:]
-    hidden_dim = double // 2
-    chips = len(groups[0])
-    flat = [part for group in groups for chip in group for part in chip]
-    shares = [sum(part.shape[0] for part in group[0]) for group in groups]
-    rows = sum(part.shape[0] for part in flat) + sum(other.shape[0] for other in others)
+def run_experts(own, other, weights, expert, top_count, slots, keep):
+    rows, model_dim = own.shape
+    rows, model_dim = 2 * rows, model_dim - 128
+    gate_up, down_proj = weights
+    double, hidden_dim = gate_up.shape[-1], down_proj.shape[-2]
     width = 256
     up_steps = hidden_dim // width
     out_width = 1024 if rows <= 512 else 512
     out_steps = model_dim // out_width
     strip = 256
 
-    def kernel(expert_ref, *refs):
-        own_refs, refs = refs[: len(flat)], refs[len(flat) :]
-        other_refs, refs = refs[: len(others)], refs[len(others) :]
-        up_hbm, down_hbm, refs = refs[0], refs[1], refs[2:]
-        out_refs, refs = refs[: chips * len(groups)], refs[chips * len(groups) :]
-        over_refs, refs = refs[: len(groups)], refs[len(groups) :]
-        up_ref, down_ref, tokens_ref, hidden_ref, sems = refs
-        up_copies, down_copies = [], []
-        for c in range(up_steps):
-            pair = []
-            for half in range(2):
-                columns = pl.ds(half * hidden_dim + c * width, width)
-                pair.append(
-                    pltpu.make_async_copy(
+    def kernel(expert_ref, own_ref, other_ref, *refs):
+        copies = {}
+        if keep:
+            up_hbm, down_hbm, out_ref, over_ref, up_ref, down_ref, tokens_ref, hidden_ref, sems = refs
+            for c in range(up_steps):
+                for half in range(2):
+                    columns = pl.ds(half * hidden_dim + c * width, width)
+                    copies["up", c, half] = pltpu.make_async_copy(
                         up_hbm.at[0, :, columns], up_ref.at[:, columns], sems.at[2 * c + half]
                     )
-                )
-                pair[-1].start()
-            up_copies.append(pair)
-        for c in range(out_steps):
-            columns = pl.ds(c * out_width, out_width)
-            down_copies.append(
-                pltpu.make_async_copy(
+            for c in range(out_steps):
+                columns = pl.ds(c * out_width, out_width)
+                copies["down", c] = pltpu.make_async_copy(
                     down_hbm.at[0, :, columns], down_ref.at[:, columns], sems.at[2 * up_steps + c]
                 )
-            )
-            down_copies[-1].start()
-
-        token_refs = list(own_refs) + list(other_refs)
+            for copy in copies.values():
+                copy.start()
+        else:
+            up_ref, down_ref, out_ref, over_ref, tokens_ref, hidden_ref = refs
+
+        def arrive(*name):
+            if keep:
+                copies[name].wait()
+
+        token_refs = [own_ref, other_ref]
         routing = stacked([ref[:, model_dim:] for ref in token_refs]).astype(jnp.float32)
         wanted = expert_ref[0].astype(jnp.float32)
         match = jnp.zeros((rows, 1), jnp.float32)
@@ -395,8 +390,8 @@
             ).astype(jnp.bfloat16)
 
         for c in range(up_steps):
-            for copy in up_copies[c]:
-                copy.wait()
+            arrive("up", c, 0)
+            arrive("up", c, 1)
             start = c * width
             tokens = tokens_ref[...]
             gated = jnp.dot(
@@ -412,43 +407,46 @@
             )
 
         for c in range(out_steps):
-            down_copies[c].wait()
+            arrive("down", c)
             columns = slice(c * out_width, (c + 1) * out_width)
             result = jnp.dot(
                 hidden_ref[...], down_ref[:, columns], preferred_element_type=jnp.float32
             )
             result = (result * gate).astype(jnp.bfloat16)
             sums = jnp.dot(place, result, preferred_element_type=jnp.float32).astype(jnp.bfloat16)
-            offset = 0
-            for i, ref in enumerate([*out_refs, *over_refs]):
-                cut = ref.shape[0]
-                ref[:, columns] = sums[offset : offset + cut]
-                offset += cut
-
-    shapes = [(share, model_dim) for share in shares for _ in range(chips)]
-    shapes += [(other.shape[0], model_dim) for other in others]
+            out_ref[:, columns] = sums[: rows // 2]
+            over_ref[:, columns] = sums[rows // 2 :]
+
+    shape = jax.ShapeDtypeStruct((rows // 2, model_dim), jnp.bfloat16)
+    kept, scratch = (), []
+    if keep:
+        kept = (
+            pltpu.VMEM((model_dim, double), jnp.bfloat16),
+            pltpu.VMEM((hidden_dim, model_dim), jnp.bfloat16),
+        )
+        scratch = [pltpu.SemaphoreType.DMA((2 * up_steps + out_steps,))]
+        weights = [in_hbm(gate_up), in_hbm(down_proj)]
+    else:
+        weights = [pltpu.with_memory_space_constraint(value, pltpu.VMEM) for value in weights]
     results = pl.pallas_call(
         kernel,
-        out_shape=tuple(jax.ShapeDtypeStruct(shape, jnp.bfloat16) for shape in shapes),
-        in_specs=[SMEM] + [VMEM] * (len(flat) + len(others)) + [HBM] * 2,
-        out_specs=(VMEM,) * len(shapes),
+        out_shape=(shape, shape) + kept,
+        in_specs=[SMEM, VMEM, VMEM] + [HBM if keep else VMEM] * 2,
+        out_specs=(VMEM,) * (2 + len(kept)),
         scratch_shapes=[
-            pltpu.VMEM((model_dim, double), jnp.bfloat16),
-            pltpu.VMEM((hidden_dim, model_dim), jnp.bfloat16),
             pltpu.VMEM((slots, model_dim), jnp.bfloat16),
             pltpu.VMEM((slots, hidden_dim), jnp.bfloat16),
-            pltpu.SemaphoreType.DMA((2 * up_steps + out_steps,)),
-        ],
-        compiler_params=pltpu.CompilerParams(vmem_limit_bytes=28 * MEBI),
+        ]
+        + scratch,
+        compiler_params=pltpu.CompilerParams(vmem_limit_bytes=EXPERT_LIMIT),
         cost_estimate=pl.CostEstimate(
             flops=6 * slots * model_dim * hidden_dim,
             bytes_accessed=20 * MEBI,
             transcendentals=slots * hidden_dim,
         ),
         name="run_experts",
-    )(expert, *flat, *others, in_hbm(gate_up), in_hbm(down_proj))
-    mine = [results[g * chips : (g + 1) * chips] for g in range(len(groups))]
-    return mine, results[chips * len(groups) :]
+    )(expert, own, other, *weights)
+    return results[0], results[1], results[2:]
 
 
 def add_up(parts, cuts, name):
@@ -608,44 +606,42 @@
     arrived[0][0] = after(arrived[0][0], arrived[2][0])
 
     def to_experts(members, tie):
-        own = [[arrived[g][c] for g in members] for c in range(len(chips))]
-        pieces = [part for chip in own for part in chip]
+        pieces = [arrived[g][c] for c in range(len(chips)) for g in members]
         if tie is not None:
             pieces[0] = after(pieces[0], tie)
-        other = layout.swapped(packed(pieces), 1)
+        own = packed(pieces)
         slots = layout.members * sum(len(groups[g]) for g in members) * capacity
-        return own, other, slots
-
-    def from_experts(own, other, slots):
-        (mine,), (over,) = run_experts(
-            [own], [other], w_gate_up, w_down, expert, top_count, slots
-        )
-        return mine, over
+        return own, layout.swapped(own, 1), slots
 
     def add_cores(mine, over):
         back = layout.swapped(over, 1)
-        cuts = [count_of_rows] * (sum(part.shape[0] for part in mine) // count_of_rows)
-        return add_up([mine, [back]], cuts, "add_cores")
+        cuts = [count_of_rows] * (mine.shape[0] // count_of_rows)
+        return add_up([[mine], [back]], cuts, "add_cores")
 
     def to_owners(sums, i):
         pieces = len(sums) // len(chips)
         return [layout.swapped(sums[c * pieces + i], chip) for c, chip in enumerate(chips)]
 
-    def from_owners(parts, by):
-        total = add_up([[part] for part in parts], [count_of_rows], "add_chips")[0]
-        return layout.shifted(total, by)
+    def total_of(parts):
+        return add_up([[part] for part in parts], [count_of_rows], "add_chips")[0]
 
     near = [s for g in (0, 1) for s in groups[g]]
-    mine, over = from_experts(*to_experts((0, 1), None))
+    own, other, slots = to_experts((0, 1), None)
+    mine, over, kept = run_experts(own, other, (w_gate_up, w_down), expert, top_count, slots, True)
     far_own, far_other, slots = to_experts((2,), over)
-    near_sums = add_cores(mine, over)
-    mine, over = from_experts(far_own, after(far_other, near_sums[0]), slots)
-    early = [(to_owners(near_sums, i), near[i]) for i in range(1, len(near))]
-    over = after(over, *[part for parts, _ in early for part in parts[1:]])
+    near_sums = list(add_cores(mine, over))
+    far_other = after(far_other, near_sums[0])
+    mine, over, _ = run_experts(far_own, far_other, kept, expert, top_count, slots, False)
+    early = [to_owners(near_sums, i) for i in range(1, len(near))]
+    over = after(over, *[part for parts in early for part in parts[1:]])
     far_sums = add_cores(mine, over)
-    late = [(to_owners(far_sums, i), s) for i, s in enumerate(groups[2])]
-    late.append((to_owners(near_sums, 0), near[0]))
-    others = [from_owners(parts, s) for parts, s in early + late]
+    totals = {s: total_of(to_owners(far_sums, i)) for i, s in enumerate(groups[2])}
+    totals.update({s: total_of(parts) for s, parts in zip(near[1:], early)})
+    pieces = len(near_sums) // len(chips)
+    for c in range(len(chips)):
+        near_sums[c * pieces] = after(near_sums[c * pieces], totals[groups[2][-1]])
+    totals[near[0]] = total_of(to_owners(near_sums, 0))
+    others = [layout.shifted(total, s) for s, total in totals.items()]
     total = merged.astype(jnp.float32) + sum(part.astype(jnp.float32) for part in others)
     layer_out = total.astype(jnp.bfloat16)
     return (attended, layer_out)

time: 103 us -> 97.9 us (0.950)
  local copies, waits for them, and re-layouts: 5.5 us -> 0.04 us
  Pallas kernels: 27.6 us -> 22.6 us
  waiting for transfers between devices: 29.2 us -> 33.5 us
    unnamed x40 -> x12, local copies, waits for them, and re-layouts: 5.5 us -> 0.04 us
    pallas_call x2, Pallas kernels: 18.4 us -> 13.4 us  [run_experts(): pl.pallas_call(kernel, out_shape=(shape, shape) + kept, in_specs=[SMEM, V...]
    ppermute x25, waiting for transfers between devices: 17.5 us -> 21.6 us  [swapped(): return lax.ppermute(value, AXES, pairs)]
  transfers between devices with their start and end apart: 33 -> 33, of which waited for: 14 -> 15; matrix products, arithmetic and copies ran while one was open for 0% -> 0% of each run, Pallas kernels for 23% -> 19%
where the time goes in v7:
time: 97.9 us; the launch traced here: 97.6 us
  starting transfers between devices  39.9 us (41%)
  waiting for transfers between devices  33.5 us (34%)
  Pallas kernels  22.6 us (23%)
    ppermute x25, starting transfers between devices, swapped(): return lax.ppermute(value, AXES, pairs)  25.3 us
    ppermute x25, waiting for transfers between devices, swapped(): return lax.ppermute(value, AXES, pairs)  21.6 us
    pallas_call x2, Pallas kernels, run_experts(): pl.pallas_call(kernel, out_shape=(shape, shape) + kept, in_specs=[SMEM, V...  13.4 us
    ppermute x6, waiting for transfers between devices, shifted(): return lax.ppermute(value, AXES, pairs)  9.87 us
    ppermute x6, starting transfers between devices, shifted(): return lax.ppermute(value, AXES, pairs)  9.48 us
    ppermute x2, starting transfers between devices, from_behind(): lax.ppermute(value, axis, [(i, (i + by) % length) for i in range(length)])  5.09 us
    pallas_call x1, Pallas kernels, own_attention(): pl.pallas_call(kernel, out_shape=(shape, shape, shape, jax.ShapeDtypeStru...  4.74 us
    ppermute x2, waiting for transfers between devices, from_behind(): lax.ppermute(value, axis, [(i, (i + by) % length) for i in range(length)])  2.06 us
  transfers between devices with their start and end apart: 33, of which 15 were waited for; matrix products, arithmetic and copies ran while one was open for 0% of the time, Pallas kernels for 19%

profile of v7, /device:TPU:0, one launch (start us, length us, event | category | flops | bytes accessed | tf_op | source)
XLA Modules:
  0.0 97.6 jit_solution(7621316453626184003)
XLA Ops:
  0.6 3.0 %collective-permute-start = (s32[16]{0:T(128)}, s32[16]{0:T(128)S(1)}, u32[]{:S(2)}, u32[]{:S(2)}) collective-permute-start(s32[16]{0:T(128)} %param.17), channel_id=1, source_target_pairs={{0,16},{16,0},{1,17},{17,1},{2,18},{18,2},{3,19},{19,3},{4,20},{20... | collective-permute-start | bytes 200 | tf_op jit(solution)/shard_map/ppermute | solution.py:68
  3.6 1.7 %collective-permute-done.slots_ref = s32[16]{0:T(128)S(1)} collective-permute-done((s32[16]{0:T(128)}, s32[16]{0:T(128)S(1)}, u32[]{:S(2)}, u32[]{:S(2)}) %collective-permute-start) | collective-permute-done | bytes 96 | tf_op jit(solution)/shard_map/ppermute | solution.py:68
  5.3 1.6 %pick_pages.1 = bf16[16,16,512]{2,1,0:T(8,128)(2,1)S(1)} custom-call(s32[16]{0:T(128)S(1)} %collective-permute-done.slots_ref, bf16[128,16,512]{2,1,0:T(8,128)(2,1)} %pages_hbm.1), custom_call_target="tpu_custom_call" | custom-call | bytes 1048576 | tf_op jit(solution)/shard_map/pick_pages/pallas_call | solution.py:84
  7.0 2.1 %collective-permute-start.1 = (bf16[16,16,512]{2,1,0:T(8,128)(2,1)S(1)}, bf16[16,16,512]{2,1,0:T(8,128)(2,1)S(1)}, u32[]{:S(2)}, u32[]{:S(2)}) collective-permute-start(bf16[16,16,512]{2,1,0:T(8,128)(2,1)S(1)} %pick_pages.1), channel_id=1, source_target_pairs={{0,16},{16,0},{1,17},{17,1},{2,18},{18,2},{3,19},{19,3},{4,20},{20... | collective-permute-start | bytes 786440 | tf_op jit(solution)/shard_map/ppermute | solution.py:68
  9.0 4.7 %own_attention.1 = (f32[512,128]{1,0:T(8,128)S(1)}, f32[512,128]{1,0:T(8,128)S(1)}, f32[512,128]{1,0:T(8,128)S(1)}, bf16[512,128]{1,0:T(8,128)(2,1)S(1)}) custom-call(bf16[16,4096]{1,0:T(8,128)(2,1)} %queries_hbm, bf16[16,512]{1,0:T(8,128)(2,1)} %new_hbm.1, bf16[128,16,512]{2,1,0:T(8,128)(2,1)} %pages_hbm.1, s32[16,16]{1,0:T(8,128)} %table_ref.1, s32[16]{0:T(128)} %lengths_ref.1), custom_call_target="tpu_custom_call" | custom-call | flops 1073741824 | bytes 16777216 | tf_op jit(solution)/shard_map/own_attention/pallas_call | solution.py:239
  14.2 1.9 %finish_attention.1 = (bf16[16,4096]{1,0:T(8,128)(2,1)}, bf16[16,4096]{1,0:T(8,128)(2,1)S(1)}, bf16[16,4224]{1,0:T(8,128)(2,1)S(1)}) custom-call(bf16[512,128]{1,0:T(8,128)(2,1)S(1)} %get-tuple-element.46.q_ref, bf16[16,16,512]{2,1,0:T(8,128)(2,1)S(1)} %collective-permute-done.1.fetched_ref, s32[16,16]{1,0:T(8,128)S(1)} %copy-done.2, s32[16]{0:T(128)S(1)} %copy-done.5, ...), custom_call_target="tpu_custom_call" | custom-call | flops 134217728 | bytes 4194304 | tf_op jit(solution)/shard_map/finish_attention/pallas_call | solution.py:538
  16.2 1.8 %collective-permute-start.4 = (bf16[16,4224]{1,0:T(8,128)(2,1)S(1)}, bf16[16,4224]{1,0:T(8,128)(2,1)S(1)}, u32[]{:S(2)}, u32[]{:S(2)}) collective-permute-start(bf16[16,4224]{1,0:T(8,128)(2,1)S(1)} %get-tuple-element.54.refs_0_), channel_id=1, source_target_pairs={{0,4},{1,5},{2,6},{3,7},{16,20},{17,21},{18,22},{19,23},{4,0},{5,1... | collective-permute-start | bytes 405512 | tf_op jit(solution)/shard_map/plane_1/ppermute | solution.py:52
  18.0 1.5 %collective-permute-start.5 = (bf16[16,4224]{1,0:T(8,128)(2,1)S(1)}, bf16[16,4224]{1,0:T(8,128)(2,1)S(1)}, u32[]{:S(2)}, u32[]{:S(2)}) collective-permute-start(bf16[16,4224]{1,0:T(8,128)(2,1)S(1)} %get-tuple-element.54.refs_0_), channel_id=1, source_target_pairs={{0,2},{1,3},{2,0},{3,1},{16,18},{17,19},{18,16},{19,17},{4,6},{5,7... | collective-permute-start | bytes 405512 | tf_op jit(solution)/shard_map/member_2/ppermute | solution.py:63
  19.5 1.5 %collective-permute-start.7 = (bf16[16,4224]{1,0:T(8,128)(2,1)S(1)}, bf16[16,4224]{1,0:T(8,128)(2,1)S(1)}, u32[]{:S(2)}, u32[]{:S(2)}) collective-permute-start(bf16[16,4224]{1,0:T(8,128)(2,1)S(1)} %get-tuple-element.54.refs_0_), channel_id=1, source_target_pairs={{0,16},{1,17},{2,18},{3,19},{16,0},{17,1},{18,2},{19,3},{4,20},{5,... | collective-permute-start | bytes 405512 | tf_op jit(solution)/shard_map/member_4/ppermute | solution.py:63
  21.5 2.6 %collective-permute-start.2 = (bf16[16,4224]{1,0:T(8,128)(2,1)S(1)}, bf16[16,4224]{1,0:T(8,128)(2,1)S(1)}, u32[]{:S(2)}, u32[]{:S(2)}) collective-permute-start(bf16[16,4224]{1,0:T(8,128)(2,1)S(1)} %get-tuple-element.54.refs_0_), channel_id=1, source_target_pairs={{0,8},{1,9},{2,10},{3,11},{16,24},{17,25},{18,26},{19,27},{4,12},{... | collective-permute-start | bytes 405512 | tf_op jit(solution)/shard_map/plane_2/ppermute | solution.py:52
  24.1 2.0 %collective-permute-start.3 = (bf16[16,4224]{1,0:T(8,128)(2,1)S(1)}, bf16[16,4224]{1,0:T(8,128)(2,1)S(1)}, u32[]{:S(2)}, u32[]{:S(2)}) collective-permute-start(bf16[16,4224]{1,0:T(8,128)(2,1)S(1)} %get-tuple-element.54.refs_0_), channel_id=1, source_target_pairs={{0,12},{1,13},{2,14},{3,15},{16,28},{17,29},{18,30},{19,31},{4,8},... | collective-permute-start | bytes 405512 | tf_op jit(solution)/shard_map/plane_3/ppermute | solution.py:52
  26.1 1.5 %collective-permute-start.6 = (bf16[16,4224]{1,0:T(8,128)(2,1)S(1)}, bf16[16,4224]{1,0:T(8,128)(2,1)S(1)}, u32[]{:S(2)}, u32[]{:S(2)}) collective-permute-start(bf16[16,4224]{1,0:T(8,128)(2,1)S(1)} %collective-permute-done.4.refs_1_), channel_id=1, source_target_pairs={{0,2},{1,3},{2,0},{3,1},{16,18},{17,19},{18,16},{19,17},{4,6},{5,7... | collective-permute-start | bytes 405512 | tf_op jit(solution)/shard_map/member_2/ppermute | solution.py:63
  27.6 1.5 %collective-permute-start.8 = (bf16[16,4224]{1,0:T(8,128)(2,1)S(1)}, bf16[16,4224]{1,0:T(8,128)(2,1)S(1)}, u32[]{:S(2)}, u32[]{:S(2)}) collective-permute-start(bf16[16,4224]{1,0:T(8,128)(2,1)S(1)} %collective-permute-done.4.refs_1_), channel_id=1, source_target_pairs={{0,16},{1,17},{2,18},{3,19},{16,0},{17,1},{18,2},{19,3},{4,20},{5,... | collective-permute-start | bytes 405512 | tf_op jit(solution)/shard_map/member_4/ppermute | solution.py:63
  29.6 2.1 %collective-permute-done.2.refs_0_ = bf16[16,4224]{1,0:T(8,128)(2,1)S(1)} collective-permute-done((bf16[16,4224]{1,0:T(8,128)(2,1)S(1)}, bf16[16,4224]{1,0:T(8,128)(2,1)S(1)}, u32[]{:S(2)}, u32[]{:S(2)}) %collective-permute-start.2) | collective-permute-done | bytes 135200 | tf_op jit(solution)/shard_map/plane_2/ppermute | solution.py:52
  32.6 2.4 %collective-permute-done.10.refs_7_ = bf16[16,4224]{1,0:T(8,128)(2,1)S(1)} collective-permute-done((bf16[16,4224]{1,0:T(8,128)(2,1)S(1)}, bf16[16,4224]{1,0:T(8,128)(2,1)S(1)}, u32[]{:S(2)}, u32[]{:S(2)}) %collective-permute-start.10) | collective-permute-done | bytes 135200 | tf_op jit(solution)/shard_map/member_6/ppermute | solution.py:63
  35.8 1.5 %collective-permute-start.13 = (bf16[32,4224]{1,0:T(8,128)(2,1)S(1)}, bf16[32,4224]{1,0:T(8,128)(2,1)S(1)}, u32[]{:S(2)}, u32[]{:S(2)}) collective-permute-start(bf16[32,4224]{1,0:T(8,128)(2,1)S(1)} %packed.3.refs_0_), channel_id=1, source_target_pairs={{0,16},{1,17},{2,18},{3,19},{16,0},{17,1},{18,2},{19,3},{4,20},{5,... | collective-permute-start | bytes 811016 | tf_op jit(solution)/shard_map/member_4/ppermute | solution.py:63
  37.3 1.5 %collective-permute-start.14 = (bf16[32,4224]{1,0:T(8,128)(2,1)S(1)}, bf16[32,4224]{1,0:T(8,128)(2,1)S(1)}, u32[]{:S(2)}, u32[]{:S(2)}) collective-permute-start(bf16[32,4224]{1,0:T(8,128)(2,1)S(1)} %packed.3.refs_0_), channel_id=1, source_target_pairs={{0,18},{1,19},{2,16},{3,17},{16,2},{17,3},{18,0},{19,1},{4,22},{5,... | collective-permute-start | bytes 811016 | tf_op jit(solution)/shard_map/member_6/ppermute | solution.py:63
  38.8 8.3 %run_experts.2 = (bf16[128,4096]{1,0:T(8,128)(2,1)S(1)}, bf16[128,4096]{1,0:T(8,128)(2,1)S(1)}, bf16[4096,1536]{1,0:T(8,128)(2,1)S(1)}, bf16[768,4096]{1,0:T(8,128)(2,1)S(1)}) custom-call(s32[1]{0:T(128)} %bitcast.3.expert_ref, bf16[128,4224]{1,0:T(8,128)(2,1)S(1)} %packed.4.own_ref, bf16[128,4224]{1,0:T(8,128)(2,1)S(1)} %collective-permute-done.11.other_ref, ...), custom_call_target="tpu_custom_call" | custom-call | flops 2415919104 | bytes 20971520 | tf_op jit(solution)/shard_map/run_experts/pallas_call | solution.py:431
  47.1 4.0 %collective-permute-done.14.refs_3_ = bf16[32,4224]{1,0:T(8,128)(2,1)S(1)} collective-permute-done((bf16[32,4224]{1,0:T(8,128)(2,1)S(1)}, bf16[32,4224]{1,0:T(8,128)(2,1)S(1)}, u32[]{:S(2)}, u32[]{:S(2)}) %collective-permute-start.14) | collective-permute-done | bytes 270368 | tf_op jit(solution)/shard_map/member_6/ppermute | solution.py:63
  51.7 3.7 %collective-permute-done.16.refs_1_ = bf16[128,4096]{1,0:T(8,128)(2,1)S(1)} collective-permute-done((bf16[128,4096]{1,0:T(8,128)(2,1)S(1)}, bf16[128,4096]{1,0:T(8,128)(2,1)S(1)}, u32[]{:S(2)}, u32[]{:S(2)}) %collective-permute-start.16) | collective-permute-done | bytes 1048608 | tf_op jit(solution)/shard_map/member_1/ppermute | solution.py:63
  56.2 1.5 %collective-permute-start.18 = (bf16[16,4096]{1,0:T(8,128)(2,1)S(1)}, bf16[16,4096]{1,0:T(8,128)(2,1)S(1)}, u32[]{:S(2)}, u32[]{:S(2)}) collective-permute-start(bf16[16,4096]{1,0:T(8,128)(2,1)S(1)} %get-tuple-element.69), channel_id=1, source_target_pairs={{0,16},{1,17},{2,18},{3,19},{16,0},{17,1},{18,2},{19,3},{4,20},{5,... | collective-permute-start | bytes 393224 | tf_op jit(solution)/shard_map/member_4/ppermute | solution.py:63
  57.7 1.5 %collective-permute-start.19 = (bf16[16,4096]{1,0:T(8,128)(2,1)S(1)}, bf16[16,4096]{1,0:T(8,128)(2,1)S(1)}, u32[]{:S(2)}, u32[]{:S(2)}) collective-permute-start(bf16[16,4096]{1,0:T(8,128)(2,1)S(1)} %get-tuple-element.70), channel_id=1, source_target_pairs={{0,18},{1,19},{2,16},{3,17},{16,2},{17,3},{18,0},{19,1},{4,22},{5,... | collective-permute-start | bytes 393224 | tf_op jit(solution)/shard_map/member_6/ppermute | solution.py:63
  59.2 5.1 %run_experts.3 = (bf16[128,4096]{1,0:T(8,128)(2,1)S(1)}, bf16[128,4096]{1,0:T(8,128)(2,1)S(1)}) custom-call(s32[1]{0:T(128)} %bitcast.3.expert_ref, bf16[128,4224]{1,0:T(8,128)(2,1)S(1)} %packed.5.own_ref, bf16[128,4224]{1,0:T(8,128)(2,1)S(1)} %collective-permute-done.15.other_ref, bf16[4096,1536]{1,0:T(8,128)(2,1)S(1)} %get-tuple-element.64.refs_0_, ...), custom_call_target="tpu_custom_call" | custom-call | flops 2415919104 | bytes 20971520 | tf_op jit(solution)/shard_map/run_experts/pallas_call | solution.py:431
  65.3 2.7 %collective-permute-done.20.refs_1_ = bf16[128,4096]{1,0:T(8,128)(2,1)S(1)} collective-permute-done((bf16[128,4096]{1,0:T(8,128)(2,1)S(1)}, bf16[128,4096]{1,0:T(8,128)(2,1)S(1)}, u32[]{:S(2)}, u32[]{:S(2)}) %collective-permute-start.20) | collective-permute-done | bytes 1048608 | tf_op jit(solution)/shard_map/member_1/ppermute | solution.py:63
  68.7 1.5 %collective-permute-start.26 = (bf16[16,4096]{1,0:T(8,128)(2,1)S(1)}, bf16[16,4096]{1,0:T(8,128)(2,1)S(1)}, u32[]{:S(2)}, u32[]{:S(2)}) collective-permute-start(bf16[16,4096]{1,0:T(8,128)(2,1)S(1)} %get-tuple-element.78), channel_id=1, source_target_pairs={{0,16},{1,17},{2,18},{3,19},{16,0},{17,1},{18,2},{19,3},{4,20},{5,... | collective-permute-start | bytes 393224 | tf_op jit(solution)/shard_map/member_4/ppermute | solution.py:63
  72.2 1.5 %collective-permute-start.22 = (bf16[16,4096]{1,0:T(8,128)(2,1)S(1)}, bf16[16,4096]{1,0:T(8,128)(2,1)S(1)}, u32[]{:S(2)}, u32[]{:S(2)}) collective-permute-start(bf16[16,4096]{1,0:T(8,128)(2,1)S(1)} %get-tuple-element.74), channel_id=1, source_target_pairs={{0,16},{1,17},{2,18},{3,19},{16,0},{17,1},{18,2},{19,3},{4,20},{5,... | collective-permute-start | bytes 393224 | tf_op jit(solution)/shard_map/member_4/ppermute | solution.py:63
  75.3 3.6 %collective-permute-done.27.refs_3_ = bf16[16,4096]{1,0:T(8,128)(2,1)S(1)} collective-permute-done((bf16[16,4096]{1,0:T(8,128)(2,1)S(1)}, bf16[16,4096]{1,0:T(8,128)(2,1)S(1)}, u32[]{:S(2)}, u32[]{:S(2)}) %collective-permute-start.27) | collective-permute-done | bytes 131104 | tf_op jit(solution)/shard_map/member_6/ppermute | solution.py:63
  79.7 1.6 %collective-permute-start.31 = (bf16[16,4096]{1,0:T(8,128)(2,1)S(1)}, bf16[16,4096]{1,0:T(8,128)(2,1)S(1)}, u32[]{:S(2)}, u32[]{:S(2)}) collective-permute-start(bf16[16,4096]{1,0:T(8,128)(2,1)S(1)} %get-tuple-element.85), channel_id=1, source_target_pairs={{0,16},{1,17},{2,18},{3,19},{16,0},{17,1},{18,2},{19,3},{4,20},{5,... | collective-permute-start | bytes 393224 | tf_op jit(solution)/shard_map/member_4/ppermute | solution.py:63
  82.7 1.8 %collective-permute-done.23.refs_3_ = bf16[16,4096]{1,0:T(8,128)(2,1)S(1)} collective-permute-done((bf16[16,4096]{1,0:T(8,128)(2,1)S(1)}, bf16[16,4096]{1,0:T(8,128)(2,1)S(1)}, u32[]{:S(2)}, u32[]{:S(2)}) %collective-permute-start.23) | collective-permute-done | bytes 131104 | tf_op jit(solution)/shard_map/member_6/ppermute | solution.py:63
  84.5 1.8 %collective-permute-start.28 = (bf16[16,4096]{1,0:T(8,128)(2,1)S(1)}, bf16[16,4096]{1,0:T(8,128)(2,1)S(1)}, u32[]{:S(2)}, u32[]{:S(2)}) collective-permute-start(bf16[16,4096]{1,0:T(8,128)(2,1)S(1)} %add_chips.5), channel_id=1, source_target_pairs={{0,12},{1,13},{2,14},{3,15},{16,28},{17,29},{18,30},{19,31},{4,8},... | collective-permute-start | bytes 393224 | tf_op jit(solution)/shard_map/plane_3/ppermute | solution.py:52
  89.1 2.3 %collective-permute-done.28 = bf16[16,4096]{1,0:T(8,128)(2,1)S(1)} collective-permute-done((bf16[16,4096]{1,0:T(8,128)(2,1)S(1)}, bf16[16,4096]{1,0:T(8,128)(2,1)S(1)}, u32[]{:S(2)}, u32[]{:S(2)}) %collective-permute-start.28) | collective-permute-done | bytes 131104 | tf_op jit(solution)/shard_map/plane_3/ppermute | solution.py:52
  91.3 5.5 %collective-permute-done.24 = bf16[16,4096]{1,0:T(8,128)(2,1)S(1)} collective-permute-done((bf16[16,4096]{1,0:T(8,128)(2,1)S(1)}, bf16[16,4096]{1,0:T(8,128)(2,1)S(1)}, u32[]{:S(2)}, u32[]{:S(2)}) %collective-permute-start.24) | collective-permute-done | bytes 131104 | tf_op jit(solution)/shard_map/plane_2/ppermute | solution.py:52
  (61 shorter events, 15.7 us)
Async XLA Ops:
  0.6 4.7 %collective-permute-start = (s32[16]{0:T(128)}, s32[16]{0:T(128)S(1)}, u32[]{:S(2)}, u32[]{:S(2)}) collective-permute-start(s32[16]{0:T(128)} %param.17), channel_id=1, source_target_pairs={{0,16},{16,0},{1,17},{17,1},{2,18},{18,2},{3,19},{19,3},{4,20},{20... | collective-permute-start | bytes 200 | tf_op jit(solution)/shard_map/ppermute | solution.py:68
  7.0 7.2 %collective-permute-start.1 = (bf16[16,16,512]{2,1,0:T(8,128)(2,1)S(1)}, bf16[16,16,512]{2,1,0:T(8,128)(2,1)S(1)}, u32[]{:S(2)}, u32[]{:S(2)}) collective-permute-start(bf16[16,16,512]{2,1,0:T(8,128)(2,1)S(1)} %pick_pages.1), channel_id=1, source_target_pairs={{0,16},{16,0},{1,17},{17,1},{2,18},{18,2},{3,19},{19,3},{4,20},{20... | collective-permute-start | bytes 786440 | tf_op jit(solution)/shard_map/ppermute | solution.py:68
  16.2 7.9 %collective-permute-start.4 = (bf16[16,4224]{1,0:T(8,128)(2,1)S(1)}, bf16[16,4224]{1,0:T(8,128)(2,1)S(1)}, u32[]{:S(2)}, u32[]{:S(2)}) collective-permute-start(bf16[16,4224]{1,0:T(8,128)(2,1)S(1)} %get-tuple-element.54.refs_0_), channel_id=1, source_target_pairs={{0,4},{1,5},{2,6},{3,7},{16,20},{17,21},{18,22},{19,23},{4,0},{5,1... | collective-permute-start | bytes 405512 | tf_op jit(solution)/shard_map/plane_1/ppermute | solution.py:52
  18.0 8.1 %collective-permute-start.5 = (bf16[16,4224]{1,0:T(8,128)(2,1)S(1)}, bf16[16,4224]{1,0:T(8,128)(2,1)S(1)}, u32[]{:S(2)}, u32[]{:S(2)}) collective-permute-start(bf16[16,4224]{1,0:T(8,128)(2,1)S(1)} %get-tuple-element.54.refs_0_), channel_id=1, source_target_pairs={{0,2},{1,3},{2,0},{3,1},{16,18},{17,19},{18,16},{19,17},{4,6},{5,7... | collective-permute-start | bytes 405512 | tf_op jit(solution)/shard_map/member_2/ppermute | solution.py:63
  19.5 8.1 %collective-permute-start.7 = (bf16[16,4224]{1,0:T(8,128)(2,1)S(1)}, bf16[16,4224]{1,0:T(8,128)(2,1)S(1)}, u32[]{:S(2)}, u32[]{:S(2)}) collective-permute-start(bf16[16,4224]{1,0:T(8,128)(2,1)S(1)} %get-tuple-element.54.refs_0_), channel_id=1, source_target_pairs={{0,16},{1,17},{2,18},{3,19},{16,0},{17,1},{18,2},{19,3},{4,20},{5,... | collective-permute-start | bytes 405512 | tf_op jit(solution)/shard_map/member_4/ppermute | solution.py:63
  21.0 8.1 %collective-permute-start.9 = (bf16[16,4224]{1,0:T(8,128)(2,1)S(1)}, bf16[16,4224]{1,0:T(8,128)(2,1)S(1)}, u32[]{:S(2)}, u32[]{:S(2)}) collective-permute-start(bf16[16,4224]{1,0:T(8,128)(2,1)S(1)} %get-tuple-element.54.refs_0_), channel_id=1, source_target_pairs={{0,18},{1,19},{2,16},{3,17},{16,2},{17,3},{18,0},{19,1},{4,22},{5,... | collective-permute-start | bytes 405512 | tf_op jit(solution)/shard_map/member_6/ppermute | solution.py:63
  21.5 10.2 %collective-permute-start.2 = (bf16[16,4224]{1,0:T(8,128)(2,1)S(1)}, bf16[16,4224]{1,0:T(8,128)(2,1)S(1)}, u32[]{:S(2)}, u32[]{:S(2)}) collective-permute-start(bf16[16,4224]{1,0:T(8,128)(2,1)S(1)} %get-tuple-element.54.refs_0_), channel_id=1, source_target_pairs={{0,8},{1,9},{2,10},{3,11},{16,24},{17,25},{18,26},{19,27},{4,12},{... | collective-permute-start | bytes 405512 | tf_op jit(solution)/shard_map/plane_2/ppermute | solution.py:52
  24.1 7.6 %collective-permute-start.3 = (bf16[16,4224]{1,0:T(8,128)(2,1)S(1)}, bf16[16,4224]{1,0:T(8,128)(2,1)S(1)}, u32[]{:S(2)}, u32[]{:S(2)}) collective-permute-start(bf16[16,4224]{1,0:T(8,128)(2,1)S(1)} %get-tuple-element.54.refs_0_), channel_id=1, source_target_pairs={{0,12},{1,13},{2,14},{3,15},{16,28},{17,29},{18,30},{19,31},{4,8},... | collective-permute-start | bytes 405512 | tf_op jit(solution)/shard_map/plane_3/ppermute | solution.py:52
  26.1 5.6 %collective-permute-start.6 = (bf16[16,4224]{1,0:T(8,128)(2,1)S(1)}, bf16[16,4224]{1,0:T(8,128)(2,1)S(1)}, u32[]{:S(2)}, u32[]{:S(2)}) collective-permute-start(bf16[16,4224]{1,0:T(8,128)(2,1)S(1)} %collective-permute-done.4.refs_1_), channel_id=1, source_target_pairs={{0,2},{1,3},{2,0},{3,1},{16,18},{17,19},{18,16},{19,17},{4,6},{5,7... | collective-permute-start | bytes 405512 | tf_op jit(solution)/shard_map/member_2/ppermute | solution.py:63
  27.6 5.0 %collective-permute-start.8 = (bf16[16,4224]{1,0:T(8,128)(2,1)S(1)}, bf16[16,4224]{1,0:T(8,128)(2,1)S(1)}, u32[]{:S(2)}, u32[]{:S(2)}) collective-permute-start(bf16[16,4224]{1,0:T(8,128)(2,1)S(1)} %collective-permute-done.4.refs_1_), channel_id=1, source_target_pairs={{0,16},{1,17},{2,18},{3,19},{16,0},{17,1},{18,2},{19,3},{4,20},{5,... | collective-permute-start | bytes 405512 | tf_op jit(solution)/shard_map/member_4/ppermute | solution.py:63
  29.1 5.9 %collective-permute-start.10 = (bf16[16,4224]{1,0:T(8,128)(2,1)S(1)}, bf16[16,4224]{1,0:T(8,128)(2,1)S(1)}, u32[]{:S(2)}, u32[]{:S(2)}) collective-permute-start(bf16[16,4224]{1,0:T(8,128)(2,1)S(1)} %collective-permute-done.4.refs_1_), channel_id=1, source_target_pairs={{0,18},{1,19},{2,16},{3,17},{16,2},{17,3},{18,0},{19,1},{4,22},{5,... | collective-permute-start | bytes 405512 | tf_op jit(solution)/shard_map/member_6/ppermute | solution.py:63
  35.1 3.6 %collective-permute-start.11 = (bf16[128,4224]{1,0:T(8,128)(2,1)S(1)}, bf16[128,4224]{1,0:T(8,128)(2,1)S(1)}, u32[]{:S(2)}, u32[]{:S(2)}) collective-permute-start(bf16[128,4224]{1,0:T(8,128)(2,1)S(1)} %packed.4.own_ref), channel_id=1, source_target_pairs={{0,1},{1,0},{2,3},{3,2},{16,17},{17,16},{18,19},{19,18},{4,5},{5,4... | collective-permute-start | bytes 3244040 | tf_op jit(solution)/shard_map/member_1/ppermute | solution.py:63
  35.2 11.9 %collective-permute-start.12 = (bf16[32,4224]{1,0:T(8,128)(2,1)S(1)}, bf16[32,4224]{1,0:T(8,128)(2,1)S(1)}, u32[]{:S(2)}, u32[]{:S(2)}) collective-permute-start(bf16[32,4224]{1,0:T(8,128)(2,1)S(1)} %packed.3.refs_0_), channel_id=1, source_target_pairs={{0,2},{1,3},{2,0},{3,1},{16,18},{17,19},{18,16},{19,17},{4,6},{5,7... | collective-permute-start | bytes 811016 | tf_op jit(solution)/shard_map/member_2/ppermute | solution.py:63
  35.8 11.3 %collective-permute-start.13 = (bf16[32,4224]{1,0:T(8,128)(2,1)S(1)}, bf16[32,4224]{1,0:T(8,128)(2,1)S(1)}, u32[]{:S(2)}, u32[]{:S(2)}) collective-permute-start(bf16[32,4224]{1,0:T(8,128)(2,1)S(1)} %packed.3.refs_0_), channel_id=1, source_target_pairs={{0,16},{1,17},{2,18},{3,19},{16,0},{17,1},{18,2},{19,3},{4,20},{5,... | collective-permute-start | bytes 811016 | tf_op jit(solution)/shard_map/member_4/ppermute | solution.py:63
  37.3 13.8 %collective-permute-start.14 = (bf16[32,4224]{1,0:T(8,128)(2,1)S(1)}, bf16[32,4224]{1,0:T(8,128)(2,1)S(1)}, u32[]{:S(2)}, u32[]{:S(2)}) collective-permute-start(bf16[32,4224]{1,0:T(8,128)(2,1)S(1)} %packed.3.refs_0_), channel_id=1, source_target_pairs={{0,18},{1,19},{2,16},{3,17},{16,2},{17,3},{18,0},{19,1},{4,22},{5,... | collective-permute-start | bytes 811016 | tf_op jit(solution)/shard_map/member_6/ppermute | solution.py:63
  51.1 8.1 %collective-permute-start.15 = (bf16[128,4224]{1,0:T(8,128)(2,1)S(1)}, bf16[128,4224]{1,0:T(8,128)(2,1)S(1)}, u32[]{:S(2)}, u32[]{:S(2)}) collective-permute-start(bf16[128,4224]{1,0:T(8,128)(2,1)S(1)} %packed.5.own_ref), channel_id=1, source_target_pairs={{0,1},{1,0},{2,3},{3,2},{16,17},{17,16},{18,19},{19,18},{4,5},{5,4... | collective-permute-start | bytes 3244040 | tf_op jit(solution)/shard_map/member_1/ppermute | solution.py:63
  51.2 4.2 %collective-permute-start.16 = (bf16[128,4096]{1,0:T(8,128)(2,1)S(1)}, bf16[128,4096]{1,0:T(8,128)(2,1)S(1)}, u32[]{:S(2)}, u32[]{:S(2)}) collective-permute-start(bf16[128,4096]{1,0:T(8,128)(2,1)S(1)} %get-tuple-element.59), channel_id=1, source_target_pairs={{0,1},{1,0},{2,3},{3,2},{16,17},{17,16},{18,19},{19,18},{4,5},{5,4... | collective-permute-start | bytes 3145736 | tf_op jit(solution)/shard_map/member_1/ppermute | solution.py:63
  55.7 8.7 %collective-permute-start.17 = (bf16[16,4096]{1,0:T(8,128)(2,1)S(1)}, bf16[16,4096]{1,0:T(8,128)(2,1)S(1)}, u32[]{:S(2)}, u32[]{:S(2)}) collective-permute-start(bf16[16,4096]{1,0:T(8,128)(2,1)S(1)} %get-tuple-element.68), channel_id=1, source_target_pairs={{0,2},{1,3},{2,0},{3,1},{16,18},{17,19},{18,16},{19,17},{4,6},{5,7... | collective-permute-start | bytes 393224 | tf_op jit(solution)/shard_map/member_2/ppermute | solution.py:63
  56.2 8.1 %collective-permute-start.18 = (bf16[16,4096]{1,0:T(8,128)(2,1)S(1)}, bf16[16,4096]{1,0:T(8,128)(2,1)S(1)}, u32[]{:S(2)}, u32[]{:S(2)}) collective-permute-start(bf16[16,4096]{1,0:T(8,128)(2,1)S(1)} %get-tuple-element.69), channel_id=1, source_target_pairs={{0,16},{1,17},{2,18},{3,19},{16,0},{17,1},{18,2},{19,3},{4,20},{5,... | collective-permute-start | bytes 393224 | tf_op jit(solution)/shard_map/member_4/ppermute | solution.py:63
  57.7 7.5 %collective-permute-start.19 = (bf16[16,4096]{1,0:T(8,128)(2,1)S(1)}, bf16[16,4096]{1,0:T(8,128)(2,1)S(1)}, u32[]{:S(2)}, u32[]{:S(2)}) collective-permute-start(bf16[16,4096]{1,0:T(8,128)(2,1)S(1)} %get-tuple-element.70), channel_id=1, source_target_pairs={{0,18},{1,19},{2,16},{3,17},{16,2},{17,3},{18,0},{19,1},{4,22},{5,... | collective-permute-start | bytes 393224 | tf_op jit(solution)/shard_map/member_6/ppermute | solution.py:63
  68.2 5.7 %collective-permute-start.25 = (bf16[16,4096]{1,0:T(8,128)(2,1)S(1)}, bf16[16,4096]{1,0:T(8,128)(2,1)S(1)}, u32[]{:S(2)}, u32[]{:S(2)}) collective-permute-start(bf16[16,4096]{1,0:T(8,128)(2,1)S(1)} %get-tuple-element.77), channel_id=1, source_target_pairs={{0,2},{1,3},{2,0},{3,1},{16,18},{17,19},{18,16},{19,17},{4,6},{5,7... | collective-permute-start | bytes 393224 | tf_op jit(solution)/shard_map/member_2/ppermute | solution.py:63
  68.7 6.6 %collective-permute-start.26 = (bf16[16,4096]{1,0:T(8,128)(2,1)S(1)}, bf16[16,4096]{1,0:T(8,128)(2,1)S(1)}, u32[]{:S(2)}, u32[]{:S(2)}) collective-permute-start(bf16[16,4096]{1,0:T(8,128)(2,1)S(1)} %get-tuple-element.78), channel_id=1, source_target_pairs={{0,16},{1,17},{2,18},{3,19},{16,0},{17,1},{18,2},{19,3},{4,20},{5,... | collective-permute-start | bytes 393224 | tf_op jit(solution)/shard_map/member_4/ppermute | solution.py:63
  70.2 8.6 %collective-permute-start.27 = (bf16[16,4096]{1,0:T(8,128)(2,1)S(1)}, bf16[16,4096]{1,0:T(8,128)(2,1)S(1)}, u32[]{:S(2)}, u32[]{:S(2)}) collective-permute-start(bf16[16,4096]{1,0:T(8,128)(2,1)S(1)} %get-tuple-element.79), channel_id=1, source_target_pairs={{0,18},{1,19},{2,16},{3,17},{16,2},{17,3},{18,0},{19,1},{4,22},{5,... | collective-permute-start | bytes 393224 | tf_op jit(solution)/shard_map/member_6/ppermute | solution.py:63
  71.7 8.0 %collective-permute-start.21 = (bf16[16,4096]{1,0:T(8,128)(2,1)S(1)}, bf16[16,4096]{1,0:T(8,128)(2,1)S(1)}, u32[]{:S(2)}, u32[]{:S(2)}) collective-permute-start(bf16[16,4096]{1,0:T(8,128)(2,1)S(1)} %get-tuple-element.73), channel_id=1, source_target_pairs={{0,2},{1,3},{2,0},{3,1},{16,18},{17,19},{18,16},{19,17},{4,6},{5,7... | collective-permute-start | bytes 393224 | tf_op jit(solution)/shard_map/member_2/ppermute | solution.py:63
  72.2 9.0 %collective-permute-start.22 = (bf16[16,4096]{1,0:T(8,128)(2,1)S(1)}, bf16[16,4096]{1,0:T(8,128)(2,1)S(1)}, u32[]{:S(2)}, u32[]{:S(2)}) collective-permute-start(bf16[16,4096]{1,0:T(8,128)(2,1)S(1)} %get-tuple-element.74), channel_id=1, source_target_pairs={{0,16},{1,17},{2,18},{3,19},{16,0},{17,1},{18,2},{19,3},{4,20},{5,... | collective-permute-start | bytes 393224 | tf_op jit(solution)/shard_map/member_4/ppermute | solution.py:63
  73.9 10.6 %collective-permute-start.23 = (bf16[16,4096]{1,0:T(8,128)(2,1)S(1)}, bf16[16,4096]{1,0:T(8,128)(2,1)S(1)}, u32[]{:S(2)}, u32[]{:S(2)}) collective-permute-start(bf16[16,4096]{1,0:T(8,128)(2,1)S(1)} %get-tuple-element.75), channel_id=1, source_target_pairs={{0,18},{1,19},{2,16},{3,17},{16,2},{17,3},{18,0},{19,1},{4,22},{5,... | collective-permute-start | bytes 393224 | tf_op jit(solution)/shard_map/member_6/ppermute | solution.py:63
  79.0 7.4 %collective-permute-start.30 = (bf16[16,4096]{1,0:T(8,128)(2,1)S(1)}, bf16[16,4096]{1,0:T(8,128)(2,1)S(1)}, u32[]{:S(2)}, u32[]{:S(2)}) collective-permute-start(bf16[16,4096]{1,0:T(8,128)(2,1)S(1)} %get-tuple-element.83), channel_id=1, source_target_pairs={{0,2},{1,3},{2,0},{3,1},{16,18},{17,19},{18,16},{19,17},{4,6},{5,7... | collective-permute-start | bytes 393224 | tf_op jit(solution)/shard_map/member_2/ppermute | solution.py:63
  79.6 9.5 %collective-permute-start.29 = (bf16[16,4096]{1,0:T(8,128)(2,1)S(1)}, bf16[16,4096]{1,0:T(8,128)(2,1)S(1)}, u32[]{:S(2)}, u32[]{:S(2)}) collective-permute-start(bf16[16,4096]{1,0:T(8,128)(2,1)S(1)} %add_chips.6), channel_id=1, source_target_pairs={{0,4},{1,5},{2,6},{3,7},{16,20},{17,21},{18,22},{19,23},{4,0},{5,1... | collective-permute-start | bytes 393224 | tf_op jit(solution)/shard_map/plane_1/ppermute | solution.py:52
  79.7 7.9 %collective-permute-start.31 = (bf16[16,4096]{1,0:T(8,128)(2,1)S(1)}, bf16[16,4096]{1,0:T(8,128)(2,1)S(1)}, u32[]{:S(2)}, u32[]{:S(2)}) collective-permute-start(bf16[16,4096]{1,0:T(8,128)(2,1)S(1)} %get-tuple-element.85), channel_id=1, source_target_pairs={{0,16},{1,17},{2,18},{3,19},{16,0},{17,1},{18,2},{19,3},{4,20},{5,... | collective-permute-start | bytes 393224 | tf_op jit(solution)/shard_map/member_4/ppermute | solution.py:63
  81.3 7.7 %collective-permute-start.32 = (bf16[16,4096]{1,0:T(8,128)(2,1)S(1)}, bf16[16,4096]{1,0:T(8,128)(2,1)S(1)}, u32[]{:S(2)}, u32[]{:S(2)}) collective-permute-start(bf16[16,4096]{1,0:T(8,128)(2,1)S(1)} %get-tuple-element.87), channel_id=1, source_target_pairs={{0,18},{1,19},{2,16},{3,17},{16,2},{17,3},{18,0},{19,1},{4,22},{5,... | collective-permute-start | bytes 393224 | tf_op jit(solution)/shard_map/member_6/ppermute | solution.py:63
  84.5 6.8 %collective-permute-start.28 = (bf16[16,4096]{1,0:T(8,128)(2,1)S(1)}, bf16[16,4096]{1,0:T(8,128)(2,1)S(1)}, u32[]{:S(2)}, u32[]{:S(2)}) collective-permute-start(bf16[16,4096]{1,0:T(8,128)(2,1)S(1)} %add_chips.5), channel_id=1, source_target_pairs={{0,12},{1,13},{2,14},{3,15},{16,28},{17,29},{18,30},{19,31},{4,8},... | collective-permute-start | bytes 393224 | tf_op jit(solution)/shard_map/plane_3/ppermute | solution.py:52
  86.4 10.5 %collective-permute-start.24 = (bf16[16,4096]{1,0:T(8,128)(2,1)S(1)}, bf16[16,4096]{1,0:T(8,128)(2,1)S(1)}, u32[]{:S(2)}, u32[]{:S(2)}) collective-permute-start(bf16[16,4096]{1,0:T(8,128)(2,1)S(1)} %add_chips.4), channel_id=1, source_target_pairs={{0,8},{1,9},{2,10},{3,11},{16,24},{17,25},{18,26},{19,27},{4,12},{... | collective-permute-start | bytes 393224 | tf_op jit(solution)/shard_map/plane_2/ppermute | solution.py:52
  (7 other events, 46.5 us)

commit v8 on v7

--- a/solution.py
+++ b/solution.py
@@ -449,7 +449,7 @@
     return results[0], results[1], results[2:]
 
 
-def add_up(parts, cuts, name):
+def add_up(parts, cuts, name, work=0):
     rows = sum(cuts)
     model_dim = parts[0][0].shape[1]
     flat = [piece for part in parts for piece in part]
@@ -482,7 +482,7 @@
         out_specs=(VMEM,) * len(cuts),
         compiler_params=pltpu.CompilerParams(vmem_limit_bytes=12 * MEBI),
         cost_estimate=pl.CostEstimate(
-            flops=0, bytes_accessed=0, transcendentals=0
+            flops=work, bytes_accessed=0, transcendentals=0
         ),
         name=name,
     )(*flat)
@@ -590,7 +590,8 @@
     )
 
     first = max(1, planes // 4)
-    groups = [range(0, first), range(first, 2 * first), range(2 * first, planes)]
+    order = sorted(range(planes), key=lambda s: (s & 1, s))
+    groups = [order[:first], order[first : 2 * first], order[2 * first :]]
     chips = range(0, layout.members, 2)
     blocks = [layout.shifted(normed, s) for s in range(planes)]
     arrived = []
@@ -614,9 +615,8 @@
         return own, layout.swapped(own, 1), slots
 
     def add_cores(mine, over):
-        back = layout.swapped(over, 1)
         cuts = [count_of_rows] * (mine.shape[0] // count_of_rows)
-        return add_up([[mine], [back]], cuts, "add_cores")
+        return list(add_up([[mine], [over]], cuts, "add_cores"))
 
     def to_owners(sums, i):
         pieces = len(sums) // len(chips)
@@ -628,20 +628,24 @@
     near = [s for g in (0, 1) for s in groups[g]]
     own, other, slots = to_experts((0, 1), None)
     mine, over, kept = run_experts(own, other, (w_gate_up, w_down), expert, top_count, slots, True)
+    near_mine, near_back = mine, layout.swapped(over, 1)
     far_own, far_other, slots = to_experts((2,), over)
-    near_sums = list(add_cores(mine, over))
-    far_other = after(far_other, near_sums[0])
+    far_other = after(far_other, near_back)
     mine, over, _ = run_experts(far_own, far_other, kept, expert, top_count, slots, False)
-    early = [to_owners(near_sums, i) for i in range(1, len(near))]
-    over = after(over, *[part for parts in early for part in parts[1:]])
-    far_sums = add_cores(mine, over)
-    totals = {s: total_of(to_owners(far_sums, i)) for i, s in enumerate(groups[2])}
-    totals.update({s: total_of(parts) for s, parts in zip(near[1:], early)})
-    pieces = len(near_sums) // len(chips)
-    for c in range(len(chips)):
-        near_sums[c * pieces] = after(near_sums[c * pieces], totals[groups[2][-1]])
-    totals[near[0]] = total_of(to_owners(near_sums, 0))
-    others = [layout.shifted(total, s) for s, total in totals.items()]
+    near_sums = add_up(
+        [[near_mine], [near_back]], [count_of_rows * len(near)] * len(chips), "add_cores"
+    )
+    far_sums = add_cores(mine, layout.swapped(over, 1))
+    parts = to_owners(near_sums, 0)
+    totals = add_up([[part] for part in parts], [count_of_rows] * len(near), "add_chips")
+    others = [layout.shifted(total, by) for total, by in zip(totals, near)]
+    for i, by in list(enumerate(groups[2]))[::-1]:
+        others.append(layout.shifted(total_of(to_owners(far_sums, i)), by))
+    count = len(near) + 1
+    merged = add_up(
+        [[merged]] + [[part] for part in others[:count]], [count_of_rows], "add_first", 10**10
+    )[0]
+    others = others[count:]
     total = merged.astype(jnp.float32) + sum(part.astype(jnp.float32) for part in others)
     layer_out = total.astype(jnp.bfloat16)
     return (attended, layer_out)

time: 97.9 us -> 97.8 us (level)
  starting transfers between devices: 39.9 us -> 35.8 us
  waiting for transfers between devices: 33.5 us -> 37.4 us
    ppermute x25 -> x22, starting transfers between devices: 25.3 us -> 22.3 us  [swapped(): return lax.ppermute(value, AXES, pairs)]
    ppermute x25 -> x22, waiting for transfers between devices: 21.6 us -> 24.3 us  [swapped(): return lax.ppermute(value, AXES, pairs)]
    ppermute x6, waiting for transfers between devices: 9.87 us -> 11.1 us  [shifted(): return lax.ppermute(value, AXES, pairs)]
    ppermute x6, starting transfers between devices: 9.48 us -> 8.41 us  [shifted(): return lax.ppermute(value, AXES, pairs)]
  transfers between devices with their start and end apart: 33 -> 30, of which waited for: 15 -> 15; matrix products, arithmetic and copies ran while one was open for 0% -> 0% of each run, Pallas kernels for 19% -> 14%
where the time goes in v8:
time: 97.8 us; the launch traced here: 97.4 us
  waiting for transfers between devices  37.4 us (38%)
  starting transfers between devices  35.8 us (37%)
  Pallas kernels  22.6 us (23%)
    ppermute x22, waiting for transfers between devices, swapped(): return lax.ppermute(value, AXES, pairs)  24.3 us
    ppermute x22, starting transfers between devices, swapped(): return lax.ppermute(value, AXES, pairs)  22.3 us
    pallas_call x2, Pallas kernels, run_experts(): pl.pallas_call(kernel, out_shape=(shape, shape) + kept, in_specs=[SMEM, V...  13.4 us
    ppermute x6, waiting for transfers between devices, shifted(): return lax.ppermute(value, AXES, pairs)  11.1 us
    ppermute x6, starting transfers between devices, shifted(): return lax.ppermute(value, AXES, pairs)  8.41 us
    ppermute x2, starting transfers between devices, from_behind(): lax.ppermute(value, axis, [(i, (i + by) % length) for i in range(length)])  5.09 us
    pallas_call x1, Pallas kernels, own_attention(): pl.pallas_call(kernel, out_shape=(shape, shape, shape, jax.ShapeDtypeStru...  4.74 us
    ppermute x2, waiting for transfers between devices, from_behind(): lax.ppermute(value, axis, [(i, (i + by) % length) for i in range(length)])  2.06 us
  transfers between devices with their start and end apart: 30, of which 15 were waited for; matrix products, arithmetic and copies ran while one was open for 0% of the time, Pallas kernels for 14%

profile of v8, /device:TPU:0, one launch (start us, length us, event | category | flops | bytes accessed | tf_op | source)
XLA Modules:
  0.0 97.4 jit_solution(2356306293111478326)
XLA Ops:
  0.6 3.0 %collective-permute-start = (s32[16]{0:T(128)}, s32[16]{0:T(128)S(1)}, u32[]{:S(2)}, u32[]{:S(2)}) collective-permute-start(s32[16]{0:T(128)} %param.17), channel_id=1, source_target_pairs={{0,16},{16,0},{1,17},{17,1},{2,18},{18,2},{3,19},{19,3},{4,20},{20... | collective-permute-start | bytes 200 | tf_op jit(solution)/shard_map/ppermute | solution.py:68
  3.6 1.7 %collective-permute-done.slots_ref = s32[16]{0:T(128)S(1)} collective-permute-done((s32[16]{0:T(128)}, s32[16]{0:T(128)S(1)}, u32[]{:S(2)}, u32[]{:S(2)}) %collective-permute-start) | collective-permute-done | bytes 96 | tf_op jit(solution)/shard_map/ppermute | solution.py:68
  5.3 1.6 %pick_pages.1 = bf16[16,16,512]{2,1,0:T(8,128)(2,1)S(1)} custom-call(s32[16]{0:T(128)S(1)} %collective-permute-done.slots_ref, bf16[128,16,512]{2,1,0:T(8,128)(2,1)} %pages_hbm.1), custom_call_target="tpu_custom_call" | custom-call | bytes 1048576 | tf_op jit(solution)/shard_map/pick_pages/pallas_call | solution.py:84
  7.0 2.1 %collective-permute-start.1 = (bf16[16,16,512]{2,1,0:T(8,128)(2,1)S(1)}, bf16[16,16,512]{2,1,0:T(8,128)(2,1)S(1)}, u32[]{:S(2)}, u32[]{:S(2)}) collective-permute-start(bf16[16,16,512]{2,1,0:T(8,128)(2,1)S(1)} %pick_pages.1), channel_id=1, source_target_pairs={{0,16},{16,0},{1,17},{17,1},{2,18},{18,2},{3,19},{19,3},{4,20},{20... | collective-permute-start | bytes 786440 | tf_op jit(solution)/shard_map/ppermute | solution.py:68
  9.0 4.7 %own_attention.1 = (f32[512,128]{1,0:T(8,128)S(1)}, f32[512,128]{1,0:T(8,128)S(1)}, f32[512,128]{1,0:T(8,128)S(1)}, bf16[512,128]{1,0:T(8,128)(2,1)S(1)}) custom-call(bf16[16,4096]{1,0:T(8,128)(2,1)} %queries_hbm, bf16[16,512]{1,0:T(8,128)(2,1)} %new_hbm.1, bf16[128,16,512]{2,1,0:T(8,128)(2,1)} %pages_hbm.1, s32[16,16]{1,0:T(8,128)} %table_ref.1, s32[16]{0:T(128)} %lengths_ref.1), custom_call_target="tpu_custom_call" | custom-call | flops 1073741824 | bytes 16777216 | tf_op jit(solution)/shard_map/own_attention/pallas_call | solution.py:239
  14.2 1.9 %finish_attention.1 = (bf16[16,4096]{1,0:T(8,128)(2,1)}, bf16[16,4096]{1,0:T(8,128)(2,1)S(1)}, bf16[16,4224]{1,0:T(8,128)(2,1)S(1)}) custom-call(bf16[512,128]{1,0:T(8,128)(2,1)S(1)} %get-tuple-element.39.q_ref, bf16[16,16,512]{2,1,0:T(8,128)(2,1)S(1)} %collective-permute-done.1.fetched_ref, s32[16,16]{1,0:T(8,128)S(1)} %copy-done.2, s32[16]{0:T(128)S(1)} %copy-done.5, ...), custom_call_target="tpu_custom_call" | custom-call | flops 134217728 | bytes 4194304 | tf_op jit(solution)/shard_map/finish_attention/pallas_call | solution.py:538
  16.2 2.7 %collective-permute-start.9 = (bf16[16,4224]{1,0:T(8,128)(2,1)S(1)}, bf16[16,4224]{1,0:T(8,128)(2,1)S(1)}, u32[]{:S(2)}, u32[]{:S(2)}) collective-permute-start(bf16[16,4224]{1,0:T(8,128)(2,1)S(1)} %get-tuple-element.47.refs_0_), channel_id=1, source_target_pairs={{0,18},{1,19},{2,16},{3,17},{16,2},{17,3},{18,0},{19,1},{4,22},{5,... | collective-permute-start | bytes 405512 | tf_op jit(solution)/shard_map/member_6/ppermute | solution.py:63
  18.9 2.6 %collective-permute-start.4 = (bf16[16,4224]{1,0:T(8,128)(2,1)S(1)}, bf16[16,4224]{1,0:T(8,128)(2,1)S(1)}, u32[]{:S(2)}, u32[]{:S(2)}) collective-permute-start(bf16[16,4224]{1,0:T(8,128)(2,1)S(1)} %get-tuple-element.47.refs_0_), channel_id=1, source_target_pairs={{0,8},{1,9},{2,10},{3,11},{16,24},{17,25},{18,26},{19,27},{4,12},{... | collective-permute-start | bytes 405512 | tf_op jit(solution)/shard_map/plane_2/ppermute | solution.py:52
  22.5 1.3 %collective-permute-start.3 = (bf16[16,4224]{1,0:T(8,128)(2,1)S(1)}, bf16[16,4224]{1,0:T(8,128)(2,1)S(1)}, u32[]{:S(2)}, u32[]{:S(2)}) collective-permute-start(bf16[16,4224]{1,0:T(8,128)(2,1)S(1)} %get-tuple-element.47.refs_0_), channel_id=1, source_target_pairs={{0,12},{1,13},{2,14},{3,15},{16,28},{17,29},{18,30},{19,31},{4,8},... | collective-permute-start | bytes 405512 | tf_op jit(solution)/shard_map/plane_3/ppermute | solution.py:52
  25.0 5.0 %collective-permute-done.4.refs_1_ = bf16[16,4224]{1,0:T(8,128)(2,1)S(1)} collective-permute-done((bf16[16,4224]{1,0:T(8,128)(2,1)S(1)}, bf16[16,4224]{1,0:T(8,128)(2,1)S(1)}, u32[]{:S(2)}, u32[]{:S(2)}) %collective-permute-start.4) | collective-permute-done | bytes 135200 | tf_op jit(solution)/shard_map/plane_2/ppermute | solution.py:52
  30.2 3.4 %collective-permute-start.10 = (bf16[16,4224]{1,0:T(8,128)(2,1)S(1)}, bf16[16,4224]{1,0:T(8,128)(2,1)S(1)}, u32[]{:S(2)}, u32[]{:S(2)}) collective-permute-start(bf16[16,4224]{1,0:T(8,128)(2,1)S(1)} %collective-permute-done.4.refs_1_), channel_id=1, source_target_pairs={{0,18},{1,19},{2,16},{3,17},{16,2},{17,3},{18,0},{19,1},{4,22},{5,... | collective-permute-start | bytes 405512 | tf_op jit(solution)/shard_map/member_6/ppermute | solution.py:63
  33.6 1.5 %collective-permute-done.6.refs_3_ = bf16[16,4224]{1,0:T(8,128)(2,1)S(1)} collective-permute-done((bf16[16,4224]{1,0:T(8,128)(2,1)S(1)}, bf16[16,4224]{1,0:T(8,128)(2,1)S(1)}, u32[]{:S(2)}, u32[]{:S(2)}) %collective-permute-start.6) | collective-permute-done | bytes 135200 | tf_op jit(solution)/shard_map/member_2/ppermute | solution.py:63
  35.2 2.8 %collective-permute-done.10.refs_7_ = bf16[16,4224]{1,0:T(8,128)(2,1)S(1)} collective-permute-done((bf16[16,4224]{1,0:T(8,128)(2,1)S(1)}, bf16[16,4224]{1,0:T(8,128)(2,1)S(1)}, u32[]{:S(2)}, u32[]{:S(2)}) %collective-permute-start.10) | collective-permute-done | bytes 135200 | tf_op jit(solution)/shard_map/member_6/ppermute | solution.py:63
  38.2 1.5 %collective-permute-start.19 = (bf16[32,4224]{1,0:T(8,128)(2,1)S(1)}, bf16[32,4224]{1,0:T(8,128)(2,1)S(1)}, u32[]{:S(2)}, u32[]{:S(2)}) collective-permute-start(bf16[32,4224]{1,0:T(8,128)(2,1)S(1)} %packed.3.refs_0_), channel_id=1, source_target_pairs={{0,18},{1,19},{2,16},{3,17},{16,2},{17,3},{18,0},{19,1},{4,22},{5,... | collective-permute-start | bytes 811016 | tf_op jit(solution)/shard_map/member_6/ppermute | solution.py:63
  39.8 2.0 %collective-permute-start.17 = (bf16[32,4224]{1,0:T(8,128)(2,1)S(1)}, bf16[32,4224]{1,0:T(8,128)(2,1)S(1)}, u32[]{:S(2)}, u32[]{:S(2)}) collective-permute-start(bf16[32,4224]{1,0:T(8,128)(2,1)S(1)} %packed.3.refs_0_), channel_id=1, source_target_pairs={{0,2},{1,3},{2,0},{3,1},{16,18},{17,19},{18,16},{19,17},{4,6},{5,7... | collective-permute-start | bytes 811016 | tf_op jit(solution)/shard_map/member_2/ppermute | solution.py:63
  41.7 8.3 %run_experts.2 = (bf16[128,4096]{1,0:T(8,128)(2,1)S(1)}, bf16[128,4096]{1,0:T(8,128)(2,1)S(1)}, bf16[4096,1536]{1,0:T(8,128)(2,1)S(1)}, bf16[768,4096]{1,0:T(8,128)(2,1)S(1)}) custom-call(s32[1]{0:T(128)} %bitcast.3.expert_ref, bf16[128,4224]{1,0:T(8,128)(2,1)S(1)} %packed.4.own_ref, bf16[128,4224]{1,0:T(8,128)(2,1)S(1)} %collective-permute-done.11.other_ref, ...), custom_call_target="tpu_custom_call" | custom-call | flops 2415919104 | bytes 20971520 | tf_op jit(solution)/shard_map/run_experts/pallas_call | solution.py:431
  50.0 2.4 %collective-permute-done.18.refs_2_ = bf16[32,4224]{1,0:T(8,128)(2,1)S(1)} collective-permute-done((bf16[32,4224]{1,0:T(8,128)(2,1)S(1)}, bf16[32,4224]{1,0:T(8,128)(2,1)S(1)}, u32[]{:S(2)}, u32[]{:S(2)}) %collective-permute-start.18) | collective-permute-done | bytes 270368 | tf_op jit(solution)/shard_map/member_4/ppermute | solution.py:63
  54.4 3.7 %collective-permute-done.12.refs_1_ = bf16[128,4096]{1,0:T(8,128)(2,1)S(1)} collective-permute-done((bf16[128,4096]{1,0:T(8,128)(2,1)S(1)}, bf16[128,4096]{1,0:T(8,128)(2,1)S(1)}, u32[]{:S(2)}, u32[]{:S(2)}) %collective-permute-start.12) | collective-permute-done | bytes 1048608 | tf_op jit(solution)/shard_map/member_1/ppermute | solution.py:63
  58.1 5.1 %run_experts.3 = (bf16[128,4096]{1,0:T(8,128)(2,1)S(1)}, bf16[128,4096]{1,0:T(8,128)(2,1)S(1)}) custom-call(s32[1]{0:T(128)} %bitcast.3.expert_ref, bf16[128,4224]{1,0:T(8,128)(2,1)S(1)} %packed.5.own_ref, bf16[128,4224]{1,0:T(8,128)(2,1)S(1)} %collective-permute-done.20.other_ref, bf16[4096,1536]{1,0:T(8,128)(2,1)S(1)} %get-tuple-element.62.refs_0_, ...), custom_call_target="tpu_custom_call" | custom-call | flops 2415919104 | bytes 20971520 | tf_op jit(solution)/shard_map/run_experts/pallas_call | solution.py:431
  64.3 1.4 %collective-permute-start.14 = (bf16[32,4096]{1,0:T(8,128)(2,1)S(1)}, bf16[32,4096]{1,0:T(8,128)(2,1)S(1)}, u32[]{:S(2)}, u32[]{:S(2)}) collective-permute-start(bf16[32,4096]{1,0:T(8,128)(2,1)S(1)} %get-tuple-element.56), channel_id=1, source_target_pairs={{0,16},{1,17},{2,18},{3,19},{16,0},{17,1},{18,2},{19,3},{4,20},{5,... | collective-permute-start | bytes 786440 | tf_op jit(solution)/shard_map/member_4/ppermute | solution.py:63
  65.8 1.4 %collective-permute-start.15 = (bf16[32,4096]{1,0:T(8,128)(2,1)S(1)}, bf16[32,4096]{1,0:T(8,128)(2,1)S(1)}, u32[]{:S(2)}, u32[]{:S(2)}) collective-permute-start(bf16[32,4096]{1,0:T(8,128)(2,1)S(1)} %get-tuple-element.57), channel_id=1, source_target_pairs={{0,18},{1,19},{2,16},{3,17},{16,2},{17,3},{18,0},{19,1},{4,22},{5,... | collective-permute-start | bytes 786440 | tf_op jit(solution)/shard_map/member_6/ppermute | solution.py:63
  68.1 1.4 %collective-permute-start.23 = (bf16[16,4096]{1,0:T(8,128)(2,1)S(1)}, bf16[16,4096]{1,0:T(8,128)(2,1)S(1)}, u32[]{:S(2)}, u32[]{:S(2)}) collective-permute-start(bf16[16,4096]{1,0:T(8,128)(2,1)S(1)} %get-tuple-element.68), channel_id=1, source_target_pairs={{0,16},{1,17},{2,18},{3,19},{16,0},{17,1},{18,2},{19,3},{4,20},{5,... | collective-permute-start | bytes 393224 | tf_op jit(solution)/shard_map/member_4/ppermute | solution.py:63
  69.6 3.5 %collective-permute-done.13.refs_1_ = bf16[32,4096]{1,0:T(8,128)(2,1)S(1)} collective-permute-done((bf16[32,4096]{1,0:T(8,128)(2,1)S(1)}, bf16[32,4096]{1,0:T(8,128)(2,1)S(1)}, u32[]{:S(2)}, u32[]{:S(2)}) %collective-permute-start.13) | collective-permute-done | bytes 262176 | tf_op jit(solution)/shard_map/member_2/ppermute | solution.py:63
  73.1 1.5 %collective-permute-start.24 = (bf16[16,4096]{1,0:T(8,128)(2,1)S(1)}, bf16[16,4096]{1,0:T(8,128)(2,1)S(1)}, u32[]{:S(2)}, u32[]{:S(2)}) collective-permute-start(bf16[16,4096]{1,0:T(8,128)(2,1)S(1)} %get-tuple-element.69), channel_id=1, source_target_pairs={{0,18},{1,19},{2,16},{3,17},{16,2},{17,3},{18,0},{19,1},{4,22},{5,... | collective-permute-start | bytes 393224 | tf_op jit(solution)/shard_map/member_6/ppermute | solution.py:63
  74.5 5.5 %collective-permute-done.15.refs_3_ = bf16[32,4096]{1,0:T(8,128)(2,1)S(1)} collective-permute-done((bf16[32,4096]{1,0:T(8,128)(2,1)S(1)}, bf16[32,4096]{1,0:T(8,128)(2,1)S(1)}, u32[]{:S(2)}, u32[]{:S(2)}) %collective-permute-start.15) | collective-permute-done | bytes 262176 | tf_op jit(solution)/shard_map/member_6/ppermute | solution.py:63
  80.8 1.4 %collective-permute-start.27 = (bf16[16,4096]{1,0:T(8,128)(2,1)S(1)}, bf16[16,4096]{1,0:T(8,128)(2,1)S(1)}, u32[]{:S(2)}, u32[]{:S(2)}) collective-permute-start(bf16[16,4096]{1,0:T(8,128)(2,1)S(1)} %get-tuple-element.72), channel_id=1, source_target_pairs={{0,16},{1,17},{2,18},{3,19},{16,0},{17,1},{18,2},{19,3},{4,20},{5,... | collective-permute-start | bytes 393224 | tf_op jit(solution)/shard_map/member_4/ppermute | solution.py:63
  82.2 1.4 %collective-permute-start.28 = (bf16[16,4096]{1,0:T(8,128)(2,1)S(1)}, bf16[16,4096]{1,0:T(8,128)(2,1)S(1)}, u32[]{:S(2)}, u32[]{:S(2)}) collective-permute-start(bf16[16,4096]{1,0:T(8,128)(2,1)S(1)} %get-tuple-element.73), channel_id=1, source_target_pairs={{0,18},{1,19},{2,16},{3,17},{16,2},{17,3},{18,0},{19,1},{4,22},{5,... | collective-permute-start | bytes 393224 | tf_op jit(solution)/shard_map/member_6/ppermute | solution.py:63
  83.8 1.9 %collective-permute-done.24.refs_3_ = bf16[16,4096]{1,0:T(8,128)(2,1)S(1)} collective-permute-done((bf16[16,4096]{1,0:T(8,128)(2,1)S(1)}, bf16[16,4096]{1,0:T(8,128)(2,1)S(1)}, u32[]{:S(2)}, u32[]{:S(2)}) %collective-permute-start.24) | collective-permute-done | bytes 131104 | tf_op jit(solution)/shard_map/member_6/ppermute | solution.py:63
  85.7 3.1 %collective-permute-start.25 = (bf16[16,4096]{1,0:T(8,128)(2,1)S(1)}, bf16[16,4096]{1,0:T(8,128)(2,1)S(1)}, u32[]{:S(2)}, u32[]{:S(2)}) collective-permute-start(bf16[16,4096]{1,0:T(8,128)(2,1)S(1)} %add_chips.4), channel_id=1, source_target_pairs={{0,12},{1,13},{2,14},{3,15},{16,28},{17,29},{18,30},{19,31},{4,8},... | collective-permute-start | bytes 393224 | tf_op jit(solution)/shard_map/plane_3/ppermute | solution.py:52
  88.8 1.6 %collective-permute-done.28.refs_3_ = bf16[16,4096]{1,0:T(8,128)(2,1)S(1)} collective-permute-done((bf16[16,4096]{1,0:T(8,128)(2,1)S(1)}, bf16[16,4096]{1,0:T(8,128)(2,1)S(1)}, u32[]{:S(2)}, u32[]{:S(2)}) %collective-permute-start.28) | collective-permute-done | bytes 131104 | tf_op jit(solution)/shard_map/member_6/ppermute | solution.py:63
  90.6 4.2 %collective-permute-done.16.refs_2_ = bf16[16,4096]{1,0:T(8,128)(2,1)S(1)} collective-permute-done((bf16[16,4096]{1,0:T(8,128)(2,1)S(1)}, bf16[16,4096]{1,0:T(8,128)(2,1)S(1)}, u32[]{:S(2)}, u32[]{:S(2)}) %collective-permute-start.16) | collective-permute-done | bytes 131104 | tf_op jit(solution)/shard_map/plane_2/ppermute | solution.py:52
  94.9 1.8 %collective-permute-done.29 = bf16[16,4096]{1,0:T(8,128)(2,1)S(1)} collective-permute-done((bf16[16,4096]{1,0:T(8,128)(2,1)S(1)}, bf16[16,4096]{1,0:T(8,128)(2,1)S(1)}, u32[]{:S(2)}, u32[]{:S(2)}) %collective-permute-start.29) | collective-permute-done | bytes 131104 | tf_op jit(solution)/shard_map/plane_1/ppermute | solution.py:52
  (55 shorter events, 9.0 us)
Async XLA Ops:
  0.6 4.7 %collective-permute-start = (s32[16]{0:T(128)}, s32[16]{0:T(128)S(1)}, u32[]{:S(2)}, u32[]{:S(2)}) collective-permute-start(s32[16]{0:T(128)} %param.17), channel_id=1, source_target_pairs={{0,16},{16,0},{1,17},{17,1},{2,18},{18,2},{3,19},{19,3},{4,20},{20... | collective-permute-start | bytes 200 | tf_op jit(solution)/shard_map/ppermute | solution.py:68
  6.9 7.3 %copy-start = (bf16[16,4096]{1,0:T(8,128)(2,1)S(1)}, bf16[16,4096]{1,0:T(8,128)(2,1)}, u32[]{:S(2)}) copy-start(bf16[16,4096]{1,0:T(8,128)(2,1)} %residual_ref.1) | copy-start | bytes 393220
  6.9 7.3 %copy-start.1 = (f32[4096]{0:T(1024)S(1)}, f32[4096]{0:T(1024)}, u32[]{:S(2)}) copy-start(f32[4096]{0:T(1024)} %param.19) | copy-start | bytes 49156
  7.0 7.2 %collective-permute-start.1 = (bf16[16,16,512]{2,1,0:T(8,128)(2,1)S(1)}, bf16[16,16,512]{2,1,0:T(8,128)(2,1)S(1)}, u32[]{:S(2)}, u32[]{:S(2)}) collective-permute-start(bf16[16,16,512]{2,1,0:T(8,128)(2,1)S(1)} %pick_pages.1), channel_id=1, source_target_pairs={{0,16},{16,0},{1,17},{17,1},{2,18},{18,2},{3,19},{19,3},{4,20},{20... | collective-permute-start | bytes 786440 | tf_op jit(solution)/shard_map/ppermute | solution.py:68
  16.2 7.7 %collective-permute-start.9 = (bf16[16,4224]{1,0:T(8,128)(2,1)S(1)}, bf16[16,4224]{1,0:T(8,128)(2,1)S(1)}, u32[]{:S(2)}, u32[]{:S(2)}) collective-permute-start(bf16[16,4224]{1,0:T(8,128)(2,1)S(1)} %get-tuple-element.47.refs_0_), channel_id=1, source_target_pairs={{0,18},{1,19},{2,16},{3,17},{16,2},{17,3},{18,0},{19,1},{4,22},{5,... | collective-permute-start | bytes 405512 | tf_op jit(solution)/shard_map/member_6/ppermute | solution.py:63
  18.9 11.2 %collective-permute-start.4 = (bf16[16,4224]{1,0:T(8,128)(2,1)S(1)}, bf16[16,4224]{1,0:T(8,128)(2,1)S(1)}, u32[]{:S(2)}, u32[]{:S(2)}) collective-permute-start(bf16[16,4224]{1,0:T(8,128)(2,1)S(1)} %get-tuple-element.47.refs_0_), channel_id=1, source_target_pairs={{0,8},{1,9},{2,10},{3,11},{16,24},{17,25},{18,26},{19,27},{4,12},{... | collective-permute-start | bytes 405512 | tf_op jit(solution)/shard_map/plane_2/ppermute | solution.py:52
  21.5 8.6 %collective-permute-start.7 = (bf16[16,4224]{1,0:T(8,128)(2,1)S(1)}, bf16[16,4224]{1,0:T(8,128)(2,1)S(1)}, u32[]{:S(2)}, u32[]{:S(2)}) collective-permute-start(bf16[16,4224]{1,0:T(8,128)(2,1)S(1)} %get-tuple-element.47.refs_0_), channel_id=1, source_target_pairs={{0,16},{1,17},{2,18},{3,19},{16,0},{17,1},{18,2},{19,3},{4,20},{5,... | collective-permute-start | bytes 405512 | tf_op jit(solution)/shard_map/member_4/ppermute | solution.py:63
  22.0 8.1 %collective-permute-start.5 = (bf16[16,4224]{1,0:T(8,128)(2,1)S(1)}, bf16[16,4224]{1,0:T(8,128)(2,1)S(1)}, u32[]{:S(2)}, u32[]{:S(2)}) collective-permute-start(bf16[16,4224]{1,0:T(8,128)(2,1)S(1)} %get-tuple-element.47.refs_0_), channel_id=1, source_target_pairs={{0,2},{1,3},{2,0},{3,1},{16,18},{17,19},{18,16},{19,17},{4,6},{5,7... | collective-permute-start | bytes 405512 | tf_op jit(solution)/shard_map/member_2/ppermute | solution.py:63
  22.5 11.1 %collective-permute-start.3 = (bf16[16,4224]{1,0:T(8,128)(2,1)S(1)}, bf16[16,4224]{1,0:T(8,128)(2,1)S(1)}, u32[]{:S(2)}, u32[]{:S(2)}) collective-permute-start(bf16[16,4224]{1,0:T(8,128)(2,1)S(1)} %get-tuple-element.47.refs_0_), channel_id=1, source_target_pairs={{0,12},{1,13},{2,14},{3,15},{16,28},{17,29},{18,30},{19,31},{4,8},... | collective-permute-start | bytes 405512 | tf_op jit(solution)/shard_map/plane_3/ppermute | solution.py:52
  23.9 9.7 %collective-permute-start.2 = (bf16[16,4224]{1,0:T(8,128)(2,1)S(1)}, bf16[16,4224]{1,0:T(8,128)(2,1)S(1)}, u32[]{:S(2)}, u32[]{:S(2)}) collective-permute-start(bf16[16,4224]{1,0:T(8,128)(2,1)S(1)} %get-tuple-element.47.refs_0_), channel_id=1, source_target_pairs={{0,4},{1,5},{2,6},{3,7},{16,20},{17,21},{18,22},{19,23},{4,0},{5,1... | collective-permute-start | bytes 405512 | tf_op jit(solution)/shard_map/plane_1/ppermute | solution.py:52
  30.1 5.0 %collective-permute-start.6 = (bf16[16,4224]{1,0:T(8,128)(2,1)S(1)}, bf16[16,4224]{1,0:T(8,128)(2,1)S(1)}, u32[]{:S(2)}, u32[]{:S(2)}) collective-permute-start(bf16[16,4224]{1,0:T(8,128)(2,1)S(1)} %collective-permute-done.4.refs_1_), channel_id=1, source_target_pairs={{0,2},{1,3},{2,0},{3,1},{16,18},{17,19},{18,16},{19,17},{4,6},{5,7... | collective-permute-start | bytes 405512 | tf_op jit(solution)/shard_map/member_2/ppermute | solution.py:63
  30.1 5.1 %collective-permute-start.8 = (bf16[16,4224]{1,0:T(8,128)(2,1)S(1)}, bf16[16,4224]{1,0:T(8,128)(2,1)S(1)}, u32[]{:S(2)}, u32[]{:S(2)}) collective-permute-start(bf16[16,4224]{1,0:T(8,128)(2,1)S(1)} %collective-permute-done.4.refs_1_), channel_id=1, source_target_pairs={{0,16},{1,17},{2,18},{3,19},{16,0},{17,1},{18,2},{19,3},{4,20},{5,... | collective-permute-start | bytes 405512 | tf_op jit(solution)/shard_map/member_4/ppermute | solution.py:63
  30.2 7.8 %collective-permute-start.10 = (bf16[16,4224]{1,0:T(8,128)(2,1)S(1)}, bf16[16,4224]{1,0:T(8,128)(2,1)S(1)}, u32[]{:S(2)}, u32[]{:S(2)}) collective-permute-start(bf16[16,4224]{1,0:T(8,128)(2,1)S(1)} %collective-permute-done.4.refs_1_), channel_id=1, source_target_pairs={{0,18},{1,19},{2,16},{3,17},{16,2},{17,3},{18,0},{19,1},{4,22},{5,... | collective-permute-start | bytes 405512 | tf_op jit(solution)/shard_map/member_6/ppermute | solution.py:63
  38.1 3.6 %collective-permute-start.11 = (bf16[128,4224]{1,0:T(8,128)(2,1)S(1)}, bf16[128,4224]{1,0:T(8,128)(2,1)S(1)}, u32[]{:S(2)}, u32[]{:S(2)}) collective-permute-start(bf16[128,4224]{1,0:T(8,128)(2,1)S(1)} %packed.4.own_ref), channel_id=1, source_target_pairs={{0,1},{1,0},{2,3},{3,2},{16,17},{17,16},{18,19},{19,18},{4,5},{5,4... | collective-permute-start | bytes 3244040 | tf_op jit(solution)/shard_map/member_1/ppermute | solution.py:63
  38.2 11.9 %collective-permute-start.19 = (bf16[32,4224]{1,0:T(8,128)(2,1)S(1)}, bf16[32,4224]{1,0:T(8,128)(2,1)S(1)}, u32[]{:S(2)}, u32[]{:S(2)}) collective-permute-start(bf16[32,4224]{1,0:T(8,128)(2,1)S(1)} %packed.3.refs_0_), channel_id=1, source_target_pairs={{0,18},{1,19},{2,16},{3,17},{16,2},{17,3},{18,0},{19,1},{4,22},{5,... | collective-permute-start | bytes 811016 | tf_op jit(solution)/shard_map/member_6/ppermute | solution.py:63
  39.7 12.7 %collective-permute-start.18 = (bf16[32,4224]{1,0:T(8,128)(2,1)S(1)}, bf16[32,4224]{1,0:T(8,128)(2,1)S(1)}, u32[]{:S(2)}, u32[]{:S(2)}) collective-permute-start(bf16[32,4224]{1,0:T(8,128)(2,1)S(1)} %packed.3.refs_0_), channel_id=1, source_target_pairs={{0,16},{1,17},{2,18},{3,19},{16,0},{17,1},{18,2},{19,3},{4,20},{5,... | collective-permute-start | bytes 811016 | tf_op jit(solution)/shard_map/member_4/ppermute | solution.py:63
  39.8 14.0 %collective-permute-start.17 = (bf16[32,4224]{1,0:T(8,128)(2,1)S(1)}, bf16[32,4224]{1,0:T(8,128)(2,1)S(1)}, u32[]{:S(2)}, u32[]{:S(2)}) collective-permute-start(bf16[32,4224]{1,0:T(8,128)(2,1)S(1)} %packed.3.refs_0_), channel_id=1, source_target_pairs={{0,2},{1,3},{2,0},{3,1},{16,18},{17,19},{18,16},{19,17},{4,6},{5,7... | collective-permute-start | bytes 811016 | tf_op jit(solution)/shard_map/member_2/ppermute | solution.py:63
  53.8 4.3 %collective-permute-start.20 = (bf16[128,4224]{1,0:T(8,128)(2,1)S(1)}, bf16[128,4224]{1,0:T(8,128)(2,1)S(1)}, u32[]{:S(2)}, u32[]{:S(2)}) collective-permute-start(bf16[128,4224]{1,0:T(8,128)(2,1)S(1)} %packed.5.own_ref), channel_id=1, source_target_pairs={{0,1},{1,0},{2,3},{3,2},{16,17},{17,16},{18,19},{19,18},{4,5},{5,4... | collective-permute-start | bytes 3244040 | tf_op jit(solution)/shard_map/member_1/ppermute | solution.py:63
  53.9 4.2 %collective-permute-start.12 = (bf16[128,4096]{1,0:T(8,128)(2,1)S(1)}, bf16[128,4096]{1,0:T(8,128)(2,1)S(1)}, u32[]{:S(2)}, u32[]{:S(2)}) collective-permute-start(bf16[128,4096]{1,0:T(8,128)(2,1)S(1)} %get-tuple-element.53), channel_id=1, source_target_pairs={{0,1},{1,0},{2,3},{3,2},{16,17},{17,16},{18,19},{19,18},{4,5},{5,4... | collective-permute-start | bytes 3145736 | tf_op jit(solution)/shard_map/member_1/ppermute | solution.py:63
  63.2 4.0 %collective-permute-start.21 = (bf16[128,4096]{1,0:T(8,128)(2,1)S(1)}, bf16[128,4096]{1,0:T(8,128)(2,1)S(1)}, u32[]{:S(2)}, u32[]{:S(2)}) collective-permute-start(bf16[128,4096]{1,0:T(8,128)(2,1)S(1)} %get-tuple-element.65), channel_id=1, source_target_pairs={{0,1},{1,0},{2,3},{3,2},{16,17},{17,16},{18,19},{19,18},{4,5},{5,4... | collective-permute-start | bytes 3145736 | tf_op jit(solution)/shard_map/member_1/ppermute | solution.py:63
  63.6 9.4 %collective-permute-start.13 = (bf16[32,4096]{1,0:T(8,128)(2,1)S(1)}, bf16[32,4096]{1,0:T(8,128)(2,1)S(1)}, u32[]{:S(2)}, u32[]{:S(2)}) collective-permute-start(bf16[32,4096]{1,0:T(8,128)(2,1)S(1)} %get-tuple-element.55), channel_id=1, source_target_pairs={{0,2},{1,3},{2,0},{3,1},{16,18},{17,19},{18,16},{19,17},{4,6},{5,7... | collective-permute-start | bytes 786440 | tf_op jit(solution)/shard_map/member_2/ppermute | solution.py:63
  64.3 10.2 %collective-permute-start.14 = (bf16[32,4096]{1,0:T(8,128)(2,1)S(1)}, bf16[32,4096]{1,0:T(8,128)(2,1)S(1)}, u32[]{:S(2)}, u32[]{:S(2)}) collective-permute-start(bf16[32,4096]{1,0:T(8,128)(2,1)S(1)} %get-tuple-element.56), channel_id=1, source_target_pairs={{0,16},{1,17},{2,18},{3,19},{16,0},{17,1},{18,2},{19,3},{4,20},{5,... | collective-permute-start | bytes 786440 | tf_op jit(solution)/shard_map/member_4/ppermute | solution.py:63
  65.8 14.2 %collective-permute-start.15 = (bf16[32,4096]{1,0:T(8,128)(2,1)S(1)}, bf16[32,4096]{1,0:T(8,128)(2,1)S(1)}, u32[]{:S(2)}, u32[]{:S(2)}) collective-permute-start(bf16[32,4096]{1,0:T(8,128)(2,1)S(1)} %get-tuple-element.57), channel_id=1, source_target_pairs={{0,18},{1,19},{2,16},{3,17},{16,2},{17,3},{18,0},{19,1},{4,22},{5,... | collective-permute-start | bytes 786440 | tf_op jit(solution)/shard_map/member_6/ppermute | solution.py:63
  67.4 14.8 %collective-permute-start.22 = (bf16[16,4096]{1,0:T(8,128)(2,1)S(1)}, bf16[16,4096]{1,0:T(8,128)(2,1)S(1)}, u32[]{:S(2)}, u32[]{:S(2)}) collective-permute-start(bf16[16,4096]{1,0:T(8,128)(2,1)S(1)} %get-tuple-element.67), channel_id=1, source_target_pairs={{0,2},{1,3},{2,0},{3,1},{16,18},{17,19},{18,16},{19,17},{4,6},{5,7... | collective-permute-start | bytes 393224 | tf_op jit(solution)/shard_map/member_2/ppermute | solution.py:63
  68.1 15.6 %collective-permute-start.23 = (bf16[16,4096]{1,0:T(8,128)(2,1)S(1)}, bf16[16,4096]{1,0:T(8,128)(2,1)S(1)}, u32[]{:S(2)}, u32[]{:S(2)}) collective-permute-start(bf16[16,4096]{1,0:T(8,128)(2,1)S(1)} %get-tuple-element.68), channel_id=1, source_target_pairs={{0,16},{1,17},{2,18},{3,19},{16,0},{17,1},{18,2},{19,3},{4,20},{5,... | collective-permute-start | bytes 393224 | tf_op jit(solution)/shard_map/member_4/ppermute | solution.py:63
  73.1 12.6 %collective-permute-start.24 = (bf16[16,4096]{1,0:T(8,128)(2,1)S(1)}, bf16[16,4096]{1,0:T(8,128)(2,1)S(1)}, u32[]{:S(2)}, u32[]{:S(2)}) collective-permute-start(bf16[16,4096]{1,0:T(8,128)(2,1)S(1)} %get-tuple-element.69), channel_id=1, source_target_pairs={{0,18},{1,19},{2,16},{3,17},{16,2},{17,3},{18,0},{19,1},{4,22},{5,... | collective-permute-start | bytes 393224 | tf_op jit(solution)/shard_map/member_6/ppermute | solution.py:63
  80.1 8.7 %collective-permute-start.26 = (bf16[16,4096]{1,0:T(8,128)(2,1)S(1)}, bf16[16,4096]{1,0:T(8,128)(2,1)S(1)}, u32[]{:S(2)}, u32[]{:S(2)}) collective-permute-start(bf16[16,4096]{1,0:T(8,128)(2,1)S(1)} %get-tuple-element.71), channel_id=1, source_target_pairs={{0,2},{1,3},{2,0},{3,1},{16,18},{17,19},{18,16},{19,17},{4,6},{5,7... | collective-permute-start | bytes 393224 | tf_op jit(solution)/shard_map/member_2/ppermute | solution.py:63
  80.8 8.0 %collective-permute-start.27 = (bf16[16,4096]{1,0:T(8,128)(2,1)S(1)}, bf16[16,4096]{1,0:T(8,128)(2,1)S(1)}, u32[]{:S(2)}, u32[]{:S(2)}) collective-permute-start(bf16[16,4096]{1,0:T(8,128)(2,1)S(1)} %get-tuple-element.72), channel_id=1, source_target_pairs={{0,16},{1,17},{2,18},{3,19},{16,0},{17,1},{18,2},{19,3},{4,20},{5,... | collective-permute-start | bytes 393224 | tf_op jit(solution)/shard_map/member_4/ppermute | solution.py:63
  82.2 8.2 %collective-permute-start.28 = (bf16[16,4096]{1,0:T(8,128)(2,1)S(1)}, bf16[16,4096]{1,0:T(8,128)(2,1)S(1)}, u32[]{:S(2)}, u32[]{:S(2)}) collective-permute-start(bf16[16,4096]{1,0:T(8,128)(2,1)S(1)} %get-tuple-element.73), channel_id=1, source_target_pairs={{0,18},{1,19},{2,16},{3,17},{16,2},{17,3},{18,0},{19,1},{4,22},{5,... | collective-permute-start | bytes 393224 | tf_op jit(solution)/shard_map/member_6/ppermute | solution.py:63
  83.7 11.2 %collective-permute-start.16 = (bf16[16,4096]{1,0:T(8,128)(2,1)S(1)}, bf16[16,4096]{1,0:T(8,128)(2,1)S(1)}, u32[]{:S(2)}, u32[]{:S(2)}) collective-permute-start(bf16[16,4096]{1,0:T(8,128)(2,1)S(1)} %get-tuple-element.59), channel_id=1, source_target_pairs={{0,8},{1,9},{2,10},{3,11},{16,24},{17,25},{18,26},{19,27},{4,12},{... | collective-permute-start | bytes 393224 | tf_op jit(solution)/shard_map/plane_2/ppermute | solution.py:52
  85.7 9.1 %collective-permute-start.25 = (bf16[16,4096]{1,0:T(8,128)(2,1)S(1)}, bf16[16,4096]{1,0:T(8,128)(2,1)S(1)}, u32[]{:S(2)}, u32[]{:S(2)}) collective-permute-start(bf16[16,4096]{1,0:T(8,128)(2,1)S(1)} %add_chips.4), channel_id=1, source_target_pairs={{0,12},{1,13},{2,14},{3,15},{16,28},{17,29},{18,30},{19,31},{4,8},... | collective-permute-start | bytes 393224 | tf_op jit(solution)/shard_map/plane_3/ppermute | solution.py:52
  90.5 6.2 %collective-permute-start.29 = (bf16[16,4096]{1,0:T(8,128)(2,1)S(1)}, bf16[16,4096]{1,0:T(8,128)(2,1)S(1)}, u32[]{:S(2)}, u32[]{:S(2)}) collective-permute-start(bf16[16,4096]{1,0:T(8,128)(2,1)S(1)} %add_chips.5), channel_id=1, source_target_pairs={{0,4},{1,5},{2,6},{3,7},{16,20},{17,21},{18,22},{19,23},{4,0},{5,1... | collective-permute-start | bytes 393224 | tf_op jit(solution)/shard_map/plane_1/ppermute | solution.py:52
  (4 other events, 29.2 us)

commit v9 on v8

--- a/solution.py
+++ b/solution.py
@@ -589,30 +589,25 @@
         kv_pages.shape[0],
     )
 
-    first = max(1, planes // 4)
-    order = sorted(range(planes), key=lambda s: (s & 1, s))
-    groups = [order[:first], order[first : 2 * first], order[2 * first :]]
+    near = list(range(1, planes // 2 + 1))
+    far = [0, *range(planes // 2 + 1, planes)]
     chips = range(0, layout.members, 2)
-    blocks = [layout.shifted(normed, s) for s in range(planes)]
+    blocks = [normed]
+    for s in range(1, planes):
+        blocks.append(layout.shifted(blocks[s ^ 1], 1) if s & 1 else layout.shifted(normed, s))
     arrived = []
-    for g, group in enumerate(groups):
-        rows = packed([blocks[s] for s in group])
-        sent = []
-        for c, chip in enumerate(chips):
-            ready = rows
-            if g == 1:
-                ready = after(rows, arrived[0][c])
-            sent.append(layout.swapped(ready, chip))
-        arrived.append(sent)
-    arrived[0][0] = after(arrived[0][0], arrived[2][0])
-
-    def to_experts(members, tie):
-        pieces = [arrived[g][c] for c in range(len(chips)) for g in members]
+    for s, block in enumerate(blocks):
+        ready = [block] * len(chips)
+        if 0 < s <= len(near):
+            ready = [after(block, part) for part in arrived[0]]
+        arrived.append([layout.swapped(rows, chip) for rows, chip in zip(ready, chips)])
+
+    def to_experts(some, tie):
+        pieces = [arrived[s][c] for c in range(len(chips)) for s in some]
         if tie is not None:
             pieces[0] = after(pieces[0], tie)
         own = packed(pieces)
-        slots = layout.members * sum(len(groups[g]) for g in members) * capacity
-        return own, layout.swapped(own, 1), slots
+        return own, layout.swapped(own, 1), layout.members * len(some) * capacity
 
     def add_cores(mine, over):
         cuts = [count_of_rows] * (mine.shape[0] // count_of_rows)
@@ -625,13 +620,12 @@
     def total_of(parts):
         return add_up([[part] for part in parts], [count_of_rows], "add_chips")[0]
 
-    near = [s for g in (0, 1) for s in groups[g]]
-    own, other, slots = to_experts((0, 1), None)
+    own, other, slots = to_experts(near, blocks[far[-1]])
     mine, over, kept = run_experts(own, other, (w_gate_up, w_down), expert, top_count, slots, True)
     near_mine, near_back = mine, layout.swapped(over, 1)
-    far_own, far_other, slots = to_experts((2,), over)
-    far_other = after(far_other, near_back)
-    mine, over, _ = run_experts(far_own, far_other, kept, expert, top_count, slots, False)
+    own, other, slots = to_experts(far, over)
+    other = after(other, near_back)
+    mine, over, _ = run_experts(own, other, kept, expert, top_count, slots, False)
     near_sums = add_up(
         [[near_mine], [near_back]], [count_of_rows * len(near)] * len(chips), "add_cores"
     )
@@ -639,13 +633,12 @@
     parts = to_owners(near_sums, 0)
     totals = add_up([[part] for part in parts], [count_of_rows] * len(near), "add_chips")
     others = [layout.shifted(total, by) for total, by in zip(totals, near)]
-    for i, by in list(enumerate(groups[2]))[::-1]:
+    for i, by in list(enumerate(far))[:0:-1]:
         others.append(layout.shifted(total_of(to_owners(far_sums, i)), by))
-    count = len(near) + 1
     merged = add_up(
-        [[merged]] + [[part] for part in others[:count]], [count_of_rows], "add_first", 10**10
+        [[merged]] + [[part] for part in others], [count_of_rows], "add_first", 10**10
     )[0]
-    others = others[count:]
+    others = [total_of(to_owners(far_sums, 0))]
     total = merged.astype(jnp.float32) + sum(part.astype(jnp.float32) for part in others)
     layer_out = total.astype(jnp.bfloat16)
     return (attended, layer_out)

time: 97.8 us -> 97.4 us (level)
  waiting for transfers between devices: 37.4 us -> 35.2 us
  starting transfers between devices: 35.8 us -> 37.6 us
    ppermute x6, waiting for transfers between devices: 11.1 us -> 8.12 us  [shifted(): return lax.ppermute(value, AXES, pairs)]
    ppermute x22 -> x25, starting transfers between devices: 22.3 us -> 23.6 us  [swapped(): return lax.ppermute(value, AXES, pairs)]
    ppermute x22 -> x25, waiting for transfers between devices: 24.3 us -> 25 us  [swapped(): return lax.ppermute(value, AXES, pairs)]
  transfers between devices with their start and end apart: 30 -> 33, of which waited for: 15 -> 16; matrix products, arithmetic and copies ran while one was open for 0% -> 0% of each run, Pallas kernels for 14% -> 14%
where the time goes in v9:
time: 97.4 us; the launch traced here: 97 us
  starting transfers between devices  37.6 us (39%)
  waiting for transfers between devices  35.2 us (36%)
  Pallas kernels  22.6 us (23%)
    ppermute x25, waiting for transfers between devices, swapped(): return lax.ppermute(value, AXES, pairs)  25 us
    ppermute x25, starting transfers between devices, swapped(): return lax.ppermute(value, AXES, pairs)  23.6 us
    pallas_call x2, Pallas kernels, run_experts(): pl.pallas_call(kernel, out_shape=(shape, shape) + kept, in_specs=[SMEM, V...  13.4 us
    ppermute x6, starting transfers between devices, shifted(): return lax.ppermute(value, AXES, pairs)  8.95 us
    ppermute x6, waiting for transfers between devices, shifted(): return lax.ppermute(value, AXES, pairs)  8.12 us
    ppermute x2, starting transfers between devices, from_behind(): lax.ppermute(value, axis, [(i, (i + by) % length) for i in range(length)])  5.09 us
    pallas_call x1, Pallas kernels, own_attention(): pl.pallas_call(kernel, out_shape=(shape, shape, shape, jax.ShapeDtypeStru...  4.74 us
    ppermute x2, waiting for transfers between devices, from_behind(): lax.ppermute(value, axis, [(i, (i + by) % length) for i in range(length)])  2.06 us
  transfers between devices with their start and end apart: 33, of which 16 were waited for; matrix products, arithmetic and copies ran while one was open for 0% of the time, Pallas kernels for 14%

profile of v9, /device:TPU:0, one launch (start us, length us, event | category | flops | bytes accessed | tf_op | source)
XLA Modules:
  0.0 97.0 jit_solution(11114731072798755562)
XLA Ops:
  0.6 3.0 %collective-permute-start = (s32[16]{0:T(128)}, s32[16]{0:T(128)S(1)}, u32[]{:S(2)}, u32[]{:S(2)}) collective-permute-start(s32[16]{0:T(128)} %param.17), channel_id=1, source_target_pairs={{0,16},{16,0},{1,17},{17,1},{2,18},{18,2},{3,19},{19,3},{4,20},{20... | collective-permute-start | bytes 200 | tf_op jit(solution)/shard_map/ppermute | solution.py:68
  3.6 1.7 %collective-permute-done.slots_ref = s32[16]{0:T(128)S(1)} collective-permute-done((s32[16]{0:T(128)}, s32[16]{0:T(128)S(1)}, u32[]{:S(2)}, u32[]{:S(2)}) %collective-permute-start) | collective-permute-done | bytes 96 | tf_op jit(solution)/shard_map/ppermute | solution.py:68
  5.3 1.6 %pick_pages.1 = bf16[16,16,512]{2,1,0:T(8,128)(2,1)S(1)} custom-call(s32[16]{0:T(128)S(1)} %collective-permute-done.slots_ref, bf16[128,16,512]{2,1,0:T(8,128)(2,1)} %pages_hbm.1), custom_call_target="tpu_custom_call" | custom-call | bytes 1048576 | tf_op jit(solution)/shard_map/pick_pages/pallas_call | solution.py:84
  7.0 2.1 %collective-permute-start.1 = (bf16[16,16,512]{2,1,0:T(8,128)(2,1)S(1)}, bf16[16,16,512]{2,1,0:T(8,128)(2,1)S(1)}, u32[]{:S(2)}, u32[]{:S(2)}) collective-permute-start(bf16[16,16,512]{2,1,0:T(8,128)(2,1)S(1)} %pick_pages.1), channel_id=1, source_target_pairs={{0,16},{16,0},{1,17},{17,1},{2,18},{18,2},{3,19},{19,3},{4,20},{20... | collective-permute-start | bytes 786440 | tf_op jit(solution)/shard_map/ppermute | solution.py:68
  9.0 4.7 %own_attention.1 = (f32[512,128]{1,0:T(8,128)S(1)}, f32[512,128]{1,0:T(8,128)S(1)}, f32[512,128]{1,0:T(8,128)S(1)}, bf16[512,128]{1,0:T(8,128)(2,1)S(1)}) custom-call(bf16[16,4096]{1,0:T(8,128)(2,1)} %queries_hbm, bf16[16,512]{1,0:T(8,128)(2,1)} %new_hbm.1, bf16[128,16,512]{2,1,0:T(8,128)(2,1)} %pages_hbm.1, s32[16,16]{1,0:T(8,128)} %table_ref.1, s32[16]{0:T(128)} %lengths_ref.1), custom_call_target="tpu_custom_call" | custom-call | flops 1073741824 | bytes 16777216 | tf_op jit(solution)/shard_map/own_attention/pallas_call | solution.py:239
  14.2 1.9 %finish_attention.1 = (bf16[16,4096]{1,0:T(8,128)(2,1)}, bf16[16,4096]{1,0:T(8,128)(2,1)S(1)}, bf16[16,4224]{1,0:T(8,128)(2,1)S(1)}) custom-call(bf16[512,128]{1,0:T(8,128)(2,1)S(1)} %get-tuple-element.43.q_ref, bf16[16,16,512]{2,1,0:T(8,128)(2,1)S(1)} %collective-permute-done.1.fetched_ref, s32[16,16]{1,0:T(8,128)S(1)} %copy-done.2, s32[16]{0:T(128)S(1)} %copy-done.5, ...), custom_call_target="tpu_custom_call" | custom-call | flops 134217728 | bytes 4194304 | tf_op jit(solution)/shard_map/finish_attention/pallas_call | solution.py:538
  16.2 1.8 %collective-permute-start.5 = (bf16[16,4224]{1,0:T(8,128)(2,1)S(1)}, bf16[16,4224]{1,0:T(8,128)(2,1)S(1)}, u32[]{:S(2)}, u32[]{:S(2)}) collective-permute-start(bf16[16,4224]{1,0:T(8,128)(2,1)S(1)} %get-tuple-element.68.refs_0_), channel_id=1, source_target_pairs={{0,2},{1,3},{2,0},{3,1},{16,18},{17,19},{18,16},{19,17},{4,6},{5,7... | collective-permute-start | bytes 405512 | tf_op jit(solution)/shard_map/member_2/ppermute | solution.py:63
  17.9 2.6 %collective-permute-start.3 = (bf16[16,4224]{1,0:T(8,128)(2,1)S(1)}, bf16[16,4224]{1,0:T(8,128)(2,1)S(1)}, u32[]{:S(2)}, u32[]{:S(2)}) collective-permute-start(bf16[16,4224]{1,0:T(8,128)(2,1)S(1)} %get-tuple-element.68.refs_0_), channel_id=1, source_target_pairs={{0,8},{1,9},{2,10},{3,11},{16,24},{17,25},{18,26},{19,27},{4,12},{... | collective-permute-start | bytes 405512 | tf_op jit(solution)/shard_map/plane_2/ppermute | solution.py:52
  20.5 1.4 %collective-permute-start.11 = (bf16[16,4224]{1,0:T(8,128)(2,1)S(1)}, bf16[16,4224]{1,0:T(8,128)(2,1)S(1)}, u32[]{:S(2)}, u32[]{:S(2)}) collective-permute-start(bf16[16,4224]{1,0:T(8,128)(2,1)S(1)} %get-tuple-element.68.refs_0_), channel_id=1, source_target_pairs={{0,18},{1,19},{2,16},{3,17},{16,2},{17,3},{18,0},{19,1},{4,22},{5,... | collective-permute-start | bytes 405512 | tf_op jit(solution)/shard_map/member_6/ppermute | solution.py:63
  22.5 1.6 %collective-permute-start.2 = (bf16[16,4224]{1,0:T(8,128)(2,1)S(1)}, bf16[16,4224]{1,0:T(8,128)(2,1)S(1)}, u32[]{:S(2)}, u32[]{:S(2)}) collective-permute-start(bf16[16,4224]{1,0:T(8,128)(2,1)S(1)} %get-tuple-element.68.refs_0_), channel_id=1, source_target_pairs={{0,4},{1,5},{2,6},{3,7},{16,20},{17,21},{18,22},{19,23},{4,0},{5,1... | collective-permute-start | bytes 405512 | tf_op jit(solution)/shard_map/plane_1/ppermute | solution.py:52
  24.1 1.4 %collective-permute-done.3.refs_1_ = bf16[16,4224]{1,0:T(8,128)(2,1)S(1)} collective-permute-done((bf16[16,4224]{1,0:T(8,128)(2,1)S(1)}, bf16[16,4224]{1,0:T(8,128)(2,1)S(1)}, u32[]{:S(2)}, u32[]{:S(2)}) %collective-permute-start.3) | collective-permute-done | bytes 135200 | tf_op jit(solution)/shard_map/plane_2/ppermute | solution.py:52
  26.5 1.4 %collective-permute-done.8.refs_4_ = bf16[16,4224]{1,0:T(8,128)(2,1)S(1)} collective-permute-done((bf16[16,4224]{1,0:T(8,128)(2,1)S(1)}, bf16[16,4224]{1,0:T(8,128)(2,1)S(1)}, u32[]{:S(2)}, u32[]{:S(2)}) %collective-permute-start.8) | collective-permute-done | bytes 135200 | tf_op jit(solution)/shard_map/member_4/ppermute | solution.py:63
  28.0 1.5 %collective-permute-start.10 = (bf16[16,4224]{1,0:T(8,128)(2,1)S(1)}, bf16[16,4224]{1,0:T(8,128)(2,1)S(1)}, u32[]{:S(2)}, u32[]{:S(2)}) collective-permute-start(bf16[16,4224]{1,0:T(8,128)(2,1)S(1)} %collective-permute-done.3.refs_1_), channel_id=1, source_target_pairs={{0,16},{1,17},{2,18},{3,19},{16,0},{17,1},{18,2},{19,3},{4,20},{5,... | collective-permute-start | bytes 405512 | tf_op jit(solution)/shard_map/member_4/ppermute | solution.py:63
  29.5 1.7 %collective-permute-start.13 = (bf16[16,4224]{1,0:T(8,128)(2,1)S(1)}, bf16[16,4224]{1,0:T(8,128)(2,1)S(1)}, u32[]{:S(2)}, u32[]{:S(2)}) collective-permute-start(bf16[16,4224]{1,0:T(8,128)(2,1)S(1)} %collective-permute-done.3.refs_1_), channel_id=1, source_target_pairs={{0,18},{1,19},{2,16},{3,17},{16,2},{17,3},{18,0},{19,1},{4,22},{5,... | collective-permute-start | bytes 405512 | tf_op jit(solution)/shard_map/member_6/ppermute | solution.py:63
  31.5 1.6 %collective-permute-done.7.refs_3_ = bf16[16,4224]{1,0:T(8,128)(2,1)S(1)} collective-permute-done((bf16[16,4224]{1,0:T(8,128)(2,1)S(1)}, bf16[16,4224]{1,0:T(8,128)(2,1)S(1)}, u32[]{:S(2)}, u32[]{:S(2)}) %collective-permute-start.7) | collective-permute-done | bytes 135200 | tf_op jit(solution)/shard_map/member_2/ppermute | solution.py:63
  33.0 1.8 %collective-permute-start.9 = (bf16[16,4224]{1,0:T(8,128)(2,1)S(1)}, bf16[16,4224]{1,0:T(8,128)(2,1)S(1)}, u32[]{:S(2)}, u32[]{:S(2)}) collective-permute-start(bf16[16,4224]{1,0:T(8,128)(2,1)S(1)} %collective-permute-done.2.refs_0_), channel_id=1, source_target_pairs={{0,16},{1,17},{2,18},{3,19},{16,0},{17,1},{18,2},{19,3},{4,20},{5,... | collective-permute-start | bytes 405512 | tf_op jit(solution)/shard_map/member_4/ppermute | solution.py:63
  35.3 1.5 %collective-permute-done.13.refs_7_ = bf16[16,4224]{1,0:T(8,128)(2,1)S(1)} collective-permute-done((bf16[16,4224]{1,0:T(8,128)(2,1)S(1)}, bf16[16,4224]{1,0:T(8,128)(2,1)S(1)}, u32[]{:S(2)}, u32[]{:S(2)}) %collective-permute-start.13) | collective-permute-done | bytes 135200 | tf_op jit(solution)/shard_map/member_6/ppermute | solution.py:63
  38.0 2.7 %collective-permute-done.12.refs_6_ = bf16[16,4224]{1,0:T(8,128)(2,1)S(1)} collective-permute-done((bf16[16,4224]{1,0:T(8,128)(2,1)S(1)}, bf16[16,4224]{1,0:T(8,128)(2,1)S(1)}, u32[]{:S(2)}, u32[]{:S(2)}) %collective-permute-start.12) | collective-permute-done | bytes 135200 | tf_op jit(solution)/shard_map/member_6/ppermute | solution.py:63
  40.9 1.5 %collective-permute-start.23 = (bf16[16,4224]{1,0:T(8,128)(2,1)S(1)}, bf16[16,4224]{1,0:T(8,128)(2,1)S(1)}, u32[]{:S(2)}, u32[]{:S(2)}) collective-permute-start(bf16[16,4224]{1,0:T(8,128)(2,1)S(1)} %collective-permute-done.4.refs_1_), channel_id=1, source_target_pairs={{0,18},{1,19},{2,16},{3,17},{16,2},{17,3},{18,0},{19,1},{4,22},{5,... | collective-permute-start | bytes 405512 | tf_op jit(solution)/shard_map/member_6/ppermute | solution.py:63
  42.9 1.5 %collective-permute-start.21 = (bf16[16,4224]{1,0:T(8,128)(2,1)S(1)}, bf16[16,4224]{1,0:T(8,128)(2,1)S(1)}, u32[]{:S(2)}, u32[]{:S(2)}) collective-permute-start(bf16[16,4224]{1,0:T(8,128)(2,1)S(1)} %collective-permute-done.4.refs_1_), channel_id=1, source_target_pairs={{0,2},{1,3},{2,0},{3,1},{16,18},{17,19},{18,16},{19,17},{4,6},{5,7... | collective-permute-start | bytes 405512 | tf_op jit(solution)/shard_map/member_2/ppermute | solution.py:63
  44.4 8.3 %run_experts.2 = (bf16[128,4096]{1,0:T(8,128)(2,1)S(1)}, bf16[128,4096]{1,0:T(8,128)(2,1)S(1)}, bf16[4096,1536]{1,0:T(8,128)(2,1)S(1)}, bf16[768,4096]{1,0:T(8,128)(2,1)S(1)}) custom-call(s32[1]{0:T(128)} %bitcast.3.expert_ref, bf16[128,4224]{1,0:T(8,128)(2,1)S(1)} %packed.2.own_ref, bf16[128,4224]{1,0:T(8,128)(2,1)S(1)} %collective-permute-done.14.other_ref, ...), custom_call_target="tpu_custom_call" | custom-call | flops 2415919104 | bytes 20971520 | tf_op jit(solution)/shard_map/run_experts/pallas_call | solution.py:431
  53.4 3.7 %collective-permute-done.15.refs_1_ = bf16[128,4096]{1,0:T(8,128)(2,1)S(1)} collective-permute-done((bf16[128,4096]{1,0:T(8,128)(2,1)S(1)}, bf16[128,4096]{1,0:T(8,128)(2,1)S(1)}, u32[]{:S(2)}, u32[]{:S(2)}) %collective-permute-start.15) | collective-permute-done | bytes 1048608 | tf_op jit(solution)/shard_map/member_1/ppermute | solution.py:63
  57.1 5.1 %run_experts.3 = (bf16[128,4096]{1,0:T(8,128)(2,1)S(1)}, bf16[128,4096]{1,0:T(8,128)(2,1)S(1)}) custom-call(s32[1]{0:T(128)} %bitcast.3.expert_ref, bf16[128,4224]{1,0:T(8,128)(2,1)S(1)} %packed.3.own_ref, bf16[128,4224]{1,0:T(8,128)(2,1)S(1)} %collective-permute-done.24.other_ref, bf16[4096,1536]{1,0:T(8,128)(2,1)S(1)} %get-tuple-element.70.refs_0_, ...), custom_call_target="tpu_custom_call" | custom-call | flops 2415919104 | bytes 20971520 | tf_op jit(solution)/shard_map/run_experts/pallas_call | solution.py:431
  63.2 1.5 %collective-permute-start.17 = (bf16[32,4096]{1,0:T(8,128)(2,1)S(1)}, bf16[32,4096]{1,0:T(8,128)(2,1)S(1)}, u32[]{:S(2)}, u32[]{:S(2)}) collective-permute-start(bf16[32,4096]{1,0:T(8,128)(2,1)S(1)} %get-tuple-element.64), channel_id=1, source_target_pairs={{0,16},{1,17},{2,18},{3,19},{16,0},{17,1},{18,2},{19,3},{4,20},{5,... | collective-permute-start | bytes 786440 | tf_op jit(solution)/shard_map/member_4/ppermute | solution.py:63
  64.7 1.5 %collective-permute-start.18 = (bf16[32,4096]{1,0:T(8,128)(2,1)S(1)}, bf16[32,4096]{1,0:T(8,128)(2,1)S(1)}, u32[]{:S(2)}, u32[]{:S(2)}) collective-permute-start(bf16[32,4096]{1,0:T(8,128)(2,1)S(1)} %get-tuple-element.65), channel_id=1, source_target_pairs={{0,18},{1,19},{2,16},{3,17},{16,2},{17,3},{18,0},{19,1},{4,22},{5,... | collective-permute-start | bytes 786440 | tf_op jit(solution)/shard_map/member_6/ppermute | solution.py:63
  67.0 1.5 %collective-permute-start.27 = (bf16[16,4096]{1,0:T(8,128)(2,1)S(1)}, bf16[16,4096]{1,0:T(8,128)(2,1)S(1)}, u32[]{:S(2)}, u32[]{:S(2)}) collective-permute-start(bf16[16,4096]{1,0:T(8,128)(2,1)S(1)} %get-tuple-element.76), channel_id=1, source_target_pairs={{0,16},{1,17},{2,18},{3,19},{16,0},{17,1},{18,2},{19,3},{4,20},{5,... | collective-permute-start | bytes 393224 | tf_op jit(solution)/shard_map/member_4/ppermute | solution.py:63
  68.5 3.6 %collective-permute-done.16.refs_1_ = bf16[32,4096]{1,0:T(8,128)(2,1)S(1)} collective-permute-done((bf16[32,4096]{1,0:T(8,128)(2,1)S(1)}, bf16[32,4096]{1,0:T(8,128)(2,1)S(1)}, u32[]{:S(2)}, u32[]{:S(2)}) %collective-permute-start.16) | collective-permute-done | bytes 262176 | tf_op jit(solution)/shard_map/member_2/ppermute | solution.py:63
  72.1 1.4 %collective-permute-start.28 = (bf16[16,4096]{1,0:T(8,128)(2,1)S(1)}, bf16[16,4096]{1,0:T(8,128)(2,1)S(1)}, u32[]{:S(2)}, u32[]{:S(2)}) collective-permute-start(bf16[16,4096]{1,0:T(8,128)(2,1)S(1)} %get-tuple-element.77), channel_id=1, source_target_pairs={{0,18},{1,19},{2,16},{3,17},{16,2},{17,3},{18,0},{19,1},{4,22},{5,... | collective-permute-start | bytes 393224 | tf_op jit(solution)/shard_map/member_6/ppermute | solution.py:63
  74.0 5.0 %collective-permute-done.18.refs_3_ = bf16[32,4096]{1,0:T(8,128)(2,1)S(1)} collective-permute-done((bf16[32,4096]{1,0:T(8,128)(2,1)S(1)}, bf16[32,4096]{1,0:T(8,128)(2,1)S(1)}, u32[]{:S(2)}, u32[]{:S(2)}) %collective-permute-start.18) | collective-permute-done | bytes 262176 | tf_op jit(solution)/shard_map/member_6/ppermute | solution.py:63
  82.4 2.2 %collective-permute-done.28.refs_3_ = bf16[16,4096]{1,0:T(8,128)(2,1)S(1)} collective-permute-done((bf16[16,4096]{1,0:T(8,128)(2,1)S(1)}, bf16[16,4096]{1,0:T(8,128)(2,1)S(1)}, u32[]{:S(2)}, u32[]{:S(2)}) %collective-permute-start.28) | collective-permute-done | bytes 131104 | tf_op jit(solution)/shard_map/member_6/ppermute | solution.py:63
  84.7 3.2 %collective-permute-start.20 = (bf16[16,4096]{1,0:T(8,128)(2,1)S(1)}, bf16[16,4096]{1,0:T(8,128)(2,1)S(1)}, u32[]{:S(2)}, u32[]{:S(2)}) collective-permute-start(bf16[16,4096]{1,0:T(8,128)(2,1)S(1)} %get-tuple-element.67), channel_id=1, source_target_pairs={{0,8},{1,9},{2,10},{3,11},{16,24},{17,25},{18,26},{19,27},{4,12},{... | collective-permute-start | bytes 393224 | tf_op jit(solution)/shard_map/plane_2/ppermute | solution.py:52
  89.5 6.7 %collective-permute-done.20.refs_2_ = bf16[16,4096]{1,0:T(8,128)(2,1)S(1)} collective-permute-done((bf16[16,4096]{1,0:T(8,128)(2,1)S(1)}, bf16[16,4096]{1,0:T(8,128)(2,1)S(1)}, u32[]{:S(2)}, u32[]{:S(2)}) %collective-permute-start.20) | collective-permute-done | bytes 131104 | tf_op jit(solution)/shard_map/plane_2/ppermute | solution.py:52
  (60 shorter events, 13.5 us)
Async XLA Ops:
  0.6 4.7 %collective-permute-start = (s32[16]{0:T(128)}, s32[16]{0:T(128)S(1)}, u32[]{:S(2)}, u32[]{:S(2)}) collective-permute-start(s32[16]{0:T(128)} %param.17), channel_id=1, source_target_pairs={{0,16},{16,0},{1,17},{17,1},{2,18},{18,2},{3,19},{19,3},{4,20},{20... | collective-permute-start | bytes 200 | tf_op jit(solution)/shard_map/ppermute | solution.py:68
  7.0 7.2 %collective-permute-start.1 = (bf16[16,16,512]{2,1,0:T(8,128)(2,1)S(1)}, bf16[16,16,512]{2,1,0:T(8,128)(2,1)S(1)}, u32[]{:S(2)}, u32[]{:S(2)}) collective-permute-start(bf16[16,16,512]{2,1,0:T(8,128)(2,1)S(1)} %pick_pages.1), channel_id=1, source_target_pairs={{0,16},{16,0},{1,17},{17,1},{2,18},{18,2},{3,19},{19,3},{4,20},{20... | collective-permute-start | bytes 786440 | tf_op jit(solution)/shard_map/ppermute | solution.py:68
  16.2 7.9 %collective-permute-start.5 = (bf16[16,4224]{1,0:T(8,128)(2,1)S(1)}, bf16[16,4224]{1,0:T(8,128)(2,1)S(1)}, u32[]{:S(2)}, u32[]{:S(2)}) collective-permute-start(bf16[16,4224]{1,0:T(8,128)(2,1)S(1)} %get-tuple-element.68.refs_0_), channel_id=1, source_target_pairs={{0,2},{1,3},{2,0},{3,1},{16,18},{17,19},{18,16},{19,17},{4,6},{5,7... | collective-permute-start | bytes 405512 | tf_op jit(solution)/shard_map/member_2/ppermute | solution.py:63
  17.9 7.5 %collective-permute-start.3 = (bf16[16,4224]{1,0:T(8,128)(2,1)S(1)}, bf16[16,4224]{1,0:T(8,128)(2,1)S(1)}, u32[]{:S(2)}, u32[]{:S(2)}) collective-permute-start(bf16[16,4224]{1,0:T(8,128)(2,1)S(1)} %get-tuple-element.68.refs_0_), channel_id=1, source_target_pairs={{0,8},{1,9},{2,10},{3,11},{16,24},{17,25},{18,26},{19,27},{4,12},{... | collective-permute-start | bytes 405512 | tf_op jit(solution)/shard_map/plane_2/ppermute | solution.py:52
  20.5 6.0 %collective-permute-start.11 = (bf16[16,4224]{1,0:T(8,128)(2,1)S(1)}, bf16[16,4224]{1,0:T(8,128)(2,1)S(1)}, u32[]{:S(2)}, u32[]{:S(2)}) collective-permute-start(bf16[16,4224]{1,0:T(8,128)(2,1)S(1)} %get-tuple-element.68.refs_0_), channel_id=1, source_target_pairs={{0,18},{1,19},{2,16},{3,17},{16,2},{17,3},{18,0},{19,1},{4,22},{5,... | collective-permute-start | bytes 405512 | tf_op jit(solution)/shard_map/member_6/ppermute | solution.py:63
  22.0 6.0 %collective-permute-start.8 = (bf16[16,4224]{1,0:T(8,128)(2,1)S(1)}, bf16[16,4224]{1,0:T(8,128)(2,1)S(1)}, u32[]{:S(2)}, u32[]{:S(2)}) collective-permute-start(bf16[16,4224]{1,0:T(8,128)(2,1)S(1)} %get-tuple-element.68.refs_0_), channel_id=1, source_target_pairs={{0,16},{1,17},{2,18},{3,19},{16,0},{17,1},{18,2},{19,3},{4,20},{5,... | collective-permute-start | bytes 405512 | tf_op jit(solution)/shard_map/member_4/ppermute | solution.py:63
  22.5 8.7 %collective-permute-start.2 = (bf16[16,4224]{1,0:T(8,128)(2,1)S(1)}, bf16[16,4224]{1,0:T(8,128)(2,1)S(1)}, u32[]{:S(2)}, u32[]{:S(2)}) collective-permute-start(bf16[16,4224]{1,0:T(8,128)(2,1)S(1)} %get-tuple-element.68.refs_0_), channel_id=1, source_target_pairs={{0,4},{1,5},{2,6},{3,7},{16,20},{17,21},{18,22},{19,23},{4,0},{5,1... | collective-permute-start | bytes 405512 | tf_op jit(solution)/shard_map/plane_1/ppermute | solution.py:52
  25.5 7.6 %collective-permute-start.7 = (bf16[16,4224]{1,0:T(8,128)(2,1)S(1)}, bf16[16,4224]{1,0:T(8,128)(2,1)S(1)}, u32[]{:S(2)}, u32[]{:S(2)}) collective-permute-start(bf16[16,4224]{1,0:T(8,128)(2,1)S(1)} %collective-permute-done.3.refs_1_), channel_id=1, source_target_pairs={{0,2},{1,3},{2,0},{3,1},{16,18},{17,19},{18,16},{19,17},{4,6},{5,7... | collective-permute-start | bytes 405512 | tf_op jit(solution)/shard_map/member_2/ppermute | solution.py:63
  25.6 9.2 %collective-permute-start.4 = (bf16[16,4224]{1,0:T(8,128)(2,1)S(1)}, bf16[16,4224]{1,0:T(8,128)(2,1)S(1)}, u32[]{:S(2)}, u32[]{:S(2)}) collective-permute-start(bf16[16,4224]{1,0:T(8,128)(2,1)S(1)} %collective-permute-done.3.refs_1_), channel_id=1, source_target_pairs={{0,4},{1,5},{2,6},{3,7},{16,20},{17,21},{18,22},{19,23},{4,0},{5,1... | collective-permute-start | bytes 405512 | tf_op jit(solution)/shard_map/plane_1/ppermute | solution.py:52
  28.0 7.3 %collective-permute-start.10 = (bf16[16,4224]{1,0:T(8,128)(2,1)S(1)}, bf16[16,4224]{1,0:T(8,128)(2,1)S(1)}, u32[]{:S(2)}, u32[]{:S(2)}) collective-permute-start(bf16[16,4224]{1,0:T(8,128)(2,1)S(1)} %collective-permute-done.3.refs_1_), channel_id=1, source_target_pairs={{0,16},{1,17},{2,18},{3,19},{16,0},{17,1},{18,2},{19,3},{4,20},{5,... | collective-permute-start | bytes 405512 | tf_op jit(solution)/shard_map/member_4/ppermute | solution.py:63
  29.5 7.3 %collective-permute-start.13 = (bf16[16,4224]{1,0:T(8,128)(2,1)S(1)}, bf16[16,4224]{1,0:T(8,128)(2,1)S(1)}, u32[]{:S(2)}, u32[]{:S(2)}) collective-permute-start(bf16[16,4224]{1,0:T(8,128)(2,1)S(1)} %collective-permute-done.3.refs_1_), channel_id=1, source_target_pairs={{0,18},{1,19},{2,16},{3,17},{16,2},{17,3},{18,0},{19,1},{4,22},{5,... | collective-permute-start | bytes 405512 | tf_op jit(solution)/shard_map/member_6/ppermute | solution.py:63
  31.2 6.5 %collective-permute-start.6 = (bf16[16,4224]{1,0:T(8,128)(2,1)S(1)}, bf16[16,4224]{1,0:T(8,128)(2,1)S(1)}, u32[]{:S(2)}, u32[]{:S(2)}) collective-permute-start(bf16[16,4224]{1,0:T(8,128)(2,1)S(1)} %collective-permute-done.2.refs_0_), channel_id=1, source_target_pairs={{0,2},{1,3},{2,0},{3,1},{16,18},{17,19},{18,16},{19,17},{4,6},{5,7... | collective-permute-start | bytes 405512 | tf_op jit(solution)/shard_map/member_2/ppermute | solution.py:63
  33.0 5.0 %collective-permute-start.9 = (bf16[16,4224]{1,0:T(8,128)(2,1)S(1)}, bf16[16,4224]{1,0:T(8,128)(2,1)S(1)}, u32[]{:S(2)}, u32[]{:S(2)}) collective-permute-start(bf16[16,4224]{1,0:T(8,128)(2,1)S(1)} %collective-permute-done.2.refs_0_), channel_id=1, source_target_pairs={{0,16},{1,17},{2,18},{3,19},{16,0},{17,1},{18,2},{19,3},{4,20},{5,... | collective-permute-start | bytes 405512 | tf_op jit(solution)/shard_map/member_4/ppermute | solution.py:63
  34.8 5.9 %collective-permute-start.12 = (bf16[16,4224]{1,0:T(8,128)(2,1)S(1)}, bf16[16,4224]{1,0:T(8,128)(2,1)S(1)}, u32[]{:S(2)}, u32[]{:S(2)}) collective-permute-start(bf16[16,4224]{1,0:T(8,128)(2,1)S(1)} %collective-permute-done.2.refs_0_), channel_id=1, source_target_pairs={{0,18},{1,19},{2,16},{3,17},{16,2},{17,3},{18,0},{19,1},{4,22},{5,... | collective-permute-start | bytes 405512 | tf_op jit(solution)/shard_map/member_6/ppermute | solution.py:63
  40.9 11.9 %collective-permute-start.23 = (bf16[16,4224]{1,0:T(8,128)(2,1)S(1)}, bf16[16,4224]{1,0:T(8,128)(2,1)S(1)}, u32[]{:S(2)}, u32[]{:S(2)}) collective-permute-start(bf16[16,4224]{1,0:T(8,128)(2,1)S(1)} %collective-permute-done.4.refs_1_), channel_id=1, source_target_pairs={{0,18},{1,19},{2,16},{3,17},{16,2},{17,3},{18,0},{19,1},{4,22},{5,... | collective-permute-start | bytes 405512 | tf_op jit(solution)/shard_map/member_6/ppermute | solution.py:63
  42.4 10.4 %collective-permute-start.22 = (bf16[16,4224]{1,0:T(8,128)(2,1)S(1)}, bf16[16,4224]{1,0:T(8,128)(2,1)S(1)}, u32[]{:S(2)}, u32[]{:S(2)}) collective-permute-start(bf16[16,4224]{1,0:T(8,128)(2,1)S(1)} %collective-permute-done.4.refs_1_), channel_id=1, source_target_pairs={{0,16},{1,17},{2,18},{3,19},{16,0},{17,1},{18,2},{19,3},{4,20},{5,... | collective-permute-start | bytes 405512 | tf_op jit(solution)/shard_map/member_4/ppermute | solution.py:63
  42.9 9.8 %collective-permute-start.21 = (bf16[16,4224]{1,0:T(8,128)(2,1)S(1)}, bf16[16,4224]{1,0:T(8,128)(2,1)S(1)}, u32[]{:S(2)}, u32[]{:S(2)}) collective-permute-start(bf16[16,4224]{1,0:T(8,128)(2,1)S(1)} %collective-permute-done.4.refs_1_), channel_id=1, source_target_pairs={{0,2},{1,3},{2,0},{3,1},{16,18},{17,19},{18,16},{19,17},{4,6},{5,7... | collective-permute-start | bytes 405512 | tf_op jit(solution)/shard_map/member_2/ppermute | solution.py:63
  52.8 4.3 %collective-permute-start.24 = (bf16[128,4224]{1,0:T(8,128)(2,1)S(1)}, bf16[128,4224]{1,0:T(8,128)(2,1)S(1)}, u32[]{:S(2)}, u32[]{:S(2)}) collective-permute-start(bf16[128,4224]{1,0:T(8,128)(2,1)S(1)} %packed.3.own_ref), channel_id=1, source_target_pairs={{0,1},{1,0},{2,3},{3,2},{16,17},{17,16},{18,19},{19,18},{4,5},{5,4... | collective-permute-start | bytes 3244040 | tf_op jit(solution)/shard_map/member_1/ppermute | solution.py:63
  52.9 4.2 %collective-permute-start.15 = (bf16[128,4096]{1,0:T(8,128)(2,1)S(1)}, bf16[128,4096]{1,0:T(8,128)(2,1)S(1)}, u32[]{:S(2)}, u32[]{:S(2)}) collective-permute-start(bf16[128,4096]{1,0:T(8,128)(2,1)S(1)} %get-tuple-element.61), channel_id=1, source_target_pairs={{0,1},{1,0},{2,3},{3,2},{16,17},{17,16},{18,19},{19,18},{4,5},{5,4... | collective-permute-start | bytes 3145736 | tf_op jit(solution)/shard_map/member_1/ppermute | solution.py:63
  62.2 4.0 %collective-permute-start.25 = (bf16[128,4096]{1,0:T(8,128)(2,1)S(1)}, bf16[128,4096]{1,0:T(8,128)(2,1)S(1)}, u32[]{:S(2)}, u32[]{:S(2)}) collective-permute-start(bf16[128,4096]{1,0:T(8,128)(2,1)S(1)} %get-tuple-element.73), channel_id=1, source_target_pairs={{0,1},{1,0},{2,3},{3,2},{16,17},{17,16},{18,19},{19,18},{4,5},{5,4... | collective-permute-start | bytes 3145736 | tf_op jit(solution)/shard_map/member_1/ppermute | solution.py:63
  62.6 9.4 %collective-permute-start.16 = (bf16[32,4096]{1,0:T(8,128)(2,1)S(1)}, bf16[32,4096]{1,0:T(8,128)(2,1)S(1)}, u32[]{:S(2)}, u32[]{:S(2)}) collective-permute-start(bf16[32,4096]{1,0:T(8,128)(2,1)S(1)} %get-tuple-element.63), channel_id=1, source_target_pairs={{0,2},{1,3},{2,0},{3,1},{16,18},{17,19},{18,16},{19,17},{4,6},{5,7... | collective-permute-start | bytes 786440 | tf_op jit(solution)/shard_map/member_2/ppermute | solution.py:63
  63.2 10.3 %collective-permute-start.17 = (bf16[32,4096]{1,0:T(8,128)(2,1)S(1)}, bf16[32,4096]{1,0:T(8,128)(2,1)S(1)}, u32[]{:S(2)}, u32[]{:S(2)}) collective-permute-start(bf16[32,4096]{1,0:T(8,128)(2,1)S(1)} %get-tuple-element.64), channel_id=1, source_target_pairs={{0,16},{1,17},{2,18},{3,19},{16,0},{17,1},{18,2},{19,3},{4,20},{5,... | collective-permute-start | bytes 786440 | tf_op jit(solution)/shard_map/member_4/ppermute | solution.py:63
  64.7 14.3 %collective-permute-start.18 = (bf16[32,4096]{1,0:T(8,128)(2,1)S(1)}, bf16[32,4096]{1,0:T(8,128)(2,1)S(1)}, u32[]{:S(2)}, u32[]{:S(2)}) collective-permute-start(bf16[32,4096]{1,0:T(8,128)(2,1)S(1)} %get-tuple-element.65), channel_id=1, source_target_pairs={{0,18},{1,19},{2,16},{3,17},{16,2},{17,3},{18,0},{19,1},{4,22},{5,... | collective-permute-start | bytes 786440 | tf_op jit(solution)/shard_map/member_6/ppermute | solution.py:63
  66.5 14.0 %collective-permute-start.26 = (bf16[16,4096]{1,0:T(8,128)(2,1)S(1)}, bf16[16,4096]{1,0:T(8,128)(2,1)S(1)}, u32[]{:S(2)}, u32[]{:S(2)}) collective-permute-start(bf16[16,4096]{1,0:T(8,128)(2,1)S(1)} %get-tuple-element.75), channel_id=1, source_target_pairs={{0,2},{1,3},{2,0},{3,1},{16,18},{17,19},{18,16},{19,17},{4,6},{5,7... | collective-permute-start | bytes 393224 | tf_op jit(solution)/shard_map/member_2/ppermute | solution.py:63
  67.0 14.2 %collective-permute-start.27 = (bf16[16,4096]{1,0:T(8,128)(2,1)S(1)}, bf16[16,4096]{1,0:T(8,128)(2,1)S(1)}, u32[]{:S(2)}, u32[]{:S(2)}) collective-permute-start(bf16[16,4096]{1,0:T(8,128)(2,1)S(1)} %get-tuple-element.76), channel_id=1, source_target_pairs={{0,16},{1,17},{2,18},{3,19},{16,0},{17,1},{18,2},{19,3},{4,20},{5,... | collective-permute-start | bytes 393224 | tf_op jit(solution)/shard_map/member_4/ppermute | solution.py:63
  72.1 12.6 %collective-permute-start.28 = (bf16[16,4096]{1,0:T(8,128)(2,1)S(1)}, bf16[16,4096]{1,0:T(8,128)(2,1)S(1)}, u32[]{:S(2)}, u32[]{:S(2)}) collective-permute-start(bf16[16,4096]{1,0:T(8,128)(2,1)S(1)} %get-tuple-element.77), channel_id=1, source_target_pairs={{0,18},{1,19},{2,16},{3,17},{16,2},{17,3},{18,0},{19,1},{4,22},{5,... | collective-permute-start | bytes 393224 | tf_op jit(solution)/shard_map/member_6/ppermute | solution.py:63
  73.5 14.5 %collective-permute-start.30 = (bf16[16,4096]{1,0:T(8,128)(2,1)S(1)}, bf16[16,4096]{1,0:T(8,128)(2,1)S(1)}, u32[]{:S(2)}, u32[]{:S(2)}) collective-permute-start(bf16[16,4096]{1,0:T(8,128)(2,1)S(1)} %get-tuple-element.79), channel_id=1, source_target_pairs={{0,2},{1,3},{2,0},{3,1},{16,18},{17,19},{18,16},{19,17},{4,6},{5,7... | collective-permute-start | bytes 393224 | tf_op jit(solution)/shard_map/member_2/ppermute | solution.py:63
  79.1 10.4 %collective-permute-start.19 = (bf16[16,4096]{1,0:T(8,128)(2,1)S(1)}, bf16[16,4096]{1,0:T(8,128)(2,1)S(1)}, u32[]{:S(2)}, u32[]{:S(2)}) collective-permute-start(bf16[16,4096]{1,0:T(8,128)(2,1)S(1)} %get-tuple-element.66), channel_id=1, source_target_pairs={{0,4},{1,5},{2,6},{3,7},{16,20},{17,21},{18,22},{19,23},{4,0},{5,1... | collective-permute-start | bytes 393224 | tf_op jit(solution)/shard_map/plane_1/ppermute | solution.py:52
  80.5 7.6 %collective-permute-start.31 = (bf16[16,4096]{1,0:T(8,128)(2,1)S(1)}, bf16[16,4096]{1,0:T(8,128)(2,1)S(1)}, u32[]{:S(2)}, u32[]{:S(2)}) collective-permute-start(bf16[16,4096]{1,0:T(8,128)(2,1)S(1)} %get-tuple-element.80), channel_id=1, source_target_pairs={{0,16},{1,17},{2,18},{3,19},{16,0},{17,1},{18,2},{19,3},{4,20},{5,... | collective-permute-start | bytes 393224 | tf_op jit(solution)/shard_map/member_4/ppermute | solution.py:63
  81.2 8.2 %collective-permute-start.32 = (bf16[16,4096]{1,0:T(8,128)(2,1)S(1)}, bf16[16,4096]{1,0:T(8,128)(2,1)S(1)}, u32[]{:S(2)}, u32[]{:S(2)}) collective-permute-start(bf16[16,4096]{1,0:T(8,128)(2,1)S(1)} %get-tuple-element.81), channel_id=1, source_target_pairs={{0,18},{1,19},{2,16},{3,17},{16,2},{17,3},{18,0},{19,1},{4,22},{5,... | collective-permute-start | bytes 393224 | tf_op jit(solution)/shard_map/member_6/ppermute | solution.py:63
  84.7 11.6 %collective-permute-start.20 = (bf16[16,4096]{1,0:T(8,128)(2,1)S(1)}, bf16[16,4096]{1,0:T(8,128)(2,1)S(1)}, u32[]{:S(2)}, u32[]{:S(2)}) collective-permute-start(bf16[16,4096]{1,0:T(8,128)(2,1)S(1)} %get-tuple-element.67), channel_id=1, source_target_pairs={{0,8},{1,9},{2,10},{3,11},{16,24},{17,25},{18,26},{19,27},{4,12},{... | collective-permute-start | bytes 393224 | tf_op jit(solution)/shard_map/plane_2/ppermute | solution.py:52
  88.0 8.2 %collective-permute-start.29 = (bf16[16,4096]{1,0:T(8,128)(2,1)S(1)}, bf16[16,4096]{1,0:T(8,128)(2,1)S(1)}, u32[]{:S(2)}, u32[]{:S(2)}) collective-permute-start(bf16[16,4096]{1,0:T(8,128)(2,1)S(1)} %add_chips.4), channel_id=1, source_target_pairs={{0,12},{1,13},{2,14},{3,15},{16,28},{17,29},{18,30},{19,31},{4,8},... | collective-permute-start | bytes 393224 | tf_op jit(solution)/shard_map/plane_3/ppermute | solution.py:52
  (7 other events, 47.4 us)

commit v10 on v9

--- a/solution.py
+++ b/solution.py
@@ -19,6 +19,8 @@
 SMEM = pl.BlockSpec(memory_space=pltpu.SMEM)
 HBM = pl.BlockSpec(memory_space=pltpu.HBM)
 MEBI = 1 << 20
+DOWN_PARTS = 4
+UP_WIDTH = 256
 EXPERT_LIMIT = 16 * MEBI
 
 
@@ -149,7 +151,7 @@
     return result
 
 
-def own_attention(queries, new_kv, pages, table, lengths):
+def own_attention(queries, new_kv, pages, table, lengths, down_proj):
     page_count, page_len, kv_width = pages.shape
     requests = new_kv.shape[0]
     rows = requests * HEADS
@@ -165,10 +167,12 @@
         pages_hbm,
         table_hbm,
         lengths_hbm,
+        down_hbm,
         out_ref,
         top_ref,
         sum_ref,
         query_ref,
+        down_ref,
         s_ref,
         fresh_ref,
         heads_ref,
@@ -192,6 +196,15 @@
             pltpu.make_async_copy(lengths_hbm, lengths_ref, sems.at[2]),
             pltpu.make_async_copy(new_hbm, fresh_ref.at[pl.ds(0, requests)], sems.at[3]),
         ]
+        down_rows = down_ref.shape[0] // DOWN_PARTS
+        down_copies = [
+            pltpu.make_async_copy(
+                down_hbm.at[0, pl.ds(c * down_rows, down_rows)],
+                down_ref.at[pl.ds(c * down_rows, down_rows)],
+                sems.at[4 + chunks + c],
+            )
+            for c in range(DOWN_PARTS)
+        ]
         fresh_ref[requests:] = jnp.zeros_like(fresh_ref[requests:])
         for copy in copies + page_copies:
             copy.start()
@@ -213,6 +226,9 @@
         top = fresh
         for c in range(chunks):
             page_copies[c].wait()
+            if c == chunks - 1:
+                for copy in down_copies:
+                    copy.start()
             keys = pages_ref[c * chunk_pages : (c + 1) * chunk_pages, :, :half].reshape(chunk, half)
             bias = token_bias(held, c * chunk_pages, chunk, page_len)
             scores = masked_scores(blocks, keys, bias, scaling)
@@ -234,13 +250,21 @@
         out_ref[...] = own_head(summed)
         top_ref[...] = jnp.broadcast_to(top, top_ref.shape)
         sum_ref[...] = jnp.broadcast_to(jnp.sum(total, axis=1, keepdims=True), sum_ref.shape)
+        for copy in down_copies:
+            copy.wait()
 
     shape = jax.ShapeDtypeStruct((rows, 128), jnp.float32)
     return pl.pallas_call(
         kernel,
-        out_shape=(shape, shape, shape, jax.ShapeDtypeStruct((rows, 128), jnp.bfloat16)),
-        in_specs=[HBM] * 5,
-        out_specs=(VMEM,) * 4,
+        out_shape=(
+            shape,
+            shape,
+            shape,
+            jax.ShapeDtypeStruct((rows, 128), jnp.bfloat16),
+            pltpu.VMEM(down_proj.shape[1:], jnp.bfloat16),
+        ),
+        in_specs=[HBM] * 6,
+        out_specs=(VMEM,) * 5,
         scratch_shapes=[
             pltpu.VMEM((rows, chunks * chunk + 128), jnp.float32),
             pltpu.VMEM((128, kv_width), jnp.bfloat16),
@@ -249,7 +273,7 @@
             pltpu.VMEM(pages.shape, jnp.bfloat16),
             pltpu.VMEM(table.shape, jnp.int32),
             pltpu.SMEM(lengths.shape, jnp.int32),
-            pltpu.SemaphoreType.DMA((4 + chunks,)),
+            pltpu.SemaphoreType.DMA((4 + chunks + DOWN_PARTS,)),
         ],
         compiler_params=pltpu.CompilerParams(vmem_limit_bytes=24 * MEBI),
         cost_estimate=pl.CostEstimate(
@@ -258,7 +282,7 @@
             transcendentals=rows * chunks * chunk,
         ),
         name="own_attention",
-    )(*[in_hbm(value) for value in (queries, new_kv, pages, table, lengths)])
+    )(*[in_hbm(value) for value in (queries, new_kv, pages, table, lengths, down_proj)])
 
 
 def routing_columns(ids, gates):
@@ -314,37 +338,23 @@
 def run_experts(own, other, weights, expert, top_count, slots, keep):
     rows, model_dim = own.shape
     rows, model_dim = 2 * rows, model_dim - 128
-    gate_up, down_proj = weights
-    double, hidden_dim = gate_up.shape[-1], down_proj.shape[-2]
-    width = 256
+    up_first, up_rest, down_proj = weights
+    hidden_dim = down_proj.shape[0]
+    width = UP_WIDTH
     up_steps = hidden_dim // width
     out_width = 1024 if rows <= 512 else 512
     out_steps = model_dim // out_width
     strip = 256
 
-    def kernel(expert_ref, own_ref, other_ref, *refs):
-        copies = {}
+    def kernel(expert_ref, own_ref, other_ref, first_ref, rest_in, down_ref, out_ref, over_ref, *refs):
         if keep:
-            up_hbm, down_hbm, out_ref, over_ref, up_ref, down_ref, tokens_ref, hidden_ref, sems = refs
-            for c in range(up_steps):
-                for half in range(2):
-                    columns = pl.ds(half * hidden_dim + c * width, width)
-                    copies["up", c, half] = pltpu.make_async_copy(
-                        up_hbm.at[0, :, columns], up_ref.at[:, columns], sems.at[2 * c + half]
-                    )
-            for c in range(out_steps):
-                columns = pl.ds(c * out_width, out_width)
-                copies["down", c] = pltpu.make_async_copy(
-                    down_hbm.at[0, :, columns], down_ref.at[:, columns], sems.at[2 * up_steps + c]
-                )
-            for copy in copies.values():
+            rest_ref, tokens_ref, hidden_ref, sems = refs
+            copies = up_parts(rest_in, rest_ref, range(1, up_steps), sems)
+            for copy in copies:
                 copy.start()
         else:
-            up_ref, down_ref, out_ref, over_ref, tokens_ref, hidden_ref = refs
-
-        def arrive(*name):
-            if keep:
-                copies[name].wait()
+            rest_ref, copies = rest_in, []
+            tokens_ref, hidden_ref = refs
 
         token_refs = [own_ref, other_ref]
         routing = stacked([ref[:, model_dim:] for ref in token_refs]).astype(jnp.float32)
@@ -390,16 +400,17 @@
             ).astype(jnp.bfloat16)
 
         for c in range(up_steps):
-            arrive("up", c, 0)
-            arrive("up", c, 1)
+            for copy in copies[2 * c - 2 : 2 * c] if c else []:
+                copy.wait()
             start = c * width
+            up_ref, place_of = (rest_ref, 2 * start - 2 * width) if c else (first_ref, 0)
             tokens = tokens_ref[...]
             gated = jnp.dot(
-                tokens, up_ref[:, start : start + width], preferred_element_type=jnp.float32
+                tokens, up_ref[:, place_of : place_of + width], preferred_element_type=jnp.float32
             )
             up = jnp.dot(
                 tokens,
-                up_ref[:, hidden_dim + start : hidden_dim + start + width],
+                up_ref[:, place_of + width : place_of + 2 * width],
                 preferred_element_type=jnp.float32,
             )
             hidden_ref[:, start : start + width] = (gated / (1.0 + jnp.exp(-gated)) * up).astype(
@@ -407,7 +418,6 @@
             )
 
         for c in range(out_steps):
-            arrive("down", c)
             columns = slice(c * out_width, (c + 1) * out_width)
             result = jnp.dot(
                 hidden_ref[...], down_ref[:, columns], preferred_element_type=jnp.float32
@@ -420,18 +430,13 @@
     shape = jax.ShapeDtypeStruct((rows // 2, model_dim), jnp.bfloat16)
     kept, scratch = (), []
     if keep:
-        kept = (
-            pltpu.VMEM((model_dim, double), jnp.bfloat16),
-            pltpu.VMEM((hidden_dim, model_dim), jnp.bfloat16),
-        )
-        scratch = [pltpu.SemaphoreType.DMA((2 * up_steps + out_steps,))]
-        weights = [in_hbm(gate_up), in_hbm(down_proj)]
-    else:
-        weights = [pltpu.with_memory_space_constraint(value, pltpu.VMEM) for value in weights]
+        kept = (pltpu.VMEM((model_dim, 2 * (hidden_dim - width)), jnp.bfloat16),)
+        scratch = [pltpu.SemaphoreType.DMA((2 * (up_steps - 1),))]
+        up_rest = in_hbm(up_rest)
     results = pl.pallas_call(
         kernel,
         out_shape=(shape, shape) + kept,
-        in_specs=[SMEM, VMEM, VMEM] + [HBM if keep else VMEM] * 2,
+        in_specs=[SMEM, VMEM, VMEM, VMEM, HBM if keep else VMEM, VMEM],
         out_specs=(VMEM,) * (2 + len(kept)),
         scratch_shapes=[
             pltpu.VMEM((slots, model_dim), jnp.bfloat16),
@@ -445,7 +450,7 @@
             transcendentals=slots * hidden_dim,
         ),
         name="run_experts",
-    )(expert, own, other, *weights)
+    )(expert, own, other, up_first, up_rest, down_proj)
     return results[0], results[1], results[2:]
 
 
@@ -488,8 +493,21 @@
     )(*flat)
 
 
+def up_parts(up_hbm, up_ref, steps, sems):
+    hidden_dim = up_hbm.shape[2] // 2
+    return [
+        pltpu.make_async_copy(
+            up_hbm.at[0, :, pl.ds(half * hidden_dim + c * UP_WIDTH, UP_WIDTH)],
+            up_ref.at[:, pl.ds((2 * i + half) * UP_WIDTH, UP_WIDTH)],
+            sems.at[2 * i + half],
+        )
+        for i, c in enumerate(steps)
+        for half in range(2)
+    ]
+
+
 def finish_attention(
-    query, fetched, table, lengths, partial, residual, gain, ids, gates, pages_own
+    query, fetched, table, lengths, partial, residual, gain, ids, gates, gate_up, pages_own
 ):
     count, page_len, kv_width = fetched.shape
     half = kv_width // 2
@@ -498,7 +516,10 @@
     rows = query.shape[0]
     scaling = 1.0 / math.sqrt(HEAD_DIMENSION)
 
-    def kernel(q_ref, fetched_ref, table_ref, lengths_ref, sum_ref, top_ref, total_ref, residual_ref, gain_ref, ids_ref, gates_ref, attended_ref, merged_ref, normed_ref, heads_ref):
+    def kernel(q_ref, fetched_ref, table_ref, lengths_ref, sum_ref, top_ref, total_ref, residual_ref, gain_ref, ids_ref, gates_ref, up_hbm, attended_ref, merged_ref, normed_ref, up_ref, heads_ref, sems):
+        up_copies = up_parts(up_hbm, up_ref, [0], sems)
+        for copy in up_copies:
+            copy.start()
         blocks = head_blocks(q_ref[...])
         held = tokens_of_pages(table_ref[...], lengths_ref, pages_own, page_len)
         bias = token_bias(held, 0, tokens, page_len)
@@ -533,20 +554,27 @@
         normed_ref[:, :model_dim] = (
             merged_ref[...].astype(jnp.float32) * inverse * gain_ref[...]
         ).astype(jnp.bfloat16)
+        for copy in up_copies:
+            copy.wait()
 
     shape = jax.ShapeDtypeStruct((requests, model_dim), jnp.bfloat16)
     return pl.pallas_call(
         kernel,
-        out_shape=(shape, shape, jax.ShapeDtypeStruct((requests, model_dim + 128), jnp.bfloat16)),
-        in_specs=[VMEM] * 3 + [SMEM] + [VMEM] * 7,
-        out_specs=(VMEM,) * 3,
-        scratch_shapes=[pltpu.VMEM((rows, 128), jnp.float32)],
+        out_shape=(
+            shape,
+            shape,
+            jax.ShapeDtypeStruct((requests, model_dim + 128), jnp.bfloat16),
+            pltpu.VMEM((model_dim, 2 * UP_WIDTH), jnp.bfloat16),
+        ),
+        in_specs=[VMEM] * 3 + [SMEM] + [VMEM] * 7 + [HBM],
+        out_specs=(VMEM,) * 4,
+        scratch_shapes=[pltpu.VMEM((rows, 128), jnp.float32), pltpu.SemaphoreType.DMA((2,))],
         compiler_params=pltpu.CompilerParams(vmem_limit_bytes=16 * MEBI),
         cost_estimate=pl.CostEstimate(
             flops=4 * rows * half * tokens, bytes_accessed=4 * MEBI, transcendentals=rows * tokens
         ),
         name="finish_attention",
-    )(query, fetched, table, lengths, *partial, residual, gain, ids, gates)
+    )(query, fetched, table, lengths, *partial, residual, gain, ids, gates, in_hbm(gate_up))
 
 
 def local(
@@ -575,8 +603,10 @@
     queries, expert_ids, picked = lax.optimization_barrier((queries, expert_ids, picked))
 
     expert = (lax.axis_index("pool") * layout.dev + lax.axis_index("dev")).reshape(1)
-    *partial, query = own_attention(queries, new_kv, kv_pages, page_table, lengths)
-    attended, merged, normed = finish_attention(
+    *partial, query, down_near = own_attention(
+        queries, new_kv, kv_pages, page_table, lengths, w_down
+    )
+    attended, merged, normed, up_first = finish_attention(
         query,
         fetched,
         page_table,
@@ -586,6 +616,7 @@
         norm_gain.reshape(1, model_dim),
         expert_ids.T,
         gate_weights.T,
+        w_gate_up,
         kv_pages.shape[0],
     )
 
@@ -621,18 +652,21 @@
         return add_up([[part] for part in parts], [count_of_rows], "add_chips")[0]
 
     own, other, slots = to_experts(near, blocks[far[-1]])
-    mine, over, kept = run_experts(own, other, (w_gate_up, w_down), expert, top_count, slots, True)
+    mine, over, (up_rest,) = run_experts(
+        own, other, (up_first, w_gate_up, down_near), expert, top_count, slots, True
+    )
     near_mine, near_back = mine, layout.swapped(over, 1)
     own, other, slots = to_experts(far, over)
-    other = after(other, near_back)
-    mine, over, _ = run_experts(own, other, kept, expert, top_count, slots, False)
+    mine, over, _ = run_experts(
+        own, other, (up_first, up_rest, down_near), expert, top_count, slots, False
+    )
     near_sums = add_up(
         [[near_mine], [near_back]], [count_of_rows * len(near)] * len(chips), "add_cores"
     )
     far_sums = add_cores(mine, layout.swapped(over, 1))
     parts = to_owners(near_sums, 0)
     totals = add_up([[part] for part in parts], [count_of_rows] * len(near), "add_chips")
-    others = [layout.shifted(total, by) for total, by in zip(totals, near)]
+    others = [layout.shifted(total, by) for total, by in list(zip(totals, near))[::-1]]
     for i, by in list(enumerate(far))[:0:-1]:
         others.append(layout.shifted(total_of(to_owners(far_sums, i)), by))
     merged = add_up(

time: 97.4 us -> 103 us (1.057)
  waiting for transfers between devices: 35.2 us -> 25.3 us
  local copies, waits for them, and re-layouts: 0.04 us -> 7.07 us
  starting transfers between devices: 37.6 us -> 43 us
  Pallas kernels: 22.6 us -> 25.8 us
    unnamed x12 -> x20, local copies, waits for them, and re-layouts: 0.04 us -> 7.07 us
    ppermute x25, waiting for transfers between devices: 25 us -> 18 us  [swapped(): return lax.ppermute(value, AXES, pairs)]
    ppermute x6, starting transfers between devices: 8.95 us -> 13.6 us  [shifted(): return lax.ppermute(value, AXES, pairs)]
    pallas_call x1, Pallas kernels: 1.93 us -> 5.03 us  [finish_attention(): pl.pallas_call(kernel, out_shape=(shape, shape, jax.ShapeDtypeStruct((req...]
    ppermute x6, waiting for transfers between devices: 8.12 us -> 5.56 us  [shifted(): return lax.ppermute(value, AXES, pairs)]
    pallas_call x1, Pallas kernels: 4.74 us -> 6.25 us  [own_attention(): pl.pallas_call(kernel, out_shape=(shape, shape, shape, jax.ShapeDtypeStru...]
    pallas_call x2, Pallas kernels: 13.4 us -> 11.9 us  [run_experts(): pl.pallas_call(kernel, out_shape=(shape, shape) + kept, in_specs=[SMEM, V...]
  transfers between devices with their start and end apart: 33 -> 33, of which waited for: 16 -> 15; matrix products, arithmetic and copies ran while one was open for 0% -> 0% of each run, Pallas kernels for 14% -> 18%
where the time goes in v10:
time: 103 us
  starting transfers between devices  43 us (42%)
  Pallas kernels  25.8 us (25%)
  waiting for transfers between devices  25.3 us (25%)
  local copies, waits for them, and re-layouts  7.07 us (7%)
    ppermute x25, starting transfers between devices, swapped(): return lax.ppermute(value, AXES, pairs)  24.2 us
    ppermute x25, waiting for transfers between devices, swapped(): return lax.ppermute(value, AXES, pairs)  18 us
    ppermute x6, starting transfers between devices, shifted(): return lax.ppermute(value, AXES, pairs)  13.6 us
    pallas_call x2, Pallas kernels, run_experts(): pl.pallas_call(kernel, out_shape=(shape, shape) + kept, in_specs=[SMEM, V...  11.9 us
    unnamed x20, local copies, waits for them, and re-layouts  7.07 us
    pallas_call x1, Pallas kernels, own_attention(): pl.pallas_call(kernel, out_shape=(shape, shape, shape, jax.ShapeDtypeStru...  6.25 us
    ppermute x6, waiting for transfers between devices, shifted(): return lax.ppermute(value, AXES, pairs)  5.56 us
    ppermute x2, starting transfers between devices, from_behind(): lax.ppermute(value, axis, [(i, (i + by) % length) for i in range(length)])  5.09 us
  transfers between devices with their start and end apart: 33, of which 15 were waited for; matrix products, arithmetic and copies ran while one was open for 0% of the time, Pallas kernels for 18%

profile of v10, /device:TPU:0, one launch (start us, length us, event | category | flops | bytes accessed | tf_op | source)
XLA Modules:
  0.0 102.7 jit_solution(11074283156716494369)
XLA Ops:
  0.6 3.0 %collective-permute-start = (s32[16]{0:T(128)}, s32[16]{0:T(128)S(1)}, u32[]{:S(2)}, u32[]{:S(2)}) collective-permute-start(s32[16]{0:T(128)} %param.17), channel_id=1, source_target_pairs={{0,16},{16,0},{1,17},{17,1},{2,18},{18,2},{3,19},{19,3},{4,20},{20... | collective-permute-start | bytes 200 | tf_op jit(solution)/shard_map/ppermute | solution.py:70
  3.6 1.7 %collective-permute-done.slots_ref = s32[16]{0:T(128)S(1)} collective-permute-done((s32[16]{0:T(128)}, s32[16]{0:T(128)S(1)}, u32[]{:S(2)}, u32[]{:S(2)}) %collective-permute-start) | collective-permute-done | bytes 96 | tf_op jit(solution)/shard_map/ppermute | solution.py:70
  5.3 1.6 %pick_pages.1 = bf16[16,16,512]{2,1,0:T(8,128)(2,1)S(1)} custom-call(s32[16]{0:T(128)S(1)} %collective-permute-done.slots_ref, bf16[128,16,512]{2,1,0:T(8,128)(2,1)} %pages_hbm.1), custom_call_target="tpu_custom_call" | custom-call | bytes 1048576 | tf_op jit(solution)/shard_map/pick_pages/pallas_call | solution.py:86
  7.0 2.1 %collective-permute-start.1 = (bf16[16,16,512]{2,1,0:T(8,128)(2,1)S(1)}, bf16[16,16,512]{2,1,0:T(8,128)(2,1)S(1)}, u32[]{:S(2)}, u32[]{:S(2)}) collective-permute-start(bf16[16,16,512]{2,1,0:T(8,128)(2,1)S(1)} %pick_pages.1), channel_id=1, source_target_pairs={{0,16},{16,0},{1,17},{17,1},{2,18},{18,2},{3,19},{19,3},{4,20},{20... | collective-permute-start | bytes 786440 | tf_op jit(solution)/shard_map/ppermute | solution.py:70
  9.0 6.2 %own_attention.1 = (f32[512,128]{1,0:T(8,128)S(1)}, f32[512,128]{1,0:T(8,128)S(1)}, f32[512,128]{1,0:T(8,128)S(1)}, bf16[512,128]{1,0:T(8,128)(2,1)S(1)}, bf16[768,4096]{1,0:T(8,128)(2,1)S(1)}) custom-call(bf16[16,4096]{1,0:T(8,128)(2,1)} %queries_hbm, bf16[16,512]{1,0:T(8,128)(2,1)} %new_hbm.1, bf16[128,16,512]{2,1,0:T(8,128)(2,1)} %pages_hbm.1, ...), custom_call_target="tpu_custom_call" | custom-call | flops 1073741824 | bytes 16777216 | tf_op jit(solution)/shard_map/own_attention/pallas_call | solution.py:257
  15.4 5.0 %finish_attention.1 = (bf16[16,4096]{1,0:T(8,128)(2,1)}, bf16[16,4096]{1,0:T(8,128)(2,1)S(1)}, bf16[16,4224]{1,0:T(8,128)(2,1)S(1)}, bf16[4096,512]{1,0:T(8,128)(2,1)S(1)}) custom-call(bf16[512,128]{1,0:T(8,128)(2,1)S(1)} %get-tuple-element.43.q_ref, bf16[16,16,512]{2,1,0:T(8,128)(2,1)S(1)} %collective-permute-done.1.fetched_ref, s32[16,16]{1,0:T(8,128)S(1)} %copy-done.5, ...), custom_call_target="tpu_custom_call" | custom-call | flops 134217728 | bytes 4194304 | tf_op jit(solution)/shard_map/finish_attention/pallas_call | solution.py:561
  20.4 2.1 %copy-done.2 = bf16[4096,512]{1,0:T(8,128)(2,1)} copy-done((bf16[4096,512]{1,0:T(8,128)(2,1)}, bf16[4096,512]{1,0:T(8,128)(2,1)S(1)}, u32[]{:S(2)}) %copy-start.2) | copy-done | bytes 4194328
  22.5 1.5 %collective-permute-start.5 = (bf16[16,4224]{1,0:T(8,128)(2,1)S(1)}, bf16[16,4224]{1,0:T(8,128)(2,1)S(1)}, u32[]{:S(2)}, u32[]{:S(2)}) collective-permute-start(bf16[16,4224]{1,0:T(8,128)(2,1)S(1)} %get-tuple-element.70.refs_0_), channel_id=1, source_target_pairs={{0,2},{1,3},{2,0},{3,1},{16,18},{17,19},{18,16},{19,17},{4,6},{5,7... | collective-permute-start | bytes 405512 | tf_op jit(solution)/shard_map/member_2/ppermute | solution.py:65
  24.0 2.6 %collective-permute-start.3 = (bf16[16,4224]{1,0:T(8,128)(2,1)S(1)}, bf16[16,4224]{1,0:T(8,128)(2,1)S(1)}, u32[]{:S(2)}, u32[]{:S(2)}) collective-permute-start(bf16[16,4224]{1,0:T(8,128)(2,1)S(1)} %get-tuple-element.70.refs_0_), channel_id=1, source_target_pairs={{0,8},{1,9},{2,10},{3,11},{16,24},{17,25},{18,26},{19,27},{4,12},{... | collective-permute-start | bytes 405512 | tf_op jit(solution)/shard_map/plane_2/ppermute | solution.py:54
  27.1 1.5 %collective-permute-start.8 = (bf16[16,4224]{1,0:T(8,128)(2,1)S(1)}, bf16[16,4224]{1,0:T(8,128)(2,1)S(1)}, u32[]{:S(2)}, u32[]{:S(2)}) collective-permute-start(bf16[16,4224]{1,0:T(8,128)(2,1)S(1)} %get-tuple-element.70.refs_0_), channel_id=1, source_target_pairs={{0,16},{1,17},{2,18},{3,19},{16,0},{17,1},{18,2},{19,3},{4,20},{5,... | collective-permute-start | bytes 405512 | tf_op jit(solution)/shard_map/member_4/ppermute | solution.py:65
  28.6 1.6 %collective-permute-start.2 = (bf16[16,4224]{1,0:T(8,128)(2,1)S(1)}, bf16[16,4224]{1,0:T(8,128)(2,1)S(1)}, u32[]{:S(2)}, u32[]{:S(2)}) collective-permute-start(bf16[16,4224]{1,0:T(8,128)(2,1)S(1)} %get-tuple-element.70.refs_0_), channel_id=1, source_target_pairs={{0,4},{1,5},{2,6},{3,7},{16,20},{17,21},{18,22},{19,23},{4,0},{5,1... | collective-permute-start | bytes 405512 | tf_op jit(solution)/shard_map/plane_1/ppermute | solution.py:54
  31.7 1.5 %collective-permute-start.4 = (bf16[16,4224]{1,0:T(8,128)(2,1)S(1)}, bf16[16,4224]{1,0:T(8,128)(2,1)S(1)}, u32[]{:S(2)}, u32[]{:S(2)}) collective-permute-start(bf16[16,4224]{1,0:T(8,128)(2,1)S(1)} %collective-permute-done.3.refs_1_), channel_id=1, source_target_pairs={{0,4},{1,5},{2,6},{3,7},{16,20},{17,21},{18,22},{19,23},{4,0},{5,1... | collective-permute-start | bytes 405512 | tf_op jit(solution)/shard_map/plane_1/ppermute | solution.py:54
  34.0 2.7 %collective-permute-start.13 = (bf16[16,4224]{1,0:T(8,128)(2,1)S(1)}, bf16[16,4224]{1,0:T(8,128)(2,1)S(1)}, u32[]{:S(2)}, u32[]{:S(2)}) collective-permute-start(bf16[16,4224]{1,0:T(8,128)(2,1)S(1)} %collective-permute-done.3.refs_1_), channel_id=1, source_target_pairs={{0,18},{1,19},{2,16},{3,17},{16,2},{17,3},{18,0},{19,1},{4,22},{5,... | collective-permute-start | bytes 405512 | tf_op jit(solution)/shard_map/member_6/ppermute | solution.py:65
  36.9 2.8 %collective-permute-done.7.refs_3_ = bf16[16,4224]{1,0:T(8,128)(2,1)S(1)} collective-permute-done((bf16[16,4224]{1,0:T(8,128)(2,1)S(1)}, bf16[16,4224]{1,0:T(8,128)(2,1)S(1)}, u32[]{:S(2)}, u32[]{:S(2)}) %collective-permute-start.7) | collective-permute-done | bytes 135200 | tf_op jit(solution)/shard_map/member_2/ppermute | solution.py:65
  40.7 2.1 %collective-permute-done.13.refs_7_ = bf16[16,4224]{1,0:T(8,128)(2,1)S(1)} collective-permute-done((bf16[16,4224]{1,0:T(8,128)(2,1)S(1)}, bf16[16,4224]{1,0:T(8,128)(2,1)S(1)}, u32[]{:S(2)}, u32[]{:S(2)}) %collective-permute-start.13) | collective-permute-done | bytes 135200 | tf_op jit(solution)/shard_map/member_6/ppermute | solution.py:65
  46.1 1.5 %collective-permute-start.23 = (bf16[16,4224]{1,0:T(8,128)(2,1)S(1)}, bf16[16,4224]{1,0:T(8,128)(2,1)S(1)}, u32[]{:S(2)}, u32[]{:S(2)}) collective-permute-start(bf16[16,4224]{1,0:T(8,128)(2,1)S(1)} %collective-permute-done.4.refs_1_), channel_id=1, source_target_pairs={{0,18},{1,19},{2,16},{3,17},{16,2},{17,3},{18,0},{19,1},{4,22},{5,... | collective-permute-start | bytes 405512 | tf_op jit(solution)/shard_map/member_6/ppermute | solution.py:65
  47.6 1.7 %collective-permute-start.22 = (bf16[16,4224]{1,0:T(8,128)(2,1)S(1)}, bf16[16,4224]{1,0:T(8,128)(2,1)S(1)}, u32[]{:S(2)}, u32[]{:S(2)}) collective-permute-start(bf16[16,4224]{1,0:T(8,128)(2,1)S(1)} %collective-permute-done.4.refs_1_), channel_id=1, source_target_pairs={{0,16},{1,17},{2,18},{3,19},{16,0},{17,1},{18,2},{19,3},{4,20},{5,... | collective-permute-start | bytes 405512 | tf_op jit(solution)/shard_map/member_4/ppermute | solution.py:65
  49.6 2.8 %copy-done.1 = bf16[768,4096]{1,0:T(8,128)(2,1)S(1)} copy-done((bf16[768,4096]{1,0:T(8,128)(2,1)S(1)}, bf16[768,4096]{1,0:T(8,128)(2,1)}, u32[]{:S(2)}) %copy-start.1) | copy-done | bytes 6291480
  52.4 2.2 %copy-done.3 = bf16[4096,512]{1,0:T(8,128)(2,1)S(1)} copy-done((bf16[4096,512]{1,0:T(8,128)(2,1)S(1)}, bf16[4096,512]{1,0:T(8,128)(2,1)}, u32[]{:S(2)}) %copy-start.3) | copy-done | bytes 4194328
  54.6 6.9 %run_experts.2 = (bf16[128,4096]{1,0:T(8,128)(2,1)S(1)}, bf16[128,4096]{1,0:T(8,128)(2,1)S(1)}, bf16[4096,1024]{1,0:T(8,128)(2,1)S(1)}) custom-call(s32[1]{0:T(128)} %bitcast.3.expert_ref, bf16[128,4224]{1,0:T(8,128)(2,1)S(1)} %packed.2.own_ref, bf16[128,4224]{1,0:T(8,128)(2,1)S(1)} %collective-permute-done.14.other_ref, bf16[4096,512]{1,0:T(8,128)(2,1)S(1)} %copy-done.3, ...), custom_call_target="tpu_custom_call" | custom-call | flops 2415919104 | bytes 20971520 | tf_op jit(solution)/shard_map/run_experts/pallas_call | solution.py:436
  62.2 2.2 %collective-permute-done.24.other_ref = bf16[128,4224]{1,0:T(8,128)(2,1)S(1)} collective-permute-done((bf16[128,4224]{1,0:T(8,128)(2,1)S(1)}, bf16[128,4224]{1,0:T(8,128)(2,1)S(1)}, u32[]{:S(2)}, u32[]{:S(2)}) %collective-permute-start.24) | collective-permute-done | bytes 1081376 | tf_op jit(solution)/shard_map/member_1/ppermute | solution.py:65
  64.4 5.0 %run_experts.3 = (bf16[128,4096]{1,0:T(8,128)(2,1)S(1)}, bf16[128,4096]{1,0:T(8,128)(2,1)S(1)}) custom-call(s32[1]{0:T(128)} %bitcast.3.expert_ref, bf16[128,4224]{1,0:T(8,128)(2,1)S(1)} %packed.3.own_ref, bf16[128,4224]{1,0:T(8,128)(2,1)S(1)} %collective-permute-done.24.other_ref, bf16[4096,512]{1,0:T(8,128)(2,1)S(1)} %copy-done.3, ...), custom_call_target="tpu_custom_call" | custom-call | flops 2415919104 | bytes 20971520 | tf_op jit(solution)/shard_map/run_experts/pallas_call | solution.py:436
  69.9 1.8 %collective-permute-start.16 = (bf16[32,4096]{1,0:T(8,128)(2,1)S(1)}, bf16[32,4096]{1,0:T(8,128)(2,1)S(1)}, u32[]{:S(2)}, u32[]{:S(2)}) collective-permute-start(bf16[32,4096]{1,0:T(8,128)(2,1)S(1)} %get-tuple-element.65), channel_id=1, source_target_pairs={{0,2},{1,3},{2,0},{3,1},{16,18},{17,19},{18,16},{19,17},{4,6},{5,7... | collective-permute-start | bytes 786440 | tf_op jit(solution)/shard_map/member_2/ppermute | solution.py:65
  73.7 1.7 %collective-permute-start.26 = (bf16[16,4096]{1,0:T(8,128)(2,1)S(1)}, bf16[16,4096]{1,0:T(8,128)(2,1)S(1)}, u32[]{:S(2)}, u32[]{:S(2)}) collective-permute-start(bf16[16,4096]{1,0:T(8,128)(2,1)S(1)} %get-tuple-element.75), channel_id=1, source_target_pairs={{0,2},{1,3},{2,0},{3,1},{16,18},{17,19},{18,16},{19,17},{4,6},{5,7... | collective-permute-start | bytes 393224 | tf_op jit(solution)/shard_map/member_2/ppermute | solution.py:65
  75.8 3.5 %collective-permute-done.16.refs_1_ = bf16[32,4096]{1,0:T(8,128)(2,1)S(1)} collective-permute-done((bf16[32,4096]{1,0:T(8,128)(2,1)S(1)}, bf16[32,4096]{1,0:T(8,128)(2,1)S(1)}, u32[]{:S(2)}, u32[]{:S(2)}) %collective-permute-start.16) | collective-permute-done | bytes 262176 | tf_op jit(solution)/shard_map/member_2/ppermute | solution.py:65
  80.8 1.7 %collective-permute-start.30 = (bf16[16,4096]{1,0:T(8,128)(2,1)S(1)}, bf16[16,4096]{1,0:T(8,128)(2,1)S(1)}, u32[]{:S(2)}, u32[]{:S(2)}) collective-permute-start(bf16[16,4096]{1,0:T(8,128)(2,1)S(1)} %get-tuple-element.79), channel_id=1, source_target_pairs={{0,2},{1,3},{2,0},{3,1},{16,18},{17,19},{18,16},{19,17},{4,6},{5,7... | collective-permute-start | bytes 393224 | tf_op jit(solution)/shard_map/member_2/ppermute | solution.py:65
  82.5 3.8 %collective-permute-done.18.refs_3_ = bf16[32,4096]{1,0:T(8,128)(2,1)S(1)} collective-permute-done((bf16[32,4096]{1,0:T(8,128)(2,1)S(1)}, bf16[32,4096]{1,0:T(8,128)(2,1)S(1)}, u32[]{:S(2)}, u32[]{:S(2)}) %collective-permute-start.18) | collective-permute-done | bytes 262176 | tf_op jit(solution)/shard_map/member_6/ppermute | solution.py:65
  86.4 3.9 %collective-permute-start.19 = (bf16[16,4096]{1,0:T(8,128)(2,1)S(1)}, bf16[16,4096]{1,0:T(8,128)(2,1)S(1)}, u32[]{:S(2)}, u32[]{:S(2)}) collective-permute-start(bf16[16,4096]{1,0:T(8,128)(2,1)S(1)} %get-tuple-element.68), channel_id=1, source_target_pairs={{0,8},{1,9},{2,10},{3,11},{16,24},{17,25},{18,26},{19,27},{4,12},{... | collective-permute-start | bytes 393224 | tf_op jit(solution)/shard_map/plane_2/ppermute | solution.py:54
  90.3 1.5 %collective-permute-start.31 = (bf16[16,4096]{1,0:T(8,128)(2,1)S(1)}, bf16[16,4096]{1,0:T(8,128)(2,1)S(1)}, u32[]{:S(2)}, u32[]{:S(2)}) collective-permute-start(bf16[16,4096]{1,0:T(8,128)(2,1)S(1)} %get-tuple-element.80), channel_id=1, source_target_pairs={{0,16},{1,17},{2,18},{3,19},{16,0},{17,1},{18,2},{19,3},{4,20},{5,... | collective-permute-start | bytes 393224 | tf_op jit(solution)/shard_map/member_4/ppermute | solution.py:65
  93.4 4.0 %collective-permute-start.29 = (bf16[16,4096]{1,0:T(8,128)(2,1)S(1)}, bf16[16,4096]{1,0:T(8,128)(2,1)S(1)}, u32[]{:S(2)}, u32[]{:S(2)}) collective-permute-start(bf16[16,4096]{1,0:T(8,128)(2,1)S(1)} %add_chips.4), channel_id=1, source_target_pairs={{0,12},{1,13},{2,14},{3,15},{16,28},{17,29},{18,30},{19,31},{4,8},... | collective-permute-start | bytes 393224 | tf_op jit(solution)/shard_map/plane_3/ppermute | solution.py:54
  97.7 1.9 %collective-permute-done.20.refs_2_ = bf16[16,4096]{1,0:T(8,128)(2,1)S(1)} collective-permute-done((bf16[16,4096]{1,0:T(8,128)(2,1)S(1)}, bf16[16,4096]{1,0:T(8,128)(2,1)S(1)}, u32[]{:S(2)}, u32[]{:S(2)}) %collective-permute-start.20) | collective-permute-done | bytes 131104 | tf_op jit(solution)/shard_map/plane_1/ppermute | solution.py:54
  99.6 2.3 %collective-permute-done.29.refs_3_ = bf16[16,4096]{1,0:T(8,128)(2,1)S(1)} collective-permute-done((bf16[16,4096]{1,0:T(8,128)(2,1)S(1)}, bf16[16,4096]{1,0:T(8,128)(2,1)S(1)}, u32[]{:S(2)}, u32[]{:S(2)}) %collective-permute-start.29) | collective-permute-done | bytes 131104 | tf_op jit(solution)/shard_map/plane_3/ppermute | solution.py:54
  (68 shorter events, 15.4 us)
Async XLA Ops:
  0.6 4.7 %collective-permute-start = (s32[16]{0:T(128)}, s32[16]{0:T(128)S(1)}, u32[]{:S(2)}, u32[]{:S(2)}) collective-permute-start(s32[16]{0:T(128)} %param.17), channel_id=1, source_target_pairs={{0,16},{16,0},{1,17},{17,1},{2,18},{18,2},{3,19},{19,3},{4,20},{20... | collective-permute-start | bytes 200 | tf_op jit(solution)/shard_map/ppermute | solution.py:70
  7.0 8.4 %collective-permute-start.1 = (bf16[16,16,512]{2,1,0:T(8,128)(2,1)S(1)}, bf16[16,16,512]{2,1,0:T(8,128)(2,1)S(1)}, u32[]{:S(2)}, u32[]{:S(2)}) collective-permute-start(bf16[16,16,512]{2,1,0:T(8,128)(2,1)S(1)} %pick_pages.1), channel_id=1, source_target_pairs={{0,16},{16,0},{1,17},{17,1},{2,18},{18,2},{3,19},{19,3},{4,20},{20... | collective-permute-start | bytes 786440 | tf_op jit(solution)/shard_map/ppermute | solution.py:70
  22.5 7.7 %collective-permute-start.5 = (bf16[16,4224]{1,0:T(8,128)(2,1)S(1)}, bf16[16,4224]{1,0:T(8,128)(2,1)S(1)}, u32[]{:S(2)}, u32[]{:S(2)}) collective-permute-start(bf16[16,4224]{1,0:T(8,128)(2,1)S(1)} %get-tuple-element.70.refs_0_), channel_id=1, source_target_pairs={{0,2},{1,3},{2,0},{3,1},{16,18},{17,19},{18,16},{19,17},{4,6},{5,7... | collective-permute-start | bytes 405512 | tf_op jit(solution)/shard_map/member_2/ppermute | solution.py:65
  24.0 7.5 %collective-permute-start.3 = (bf16[16,4224]{1,0:T(8,128)(2,1)S(1)}, bf16[16,4224]{1,0:T(8,128)(2,1)S(1)}, u32[]{:S(2)}, u32[]{:S(2)}) collective-permute-start(bf16[16,4224]{1,0:T(8,128)(2,1)S(1)} %get-tuple-element.70.refs_0_), channel_id=1, source_target_pairs={{0,8},{1,9},{2,10},{3,11},{16,24},{17,25},{18,26},{19,27},{4,12},{... | collective-permute-start | bytes 405512 | tf_op jit(solution)/shard_map/plane_2/ppermute | solution.py:54
  26.6 6.6 %collective-permute-start.11 = (bf16[16,4224]{1,0:T(8,128)(2,1)S(1)}, bf16[16,4224]{1,0:T(8,128)(2,1)S(1)}, u32[]{:S(2)}, u32[]{:S(2)}) collective-permute-start(bf16[16,4224]{1,0:T(8,128)(2,1)S(1)} %get-tuple-element.70.refs_0_), channel_id=1, source_target_pairs={{0,18},{1,19},{2,16},{3,17},{16,2},{17,3},{18,0},{19,1},{4,22},{5,... | collective-permute-start | bytes 405512 | tf_op jit(solution)/shard_map/member_6/ppermute | solution.py:65
  27.1 6.3 %collective-permute-start.8 = (bf16[16,4224]{1,0:T(8,128)(2,1)S(1)}, bf16[16,4224]{1,0:T(8,128)(2,1)S(1)}, u32[]{:S(2)}, u32[]{:S(2)}) collective-permute-start(bf16[16,4224]{1,0:T(8,128)(2,1)S(1)} %get-tuple-element.70.refs_0_), channel_id=1, source_target_pairs={{0,16},{1,17},{2,18},{3,19},{16,0},{17,1},{18,2},{19,3},{4,20},{5,... | collective-permute-start | bytes 405512 | tf_op jit(solution)/shard_map/member_4/ppermute | solution.py:65
  28.6 8.1 %collective-permute-start.2 = (bf16[16,4224]{1,0:T(8,128)(2,1)S(1)}, bf16[16,4224]{1,0:T(8,128)(2,1)S(1)}, u32[]{:S(2)}, u32[]{:S(2)}) collective-permute-start(bf16[16,4224]{1,0:T(8,128)(2,1)S(1)} %get-tuple-element.70.refs_0_), channel_id=1, source_target_pairs={{0,4},{1,5},{2,6},{3,7},{16,20},{17,21},{18,22},{19,23},{4,0},{5,1... | collective-permute-start | bytes 405512 | tf_op jit(solution)/shard_map/plane_1/ppermute | solution.py:54
  31.5 8.1 %collective-permute-start.7 = (bf16[16,4224]{1,0:T(8,128)(2,1)S(1)}, bf16[16,4224]{1,0:T(8,128)(2,1)S(1)}, u32[]{:S(2)}, u32[]{:S(2)}) collective-permute-start(bf16[16,4224]{1,0:T(8,128)(2,1)S(1)} %collective-permute-done.3.refs_1_), channel_id=1, source_target_pairs={{0,2},{1,3},{2,0},{3,1},{16,18},{17,19},{18,16},{19,17},{4,6},{5,7... | collective-permute-start | bytes 405512 | tf_op jit(solution)/shard_map/member_2/ppermute | solution.py:65
  31.7 8.3 %collective-permute-start.4 = (bf16[16,4224]{1,0:T(8,128)(2,1)S(1)}, bf16[16,4224]{1,0:T(8,128)(2,1)S(1)}, u32[]{:S(2)}, u32[]{:S(2)}) collective-permute-start(bf16[16,4224]{1,0:T(8,128)(2,1)S(1)} %collective-permute-done.3.refs_1_), channel_id=1, source_target_pairs={{0,4},{1,5},{2,6},{3,7},{16,20},{17,21},{18,22},{19,23},{4,0},{5,1... | collective-permute-start | bytes 405512 | tf_op jit(solution)/shard_map/plane_1/ppermute | solution.py:54
  33.4 7.3 %collective-permute-start.10 = (bf16[16,4224]{1,0:T(8,128)(2,1)S(1)}, bf16[16,4224]{1,0:T(8,128)(2,1)S(1)}, u32[]{:S(2)}, u32[]{:S(2)}) collective-permute-start(bf16[16,4224]{1,0:T(8,128)(2,1)S(1)} %collective-permute-done.3.refs_1_), channel_id=1, source_target_pairs={{0,16},{1,17},{2,18},{3,19},{16,0},{17,1},{18,2},{19,3},{4,20},{5,... | collective-permute-start | bytes 405512 | tf_op jit(solution)/shard_map/member_4/ppermute | solution.py:65
  34.0 8.8 %collective-permute-start.13 = (bf16[16,4224]{1,0:T(8,128)(2,1)S(1)}, bf16[16,4224]{1,0:T(8,128)(2,1)S(1)}, u32[]{:S(2)}, u32[]{:S(2)}) collective-permute-start(bf16[16,4224]{1,0:T(8,128)(2,1)S(1)} %collective-permute-done.3.refs_1_), channel_id=1, source_target_pairs={{0,18},{1,19},{2,16},{3,17},{16,2},{17,3},{18,0},{19,1},{4,22},{5,... | collective-permute-start | bytes 405512 | tf_op jit(solution)/shard_map/member_6/ppermute | solution.py:65
  36.7 7.0 %collective-permute-start.6 = (bf16[16,4224]{1,0:T(8,128)(2,1)S(1)}, bf16[16,4224]{1,0:T(8,128)(2,1)S(1)}, u32[]{:S(2)}, u32[]{:S(2)}) collective-permute-start(bf16[16,4224]{1,0:T(8,128)(2,1)S(1)} %collective-permute-done.2.refs_0_), channel_id=1, source_target_pairs={{0,2},{1,3},{2,0},{3,1},{16,18},{17,19},{18,16},{19,17},{4,6},{5,7... | collective-permute-start | bytes 405512 | tf_op jit(solution)/shard_map/member_2/ppermute | solution.py:65
  39.7 5.0 %collective-permute-start.9 = (bf16[16,4224]{1,0:T(8,128)(2,1)S(1)}, bf16[16,4224]{1,0:T(8,128)(2,1)S(1)}, u32[]{:S(2)}, u32[]{:S(2)}) collective-permute-start(bf16[16,4224]{1,0:T(8,128)(2,1)S(1)} %collective-permute-done.2.refs_0_), channel_id=1, source_target_pairs={{0,16},{1,17},{2,18},{3,19},{16,0},{17,1},{18,2},{19,3},{4,20},{5,... | collective-permute-start | bytes 405512 | tf_op jit(solution)/shard_map/member_4/ppermute | solution.py:65
  40.0 5.9 %collective-permute-start.12 = (bf16[16,4224]{1,0:T(8,128)(2,1)S(1)}, bf16[16,4224]{1,0:T(8,128)(2,1)S(1)}, u32[]{:S(2)}, u32[]{:S(2)}) collective-permute-start(bf16[16,4224]{1,0:T(8,128)(2,1)S(1)} %collective-permute-done.2.refs_0_), channel_id=1, source_target_pairs={{0,18},{1,19},{2,16},{3,17},{16,2},{17,3},{18,0},{19,1},{4,22},{5,... | collective-permute-start | bytes 405512 | tf_op jit(solution)/shard_map/member_6/ppermute | solution.py:65
  46.0 3.6 %collective-permute-start.14 = (bf16[128,4224]{1,0:T(8,128)(2,1)S(1)}, bf16[128,4224]{1,0:T(8,128)(2,1)S(1)}, u32[]{:S(2)}, u32[]{:S(2)}) collective-permute-start(bf16[128,4224]{1,0:T(8,128)(2,1)S(1)} %packed.2.own_ref), channel_id=1, source_target_pairs={{0,1},{1,0},{2,3},{3,2},{16,17},{17,16},{18,19},{19,18},{4,5},{5,4... | collective-permute-start | bytes 3244040 | tf_op jit(solution)/shard_map/member_1/ppermute | solution.py:65
  46.1 15.4 %collective-permute-start.23 = (bf16[16,4224]{1,0:T(8,128)(2,1)S(1)}, bf16[16,4224]{1,0:T(8,128)(2,1)S(1)}, u32[]{:S(2)}, u32[]{:S(2)}) collective-permute-start(bf16[16,4224]{1,0:T(8,128)(2,1)S(1)} %collective-permute-done.4.refs_1_), channel_id=1, source_target_pairs={{0,18},{1,19},{2,16},{3,17},{16,2},{17,3},{18,0},{19,1},{4,22},{5,... | collective-permute-start | bytes 405512 | tf_op jit(solution)/shard_map/member_6/ppermute | solution.py:65
  47.6 13.9 %collective-permute-start.22 = (bf16[16,4224]{1,0:T(8,128)(2,1)S(1)}, bf16[16,4224]{1,0:T(8,128)(2,1)S(1)}, u32[]{:S(2)}, u32[]{:S(2)}) collective-permute-start(bf16[16,4224]{1,0:T(8,128)(2,1)S(1)} %collective-permute-done.4.refs_1_), channel_id=1, source_target_pairs={{0,16},{1,17},{2,18},{3,19},{16,0},{17,1},{18,2},{19,3},{4,20},{5,... | collective-permute-start | bytes 405512 | tf_op jit(solution)/shard_map/member_4/ppermute | solution.py:65
  49.3 12.3 %collective-permute-start.21 = (bf16[16,4224]{1,0:T(8,128)(2,1)S(1)}, bf16[16,4224]{1,0:T(8,128)(2,1)S(1)}, u32[]{:S(2)}, u32[]{:S(2)}) collective-permute-start(bf16[16,4224]{1,0:T(8,128)(2,1)S(1)} %collective-permute-done.4.refs_1_), channel_id=1, source_target_pairs={{0,2},{1,3},{2,0},{3,1},{16,18},{17,19},{18,16},{19,17},{4,6},{5,7... | collective-permute-start | bytes 405512 | tf_op jit(solution)/shard_map/member_2/ppermute | solution.py:65
  61.7 8.0 %collective-permute-start.15 = (bf16[128,4096]{1,0:T(8,128)(2,1)S(1)}, bf16[128,4096]{1,0:T(8,128)(2,1)S(1)}, u32[]{:S(2)}, u32[]{:S(2)}) collective-permute-start(bf16[128,4096]{1,0:T(8,128)(2,1)S(1)} %get-tuple-element.63), channel_id=1, source_target_pairs={{0,1},{1,0},{2,3},{3,2},{16,17},{17,16},{18,19},{19,18},{4,5},{5,4... | collective-permute-start | bytes 3145736 | tf_op jit(solution)/shard_map/member_1/ppermute | solution.py:65
  69.5 4.0 %collective-permute-start.25 = (bf16[128,4096]{1,0:T(8,128)(2,1)S(1)}, bf16[128,4096]{1,0:T(8,128)(2,1)S(1)}, u32[]{:S(2)}, u32[]{:S(2)}) collective-permute-start(bf16[128,4096]{1,0:T(8,128)(2,1)S(1)} %get-tuple-element.73), channel_id=1, source_target_pairs={{0,1},{1,0},{2,3},{3,2},{16,17},{17,16},{18,19},{19,18},{4,5},{5,4... | collective-permute-start | bytes 3145736 | tf_op jit(solution)/shard_map/member_1/ppermute | solution.py:65
  69.9 9.4 %collective-permute-start.16 = (bf16[32,4096]{1,0:T(8,128)(2,1)S(1)}, bf16[32,4096]{1,0:T(8,128)(2,1)S(1)}, u32[]{:S(2)}, u32[]{:S(2)}) collective-permute-start(bf16[32,4096]{1,0:T(8,128)(2,1)S(1)} %get-tuple-element.65), channel_id=1, source_target_pairs={{0,2},{1,3},{2,0},{3,1},{16,18},{17,19},{18,16},{19,17},{4,6},{5,7... | collective-permute-start | bytes 786440 | tf_op jit(solution)/shard_map/member_2/ppermute | solution.py:65
  71.7 9.2 %collective-permute-start.17 = (bf16[32,4096]{1,0:T(8,128)(2,1)S(1)}, bf16[32,4096]{1,0:T(8,128)(2,1)S(1)}, u32[]{:S(2)}, u32[]{:S(2)}) collective-permute-start(bf16[32,4096]{1,0:T(8,128)(2,1)S(1)} %get-tuple-element.66), channel_id=1, source_target_pairs={{0,16},{1,17},{2,18},{3,19},{16,0},{17,1},{18,2},{19,3},{4,20},{5,... | collective-permute-start | bytes 786440 | tf_op jit(solution)/shard_map/member_4/ppermute | solution.py:65
  72.0 14.3 %collective-permute-start.18 = (bf16[32,4096]{1,0:T(8,128)(2,1)S(1)}, bf16[32,4096]{1,0:T(8,128)(2,1)S(1)}, u32[]{:S(2)}, u32[]{:S(2)}) collective-permute-start(bf16[32,4096]{1,0:T(8,128)(2,1)S(1)} %get-tuple-element.67), channel_id=1, source_target_pairs={{0,18},{1,19},{2,16},{3,17},{16,2},{17,3},{18,0},{19,1},{4,22},{5,... | collective-permute-start | bytes 786440 | tf_op jit(solution)/shard_map/member_6/ppermute | solution.py:65
  73.7 16.6 %collective-permute-start.26 = (bf16[16,4096]{1,0:T(8,128)(2,1)S(1)}, bf16[16,4096]{1,0:T(8,128)(2,1)S(1)}, u32[]{:S(2)}, u32[]{:S(2)}) collective-permute-start(bf16[16,4096]{1,0:T(8,128)(2,1)S(1)} %get-tuple-element.75), channel_id=1, source_target_pairs={{0,2},{1,3},{2,0},{3,1},{16,18},{17,19},{18,16},{19,17},{4,6},{5,7... | collective-permute-start | bytes 393224 | tf_op jit(solution)/shard_map/member_2/ppermute | solution.py:65
  75.5 16.3 %collective-permute-start.27 = (bf16[16,4096]{1,0:T(8,128)(2,1)S(1)}, bf16[16,4096]{1,0:T(8,128)(2,1)S(1)}, u32[]{:S(2)}, u32[]{:S(2)}) collective-permute-start(bf16[16,4096]{1,0:T(8,128)(2,1)S(1)} %get-tuple-element.76), channel_id=1, source_target_pairs={{0,16},{1,17},{2,18},{3,19},{16,0},{17,1},{18,2},{19,3},{4,20},{5,... | collective-permute-start | bytes 393224 | tf_op jit(solution)/shard_map/member_4/ppermute | solution.py:65
  79.3 13.9 %collective-permute-start.28 = (bf16[16,4096]{1,0:T(8,128)(2,1)S(1)}, bf16[16,4096]{1,0:T(8,128)(2,1)S(1)}, u32[]{:S(2)}, u32[]{:S(2)}) collective-permute-start(bf16[16,4096]{1,0:T(8,128)(2,1)S(1)} %get-tuple-element.77), channel_id=1, source_target_pairs={{0,18},{1,19},{2,16},{3,17},{16,2},{17,3},{18,0},{19,1},{4,22},{5,... | collective-permute-start | bytes 393224 | tf_op jit(solution)/shard_map/member_6/ppermute | solution.py:65
  80.8 12.5 %collective-permute-start.30 = (bf16[16,4096]{1,0:T(8,128)(2,1)S(1)}, bf16[16,4096]{1,0:T(8,128)(2,1)S(1)}, u32[]{:S(2)}, u32[]{:S(2)}) collective-permute-start(bf16[16,4096]{1,0:T(8,128)(2,1)S(1)} %get-tuple-element.79), channel_id=1, source_target_pairs={{0,2},{1,3},{2,0},{3,1},{16,18},{17,19},{18,16},{19,17},{4,6},{5,7... | collective-permute-start | bytes 393224 | tf_op jit(solution)/shard_map/member_2/ppermute | solution.py:65
  86.4 11.3 %collective-permute-start.19 = (bf16[16,4096]{1,0:T(8,128)(2,1)S(1)}, bf16[16,4096]{1,0:T(8,128)(2,1)S(1)}, u32[]{:S(2)}, u32[]{:S(2)}) collective-permute-start(bf16[16,4096]{1,0:T(8,128)(2,1)S(1)} %get-tuple-element.68), channel_id=1, source_target_pairs={{0,8},{1,9},{2,10},{3,11},{16,24},{17,25},{18,26},{19,27},{4,12},{... | collective-permute-start | bytes 393224 | tf_op jit(solution)/shard_map/plane_2/ppermute | solution.py:54
  90.3 7.1 %collective-permute-start.31 = (bf16[16,4096]{1,0:T(8,128)(2,1)S(1)}, bf16[16,4096]{1,0:T(8,128)(2,1)S(1)}, u32[]{:S(2)}, u32[]{:S(2)}) collective-permute-start(bf16[16,4096]{1,0:T(8,128)(2,1)S(1)} %get-tuple-element.80), channel_id=1, source_target_pairs={{0,16},{1,17},{2,18},{3,19},{16,0},{17,1},{18,2},{19,3},{4,20},{5,... | collective-permute-start | bytes 393224 | tf_op jit(solution)/shard_map/member_4/ppermute | solution.py:65
  91.8 5.9 %collective-permute-start.32 = (bf16[16,4096]{1,0:T(8,128)(2,1)S(1)}, bf16[16,4096]{1,0:T(8,128)(2,1)S(1)}, u32[]{:S(2)}, u32[]{:S(2)}) collective-permute-start(bf16[16,4096]{1,0:T(8,128)(2,1)S(1)} %get-tuple-element.81), channel_id=1, source_target_pairs={{0,18},{1,19},{2,16},{3,17},{16,2},{17,3},{18,0},{19,1},{4,22},{5,... | collective-permute-start | bytes 393224 | tf_op jit(solution)/shard_map/member_6/ppermute | solution.py:65
  93.2 6.4 %collective-permute-start.20 = (bf16[16,4096]{1,0:T(8,128)(2,1)S(1)}, bf16[16,4096]{1,0:T(8,128)(2,1)S(1)}, u32[]{:S(2)}, u32[]{:S(2)}) collective-permute-start(bf16[16,4096]{1,0:T(8,128)(2,1)S(1)} %get-tuple-element.69), channel_id=1, source_target_pairs={{0,4},{1,5},{2,6},{3,7},{16,20},{17,21},{18,22},{19,23},{4,0},{5,1... | collective-permute-start | bytes 393224 | tf_op jit(solution)/shard_map/plane_1/ppermute | solution.py:54
  93.4 8.6 %collective-permute-start.29 = (bf16[16,4096]{1,0:T(8,128)(2,1)S(1)}, bf16[16,4096]{1,0:T(8,128)(2,1)S(1)}, u32[]{:S(2)}, u32[]{:S(2)}) collective-permute-start(bf16[16,4096]{1,0:T(8,128)(2,1)S(1)} %add_chips.4), channel_id=1, source_target_pairs={{0,12},{1,13},{2,14},{3,15},{16,28},{17,29},{18,30},{19,31},{4,8},... | collective-permute-start | bytes 393224 | tf_op jit(solution)/shard_map/plane_3/ppermute | solution.py:54
  (11 other events, 65.5 us)

commit v11 on v9

--- a/solution.py
+++ b/solution.py
@@ -624,15 +624,16 @@
     mine, over, kept = run_experts(own, other, (w_gate_up, w_down), expert, top_count, slots, True)
     near_mine, near_back = mine, layout.swapped(over, 1)
     own, other, slots = to_experts(far, over)
-    other = after(other, near_back)
-    mine, over, _ = run_experts(own, other, kept, expert, top_count, slots, False)
     near_sums = add_up(
         [[near_mine], [near_back]], [count_of_rows * len(near)] * len(chips), "add_cores"
     )
+    other = after(other, near_sums[0])
+    mine, over, _ = run_experts(own, other, kept, expert, top_count, slots, False)
+    parts = to_owners(near_sums, 0)
+    over = after(over, parts[1], parts[2])
     far_sums = add_cores(mine, layout.swapped(over, 1))
-    parts = to_owners(near_sums, 0)
     totals = add_up([[part] for part in parts], [count_of_rows] * len(near), "add_chips")
-    others = [layout.shifted(total, by) for total, by in zip(totals, near)]
+    others = [layout.shifted(total, by) for total, by in list(zip(totals, near))[::-1]]
     for i, by in list(enumerate(far))[:0:-1]:
         others.append(layout.shifted(total_of(to_owners(far_sums, i)), by))
     merged = add_up(

time: 97.4 us -> 89.8 us (0.922)
  waiting for transfers between devices: 35.2 us -> 22.4 us
  starting transfers between devices: 37.6 us -> 42.9 us
    ppermute x25, waiting for transfers between devices: 25 us -> 15.6 us  [swapped(): return lax.ppermute(value, AXES, pairs)]
    ppermute x25, starting transfers between devices: 23.6 us -> 27.4 us  [swapped(): return lax.ppermute(value, AXES, pairs)]
    ppermute x6, waiting for transfers between devices: 8.12 us -> 4.77 us  [shifted(): return lax.ppermute(value, AXES, pairs)]
    ppermute x6, starting transfers between devices: 8.95 us -> 10.4 us  [shifted(): return lax.ppermute(value, AXES, pairs)]
  transfers between devices with their start and end apart: 33 -> 33, of which waited for: 16 -> 18; matrix products, arithmetic and copies ran while one was open for 0% -> 0% of each run, Pallas kernels for 14% -> 21%
where the time goes in v11:
time: 89.8 us; the launch traced here: 89.5 us
  starting transfers between devices  42.9 us (48%)
  Pallas kernels  22.6 us (25%)
  waiting for transfers between devices  22.4 us (25%)
    ppermute x25, starting transfers between devices, swapped(): return lax.ppermute(value, AXES, pairs)  27.4 us
    ppermute x25, waiting for transfers between devices, swapped(): return lax.ppermute(value, AXES, pairs)  15.6 us
    pallas_call x2, Pallas kernels, run_experts(): pl.pallas_call(kernel, out_shape=(shape, shape) + kept, in_specs=[SMEM, V...  13.4 us
    ppermute x6, starting transfers between devices, shifted(): return lax.ppermute(value, AXES, pairs)  10.4 us
    ppermute x2, starting transfers between devices, from_behind(): lax.ppermute(value, axis, [(i, (i + by) % length) for i in range(length)])  5.09 us
    ppermute x6, waiting for transfers between devices, shifted(): return lax.ppermute(value, AXES, pairs)  4.77 us
    pallas_call x1, Pallas kernels, own_attention(): pl.pallas_call(kernel, out_shape=(shape, shape, shape, jax.ShapeDtypeStru...  4.74 us
    ppermute x2, waiting for transfers between devices, from_behind(): lax.ppermute(value, axis, [(i, (i + by) % length) for i in range(length)])  2.06 us
  transfers between devices with their start and end apart: 33, of which 18 were waited for; matrix products, arithmetic and copies ran while one was open for 0% of the time, Pallas kernels for 21%

profile of v11, /device:TPU:0, one launch (start us, length us, event | category | flops | bytes accessed | tf_op | source)
XLA Modules:
  0.0 89.5 jit_solution(11103230636840463118)
XLA Ops:
  0.6 3.0 %collective-permute-start = (s32[16]{0:T(128)}, s32[16]{0:T(128)S(1)}, u32[]{:S(2)}, u32[]{:S(2)}) collective-permute-start(s32[16]{0:T(128)} %param.17), channel_id=1, source_target_pairs={{0,16},{16,0},{1,17},{17,1},{2,18},{18,2},{3,19},{19,3},{4,20},{20... | collective-permute-start | bytes 200 | tf_op jit(solution)/shard_map/ppermute | solution.py:68
  3.6 1.7 %collective-permute-done.slots_ref = s32[16]{0:T(128)S(1)} collective-permute-done((s32[16]{0:T(128)}, s32[16]{0:T(128)S(1)}, u32[]{:S(2)}, u32[]{:S(2)}) %collective-permute-start) | collective-permute-done | bytes 96 | tf_op jit(solution)/shard_map/ppermute | solution.py:68
  5.3 1.6 %pick_pages.1 = bf16[16,16,512]{2,1,0:T(8,128)(2,1)S(1)} custom-call(s32[16]{0:T(128)S(1)} %collective-permute-done.slots_ref, bf16[128,16,512]{2,1,0:T(8,128)(2,1)} %pages_hbm.1), custom_call_target="tpu_custom_call" | custom-call | bytes 1048576 | tf_op jit(solution)/shard_map/pick_pages/pallas_call | solution.py:84
  7.0 2.1 %collective-permute-start.1 = (bf16[16,16,512]{2,1,0:T(8,128)(2,1)S(1)}, bf16[16,16,512]{2,1,0:T(8,128)(2,1)S(1)}, u32[]{:S(2)}, u32[]{:S(2)}) collective-permute-start(bf16[16,16,512]{2,1,0:T(8,128)(2,1)S(1)} %pick_pages.1), channel_id=1, source_target_pairs={{0,16},{16,0},{1,17},{17,1},{2,18},{18,2},{3,19},{19,3},{4,20},{20... | collective-permute-start | bytes 786440 | tf_op jit(solution)/shard_map/ppermute | solution.py:68
  9.0 4.7 %own_attention.1 = (f32[512,128]{1,0:T(8,128)S(1)}, f32[512,128]{1,0:T(8,128)S(1)}, f32[512,128]{1,0:T(8,128)S(1)}, bf16[512,128]{1,0:T(8,128)(2,1)S(1)}) custom-call(bf16[16,4096]{1,0:T(8,128)(2,1)} %queries_hbm, bf16[16,512]{1,0:T(8,128)(2,1)} %new_hbm.1, bf16[128,16,512]{2,1,0:T(8,128)(2,1)} %pages_hbm.1, s32[16,16]{1,0:T(8,128)} %table_ref.1, s32[16]{0:T(128)} %lengths_ref.1), custom_call_target="tpu_custom_call" | custom-call | flops 1073741824 | bytes 16777216 | tf_op jit(solution)/shard_map/own_attention/pallas_call | solution.py:239
  14.2 1.9 %finish_attention.1 = (bf16[16,4096]{1,0:T(8,128)(2,1)}, bf16[16,4096]{1,0:T(8,128)(2,1)S(1)}, bf16[16,4224]{1,0:T(8,128)(2,1)S(1)}) custom-call(bf16[512,128]{1,0:T(8,128)(2,1)S(1)} %get-tuple-element.44.q_ref, bf16[16,16,512]{2,1,0:T(8,128)(2,1)S(1)} %collective-permute-done.1.fetched_ref, s32[16,16]{1,0:T(8,128)S(1)} %copy-done.2, s32[16]{0:T(128)S(1)} %copy-done.5, ...), custom_call_target="tpu_custom_call" | custom-call | flops 134217728 | bytes 4194304 | tf_op jit(solution)/shard_map/finish_attention/pallas_call | solution.py:538
  16.2 2.8 %collective-permute-start.3 = (bf16[16,4224]{1,0:T(8,128)(2,1)S(1)}, bf16[16,4224]{1,0:T(8,128)(2,1)S(1)}, u32[]{:S(2)}, u32[]{:S(2)}) collective-permute-start(bf16[16,4224]{1,0:T(8,128)(2,1)S(1)} %get-tuple-element.69.refs_0_), channel_id=1, source_target_pairs={{0,8},{1,9},{2,10},{3,11},{16,24},{17,25},{18,26},{19,27},{4,12},{... | collective-permute-start | bytes 405512 | tf_op jit(solution)/shard_map/plane_2/ppermute | solution.py:52
  19.0 2.4 %collective-permute-start.11 = (bf16[16,4224]{1,0:T(8,128)(2,1)S(1)}, bf16[16,4224]{1,0:T(8,128)(2,1)S(1)}, u32[]{:S(2)}, u32[]{:S(2)}) collective-permute-start(bf16[16,4224]{1,0:T(8,128)(2,1)S(1)} %get-tuple-element.69.refs_0_), channel_id=1, source_target_pairs={{0,18},{1,19},{2,16},{3,17},{16,2},{17,3},{18,0},{19,1},{4,22},{5,... | collective-permute-start | bytes 405512 | tf_op jit(solution)/shard_map/member_6/ppermute | solution.py:63
  22.5 1.6 %collective-permute-start.2 = (bf16[16,4224]{1,0:T(8,128)(2,1)S(1)}, bf16[16,4224]{1,0:T(8,128)(2,1)S(1)}, u32[]{:S(2)}, u32[]{:S(2)}) collective-permute-start(bf16[16,4224]{1,0:T(8,128)(2,1)S(1)} %get-tuple-element.69.refs_0_), channel_id=1, source_target_pairs={{0,4},{1,5},{2,6},{3,7},{16,20},{17,21},{18,22},{19,23},{4,0},{5,1... | collective-permute-start | bytes 405512 | tf_op jit(solution)/shard_map/plane_1/ppermute | solution.py:52
  25.0 2.4 %collective-permute-start.13 = (bf16[16,4224]{1,0:T(8,128)(2,1)S(1)}, bf16[16,4224]{1,0:T(8,128)(2,1)S(1)}, u32[]{:S(2)}, u32[]{:S(2)}) collective-permute-start(bf16[16,4224]{1,0:T(8,128)(2,1)S(1)} %collective-permute-done.3.refs_1_), channel_id=1, source_target_pairs={{0,18},{1,19},{2,16},{3,17},{16,2},{17,3},{18,0},{19,1},{4,22},{5,... | collective-permute-start | bytes 405512 | tf_op jit(solution)/shard_map/member_6/ppermute | solution.py:63
  27.8 1.4 %collective-permute-start.10 = (bf16[16,4224]{1,0:T(8,128)(2,1)S(1)}, bf16[16,4224]{1,0:T(8,128)(2,1)S(1)}, u32[]{:S(2)}, u32[]{:S(2)}) collective-permute-start(bf16[16,4224]{1,0:T(8,128)(2,1)S(1)} %collective-permute-done.3.refs_1_), channel_id=1, source_target_pairs={{0,16},{1,17},{2,18},{3,19},{16,0},{17,1},{18,2},{19,3},{4,20},{5,... | collective-permute-start | bytes 405512 | tf_op jit(solution)/shard_map/member_4/ppermute | solution.py:63
  30.2 1.9 %collective-permute-start.12 = (bf16[16,4224]{1,0:T(8,128)(2,1)S(1)}, bf16[16,4224]{1,0:T(8,128)(2,1)S(1)}, u32[]{:S(2)}, u32[]{:S(2)}) collective-permute-start(bf16[16,4224]{1,0:T(8,128)(2,1)S(1)} %collective-permute-done.2.refs_0_), channel_id=1, source_target_pairs={{0,18},{1,19},{2,16},{3,17},{16,2},{17,3},{18,0},{19,1},{4,22},{5,... | collective-permute-start | bytes 405512 | tf_op jit(solution)/shard_map/member_6/ppermute | solution.py:63
  32.7 1.3 %collective-permute-start.6 = (bf16[16,4224]{1,0:T(8,128)(2,1)S(1)}, bf16[16,4224]{1,0:T(8,128)(2,1)S(1)}, u32[]{:S(2)}, u32[]{:S(2)}) collective-permute-start(bf16[16,4224]{1,0:T(8,128)(2,1)S(1)} %collective-permute-done.2.refs_0_), channel_id=1, source_target_pairs={{0,2},{1,3},{2,0},{3,1},{16,18},{17,19},{18,16},{19,17},{4,6},{5,7... | collective-permute-start | bytes 405512 | tf_op jit(solution)/shard_map/member_2/ppermute | solution.py:63
  34.0 1.2 %collective-permute-done.10.refs_5_ = bf16[16,4224]{1,0:T(8,128)(2,1)S(1)} collective-permute-done((bf16[16,4224]{1,0:T(8,128)(2,1)S(1)}, bf16[16,4224]{1,0:T(8,128)(2,1)S(1)}, u32[]{:S(2)}, u32[]{:S(2)}) %collective-permute-start.10) | collective-permute-done | bytes 135200 | tf_op jit(solution)/shard_map/member_4/ppermute | solution.py:63
  35.2 1.7 %collective-permute-done.7.refs_3_ = bf16[16,4224]{1,0:T(8,128)(2,1)S(1)} collective-permute-done((bf16[16,4224]{1,0:T(8,128)(2,1)S(1)}, bf16[16,4224]{1,0:T(8,128)(2,1)S(1)}, u32[]{:S(2)}, u32[]{:S(2)}) %collective-permute-start.7) | collective-permute-done | bytes 135200 | tf_op jit(solution)/shard_map/member_2/ppermute | solution.py:63
  36.9 1.2 %collective-permute-done.9.refs_4_ = bf16[16,4224]{1,0:T(8,128)(2,1)S(1)} collective-permute-done((bf16[16,4224]{1,0:T(8,128)(2,1)S(1)}, bf16[16,4224]{1,0:T(8,128)(2,1)S(1)}, u32[]{:S(2)}, u32[]{:S(2)}) %collective-permute-start.9) | collective-permute-done | bytes 135200 | tf_op jit(solution)/shard_map/member_4/ppermute | solution.py:63
  38.5 1.3 %collective-permute-start.21 = (bf16[16,4224]{1,0:T(8,128)(2,1)S(1)}, bf16[16,4224]{1,0:T(8,128)(2,1)S(1)}, u32[]{:S(2)}, u32[]{:S(2)}) collective-permute-start(bf16[16,4224]{1,0:T(8,128)(2,1)S(1)} %collective-permute-done.4.refs_1_), channel_id=1, source_target_pairs={{0,2},{1,3},{2,0},{3,1},{16,18},{17,19},{18,16},{19,17},{4,6},{5,7... | collective-permute-start | bytes 405512 | tf_op jit(solution)/shard_map/member_2/ppermute | solution.py:63
  39.8 1.4 %collective-permute-start.22 = (bf16[16,4224]{1,0:T(8,128)(2,1)S(1)}, bf16[16,4224]{1,0:T(8,128)(2,1)S(1)}, u32[]{:S(2)}, u32[]{:S(2)}) collective-permute-start(bf16[16,4224]{1,0:T(8,128)(2,1)S(1)} %collective-permute-done.4.refs_1_), channel_id=1, source_target_pairs={{0,16},{1,17},{2,18},{3,19},{16,0},{17,1},{18,2},{19,3},{4,20},{5,... | collective-permute-start | bytes 405512 | tf_op jit(solution)/shard_map/member_4/ppermute | solution.py:63
  42.1 8.3 %run_experts.2 = (bf16[128,4096]{1,0:T(8,128)(2,1)S(1)}, bf16[128,4096]{1,0:T(8,128)(2,1)S(1)}, bf16[4096,1536]{1,0:T(8,128)(2,1)S(1)}, bf16[768,4096]{1,0:T(8,128)(2,1)S(1)}) custom-call(s32[1]{0:T(128)} %bitcast.3.expert_ref, bf16[128,4224]{1,0:T(8,128)(2,1)S(1)} %packed.2.own_ref, bf16[128,4224]{1,0:T(8,128)(2,1)S(1)} %collective-permute-done.14.other_ref, ...), custom_call_target="tpu_custom_call" | custom-call | flops 2415919104 | bytes 20971520 | tf_op jit(solution)/shard_map/run_experts/pallas_call | solution.py:431
  51.1 2.0 %collective-permute-done.15.refs_1_ = bf16[128,4096]{1,0:T(8,128)(2,1)S(1)} collective-permute-done((bf16[128,4096]{1,0:T(8,128)(2,1)S(1)}, bf16[128,4096]{1,0:T(8,128)(2,1)S(1)}, u32[]{:S(2)}, u32[]{:S(2)}) %collective-permute-start.15) | collective-permute-done | bytes 1048608 | tf_op jit(solution)/shard_map/member_1/ppermute | solution.py:63
  53.3 1.3 %collective-permute-start.16 = (bf16[32,4096]{1,0:T(8,128)(2,1)S(1)}, bf16[32,4096]{1,0:T(8,128)(2,1)S(1)}, u32[]{:S(2)}, u32[]{:S(2)}) collective-permute-start(bf16[32,4096]{1,0:T(8,128)(2,1)S(1)} %get-tuple-element.64), channel_id=1, source_target_pairs={{0,2},{1,3},{2,0},{3,1},{16,18},{17,19},{18,16},{19,17},{4,6},{5,7... | collective-permute-start | bytes 786440 | tf_op jit(solution)/shard_map/member_2/ppermute | solution.py:63
  54.6 1.4 %collective-permute-start.17 = (bf16[32,4096]{1,0:T(8,128)(2,1)S(1)}, bf16[32,4096]{1,0:T(8,128)(2,1)S(1)}, u32[]{:S(2)}, u32[]{:S(2)}) collective-permute-start(bf16[32,4096]{1,0:T(8,128)(2,1)S(1)} %get-tuple-element.65), channel_id=1, source_target_pairs={{0,16},{1,17},{2,18},{3,19},{16,0},{17,1},{18,2},{19,3},{4,20},{5,... | collective-permute-start | bytes 786440 | tf_op jit(solution)/shard_map/member_4/ppermute | solution.py:63
  56.0 5.1 %run_experts.3 = (bf16[128,4096]{1,0:T(8,128)(2,1)S(1)}, bf16[128,4096]{1,0:T(8,128)(2,1)S(1)}) custom-call(s32[1]{0:T(128)} %bitcast.3.expert_ref, bf16[128,4224]{1,0:T(8,128)(2,1)S(1)} %packed.3.own_ref, bf16[128,4224]{1,0:T(8,128)(2,1)S(1)} %collective-permute-done.24.other_ref, bf16[4096,1536]{1,0:T(8,128)(2,1)S(1)} %get-tuple-element.71.refs_0_, ...), custom_call_target="tpu_custom_call" | custom-call | flops 2415919104 | bytes 20971520 | tf_op jit(solution)/shard_map/run_experts/pallas_call | solution.py:431
  62.7 1.8 %collective-permute-start.18 = (bf16[32,4096]{1,0:T(8,128)(2,1)S(1)}, bf16[32,4096]{1,0:T(8,128)(2,1)S(1)}, u32[]{:S(2)}, u32[]{:S(2)}) collective-permute-start(bf16[32,4096]{1,0:T(8,128)(2,1)S(1)} %get-tuple-element.66), channel_id=1, source_target_pairs={{0,18},{1,19},{2,16},{3,17},{16,2},{17,3},{18,0},{19,1},{4,22},{5,... | collective-permute-start | bytes 786440 | tf_op jit(solution)/shard_map/member_6/ppermute | solution.py:63
  66.5 1.5 %collective-permute-start.27 = (bf16[16,4096]{1,0:T(8,128)(2,1)S(1)}, bf16[16,4096]{1,0:T(8,128)(2,1)S(1)}, u32[]{:S(2)}, u32[]{:S(2)}) collective-permute-start(bf16[16,4096]{1,0:T(8,128)(2,1)S(1)} %get-tuple-element.78), channel_id=1, source_target_pairs={{0,16},{1,17},{2,18},{3,19},{16,0},{17,1},{18,2},{19,3},{4,20},{5,... | collective-permute-start | bytes 393224 | tf_op jit(solution)/shard_map/member_4/ppermute | solution.py:63
  70.0 2.8 %collective-permute-done.18.refs_3_ = bf16[32,4096]{1,0:T(8,128)(2,1)S(1)} collective-permute-done((bf16[32,4096]{1,0:T(8,128)(2,1)S(1)}, bf16[32,4096]{1,0:T(8,128)(2,1)S(1)}, u32[]{:S(2)}, u32[]{:S(2)}) %collective-permute-start.18) | collective-permute-done | bytes 262176 | tf_op jit(solution)/shard_map/member_6/ppermute | solution.py:63
  72.9 2.1 %collective-permute-start.19 = (bf16[16,4096]{1,0:T(8,128)(2,1)S(1)}, bf16[16,4096]{1,0:T(8,128)(2,1)S(1)}, u32[]{:S(2)}, u32[]{:S(2)}) collective-permute-start(bf16[16,4096]{1,0:T(8,128)(2,1)S(1)} %get-tuple-element.67), channel_id=1, source_target_pairs={{0,8},{1,9},{2,10},{3,11},{16,24},{17,25},{18,26},{19,27},{4,12},{... | collective-permute-start | bytes 393224 | tf_op jit(solution)/shard_map/plane_2/ppermute | solution.py:52
  75.6 1.4 %collective-permute-start.31 = (bf16[16,4096]{1,0:T(8,128)(2,1)S(1)}, bf16[16,4096]{1,0:T(8,128)(2,1)S(1)}, u32[]{:S(2)}, u32[]{:S(2)}) collective-permute-start(bf16[16,4096]{1,0:T(8,128)(2,1)S(1)} %get-tuple-element.82), channel_id=1, source_target_pairs={{0,16},{1,17},{2,18},{3,19},{16,0},{17,1},{18,2},{19,3},{4,20},{5,... | collective-permute-start | bytes 393224 | tf_op jit(solution)/shard_map/member_4/ppermute | solution.py:63
  78.1 1.6 %collective-permute-start.20 = (bf16[16,4096]{1,0:T(8,128)(2,1)S(1)}, bf16[16,4096]{1,0:T(8,128)(2,1)S(1)}, u32[]{:S(2)}, u32[]{:S(2)}) collective-permute-start(bf16[16,4096]{1,0:T(8,128)(2,1)S(1)} %get-tuple-element.68), channel_id=1, source_target_pairs={{0,4},{1,5},{2,6},{3,7},{16,20},{17,21},{18,22},{19,23},{4,0},{5,1... | collective-permute-start | bytes 393224 | tf_op jit(solution)/shard_map/plane_1/ppermute | solution.py:52
  79.7 1.7 %collective-permute-done.30.refs_1_ = bf16[16,4096]{1,0:T(8,128)(2,1)S(1)} collective-permute-done((bf16[16,4096]{1,0:T(8,128)(2,1)S(1)}, bf16[16,4096]{1,0:T(8,128)(2,1)S(1)}, u32[]{:S(2)}, u32[]{:S(2)}) %collective-permute-start.30) | collective-permute-done | bytes 131104 | tf_op jit(solution)/shard_map/member_2/ppermute | solution.py:63
  81.4 1.4 %collective-permute-start.29 = (bf16[16,4096]{1,0:T(8,128)(2,1)S(1)}, bf16[16,4096]{1,0:T(8,128)(2,1)S(1)}, u32[]{:S(2)}, u32[]{:S(2)}) collective-permute-start(bf16[16,4096]{1,0:T(8,128)(2,1)S(1)} %add_chips.4), channel_id=1, source_target_pairs={{0,12},{1,13},{2,14},{3,15},{16,28},{17,29},{18,30},{19,31},{4,8},... | collective-permute-start | bytes 393224 | tf_op jit(solution)/shard_map/plane_3/ppermute | solution.py:52
  84.2 4.5 %collective-permute-done.29.refs_3_ = bf16[16,4096]{1,0:T(8,128)(2,1)S(1)} collective-permute-done((bf16[16,4096]{1,0:T(8,128)(2,1)S(1)}, bf16[16,4096]{1,0:T(8,128)(2,1)S(1)}, u32[]{:S(2)}, u32[]{:S(2)}) %collective-permute-start.29) | collective-permute-done | bytes 131104 | tf_op jit(solution)/shard_map/plane_3/ppermute | solution.py:52
  (60 shorter events, 16.1 us)
Async XLA Ops:
  0.6 4.7 %collective-permute-start = (s32[16]{0:T(128)}, s32[16]{0:T(128)S(1)}, u32[]{:S(2)}, u32[]{:S(2)}) collective-permute-start(s32[16]{0:T(128)} %param.17), channel_id=1, source_target_pairs={{0,16},{16,0},{1,17},{17,1},{2,18},{18,2},{3,19},{19,3},{4,20},{20... | collective-permute-start | bytes 200 | tf_op jit(solution)/shard_map/ppermute | solution.py:68
  7.0 7.2 %collective-permute-start.1 = (bf16[16,16,512]{2,1,0:T(8,128)(2,1)S(1)}, bf16[16,16,512]{2,1,0:T(8,128)(2,1)S(1)}, u32[]{:S(2)}, u32[]{:S(2)}) collective-permute-start(bf16[16,16,512]{2,1,0:T(8,128)(2,1)S(1)} %pick_pages.1), channel_id=1, source_target_pairs={{0,16},{16,0},{1,17},{17,1},{2,18},{18,2},{3,19},{19,3},{4,20},{20... | collective-permute-start | bytes 786440 | tf_op jit(solution)/shard_map/ppermute | solution.py:68
  16.2 7.9 %collective-permute-start.3 = (bf16[16,4224]{1,0:T(8,128)(2,1)S(1)}, bf16[16,4224]{1,0:T(8,128)(2,1)S(1)}, u32[]{:S(2)}, u32[]{:S(2)}) collective-permute-start(bf16[16,4224]{1,0:T(8,128)(2,1)S(1)} %get-tuple-element.69.refs_0_), channel_id=1, source_target_pairs={{0,8},{1,9},{2,10},{3,11},{16,24},{17,25},{18,26},{19,27},{4,12},{... | collective-permute-start | bytes 405512 | tf_op jit(solution)/shard_map/plane_2/ppermute | solution.py:52
  19.0 6.0 %collective-permute-start.11 = (bf16[16,4224]{1,0:T(8,128)(2,1)S(1)}, bf16[16,4224]{1,0:T(8,128)(2,1)S(1)}, u32[]{:S(2)}, u32[]{:S(2)}) collective-permute-start(bf16[16,4224]{1,0:T(8,128)(2,1)S(1)} %get-tuple-element.69.refs_0_), channel_id=1, source_target_pairs={{0,18},{1,19},{2,16},{3,17},{16,2},{17,3},{18,0},{19,1},{4,22},{5,... | collective-permute-start | bytes 405512 | tf_op jit(solution)/shard_map/member_6/ppermute | solution.py:63
  21.5 6.4 %collective-permute-start.8 = (bf16[16,4224]{1,0:T(8,128)(2,1)S(1)}, bf16[16,4224]{1,0:T(8,128)(2,1)S(1)}, u32[]{:S(2)}, u32[]{:S(2)}) collective-permute-start(bf16[16,4224]{1,0:T(8,128)(2,1)S(1)} %get-tuple-element.69.refs_0_), channel_id=1, source_target_pairs={{0,16},{1,17},{2,18},{3,19},{16,0},{17,1},{18,2},{19,3},{4,20},{5,... | collective-permute-start | bytes 405512 | tf_op jit(solution)/shard_map/member_4/ppermute | solution.py:63
  22.0 7.2 %collective-permute-start.5 = (bf16[16,4224]{1,0:T(8,128)(2,1)S(1)}, bf16[16,4224]{1,0:T(8,128)(2,1)S(1)}, u32[]{:S(2)}, u32[]{:S(2)}) collective-permute-start(bf16[16,4224]{1,0:T(8,128)(2,1)S(1)} %get-tuple-element.69.refs_0_), channel_id=1, source_target_pairs={{0,2},{1,3},{2,0},{3,1},{16,18},{17,19},{18,16},{19,17},{4,6},{5,7... | collective-permute-start | bytes 405512 | tf_op jit(solution)/shard_map/member_2/ppermute | solution.py:63
  22.5 7.7 %collective-permute-start.2 = (bf16[16,4224]{1,0:T(8,128)(2,1)S(1)}, bf16[16,4224]{1,0:T(8,128)(2,1)S(1)}, u32[]{:S(2)}, u32[]{:S(2)}) collective-permute-start(bf16[16,4224]{1,0:T(8,128)(2,1)S(1)} %get-tuple-element.69.refs_0_), channel_id=1, source_target_pairs={{0,4},{1,5},{2,6},{3,7},{16,20},{17,21},{18,22},{19,23},{4,0},{5,1... | collective-permute-start | bytes 405512 | tf_op jit(solution)/shard_map/plane_1/ppermute | solution.py:52
  24.1 8.0 %collective-permute-start.4 = (bf16[16,4224]{1,0:T(8,128)(2,1)S(1)}, bf16[16,4224]{1,0:T(8,128)(2,1)S(1)}, u32[]{:S(2)}, u32[]{:S(2)}) collective-permute-start(bf16[16,4224]{1,0:T(8,128)(2,1)S(1)} %collective-permute-done.3.refs_1_), channel_id=1, source_target_pairs={{0,4},{1,5},{2,6},{3,7},{16,20},{17,21},{18,22},{19,23},{4,0},{5,1... | collective-permute-start | bytes 405512 | tf_op jit(solution)/shard_map/plane_1/ppermute | solution.py:52
  25.0 7.7 %collective-permute-start.13 = (bf16[16,4224]{1,0:T(8,128)(2,1)S(1)}, bf16[16,4224]{1,0:T(8,128)(2,1)S(1)}, u32[]{:S(2)}, u32[]{:S(2)}) collective-permute-start(bf16[16,4224]{1,0:T(8,128)(2,1)S(1)} %collective-permute-done.3.refs_1_), channel_id=1, source_target_pairs={{0,18},{1,19},{2,16},{3,17},{16,2},{17,3},{18,0},{19,1},{4,22},{5,... | collective-permute-start | bytes 405512 | tf_op jit(solution)/shard_map/member_6/ppermute | solution.py:63
  27.8 7.4 %collective-permute-start.10 = (bf16[16,4224]{1,0:T(8,128)(2,1)S(1)}, bf16[16,4224]{1,0:T(8,128)(2,1)S(1)}, u32[]{:S(2)}, u32[]{:S(2)}) collective-permute-start(bf16[16,4224]{1,0:T(8,128)(2,1)S(1)} %collective-permute-done.3.refs_1_), channel_id=1, source_target_pairs={{0,16},{1,17},{2,18},{3,19},{16,0},{17,1},{18,2},{19,3},{4,20},{5,... | collective-permute-start | bytes 405512 | tf_op jit(solution)/shard_map/member_4/ppermute | solution.py:63
  29.2 7.7 %collective-permute-start.7 = (bf16[16,4224]{1,0:T(8,128)(2,1)S(1)}, bf16[16,4224]{1,0:T(8,128)(2,1)S(1)}, u32[]{:S(2)}, u32[]{:S(2)}) collective-permute-start(bf16[16,4224]{1,0:T(8,128)(2,1)S(1)} %collective-permute-done.3.refs_1_), channel_id=1, source_target_pairs={{0,2},{1,3},{2,0},{3,1},{16,18},{17,19},{18,16},{19,17},{4,6},{5,7... | collective-permute-start | bytes 405512 | tf_op jit(solution)/shard_map/member_2/ppermute | solution.py:63
  30.2 6.7 %collective-permute-start.12 = (bf16[16,4224]{1,0:T(8,128)(2,1)S(1)}, bf16[16,4224]{1,0:T(8,128)(2,1)S(1)}, u32[]{:S(2)}, u32[]{:S(2)}) collective-permute-start(bf16[16,4224]{1,0:T(8,128)(2,1)S(1)} %collective-permute-done.2.refs_0_), channel_id=1, source_target_pairs={{0,18},{1,19},{2,16},{3,17},{16,2},{17,3},{18,0},{19,1},{4,22},{5,... | collective-permute-start | bytes 405512 | tf_op jit(solution)/shard_map/member_6/ppermute | solution.py:63
  32.1 6.0 %collective-permute-start.9 = (bf16[16,4224]{1,0:T(8,128)(2,1)S(1)}, bf16[16,4224]{1,0:T(8,128)(2,1)S(1)}, u32[]{:S(2)}, u32[]{:S(2)}) collective-permute-start(bf16[16,4224]{1,0:T(8,128)(2,1)S(1)} %collective-permute-done.2.refs_0_), channel_id=1, source_target_pairs={{0,16},{1,17},{2,18},{3,19},{16,0},{17,1},{18,2},{19,3},{4,20},{5,... | collective-permute-start | bytes 405512 | tf_op jit(solution)/shard_map/member_4/ppermute | solution.py:63
  32.7 5.7 %collective-permute-start.6 = (bf16[16,4224]{1,0:T(8,128)(2,1)S(1)}, bf16[16,4224]{1,0:T(8,128)(2,1)S(1)}, u32[]{:S(2)}, u32[]{:S(2)}) collective-permute-start(bf16[16,4224]{1,0:T(8,128)(2,1)S(1)} %collective-permute-done.2.refs_0_), channel_id=1, source_target_pairs={{0,2},{1,3},{2,0},{3,1},{16,18},{17,19},{18,16},{19,17},{4,6},{5,7... | collective-permute-start | bytes 405512 | tf_op jit(solution)/shard_map/member_2/ppermute | solution.py:63
  38.4 3.6 %collective-permute-start.14 = (bf16[128,4224]{1,0:T(8,128)(2,1)S(1)}, bf16[128,4224]{1,0:T(8,128)(2,1)S(1)}, u32[]{:S(2)}, u32[]{:S(2)}) collective-permute-start(bf16[128,4224]{1,0:T(8,128)(2,1)S(1)} %packed.2.own_ref), channel_id=1, source_target_pairs={{0,1},{1,0},{2,3},{3,2},{16,17},{17,16},{18,19},{19,18},{4,5},{5,4... | collective-permute-start | bytes 3244040 | tf_op jit(solution)/shard_map/member_1/ppermute | solution.py:63
  38.5 11.9 %collective-permute-start.21 = (bf16[16,4224]{1,0:T(8,128)(2,1)S(1)}, bf16[16,4224]{1,0:T(8,128)(2,1)S(1)}, u32[]{:S(2)}, u32[]{:S(2)}) collective-permute-start(bf16[16,4224]{1,0:T(8,128)(2,1)S(1)} %collective-permute-done.4.refs_1_), channel_id=1, source_target_pairs={{0,2},{1,3},{2,0},{3,1},{16,18},{17,19},{18,16},{19,17},{4,6},{5,7... | collective-permute-start | bytes 405512 | tf_op jit(solution)/shard_map/member_2/ppermute | solution.py:63
  39.8 10.7 %collective-permute-start.22 = (bf16[16,4224]{1,0:T(8,128)(2,1)S(1)}, bf16[16,4224]{1,0:T(8,128)(2,1)S(1)}, u32[]{:S(2)}, u32[]{:S(2)}) collective-permute-start(bf16[16,4224]{1,0:T(8,128)(2,1)S(1)} %collective-permute-done.4.refs_1_), channel_id=1, source_target_pairs={{0,16},{1,17},{2,18},{3,19},{16,0},{17,1},{18,2},{19,3},{4,20},{5,... | collective-permute-start | bytes 405512 | tf_op jit(solution)/shard_map/member_4/ppermute | solution.py:63
  41.2 9.3 %collective-permute-start.23 = (bf16[16,4224]{1,0:T(8,128)(2,1)S(1)}, bf16[16,4224]{1,0:T(8,128)(2,1)S(1)}, u32[]{:S(2)}, u32[]{:S(2)}) collective-permute-start(bf16[16,4224]{1,0:T(8,128)(2,1)S(1)} %collective-permute-done.4.refs_1_), channel_id=1, source_target_pairs={{0,18},{1,19},{2,16},{3,17},{16,2},{17,3},{18,0},{19,1},{4,22},{5,... | collective-permute-start | bytes 405512 | tf_op jit(solution)/shard_map/member_6/ppermute | solution.py:63
  50.4 2.7 %collective-permute-start.15 = (bf16[128,4096]{1,0:T(8,128)(2,1)S(1)}, bf16[128,4096]{1,0:T(8,128)(2,1)S(1)}, u32[]{:S(2)}, u32[]{:S(2)}) collective-permute-start(bf16[128,4096]{1,0:T(8,128)(2,1)S(1)} %get-tuple-element.62), channel_id=1, source_target_pairs={{0,1},{1,0},{2,3},{3,2},{16,17},{17,16},{18,19},{19,18},{4,5},{5,4... | collective-permute-start | bytes 3145736 | tf_op jit(solution)/shard_map/member_1/ppermute | solution.py:63
  50.6 5.5 %collective-permute-start.24 = (bf16[128,4224]{1,0:T(8,128)(2,1)S(1)}, bf16[128,4224]{1,0:T(8,128)(2,1)S(1)}, u32[]{:S(2)}, u32[]{:S(2)}) collective-permute-start(bf16[128,4224]{1,0:T(8,128)(2,1)S(1)} %packed.3.own_ref), channel_id=1, source_target_pairs={{0,1},{1,0},{2,3},{3,2},{16,17},{17,16},{18,19},{19,18},{4,5},{5,4... | collective-permute-start | bytes 3244040 | tf_op jit(solution)/shard_map/member_1/ppermute | solution.py:63
  53.3 8.4 %collective-permute-start.16 = (bf16[32,4096]{1,0:T(8,128)(2,1)S(1)}, bf16[32,4096]{1,0:T(8,128)(2,1)S(1)}, u32[]{:S(2)}, u32[]{:S(2)}) collective-permute-start(bf16[32,4096]{1,0:T(8,128)(2,1)S(1)} %get-tuple-element.64), channel_id=1, source_target_pairs={{0,2},{1,3},{2,0},{3,1},{16,18},{17,19},{18,16},{19,17},{4,6},{5,7... | collective-permute-start | bytes 786440 | tf_op jit(solution)/shard_map/member_2/ppermute | solution.py:63
  54.6 8.1 %collective-permute-start.17 = (bf16[32,4096]{1,0:T(8,128)(2,1)S(1)}, bf16[32,4096]{1,0:T(8,128)(2,1)S(1)}, u32[]{:S(2)}, u32[]{:S(2)}) collective-permute-start(bf16[32,4096]{1,0:T(8,128)(2,1)S(1)} %get-tuple-element.65), channel_id=1, source_target_pairs={{0,16},{1,17},{2,18},{3,19},{16,0},{17,1},{18,2},{19,3},{4,20},{5,... | collective-permute-start | bytes 786440 | tf_op jit(solution)/shard_map/member_4/ppermute | solution.py:63
  62.7 10.0 %collective-permute-start.18 = (bf16[32,4096]{1,0:T(8,128)(2,1)S(1)}, bf16[32,4096]{1,0:T(8,128)(2,1)S(1)}, u32[]{:S(2)}, u32[]{:S(2)}) collective-permute-start(bf16[32,4096]{1,0:T(8,128)(2,1)S(1)} %get-tuple-element.66), channel_id=1, source_target_pairs={{0,18},{1,19},{2,16},{3,17},{16,2},{17,3},{18,0},{19,1},{4,22},{5,... | collective-permute-start | bytes 786440 | tf_op jit(solution)/shard_map/member_6/ppermute | solution.py:63
  65.6 10.0 %collective-permute-start.26 = (bf16[16,4096]{1,0:T(8,128)(2,1)S(1)}, bf16[16,4096]{1,0:T(8,128)(2,1)S(1)}, u32[]{:S(2)}, u32[]{:S(2)}) collective-permute-start(bf16[16,4096]{1,0:T(8,128)(2,1)S(1)} %get-tuple-element.77), channel_id=1, source_target_pairs={{0,2},{1,3},{2,0},{3,1},{16,18},{17,19},{18,16},{19,17},{4,6},{5,7... | collective-permute-start | bytes 393224 | tf_op jit(solution)/shard_map/member_2/ppermute | solution.py:63
  66.5 10.5 %collective-permute-start.27 = (bf16[16,4096]{1,0:T(8,128)(2,1)S(1)}, bf16[16,4096]{1,0:T(8,128)(2,1)S(1)}, u32[]{:S(2)}, u32[]{:S(2)}) collective-permute-start(bf16[16,4096]{1,0:T(8,128)(2,1)S(1)} %get-tuple-element.78), channel_id=1, source_target_pairs={{0,16},{1,17},{2,18},{3,19},{16,0},{17,1},{18,2},{19,3},{4,20},{5,... | collective-permute-start | bytes 393224 | tf_op jit(solution)/shard_map/member_4/ppermute | solution.py:63
  68.0 10.1 %collective-permute-start.28 = (bf16[16,4096]{1,0:T(8,128)(2,1)S(1)}, bf16[16,4096]{1,0:T(8,128)(2,1)S(1)}, u32[]{:S(2)}, u32[]{:S(2)}) collective-permute-start(bf16[16,4096]{1,0:T(8,128)(2,1)S(1)} %get-tuple-element.79), channel_id=1, source_target_pairs={{0,18},{1,19},{2,16},{3,17},{16,2},{17,3},{18,0},{19,1},{4,22},{5,... | collective-permute-start | bytes 393224 | tf_op jit(solution)/shard_map/member_6/ppermute | solution.py:63
  69.1 12.3 %collective-permute-start.30 = (bf16[16,4096]{1,0:T(8,128)(2,1)S(1)}, bf16[16,4096]{1,0:T(8,128)(2,1)S(1)}, u32[]{:S(2)}, u32[]{:S(2)}) collective-permute-start(bf16[16,4096]{1,0:T(8,128)(2,1)S(1)} %get-tuple-element.81), channel_id=1, source_target_pairs={{0,2},{1,3},{2,0},{3,1},{16,18},{17,19},{18,16},{19,17},{4,6},{5,7... | collective-permute-start | bytes 393224 | tf_op jit(solution)/shard_map/member_2/ppermute | solution.py:63
  72.9 11.1 %collective-permute-start.19 = (bf16[16,4096]{1,0:T(8,128)(2,1)S(1)}, bf16[16,4096]{1,0:T(8,128)(2,1)S(1)}, u32[]{:S(2)}, u32[]{:S(2)}) collective-permute-start(bf16[16,4096]{1,0:T(8,128)(2,1)S(1)} %get-tuple-element.67), channel_id=1, source_target_pairs={{0,8},{1,9},{2,10},{3,11},{16,24},{17,25},{18,26},{19,27},{4,12},{... | collective-permute-start | bytes 393224 | tf_op jit(solution)/shard_map/plane_2/ppermute | solution.py:52
  75.6 7.2 %collective-permute-start.31 = (bf16[16,4096]{1,0:T(8,128)(2,1)S(1)}, bf16[16,4096]{1,0:T(8,128)(2,1)S(1)}, u32[]{:S(2)}, u32[]{:S(2)}) collective-permute-start(bf16[16,4096]{1,0:T(8,128)(2,1)S(1)} %get-tuple-element.82), channel_id=1, source_target_pairs={{0,16},{1,17},{2,18},{3,19},{16,0},{17,1},{18,2},{19,3},{4,20},{5,... | collective-permute-start | bytes 393224 | tf_op jit(solution)/shard_map/member_4/ppermute | solution.py:63
  77.0 6.9 %collective-permute-start.32 = (bf16[16,4096]{1,0:T(8,128)(2,1)S(1)}, bf16[16,4096]{1,0:T(8,128)(2,1)S(1)}, u32[]{:S(2)}, u32[]{:S(2)}) collective-permute-start(bf16[16,4096]{1,0:T(8,128)(2,1)S(1)} %get-tuple-element.83), channel_id=1, source_target_pairs={{0,18},{1,19},{2,16},{3,17},{16,2},{17,3},{18,0},{19,1},{4,22},{5,... | collective-permute-start | bytes 393224 | tf_op jit(solution)/shard_map/member_6/ppermute | solution.py:63
  78.1 6.1 %collective-permute-start.20 = (bf16[16,4096]{1,0:T(8,128)(2,1)S(1)}, bf16[16,4096]{1,0:T(8,128)(2,1)S(1)}, u32[]{:S(2)}, u32[]{:S(2)}) collective-permute-start(bf16[16,4096]{1,0:T(8,128)(2,1)S(1)} %get-tuple-element.68), channel_id=1, source_target_pairs={{0,4},{1,5},{2,6},{3,7},{16,20},{17,21},{18,22},{19,23},{4,0},{5,1... | collective-permute-start | bytes 393224 | tf_op jit(solution)/shard_map/plane_1/ppermute | solution.py:52
  81.4 7.3 %collective-permute-start.29 = (bf16[16,4096]{1,0:T(8,128)(2,1)S(1)}, bf16[16,4096]{1,0:T(8,128)(2,1)S(1)}, u32[]{:S(2)}, u32[]{:S(2)}) collective-permute-start(bf16[16,4096]{1,0:T(8,128)(2,1)S(1)} %add_chips.4), channel_id=1, source_target_pairs={{0,12},{1,13},{2,14},{3,15},{16,28},{17,29},{18,30},{19,31},{4,8},... | collective-permute-start | bytes 393224 | tf_op jit(solution)/shard_map/plane_3/ppermute | solution.py:52
  (7 other events, 46.5 us)

commit v12 on v11

--- a/solution.py
+++ b/solution.py
@@ -68,29 +68,55 @@
     return lax.ppermute(value, axis, [(i, (i + by) % length) for i in range(length)])
 
 
+def in_fast_memory(value, parts, name):
+    rows = value.shape[0] // parts
+
+    def kernel(in_ref, out_ref, sign_ref, sems):
+        copies = [
+            pltpu.make_async_copy(
+                in_ref.at[pl.ds(c * rows, rows)], out_ref.at[pl.ds(c * rows, rows)], sems.at[c]
+            )
+            for c in range(parts)
+        ]
+        for copy in copies:
+            copy.start()
+        sign_ref[...] = jnp.zeros_like(sign_ref)
+        for copy in copies:
+            copy.wait()
+
+    size = math.prod(value.shape) * 2
+    return pl.pallas_call(
+        kernel,
+        out_shape=(
+            pltpu.VMEM(value.shape, value.dtype),
+            jax.ShapeDtypeStruct((8, 128), jnp.float32),
+        ),
+        in_specs=[HBM],
+        out_specs=(VMEM, VMEM),
+        scratch_shapes=[pltpu.SemaphoreType.DMA((parts,))],
+        compiler_params=pltpu.CompilerParams(vmem_limit_bytes=2 * MEBI),
+        cost_estimate=pl.CostEstimate(flops=0, bytes_accessed=2 * size, transcendentals=0),
+        name=name,
+    )(in_hbm(value))
+
+
 def pick_pages(slots, pages):
     count = slots.shape[0]
     last = pages.shape[0] - 1
 
-    def kernel(slots_ref, pages_ref, out_ref, sems):
-        copies = []
+    def kernel(slots_ref, pages_ref, out_ref):
         for i in range(count):
-            page = jnp.clip(slots_ref[i], 0, last)
-            copies.append(pltpu.make_async_copy(pages_ref.at[page], out_ref.at[i], sems.at[i]))
-            copies[-1].start()
-        for copy in copies:
-            copy.wait()
+            out_ref[i] = pages_ref[jnp.clip(slots_ref[i], 0, last)]
 
     return pl.pallas_call(
         kernel,
         out_shape=jax.ShapeDtypeStruct((count,) + pages.shape[1:], pages.dtype),
-        in_specs=[SMEM, HBM],
+        in_specs=[SMEM, VMEM],
         out_specs=VMEM,
-        scratch_shapes=[pltpu.SemaphoreType.DMA((count,))],
-        compiler_params=pltpu.CompilerParams(vmem_limit_bytes=4 * MEBI),
+        compiler_params=pltpu.CompilerParams(vmem_limit_bytes=8 * MEBI),
         cost_estimate=pl.CostEstimate(flops=0, bytes_accessed=MEBI, transcendentals=0),
         name="pick_pages",
-    )(slots, in_hbm(pages))
+    )(slots, pages)
 
 
 def head_blocks(query):
@@ -162,7 +188,7 @@
     def kernel(
         queries_hbm,
         new_hbm,
-        pages_hbm,
+        pages_ref,
         table_hbm,
         lengths_hbm,
         out_ref,
@@ -173,19 +199,10 @@
         fresh_ref,
         heads_ref,
         flat_ref,
-        pages_ref,
         table_ref,
         lengths_ref,
         sems,
     ):
-        page_copies = [
-            pltpu.make_async_copy(
-                pages_hbm.at[pl.ds(c * chunk_pages, chunk_pages)],
-                pages_ref.at[pl.ds(c * chunk_pages, chunk_pages)],
-                sems.at[4 + c],
-            )
-            for c in range(chunks)
-        ]
         copies = [
             pltpu.make_async_copy(queries_hbm, flat_ref, sems.at[0]),
             pltpu.make_async_copy(table_hbm, table_ref, sems.at[1]),
@@ -193,7 +210,7 @@
             pltpu.make_async_copy(new_hbm, fresh_ref.at[pl.ds(0, requests)], sems.at[3]),
         ]
         fresh_ref[requests:] = jnp.zeros_like(fresh_ref[requests:])
-        for copy in copies + page_copies:
+        for copy in copies:
             copy.start()
         for copy in copies:
             copy.wait()
@@ -212,7 +229,6 @@
         s_ref[:, chunks * chunk :] = fresh
         top = fresh
         for c in range(chunks):
-            page_copies[c].wait()
             keys = pages_ref[c * chunk_pages : (c + 1) * chunk_pages, :, :half].reshape(chunk, half)
             bias = token_bias(held, c * chunk_pages, chunk, page_len)
             scores = masked_scores(blocks, keys, bias, scaling)
@@ -239,17 +255,16 @@
     return pl.pallas_call(
         kernel,
         out_shape=(shape, shape, shape, jax.ShapeDtypeStruct((rows, 128), jnp.bfloat16)),
-        in_specs=[HBM] * 5,
+        in_specs=[HBM, HBM, VMEM, HBM, HBM],
         out_specs=(VMEM,) * 4,
         scratch_shapes=[
             pltpu.VMEM((rows, chunks * chunk + 128), jnp.float32),
             pltpu.VMEM((128, kv_width), jnp.bfloat16),
             pltpu.VMEM((rows, 128), jnp.float32),
             pltpu.VMEM(queries.shape, jnp.bfloat16),
-            pltpu.VMEM(pages.shape, jnp.bfloat16),
             pltpu.VMEM(table.shape, jnp.int32),
             pltpu.SMEM(lengths.shape, jnp.int32),
-            pltpu.SemaphoreType.DMA((4 + chunks,)),
+            pltpu.SemaphoreType.DMA((4,)),
         ],
         compiler_params=pltpu.CompilerParams(vmem_limit_bytes=24 * MEBI),
         cost_estimate=pl.CostEstimate(
@@ -258,7 +273,7 @@
             transcendentals=rows * chunks * chunk,
         ),
         name="own_attention",
-    )(*[in_hbm(value) for value in (queries, new_kv, pages, table, lengths)])
+    )(in_hbm(queries), in_hbm(new_kv), pages, in_hbm(table), in_hbm(lengths))
 
 
 def routing_columns(ids, gates):
@@ -284,27 +299,25 @@
     return jnp.concatenate(parts, axis=0)
 
 
-def packed(parts, work=0):
-    if len(parts) == 1 and not work:
-        return parts[0]
+def packed(parts, *signs):
     rows = sum(part.shape[0] for part in parts)
     columns = parts[0].shape[1]
 
     def kernel(*refs):
         out_ref, offset = refs[-1], 0
-        for ref in refs[:-1]:
+        for ref in refs[: len(parts)]:
             out_ref[offset : offset + ref.shape[0]] = ref[...]
             offset += ref.shape[0]
 
     return pl.pallas_call(
         kernel,
         out_shape=jax.ShapeDtypeStruct((rows, columns), parts[0].dtype),
-        in_specs=[VMEM] * len(parts),
+        in_specs=[VMEM] * (len(parts) + len(signs)),
         out_specs=VMEM,
         compiler_params=pltpu.CompilerParams(vmem_limit_bytes=12 * MEBI),
-        cost_estimate=pl.CostEstimate(flops=work, bytes_accessed=0, transcendentals=0),
+        cost_estimate=pl.CostEstimate(flops=0, bytes_accessed=0, transcendentals=0),
         name="packed",
-    )(*parts)
+    )(*parts, *signs)
 
 
 def after(value, *others):
@@ -325,18 +338,13 @@
     def kernel(expert_ref, own_ref, other_ref, *refs):
         copies = {}
         if keep:
-            up_hbm, down_hbm, out_ref, over_ref, up_ref, down_ref, tokens_ref, hidden_ref, sems = refs
+            up_hbm, down_ref, out_ref, over_ref, up_ref, tokens_ref, hidden_ref, sems = refs
             for c in range(up_steps):
                 for half in range(2):
                     columns = pl.ds(half * hidden_dim + c * width, width)
                     copies["up", c, half] = pltpu.make_async_copy(
                         up_hbm.at[0, :, columns], up_ref.at[:, columns], sems.at[2 * c + half]
                     )
-            for c in range(out_steps):
-                columns = pl.ds(c * out_width, out_width)
-                copies["down", c] = pltpu.make_async_copy(
-                    down_hbm.at[0, :, columns], down_ref.at[:, columns], sems.at[2 * up_steps + c]
-                )
             for copy in copies.values():
                 copy.start()
         else:
@@ -407,7 +415,6 @@
             )
 
         for c in range(out_steps):
-            arrive("down", c)
             columns = slice(c * out_width, (c + 1) * out_width)
             result = jnp.dot(
                 hidden_ref[...], down_ref[:, columns], preferred_element_type=jnp.float32
@@ -420,18 +427,13 @@
     shape = jax.ShapeDtypeStruct((rows // 2, model_dim), jnp.bfloat16)
     kept, scratch = (), []
     if keep:
-        kept = (
-            pltpu.VMEM((model_dim, double), jnp.bfloat16),
-            pltpu.VMEM((hidden_dim, model_dim), jnp.bfloat16),
-        )
-        scratch = [pltpu.SemaphoreType.DMA((2 * up_steps + out_steps,))]
-        weights = [in_hbm(gate_up), in_hbm(down_proj)]
-    else:
-        weights = [pltpu.with_memory_space_constraint(value, pltpu.VMEM) for value in weights]
+        kept = (pltpu.VMEM((model_dim, double), jnp.bfloat16),)
+        scratch = [pltpu.SemaphoreType.DMA((2 * up_steps,))]
+        gate_up = in_hbm(gate_up)
     results = pl.pallas_call(
         kernel,
         out_shape=(shape, shape) + kept,
-        in_specs=[SMEM, VMEM, VMEM] + [HBM if keep else VMEM] * 2,
+        in_specs=[SMEM, VMEM, VMEM, HBM if keep else VMEM, VMEM],
         out_specs=(VMEM,) * (2 + len(kept)),
         scratch_shapes=[
             pltpu.VMEM((slots, model_dim), jnp.bfloat16),
@@ -445,7 +447,7 @@
             transcendentals=slots * hidden_dim,
         ),
         name="run_experts",
-    )(expert, own, other, *weights)
+    )(expert, own, other, gate_up, down_proj)
     return results[0], results[1], results[2:]
 
 
@@ -570,12 +572,13 @@
     planes = layout.planes
 
     requested = from_behind(shed_slots, "pool", 1)
-    picked = pick_pages(requested, kv_pages)
+    fast_pages, _ = in_fast_memory(kv_pages, 4, "pages_in")
+    picked = pick_pages(requested, fast_pages)
     fetched = from_behind(picked, "pool", 1)
     queries, expert_ids, picked = lax.optimization_barrier((queries, expert_ids, picked))
 
     expert = (lax.axis_index("pool") * layout.dev + lax.axis_index("dev")).reshape(1)
-    *partial, query = own_attention(queries, new_kv, kv_pages, page_table, lengths)
+    *partial, query = own_attention(queries, new_kv, fast_pages, page_table, lengths)
     attended, merged, normed = finish_attention(
         query,
         fetched,
@@ -602,11 +605,10 @@
             ready = [after(block, part) for part in arrived[0]]
         arrived.append([layout.swapped(rows, chip) for rows, chip in zip(ready, chips)])
 
-    def to_experts(some, tie):
+    def to_experts(some, tie, *signs):
         pieces = [arrived[s][c] for c in range(len(chips)) for s in some]
-        if tie is not None:
-            pieces[0] = after(pieces[0], tie)
-        own = packed(pieces)
+        pieces[0] = after(pieces[0], tie)
+        own = packed(pieces, *signs)
         return own, layout.swapped(own, 1), layout.members * len(some) * capacity
 
     def add_cores(mine, over):
@@ -620,26 +622,30 @@
     def total_of(parts):
         return add_up([[part] for part in parts], [count_of_rows], "add_chips")[0]
 
-    own, other, slots = to_experts(near, blocks[far[-1]])
-    mine, over, kept = run_experts(own, other, (w_gate_up, w_down), expert, top_count, slots, True)
+    down, sign = in_fast_memory(after(w_down[0], blocks[far[-1]]), 4, "weights_in")
+    own, other, slots = to_experts(near, blocks[far[-1]], sign)
+    mine, over, (up,) = run_experts(own, other, (w_gate_up, down), expert, top_count, slots, True)
     near_mine, near_back = mine, layout.swapped(over, 1)
     own, other, slots = to_experts(far, over)
     near_sums = add_up(
         [[near_mine], [near_back]], [count_of_rows * len(near)] * len(chips), "add_cores"
     )
     other = after(other, near_sums[0])
-    mine, over, _ = run_experts(own, other, kept, expert, top_count, slots, False)
+    mine, over, _ = run_experts(own, other, (up, down), expert, top_count, slots, False)
     parts = to_owners(near_sums, 0)
     over = after(over, parts[1], parts[2])
     far_sums = add_cores(mine, layout.swapped(over, 1))
     totals = add_up([[part] for part in parts], [count_of_rows] * len(near), "add_chips")
-    others = [layout.shifted(total, by) for total, by in list(zip(totals, near))[::-1]]
+    last = to_owners(far_sums, 0)
+    others = []
+    for total, by in list(zip(totals, near))[::-1]:
+        others.append(layout.shifted(after(total, last[1]) if by == 1 else total, by))
     for i, by in list(enumerate(far))[:0:-1]:
         others.append(layout.shifted(total_of(to_owners(far_sums, i)), by))
     merged = add_up(
         [[merged]] + [[part] for part in others], [count_of_rows], "add_first", 10**10
     )[0]
-    others = [total_of(to_owners(far_sums, 0))]
+    others = [total_of(last)]
     total = merged.astype(jnp.float32) + sum(part.astype(jnp.float32) for part in others)
     layer_out = total.astype(jnp.bfloat16)
     return (attended, layer_out)

time: 89.8 us -> 92.7 us (1.032)
  local copies, waits for them, and re-layouts: 0.04 us -> 5.5 us
  waiting for transfers between devices: 22.4 us -> 17 us
  Pallas kernels: 22.6 us -> 26.2 us
    unnamed x12 -> x18, local copies, waits for them, and re-layouts: 0.04 us -> 5.5 us
    pallas_call x0 -> x2, Pallas kernels: none -> 5.01 us  [in_fast_memory(): pl.pallas_call(kernel, out_shape=(pltpu.VMEM(value.shape, value.dtype), j...]
    ppermute x25, waiting for transfers between devices: 15.6 us -> 11.1 us  [swapped(): return lax.ppermute(value, AXES, pairs)]
    ppermute x25, starting transfers between devices: 27.4 us -> 26.3 us  [swapped(): return lax.ppermute(value, AXES, pairs)]
    ppermute x6, starting transfers between devices: 10.4 us -> 11.4 us  [shifted(): return lax.ppermute(value, AXES, pairs)]
    pallas_call x1, Pallas kernels: 1.59 us -> 0.58 us  [pick_pages(): pl.pallas_call(kernel, out_shape=jax.ShapeDtypeStruct((count,) + pages.sh...]
    ppermute x6, waiting for transfers between devices: 4.77 us -> 3.81 us  [shifted(): return lax.ppermute(value, AXES, pairs)]
  transfers between devices with their start and end apart: 33 -> 33, of which waited for: 18 -> 14; matrix products, arithmetic and copies ran while one was open for 0% -> 0% of each run, Pallas kernels for 21% -> 25%
where the time goes in v12:
time: 92.7 us; the launch traced here: 92.5 us
  starting transfers between devices  42.3 us (46%)
  Pallas kernels  26.2 us (28%)
  waiting for transfers between devices  17 us (18%)
  local copies, waits for them, and re-layouts  5.5 us (6%)
    ppermute x25, starting transfers between devices, swapped(): return lax.ppermute(value, AXES, pairs)  26.3 us
    pallas_call x2, Pallas kernels, run_experts(): pl.pallas_call(kernel, out_shape=(shape, shape) + kept, in_specs=[SMEM, V...  13.5 us
    ppermute x6, starting transfers between devices, shifted(): return lax.ppermute(value, AXES, pairs)  11.4 us
    ppermute x25, waiting for transfers between devices, swapped(): return lax.ppermute(value, AXES, pairs)  11.1 us
    unnamed x18, local copies, waits for them, and re-layouts  5.5 us
    pallas_call x2, Pallas kernels, in_fast_memory(): pl.pallas_call(kernel, out_shape=(pltpu.VMEM(value.shape, value.dtype), j...  5.01 us
    ppermute x2, starting transfers between devices, from_behind(): lax.ppermute(value, axis, [(i, (i + by) % length) for i in range(length)])  4.58 us
    pallas_call x1, Pallas kernels, own_attention(): pl.pallas_call(kernel, out_shape=(shape, shape, shape, jax.ShapeDtypeStru...  4.18 us
  transfers between devices with their start and end apart: 33, of which 14 were waited for; matrix products, arithmetic and copies ran while one was open for 0% of the time, Pallas kernels for 25%

profile of v12, /device:TPU:0, one launch (start us, length us, event | category | flops | bytes accessed | tf_op | source)
XLA Modules:
  0.0 92.5 jit_solution(11568077098008430348)
XLA Ops:
  0.6 3.0 %collective-permute-start = (s32[16]{0:T(128)}, s32[16]{0:T(128)S(1)}, u32[]{:S(2)}, u32[]{:S(2)}) collective-permute-start(s32[16]{0:T(128)} %param.17), channel_id=1, source_target_pairs={{0,16},{16,0},{1,17},{17,1},{2,18},{18,2},{3,19},{19,3},{4,20},{20... | collective-permute-start | bytes 200 | tf_op jit(solution)/shard_map/ppermute | solution.py:68
  3.6 2.1 %pages_in.1 = (bf16[128,16,512]{2,1,0:T(8,128)(2,1)S(1)}, f32[8,128]{1,0:T(8,128)}) custom-call(bf16[128,16,512]{2,1,0:T(8,128)(2,1)} %in_ref.1), custom_call_target="tpu_custom_call" | custom-call | bytes 4194304 | tf_op jit(solution)/shard_map/pages_in/pallas_call | solution.py:88
  6.4 1.6 %collective-permute-start.1 = (bf16[16,16,512]{2,1,0:T(8,128)(2,1)S(1)}, bf16[16,16,512]{2,1,0:T(8,128)(2,1)S(1)}, u32[]{:S(2)}, u32[]{:S(2)}) collective-permute-start(bf16[16,16,512]{2,1,0:T(8,128)(2,1)S(1)} %pick_pages.1), channel_id=1, source_target_pairs={{0,16},{16,0},{1,17},{17,1},{2,18},{18,2},{3,19},{19,3},{4,20},{20... | collective-permute-start | bytes 786440 | tf_op jit(solution)/shard_map/ppermute | solution.py:68
  8.0 4.2 %own_attention.1 = (f32[512,128]{1,0:T(8,128)S(1)}, f32[512,128]{1,0:T(8,128)S(1)}, f32[512,128]{1,0:T(8,128)S(1)}, bf16[512,128]{1,0:T(8,128)(2,1)S(1)}) custom-call(bf16[16,4096]{1,0:T(8,128)(2,1)} %queries_hbm, bf16[16,512]{1,0:T(8,128)(2,1)} %new_hbm.1, bf16[128,16,512]{2,1,0:T(8,128)(2,1)S(1)} %get-tuple-element.47.pages_ref, s32[16,16]{1,0:T(8,128)} %table_ref.1, ...), custom_call_target="tpu_custom_call" | custom-call | flops 1073741824 | bytes 16777216 | tf_op jit(solution)/shard_map/own_attention/pallas_call | solution.py:255
  12.2 2.1 %collective-permute-done.1.fetched_ref = bf16[16,16,512]{2,1,0:T(8,128)(2,1)S(1)} collective-permute-done((bf16[16,16,512]{2,1,0:T(8,128)(2,1)S(1)}, bf16[16,16,512]{2,1,0:T(8,128)(2,1)S(1)}, u32[]{:S(2)}, u32[]{:S(2)}) %collective-permute-start.1) | collective-permute-done | bytes 262176 | tf_op jit(solution)/shard_map/ppermute | solution.py:68
  14.3 1.9 %finish_attention.1 = (bf16[16,4096]{1,0:T(8,128)(2,1)}, bf16[16,4096]{1,0:T(8,128)(2,1)S(1)}, bf16[16,4224]{1,0:T(8,128)(2,1)S(1)}) custom-call(bf16[512,128]{1,0:T(8,128)(2,1)S(1)} %get-tuple-element.49.q_ref, bf16[16,16,512]{2,1,0:T(8,128)(2,1)S(1)} %collective-permute-done.1.fetched_ref, s32[16,16]{1,0:T(8,128)S(1)} %copy-done.5, s32[16]{0:T(128)S(1)} %copy-done.8, ...), custom_call_target="tpu_custom_call" | custom-call | flops 134217728 | bytes 4194304 | tf_op jit(solution)/shard_map/finish_attention/pallas_call | solution.py:540
  16.3 2.6 %collective-permute-start.3 = (bf16[16,4224]{1,0:T(8,128)(2,1)S(1)}, bf16[16,4224]{1,0:T(8,128)(2,1)S(1)}, u32[]{:S(2)}, u32[]{:S(2)}) collective-permute-start(bf16[16,4224]{1,0:T(8,128)(2,1)S(1)} %get-tuple-element.77.refs_0_), channel_id=1, source_target_pairs={{0,8},{1,9},{2,10},{3,11},{16,24},{17,25},{18,26},{19,27},{4,12},{... | collective-permute-start | bytes 405512 | tf_op jit(solution)/shard_map/plane_2/ppermute | solution.py:52
  18.8 1.6 %collective-permute-start.11 = (bf16[16,4224]{1,0:T(8,128)(2,1)S(1)}, bf16[16,4224]{1,0:T(8,128)(2,1)S(1)}, u32[]{:S(2)}, u32[]{:S(2)}) collective-permute-start(bf16[16,4224]{1,0:T(8,128)(2,1)S(1)} %get-tuple-element.77.refs_0_), channel_id=1, source_target_pairs={{0,18},{1,19},{2,16},{3,17},{16,2},{17,3},{18,0},{19,1},{4,22},{5,... | collective-permute-start | bytes 405512 | tf_op jit(solution)/shard_map/member_6/ppermute | solution.py:63
  20.4 1.4 %collective-permute-start.8 = (bf16[16,4224]{1,0:T(8,128)(2,1)S(1)}, bf16[16,4224]{1,0:T(8,128)(2,1)S(1)}, u32[]{:S(2)}, u32[]{:S(2)}) collective-permute-start(bf16[16,4224]{1,0:T(8,128)(2,1)S(1)} %get-tuple-element.77.refs_0_), channel_id=1, source_target_pairs={{0,16},{1,17},{2,18},{3,19},{16,0},{17,1},{18,2},{19,3},{4,20},{5,... | collective-permute-start | bytes 405512 | tf_op jit(solution)/shard_map/member_4/ppermute | solution.py:63
  22.3 1.6 %collective-permute-start.2 = (bf16[16,4224]{1,0:T(8,128)(2,1)S(1)}, bf16[16,4224]{1,0:T(8,128)(2,1)S(1)}, u32[]{:S(2)}, u32[]{:S(2)}) collective-permute-start(bf16[16,4224]{1,0:T(8,128)(2,1)S(1)} %get-tuple-element.77.refs_0_), channel_id=1, source_target_pairs={{0,4},{1,5},{2,6},{3,7},{16,20},{17,21},{18,22},{19,23},{4,0},{5,1... | collective-permute-start | bytes 405512 | tf_op jit(solution)/shard_map/plane_1/ppermute | solution.py:52
  25.1 1.6 %collective-permute-start.13 = (bf16[16,4224]{1,0:T(8,128)(2,1)S(1)}, bf16[16,4224]{1,0:T(8,128)(2,1)S(1)}, u32[]{:S(2)}, u32[]{:S(2)}) collective-permute-start(bf16[16,4224]{1,0:T(8,128)(2,1)S(1)} %collective-permute-done.3.refs_1_), channel_id=1, source_target_pairs={{0,18},{1,19},{2,16},{3,17},{16,2},{17,3},{18,0},{19,1},{4,22},{5,... | collective-permute-start | bytes 405512 | tf_op jit(solution)/shard_map/member_6/ppermute | solution.py:63
  28.6 1.6 %collective-permute-start.12 = (bf16[16,4224]{1,0:T(8,128)(2,1)S(1)}, bf16[16,4224]{1,0:T(8,128)(2,1)S(1)}, u32[]{:S(2)}, u32[]{:S(2)}) collective-permute-start(bf16[16,4224]{1,0:T(8,128)(2,1)S(1)} %collective-permute-done.2.refs_0_), channel_id=1, source_target_pairs={{0,18},{1,19},{2,16},{3,17},{16,2},{17,3},{18,0},{19,1},{4,22},{5,... | collective-permute-start | bytes 405512 | tf_op jit(solution)/shard_map/member_6/ppermute | solution.py:63
  30.2 1.4 %collective-permute-start.9 = (bf16[16,4224]{1,0:T(8,128)(2,1)S(1)}, bf16[16,4224]{1,0:T(8,128)(2,1)S(1)}, u32[]{:S(2)}, u32[]{:S(2)}) collective-permute-start(bf16[16,4224]{1,0:T(8,128)(2,1)S(1)} %collective-permute-done.2.refs_0_), channel_id=1, source_target_pairs={{0,16},{1,17},{2,18},{3,19},{16,0},{17,1},{18,2},{19,3},{4,20},{5,... | collective-permute-start | bytes 405512 | tf_op jit(solution)/shard_map/member_4/ppermute | solution.py:63
  32.6 1.5 %collective-permute-start.6 = (bf16[16,4224]{1,0:T(8,128)(2,1)S(1)}, bf16[16,4224]{1,0:T(8,128)(2,1)S(1)}, u32[]{:S(2)}, u32[]{:S(2)}) collective-permute-start(bf16[16,4224]{1,0:T(8,128)(2,1)S(1)} %collective-permute-done.2.refs_0_), channel_id=1, source_target_pairs={{0,2},{1,3},{2,0},{3,1},{16,18},{17,19},{18,16},{19,17},{4,6},{5,7... | collective-permute-start | bytes 405512 | tf_op jit(solution)/shard_map/member_2/ppermute | solution.py:63
  34.1 2.9 %weights_in.1 = (bf16[768,4096]{1,0:T(8,128)(2,1)S(1)}, f32[8,128]{1,0:T(8,128)S(1)}) custom-call(bf16[768,4096]{1,0:T(8,128)(2,1)} %bitcast.8), custom_call_target="tpu_custom_call" | custom-call | bytes 12582912 | tf_op jit(solution)/shard_map/weights_in/pallas_call | solution.py:88
  37.0 2.7 %copy-done = bf16[768,4096]{1,0:T(8,128)(2,1)} copy-done((bf16[768,4096]{1,0:T(8,128)(2,1)}, bf16[768,4096]{1,0:T(8,128)(2,1)S(1)}, u32[]{:S(2)}) %copy-start) | copy-done | bytes 6291480
  41.1 2.4 %collective-permute-start.22 = (bf16[16,4224]{1,0:T(8,128)(2,1)S(1)}, bf16[16,4224]{1,0:T(8,128)(2,1)S(1)}, u32[]{:S(2)}, u32[]{:S(2)}) collective-permute-start(bf16[16,4224]{1,0:T(8,128)(2,1)S(1)} %collective-permute-done.4.refs_1_), channel_id=1, source_target_pairs={{0,18},{1,19},{2,16},{3,17},{16,2},{17,3},{18,0},{19,1},{4,22},{5,... | collective-permute-start | bytes 405512 | tf_op jit(solution)/shard_map/member_6/ppermute | solution.py:63
  43.4 2.8 %copy-done.1 = bf16[768,4096]{1,0:T(8,128)(2,1)S(1)} copy-done((bf16[768,4096]{1,0:T(8,128)(2,1)S(1)}, bf16[768,4096]{1,0:T(8,128)(2,1)}, u32[]{:S(2)}) %copy-start.1) | copy-done | bytes 6291480
  46.2 8.4 %run_experts.2 = (bf16[128,4096]{1,0:T(8,128)(2,1)S(1)}, bf16[128,4096]{1,0:T(8,128)(2,1)S(1)}, bf16[4096,1536]{1,0:T(8,128)(2,1)S(1)}) custom-call(s32[1]{0:T(128)} %bitcast.3.expert_ref, bf16[128,4224]{1,0:T(8,128)(2,1)S(1)} %packed.2.own_ref, bf16[128,4224]{1,0:T(8,128)(2,1)S(1)} %collective-permute-done.14.other_ref, bf16[1,4096,1536]{2,1,0:T(8,128)(2,1)} %refs_0_.1, ...), custom_call_target="tpu_custom_call" | custom-call | flops 2415919104 | bytes 20971520 | tf_op jit(solution)/shard_map/run_experts/pallas_call | solution.py:433
  55.4 2.0 %collective-permute-done.15.refs_1_ = bf16[128,4096]{1,0:T(8,128)(2,1)S(1)} collective-permute-done((bf16[128,4096]{1,0:T(8,128)(2,1)S(1)}, bf16[128,4096]{1,0:T(8,128)(2,1)S(1)}, u32[]{:S(2)}, u32[]{:S(2)}) %collective-permute-start.15) | collective-permute-done | bytes 1048608 | tf_op jit(solution)/shard_map/member_1/ppermute | solution.py:63
  58.9 5.1 %run_experts.3 = (bf16[128,4096]{1,0:T(8,128)(2,1)S(1)}, bf16[128,4096]{1,0:T(8,128)(2,1)S(1)}) custom-call(s32[1]{0:T(128)} %bitcast.3.expert_ref, bf16[128,4224]{1,0:T(8,128)(2,1)S(1)} %packed.3.own_ref, bf16[128,4224]{1,0:T(8,128)(2,1)S(1)} %collective-permute-done.23.other_ref, bf16[4096,1536]{1,0:T(8,128)(2,1)S(1)} %get-tuple-element.79.refs_0_, ...), custom_call_target="tpu_custom_call" | custom-call | flops 2415919104 | bytes 20971520 | tf_op jit(solution)/shard_map/run_experts/pallas_call | solution.py:433
  64.0 2.0 %collective-permute-done.16.refs_1_ = bf16[32,4096]{1,0:T(8,128)(2,1)S(1)} collective-permute-done((bf16[32,4096]{1,0:T(8,128)(2,1)S(1)}, bf16[32,4096]{1,0:T(8,128)(2,1)S(1)}, u32[]{:S(2)}, u32[]{:S(2)}) %collective-permute-start.16) | collective-permute-done | bytes 262176 | tf_op jit(solution)/shard_map/member_2/ppermute | solution.py:63
  66.3 1.6 %collective-permute-start.18 = (bf16[32,4096]{1,0:T(8,128)(2,1)S(1)}, bf16[32,4096]{1,0:T(8,128)(2,1)S(1)}, u32[]{:S(2)}, u32[]{:S(2)}) collective-permute-start(bf16[32,4096]{1,0:T(8,128)(2,1)S(1)} %get-tuple-element.74), channel_id=1, source_target_pairs={{0,18},{1,19},{2,16},{3,17},{16,2},{17,3},{18,0},{19,1},{4,22},{5,... | collective-permute-start | bytes 786440 | tf_op jit(solution)/shard_map/member_6/ppermute | solution.py:63
  69.2 1.6 %collective-permute-start.27 = (bf16[16,4096]{1,0:T(8,128)(2,1)S(1)}, bf16[16,4096]{1,0:T(8,128)(2,1)S(1)}, u32[]{:S(2)}, u32[]{:S(2)}) collective-permute-start(bf16[16,4096]{1,0:T(8,128)(2,1)S(1)} %get-tuple-element.86), channel_id=1, source_target_pairs={{0,2},{1,3},{2,0},{3,1},{16,18},{17,19},{18,16},{19,17},{4,6},{5,7... | collective-permute-start | bytes 393224 | tf_op jit(solution)/shard_map/member_2/ppermute | solution.py:63
  72.7 1.5 %collective-permute-start.25 = (bf16[16,4096]{1,0:T(8,128)(2,1)S(1)}, bf16[16,4096]{1,0:T(8,128)(2,1)S(1)}, u32[]{:S(2)}, u32[]{:S(2)}) collective-permute-start(bf16[16,4096]{1,0:T(8,128)(2,1)S(1)} %get-tuple-element.83), channel_id=1, source_target_pairs={{0,2},{1,3},{2,0},{3,1},{16,18},{17,19},{18,16},{19,17},{4,6},{5,7... | collective-permute-start | bytes 393224 | tf_op jit(solution)/shard_map/member_2/ppermute | solution.py:63
  74.2 2.1 %collective-permute-done.18.refs_3_ = bf16[32,4096]{1,0:T(8,128)(2,1)S(1)} collective-permute-done((bf16[32,4096]{1,0:T(8,128)(2,1)S(1)}, bf16[32,4096]{1,0:T(8,128)(2,1)S(1)}, u32[]{:S(2)}, u32[]{:S(2)}) %collective-permute-start.18) | collective-permute-done | bytes 262176 | tf_op jit(solution)/shard_map/member_6/ppermute | solution.py:63
  76.4 3.4 %collective-permute-start.19 = (bf16[16,4096]{1,0:T(8,128)(2,1)S(1)}, bf16[16,4096]{1,0:T(8,128)(2,1)S(1)}, u32[]{:S(2)}, u32[]{:S(2)}) collective-permute-start(bf16[16,4096]{1,0:T(8,128)(2,1)S(1)} %get-tuple-element.75), channel_id=1, source_target_pairs={{0,8},{1,9},{2,10},{3,11},{16,24},{17,25},{18,26},{19,27},{4,12},{... | collective-permute-start | bytes 393224 | tf_op jit(solution)/shard_map/plane_2/ppermute | solution.py:52
  80.1 2.5 %collective-permute-start.32 = (bf16[16,4096]{1,0:T(8,128)(2,1)S(1)}, bf16[16,4096]{1,0:T(8,128)(2,1)S(1)}, u32[]{:S(2)}, u32[]{:S(2)}) collective-permute-start(bf16[16,4096]{1,0:T(8,128)(2,1)S(1)} %get-tuple-element.91), channel_id=1, source_target_pairs={{0,18},{1,19},{2,16},{3,17},{16,2},{17,3},{18,0},{19,1},{4,22},{5,... | collective-permute-start | bytes 393224 | tf_op jit(solution)/shard_map/member_6/ppermute | solution.py:63
  82.7 2.2 %collective-permute-start.30 = (bf16[16,4096]{1,0:T(8,128)(2,1)S(1)}, bf16[16,4096]{1,0:T(8,128)(2,1)S(1)}, u32[]{:S(2)}, u32[]{:S(2)}) collective-permute-start(bf16[16,4096]{1,0:T(8,128)(2,1)S(1)} %add_chips.4), channel_id=1, source_target_pairs={{0,12},{1,13},{2,14},{3,15},{16,28},{17,29},{18,30},{19,31},{4,8},... | collective-permute-start | bytes 393224 | tf_op jit(solution)/shard_map/plane_3/ppermute | solution.py:52
  86.0 2.1 %collective-permute-done.32.refs_3_ = bf16[16,4096]{1,0:T(8,128)(2,1)S(1)} collective-permute-done((bf16[16,4096]{1,0:T(8,128)(2,1)S(1)}, bf16[16,4096]{1,0:T(8,128)(2,1)S(1)}, u32[]{:S(2)}, u32[]{:S(2)}) %collective-permute-start.32) | collective-permute-done | bytes 131104 | tf_op jit(solution)/shard_map/member_6/ppermute | solution.py:63
  88.2 1.5 %collective-permute-done.30.refs_3_ = bf16[16,4096]{1,0:T(8,128)(2,1)S(1)} collective-permute-done((bf16[16,4096]{1,0:T(8,128)(2,1)S(1)}, bf16[16,4096]{1,0:T(8,128)(2,1)S(1)}, u32[]{:S(2)}, u32[]{:S(2)}) %collective-permute-start.30) | collective-permute-done | bytes 131104 | tf_op jit(solution)/shard_map/plane_3/ppermute | solution.py:52
  89.7 2.1 %collective-permute-done.26.refs_2_ = bf16[16,4096]{1,0:T(8,128)(2,1)S(1)} collective-permute-done((bf16[16,4096]{1,0:T(8,128)(2,1)S(1)}, bf16[16,4096]{1,0:T(8,128)(2,1)S(1)}, u32[]{:S(2)}, u32[]{:S(2)}) %collective-permute-start.26) | collective-permute-done | bytes 131104 | tf_op jit(solution)/shard_map/plane_1/ppermute | solution.py:52
  (68 shorter events, 14.8 us)
Async XLA Ops:
  0.6 5.2 %collective-permute-start = (s32[16]{0:T(128)}, s32[16]{0:T(128)S(1)}, u32[]{:S(2)}, u32[]{:S(2)}) collective-permute-start(s32[16]{0:T(128)} %param.17), channel_id=1, source_target_pairs={{0,16},{16,0},{1,17},{17,1},{2,18},{18,2},{3,19},{19,3},{4,20},{20... | collective-permute-start | bytes 200 | tf_op jit(solution)/shard_map/ppermute | solution.py:68
  6.4 7.8 %collective-permute-start.1 = (bf16[16,16,512]{2,1,0:T(8,128)(2,1)S(1)}, bf16[16,16,512]{2,1,0:T(8,128)(2,1)S(1)}, u32[]{:S(2)}, u32[]{:S(2)}) collective-permute-start(bf16[16,16,512]{2,1,0:T(8,128)(2,1)S(1)} %pick_pages.1), channel_id=1, source_target_pairs={{0,16},{16,0},{1,17},{17,1},{2,18},{18,2},{3,19},{19,3},{4,20},{20... | collective-permute-start | bytes 786440 | tf_op jit(solution)/shard_map/ppermute | solution.py:68
  16.3 7.9 %collective-permute-start.3 = (bf16[16,4224]{1,0:T(8,128)(2,1)S(1)}, bf16[16,4224]{1,0:T(8,128)(2,1)S(1)}, u32[]{:S(2)}, u32[]{:S(2)}) collective-permute-start(bf16[16,4224]{1,0:T(8,128)(2,1)S(1)} %get-tuple-element.77.refs_0_), channel_id=1, source_target_pairs={{0,8},{1,9},{2,10},{3,11},{16,24},{17,25},{18,26},{19,27},{4,12},{... | collective-permute-start | bytes 405512 | tf_op jit(solution)/shard_map/plane_2/ppermute | solution.py:52
  18.8 6.2 %collective-permute-start.11 = (bf16[16,4224]{1,0:T(8,128)(2,1)S(1)}, bf16[16,4224]{1,0:T(8,128)(2,1)S(1)}, u32[]{:S(2)}, u32[]{:S(2)}) collective-permute-start(bf16[16,4224]{1,0:T(8,128)(2,1)S(1)} %get-tuple-element.77.refs_0_), channel_id=1, source_target_pairs={{0,18},{1,19},{2,16},{3,17},{16,2},{17,3},{18,0},{19,1},{4,22},{5,... | collective-permute-start | bytes 405512 | tf_op jit(solution)/shard_map/member_6/ppermute | solution.py:63
  20.4 6.2 %collective-permute-start.8 = (bf16[16,4224]{1,0:T(8,128)(2,1)S(1)}, bf16[16,4224]{1,0:T(8,128)(2,1)S(1)}, u32[]{:S(2)}, u32[]{:S(2)}) collective-permute-start(bf16[16,4224]{1,0:T(8,128)(2,1)S(1)} %get-tuple-element.77.refs_0_), channel_id=1, source_target_pairs={{0,16},{1,17},{2,18},{3,19},{16,0},{17,1},{18,2},{19,3},{4,20},{5,... | collective-permute-start | bytes 405512 | tf_op jit(solution)/shard_map/member_4/ppermute | solution.py:63
  21.8 6.2 %collective-permute-start.5 = (bf16[16,4224]{1,0:T(8,128)(2,1)S(1)}, bf16[16,4224]{1,0:T(8,128)(2,1)S(1)}, u32[]{:S(2)}, u32[]{:S(2)}) collective-permute-start(bf16[16,4224]{1,0:T(8,128)(2,1)S(1)} %get-tuple-element.77.refs_0_), channel_id=1, source_target_pairs={{0,2},{1,3},{2,0},{3,1},{16,18},{17,19},{18,16},{19,17},{4,6},{5,7... | collective-permute-start | bytes 405512 | tf_op jit(solution)/shard_map/member_2/ppermute | solution.py:63
  22.3 6.3 %collective-permute-start.2 = (bf16[16,4224]{1,0:T(8,128)(2,1)S(1)}, bf16[16,4224]{1,0:T(8,128)(2,1)S(1)}, u32[]{:S(2)}, u32[]{:S(2)}) collective-permute-start(bf16[16,4224]{1,0:T(8,128)(2,1)S(1)} %get-tuple-element.77.refs_0_), channel_id=1, source_target_pairs={{0,4},{1,5},{2,6},{3,7},{16,20},{17,21},{18,22},{19,23},{4,0},{5,1... | collective-permute-start | bytes 405512 | tf_op jit(solution)/shard_map/plane_1/ppermute | solution.py:52
  24.2 6.0 %collective-permute-start.4 = (bf16[16,4224]{1,0:T(8,128)(2,1)S(1)}, bf16[16,4224]{1,0:T(8,128)(2,1)S(1)}, u32[]{:S(2)}, u32[]{:S(2)}) collective-permute-start(bf16[16,4224]{1,0:T(8,128)(2,1)S(1)} %collective-permute-done.3.refs_1_), channel_id=1, source_target_pairs={{0,4},{1,5},{2,6},{3,7},{16,20},{17,21},{18,22},{19,23},{4,0},{5,1... | collective-permute-start | bytes 405512 | tf_op jit(solution)/shard_map/plane_1/ppermute | solution.py:52
  25.1 7.5 %collective-permute-start.13 = (bf16[16,4224]{1,0:T(8,128)(2,1)S(1)}, bf16[16,4224]{1,0:T(8,128)(2,1)S(1)}, u32[]{:S(2)}, u32[]{:S(2)}) collective-permute-start(bf16[16,4224]{1,0:T(8,128)(2,1)S(1)} %collective-permute-done.3.refs_1_), channel_id=1, source_target_pairs={{0,18},{1,19},{2,16},{3,17},{16,2},{17,3},{18,0},{19,1},{4,22},{5,... | collective-permute-start | bytes 405512 | tf_op jit(solution)/shard_map/member_6/ppermute | solution.py:63
  26.7 13.0 %collective-permute-start.10 = (bf16[16,4224]{1,0:T(8,128)(2,1)S(1)}, bf16[16,4224]{1,0:T(8,128)(2,1)S(1)}, u32[]{:S(2)}, u32[]{:S(2)}) collective-permute-start(bf16[16,4224]{1,0:T(8,128)(2,1)S(1)} %collective-permute-done.3.refs_1_), channel_id=1, source_target_pairs={{0,16},{1,17},{2,18},{3,19},{16,0},{17,1},{18,2},{19,3},{4,20},{5,... | collective-permute-start | bytes 405512 | tf_op jit(solution)/shard_map/member_4/ppermute | solution.py:63
  28.1 11.6 %collective-permute-start.7 = (bf16[16,4224]{1,0:T(8,128)(2,1)S(1)}, bf16[16,4224]{1,0:T(8,128)(2,1)S(1)}, u32[]{:S(2)}, u32[]{:S(2)}) collective-permute-start(bf16[16,4224]{1,0:T(8,128)(2,1)S(1)} %collective-permute-done.3.refs_1_), channel_id=1, source_target_pairs={{0,2},{1,3},{2,0},{3,1},{16,18},{17,19},{18,16},{19,17},{4,6},{5,7... | collective-permute-start | bytes 405512 | tf_op jit(solution)/shard_map/member_2/ppermute | solution.py:63
  28.6 11.1 %collective-permute-start.12 = (bf16[16,4224]{1,0:T(8,128)(2,1)S(1)}, bf16[16,4224]{1,0:T(8,128)(2,1)S(1)}, u32[]{:S(2)}, u32[]{:S(2)}) collective-permute-start(bf16[16,4224]{1,0:T(8,128)(2,1)S(1)} %collective-permute-done.2.refs_0_), channel_id=1, source_target_pairs={{0,18},{1,19},{2,16},{3,17},{16,2},{17,3},{18,0},{19,1},{4,22},{5,... | collective-permute-start | bytes 405512 | tf_op jit(solution)/shard_map/member_6/ppermute | solution.py:63
  30.2 9.5 %collective-permute-start.9 = (bf16[16,4224]{1,0:T(8,128)(2,1)S(1)}, bf16[16,4224]{1,0:T(8,128)(2,1)S(1)}, u32[]{:S(2)}, u32[]{:S(2)}) collective-permute-start(bf16[16,4224]{1,0:T(8,128)(2,1)S(1)} %collective-permute-done.2.refs_0_), channel_id=1, source_target_pairs={{0,16},{1,17},{2,18},{3,19},{16,0},{17,1},{18,2},{19,3},{4,20},{5,... | collective-permute-start | bytes 405512 | tf_op jit(solution)/shard_map/member_4/ppermute | solution.py:63
  32.6 7.1 %collective-permute-start.6 = (bf16[16,4224]{1,0:T(8,128)(2,1)S(1)}, bf16[16,4224]{1,0:T(8,128)(2,1)S(1)}, u32[]{:S(2)}, u32[]{:S(2)}) collective-permute-start(bf16[16,4224]{1,0:T(8,128)(2,1)S(1)} %collective-permute-done.2.refs_0_), channel_id=1, source_target_pairs={{0,2},{1,3},{2,0},{3,1},{16,18},{17,19},{18,16},{19,17},{4,6},{5,7... | collective-permute-start | bytes 405512 | tf_op jit(solution)/shard_map/member_2/ppermute | solution.py:63
  39.8 3.6 %collective-permute-start.14 = (bf16[128,4224]{1,0:T(8,128)(2,1)S(1)}, bf16[128,4224]{1,0:T(8,128)(2,1)S(1)}, u32[]{:S(2)}, u32[]{:S(2)}) collective-permute-start(bf16[128,4224]{1,0:T(8,128)(2,1)S(1)} %packed.2.own_ref), channel_id=1, source_target_pairs={{0,1},{1,0},{2,3},{3,2},{16,17},{17,16},{18,19},{19,18},{4,5},{5,4... | collective-permute-start | bytes 3244040 | tf_op jit(solution)/shard_map/member_1/ppermute | solution.py:63
  39.9 14.8 %collective-permute-start.20 = (bf16[16,4224]{1,0:T(8,128)(2,1)S(1)}, bf16[16,4224]{1,0:T(8,128)(2,1)S(1)}, u32[]{:S(2)}, u32[]{:S(2)}) collective-permute-start(bf16[16,4224]{1,0:T(8,128)(2,1)S(1)} %collective-permute-done.4.refs_1_), channel_id=1, source_target_pairs={{0,2},{1,3},{2,0},{3,1},{16,18},{17,19},{18,16},{19,17},{4,6},{5,7... | collective-permute-start | bytes 405512 | tf_op jit(solution)/shard_map/member_2/ppermute | solution.py:63
  40.5 14.3 %collective-permute-start.21 = (bf16[16,4224]{1,0:T(8,128)(2,1)S(1)}, bf16[16,4224]{1,0:T(8,128)(2,1)S(1)}, u32[]{:S(2)}, u32[]{:S(2)}) collective-permute-start(bf16[16,4224]{1,0:T(8,128)(2,1)S(1)} %collective-permute-done.4.refs_1_), channel_id=1, source_target_pairs={{0,16},{1,17},{2,18},{3,19},{16,0},{17,1},{18,2},{19,3},{4,20},{5,... | collective-permute-start | bytes 405512 | tf_op jit(solution)/shard_map/member_4/ppermute | solution.py:63
  41.1 13.7 %collective-permute-start.22 = (bf16[16,4224]{1,0:T(8,128)(2,1)S(1)}, bf16[16,4224]{1,0:T(8,128)(2,1)S(1)}, u32[]{:S(2)}, u32[]{:S(2)}) collective-permute-start(bf16[16,4224]{1,0:T(8,128)(2,1)S(1)} %collective-permute-done.4.refs_1_), channel_id=1, source_target_pairs={{0,18},{1,19},{2,16},{3,17},{16,2},{17,3},{18,0},{19,1},{4,22},{5,... | collective-permute-start | bytes 405512 | tf_op jit(solution)/shard_map/member_6/ppermute | solution.py:63
  54.6 2.7 %collective-permute-start.15 = (bf16[128,4096]{1,0:T(8,128)(2,1)S(1)}, bf16[128,4096]{1,0:T(8,128)(2,1)S(1)}, u32[]{:S(2)}, u32[]{:S(2)}) collective-permute-start(bf16[128,4096]{1,0:T(8,128)(2,1)S(1)} %get-tuple-element.70), channel_id=1, source_target_pairs={{0,1},{1,0},{2,3},{3,2},{16,17},{17,16},{18,19},{19,18},{4,5},{5,4... | collective-permute-start | bytes 3145736 | tf_op jit(solution)/shard_map/member_1/ppermute | solution.py:63
  54.8 4.1 %collective-permute-start.23 = (bf16[128,4224]{1,0:T(8,128)(2,1)S(1)}, bf16[128,4224]{1,0:T(8,128)(2,1)S(1)}, u32[]{:S(2)}, u32[]{:S(2)}) collective-permute-start(bf16[128,4224]{1,0:T(8,128)(2,1)S(1)} %packed.3.own_ref), channel_id=1, source_target_pairs={{0,1},{1,0},{2,3},{3,2},{16,17},{17,16},{18,19},{19,18},{4,5},{5,4... | collective-permute-start | bytes 3244040 | tf_op jit(solution)/shard_map/member_1/ppermute | solution.py:63
  57.6 8.4 %collective-permute-start.16 = (bf16[32,4096]{1,0:T(8,128)(2,1)S(1)}, bf16[32,4096]{1,0:T(8,128)(2,1)S(1)}, u32[]{:S(2)}, u32[]{:S(2)}) collective-permute-start(bf16[32,4096]{1,0:T(8,128)(2,1)S(1)} %get-tuple-element.72), channel_id=1, source_target_pairs={{0,2},{1,3},{2,0},{3,1},{16,18},{17,19},{18,16},{19,17},{4,6},{5,7... | collective-permute-start | bytes 786440 | tf_op jit(solution)/shard_map/member_2/ppermute | solution.py:63
  58.2 8.1 %collective-permute-start.17 = (bf16[32,4096]{1,0:T(8,128)(2,1)S(1)}, bf16[32,4096]{1,0:T(8,128)(2,1)S(1)}, u32[]{:S(2)}, u32[]{:S(2)}) collective-permute-start(bf16[32,4096]{1,0:T(8,128)(2,1)S(1)} %get-tuple-element.73), channel_id=1, source_target_pairs={{0,16},{1,17},{2,18},{3,19},{16,0},{17,1},{18,2},{19,3},{4,20},{5,... | collective-permute-start | bytes 786440 | tf_op jit(solution)/shard_map/member_4/ppermute | solution.py:63
  66.3 10.0 %collective-permute-start.18 = (bf16[32,4096]{1,0:T(8,128)(2,1)S(1)}, bf16[32,4096]{1,0:T(8,128)(2,1)S(1)}, u32[]{:S(2)}, u32[]{:S(2)}) collective-permute-start(bf16[32,4096]{1,0:T(8,128)(2,1)S(1)} %get-tuple-element.74), channel_id=1, source_target_pairs={{0,18},{1,19},{2,16},{3,17},{16,2},{17,3},{18,0},{19,1},{4,22},{5,... | collective-permute-start | bytes 786440 | tf_op jit(solution)/shard_map/member_6/ppermute | solution.py:63
  69.2 10.7 %collective-permute-start.27 = (bf16[16,4096]{1,0:T(8,128)(2,1)S(1)}, bf16[16,4096]{1,0:T(8,128)(2,1)S(1)}, u32[]{:S(2)}, u32[]{:S(2)}) collective-permute-start(bf16[16,4096]{1,0:T(8,128)(2,1)S(1)} %get-tuple-element.86), channel_id=1, source_target_pairs={{0,2},{1,3},{2,0},{3,1},{16,18},{17,19},{18,16},{19,17},{4,6},{5,7... | collective-permute-start | bytes 393224 | tf_op jit(solution)/shard_map/member_2/ppermute | solution.py:63
  70.7 9.4 %collective-permute-start.28 = (bf16[16,4096]{1,0:T(8,128)(2,1)S(1)}, bf16[16,4096]{1,0:T(8,128)(2,1)S(1)}, u32[]{:S(2)}, u32[]{:S(2)}) collective-permute-start(bf16[16,4096]{1,0:T(8,128)(2,1)S(1)} %get-tuple-element.87), channel_id=1, source_target_pairs={{0,16},{1,17},{2,18},{3,19},{16,0},{17,1},{18,2},{19,3},{4,20},{5,... | collective-permute-start | bytes 393224 | tf_op jit(solution)/shard_map/member_4/ppermute | solution.py:63
  71.4 11.3 %collective-permute-start.29 = (bf16[16,4096]{1,0:T(8,128)(2,1)S(1)}, bf16[16,4096]{1,0:T(8,128)(2,1)S(1)}, u32[]{:S(2)}, u32[]{:S(2)}) collective-permute-start(bf16[16,4096]{1,0:T(8,128)(2,1)S(1)} %get-tuple-element.88), channel_id=1, source_target_pairs={{0,18},{1,19},{2,16},{3,17},{16,2},{17,3},{18,0},{19,1},{4,22},{5,... | collective-permute-start | bytes 393224 | tf_op jit(solution)/shard_map/member_6/ppermute | solution.py:63
  72.7 12.3 %collective-permute-start.25 = (bf16[16,4096]{1,0:T(8,128)(2,1)S(1)}, bf16[16,4096]{1,0:T(8,128)(2,1)S(1)}, u32[]{:S(2)}, u32[]{:S(2)}) collective-permute-start(bf16[16,4096]{1,0:T(8,128)(2,1)S(1)} %get-tuple-element.83), channel_id=1, source_target_pairs={{0,2},{1,3},{2,0},{3,1},{16,18},{17,19},{18,16},{19,17},{4,6},{5,7... | collective-permute-start | bytes 393224 | tf_op jit(solution)/shard_map/member_2/ppermute | solution.py:63
  76.4 11.8 %collective-permute-start.19 = (bf16[16,4096]{1,0:T(8,128)(2,1)S(1)}, bf16[16,4096]{1,0:T(8,128)(2,1)S(1)}, u32[]{:S(2)}, u32[]{:S(2)}) collective-permute-start(bf16[16,4096]{1,0:T(8,128)(2,1)S(1)} %get-tuple-element.75), channel_id=1, source_target_pairs={{0,8},{1,9},{2,10},{3,11},{16,24},{17,25},{18,26},{19,27},{4,12},{... | collective-permute-start | bytes 393224 | tf_op jit(solution)/shard_map/plane_2/ppermute | solution.py:52
  79.9 6.2 %collective-permute-start.31 = (bf16[16,4096]{1,0:T(8,128)(2,1)S(1)}, bf16[16,4096]{1,0:T(8,128)(2,1)S(1)}, u32[]{:S(2)}, u32[]{:S(2)}) collective-permute-start(bf16[16,4096]{1,0:T(8,128)(2,1)S(1)} %get-tuple-element.90), channel_id=1, source_target_pairs={{0,16},{1,17},{2,18},{3,19},{16,0},{17,1},{18,2},{19,3},{4,20},{5,... | collective-permute-start | bytes 393224 | tf_op jit(solution)/shard_map/member_4/ppermute | solution.py:63
  80.1 8.0 %collective-permute-start.32 = (bf16[16,4096]{1,0:T(8,128)(2,1)S(1)}, bf16[16,4096]{1,0:T(8,128)(2,1)S(1)}, u32[]{:S(2)}, u32[]{:S(2)}) collective-permute-start(bf16[16,4096]{1,0:T(8,128)(2,1)S(1)} %get-tuple-element.91), channel_id=1, source_target_pairs={{0,18},{1,19},{2,16},{3,17},{16,2},{17,3},{18,0},{19,1},{4,22},{5,... | collective-permute-start | bytes 393224 | tf_op jit(solution)/shard_map/member_6/ppermute | solution.py:63
  82.7 7.0 %collective-permute-start.30 = (bf16[16,4096]{1,0:T(8,128)(2,1)S(1)}, bf16[16,4096]{1,0:T(8,128)(2,1)S(1)}, u32[]{:S(2)}, u32[]{:S(2)}) collective-permute-start(bf16[16,4096]{1,0:T(8,128)(2,1)S(1)} %add_chips.4), channel_id=1, source_target_pairs={{0,12},{1,13},{2,14},{3,15},{16,28},{17,29},{18,30},{19,31},{4,8},... | collective-permute-start | bytes 393224 | tf_op jit(solution)/shard_map/plane_3/ppermute | solution.py:52
  85.0 6.8 %collective-permute-start.26 = (bf16[16,4096]{1,0:T(8,128)(2,1)S(1)}, bf16[16,4096]{1,0:T(8,128)(2,1)S(1)}, u32[]{:S(2)}, u32[]{:S(2)}) collective-permute-start(bf16[16,4096]{1,0:T(8,128)(2,1)S(1)} %get-tuple-element.84), channel_id=1, source_target_pairs={{0,4},{1,5},{2,6},{3,7},{16,20},{17,21},{18,22},{19,23},{4,0},{5,1... | collective-permute-start | bytes 393224 | tf_op jit(solution)/shard_map/plane_1/ppermute | solution.py:52
  (10 other events, 68.1 us)

commit v13 on v11

--- a/solution.py
+++ b/solution.py
@@ -633,15 +633,16 @@
     over = after(over, parts[1], parts[2])
     far_sums = add_cores(mine, layout.swapped(over, 1))
     totals = add_up([[part] for part in parts], [count_of_rows] * len(near), "add_chips")
-    others = [layout.shifted(total, by) for total, by in list(zip(totals, near))[::-1]]
-    for i, by in list(enumerate(far))[:0:-1]:
-        others.append(layout.shifted(total_of(to_owners(far_sums, i)), by))
+    far_totals = [total_of(to_owners(far_sums, i)) for i in range(len(far) - 1, 0, -1)]
+    last = to_owners(far_sums, 0)
+    others = []
+    for total, by in list(zip(totals, near))[::-1]:
+        others.append(layout.shifted(total, by))
+    others += [layout.shifted(total, by) for total, by in zip(far_totals, far[:0:-1])]
     merged = add_up(
         [[merged]] + [[part] for part in others], [count_of_rows], "add_first", 10**10
     )[0]
-    others = [total_of(to_owners(far_sums, 0))]
-    total = merged.astype(jnp.float32) + sum(part.astype(jnp.float32) for part in others)
-    layer_out = total.astype(jnp.bfloat16)
+    layer_out = add_up([[merged]] + [[part] for part in last], [count_of_rows], "add_last")[0]
     return (attended, layer_out)
 
 

time: 89.8 us -> 91.8 us (1.022)
  waiting for transfers between devices: 22.4 us -> 30.2 us
  starting transfers between devices: 42.9 us -> 37 us
    ppermute x25, waiting for transfers between devices: 15.6 us -> 24.3 us  [swapped(): return lax.ppermute(value, AXES, pairs)]
    ppermute x6, starting transfers between devices: 10.4 us -> 5.73 us  [shifted(): return lax.ppermute(value, AXES, pairs)]
    ppermute x25, starting transfers between devices: 27.4 us -> 26.2 us  [swapped(): return lax.ppermute(value, AXES, pairs)]
  transfers between devices with their start and end apart: 33 -> 33, of which waited for: 18 -> 17; matrix products, arithmetic and copies ran while one was open for 0% -> 0% of each run, Pallas kernels for 21% -> 21%
where the time goes in v13:
time: 91.8 us; the launch traced here: 91.4 us
  starting transfers between devices  37 us (40%)
  waiting for transfers between devices  30.2 us (33%)
  Pallas kernels  23.3 us (25%)
    ppermute x25, starting transfers between devices, swapped(): return lax.ppermute(value, AXES, pairs)  26.2 us
    ppermute x25, waiting for transfers between devices, swapped(): return lax.ppermute(value, AXES, pairs)  24.3 us
    pallas_call x2, Pallas kernels, run_experts(): pl.pallas_call(kernel, out_shape=(shape, shape) + kept, in_specs=[SMEM, V...  13.4 us
    ppermute x6, starting transfers between devices, shifted(): return lax.ppermute(value, AXES, pairs)  5.73 us
    ppermute x2, starting transfers between devices, from_behind(): lax.ppermute(value, axis, [(i, (i + by) % length) for i in range(length)])  5.09 us
    pallas_call x1, Pallas kernels, own_attention(): pl.pallas_call(kernel, out_shape=(shape, shape, shape, jax.ShapeDtypeStru...  4.74 us
    ppermute x6, waiting for transfers between devices, shifted(): return lax.ppermute(value, AXES, pairs)  3.86 us
    ppermute x2, waiting for transfers between devices, from_behind(): lax.ppermute(value, axis, [(i, (i + by) % length) for i in range(length)])  2.06 us
  transfers between devices with their start and end apart: 33, of which 17 were waited for; matrix products, arithmetic and copies ran while one was open for 0% of the time, Pallas kernels for 21%

profile of v13, /device:TPU:0, one launch (start us, length us, event | category | flops | bytes accessed | tf_op | source)
XLA Modules:
  0.0 91.4 jit_solution(8763710104420039722)
XLA Ops:
  0.6 3.0 %collective-permute-start = (s32[16]{0:T(128)}, s32[16]{0:T(128)S(1)}, u32[]{:S(2)}, u32[]{:S(2)}) collective-permute-start(s32[16]{0:T(128)} %param.17), channel_id=1, source_target_pairs={{0,16},{16,0},{1,17},{17,1},{2,18},{18,2},{3,19},{19,3},{4,20},{20... | collective-permute-start | bytes 200 | tf_op jit(solution)/shard_map/ppermute | solution.py:68
  3.6 1.7 %collective-permute-done.slots_ref = s32[16]{0:T(128)S(1)} collective-permute-done((s32[16]{0:T(128)}, s32[16]{0:T(128)S(1)}, u32[]{:S(2)}, u32[]{:S(2)}) %collective-permute-start) | collective-permute-done | bytes 96 | tf_op jit(solution)/shard_map/ppermute | solution.py:68
  5.3 1.6 %pick_pages.1 = bf16[16,16,512]{2,1,0:T(8,128)(2,1)S(1)} custom-call(s32[16]{0:T(128)S(1)} %collective-permute-done.slots_ref, bf16[128,16,512]{2,1,0:T(8,128)(2,1)} %pages_hbm.1), custom_call_target="tpu_custom_call" | custom-call | bytes 1048576 | tf_op jit(solution)/shard_map/pick_pages/pallas_call | solution.py:84
  7.0 2.1 %collective-permute-start.1 = (bf16[16,16,512]{2,1,0:T(8,128)(2,1)S(1)}, bf16[16,16,512]{2,1,0:T(8,128)(2,1)S(1)}, u32[]{:S(2)}, u32[]{:S(2)}) collective-permute-start(bf16[16,16,512]{2,1,0:T(8,128)(2,1)S(1)} %pick_pages.1), channel_id=1, source_target_pairs={{0,16},{16,0},{1,17},{17,1},{2,18},{18,2},{3,19},{19,3},{4,20},{20... | collective-permute-start | bytes 786440 | tf_op jit(solution)/shard_map/ppermute | solution.py:68
  9.0 4.7 %own_attention.1 = (f32[512,128]{1,0:T(8,128)S(1)}, f32[512,128]{1,0:T(8,128)S(1)}, f32[512,128]{1,0:T(8,128)S(1)}, bf16[512,128]{1,0:T(8,128)(2,1)S(1)}) custom-call(bf16[16,4096]{1,0:T(8,128)(2,1)} %queries_hbm, bf16[16,512]{1,0:T(8,128)(2,1)} %new_hbm.1, bf16[128,16,512]{2,1,0:T(8,128)(2,1)} %pages_hbm.1, s32[16,16]{1,0:T(8,128)} %table_ref.1, s32[16]{0:T(128)} %lengths_ref.1), custom_call_target="tpu_custom_call" | custom-call | flops 1073741824 | bytes 16777216 | tf_op jit(solution)/shard_map/own_attention/pallas_call | solution.py:239
  14.2 1.9 %finish_attention.1 = (bf16[16,4096]{1,0:T(8,128)(2,1)}, bf16[16,4096]{1,0:T(8,128)(2,1)S(1)}, bf16[16,4224]{1,0:T(8,128)(2,1)S(1)}) custom-call(bf16[512,128]{1,0:T(8,128)(2,1)S(1)} %get-tuple-element.44.q_ref, bf16[16,16,512]{2,1,0:T(8,128)(2,1)S(1)} %collective-permute-done.1.fetched_ref, s32[16,16]{1,0:T(8,128)S(1)} %copy-done.2, s32[16]{0:T(128)S(1)} %copy-done.5, ...), custom_call_target="tpu_custom_call" | custom-call | flops 134217728 | bytes 4194304 | tf_op jit(solution)/shard_map/finish_attention/pallas_call | solution.py:538
  16.2 2.8 %collective-permute-start.3 = (bf16[16,4224]{1,0:T(8,128)(2,1)S(1)}, bf16[16,4224]{1,0:T(8,128)(2,1)S(1)}, u32[]{:S(2)}, u32[]{:S(2)}) collective-permute-start(bf16[16,4224]{1,0:T(8,128)(2,1)S(1)} %get-tuple-element.69.refs_0_), channel_id=1, source_target_pairs={{0,8},{1,9},{2,10},{3,11},{16,24},{17,25},{18,26},{19,27},{4,12},{... | collective-permute-start | bytes 405512 | tf_op jit(solution)/shard_map/plane_2/ppermute | solution.py:52
  19.0 1.6 %collective-permute-start.2 = (bf16[16,4224]{1,0:T(8,128)(2,1)S(1)}, bf16[16,4224]{1,0:T(8,128)(2,1)S(1)}, u32[]{:S(2)}, u32[]{:S(2)}) collective-permute-start(bf16[16,4224]{1,0:T(8,128)(2,1)S(1)} %get-tuple-element.69.refs_0_), channel_id=1, source_target_pairs={{0,4},{1,5},{2,6},{3,7},{16,20},{17,21},{18,22},{19,23},{4,0},{5,1... | collective-permute-start | bytes 405512 | tf_op jit(solution)/shard_map/plane_1/ppermute | solution.py:52
  20.6 1.5 %collective-permute-start.5 = (bf16[16,4224]{1,0:T(8,128)(2,1)S(1)}, bf16[16,4224]{1,0:T(8,128)(2,1)S(1)}, u32[]{:S(2)}, u32[]{:S(2)}) collective-permute-start(bf16[16,4224]{1,0:T(8,128)(2,1)S(1)} %get-tuple-element.69.refs_0_), channel_id=1, source_target_pairs={{0,2},{1,3},{2,0},{3,1},{16,18},{17,19},{18,16},{19,17},{4,6},{5,7... | collective-permute-start | bytes 405512 | tf_op jit(solution)/shard_map/member_2/ppermute | solution.py:63
  22.1 1.5 %collective-permute-start.8 = (bf16[16,4224]{1,0:T(8,128)(2,1)S(1)}, bf16[16,4224]{1,0:T(8,128)(2,1)S(1)}, u32[]{:S(2)}, u32[]{:S(2)}) collective-permute-start(bf16[16,4224]{1,0:T(8,128)(2,1)S(1)} %get-tuple-element.69.refs_0_), channel_id=1, source_target_pairs={{0,16},{1,17},{2,18},{3,19},{16,0},{17,1},{18,2},{19,3},{4,20},{5,... | collective-permute-start | bytes 405512 | tf_op jit(solution)/shard_map/member_4/ppermute | solution.py:63
  25.1 2.9 %collective-permute-done.5.refs_2_ = bf16[16,4224]{1,0:T(8,128)(2,1)S(1)} collective-permute-done((bf16[16,4224]{1,0:T(8,128)(2,1)S(1)}, bf16[16,4224]{1,0:T(8,128)(2,1)S(1)}, u32[]{:S(2)}, u32[]{:S(2)}) %collective-permute-start.5) | collective-permute-done | bytes 135200 | tf_op jit(solution)/shard_map/member_2/ppermute | solution.py:63
  28.8 1.2 %collective-permute-start.7 = (bf16[16,4224]{1,0:T(8,128)(2,1)S(1)}, bf16[16,4224]{1,0:T(8,128)(2,1)S(1)}, u32[]{:S(2)}, u32[]{:S(2)}) collective-permute-start(bf16[16,4224]{1,0:T(8,128)(2,1)S(1)} %collective-permute-done.3.refs_1_), channel_id=1, source_target_pairs={{0,2},{1,3},{2,0},{3,1},{16,18},{17,19},{18,16},{19,17},{4,6},{5,7... | collective-permute-start | bytes 405512 | tf_op jit(solution)/shard_map/member_2/ppermute | solution.py:63
  32.1 1.7 %collective-permute-start.12 = (bf16[16,4224]{1,0:T(8,128)(2,1)S(1)}, bf16[16,4224]{1,0:T(8,128)(2,1)S(1)}, u32[]{:S(2)}, u32[]{:S(2)}) collective-permute-start(bf16[16,4224]{1,0:T(8,128)(2,1)S(1)} %collective-permute-done.2.refs_0_), channel_id=1, source_target_pairs={{0,18},{1,19},{2,16},{3,17},{16,2},{17,3},{18,0},{19,1},{4,22},{5,... | collective-permute-start | bytes 405512 | tf_op jit(solution)/shard_map/member_6/ppermute | solution.py:63
  33.8 2.0 %collective-permute-done.6.refs_2_ = bf16[16,4224]{1,0:T(8,128)(2,1)S(1)} collective-permute-done((bf16[16,4224]{1,0:T(8,128)(2,1)S(1)}, bf16[16,4224]{1,0:T(8,128)(2,1)S(1)}, u32[]{:S(2)}, u32[]{:S(2)}) %collective-permute-start.6) | collective-permute-done | bytes 135200 | tf_op jit(solution)/shard_map/member_2/ppermute | solution.py:63
  35.8 1.6 %collective-permute-start.13 = (bf16[16,4224]{1,0:T(8,128)(2,1)S(1)}, bf16[16,4224]{1,0:T(8,128)(2,1)S(1)}, u32[]{:S(2)}, u32[]{:S(2)}) collective-permute-start(bf16[16,4224]{1,0:T(8,128)(2,1)S(1)} %collective-permute-done.3.refs_1_), channel_id=1, source_target_pairs={{0,18},{1,19},{2,16},{3,17},{16,2},{17,3},{18,0},{19,1},{4,22},{5,... | collective-permute-start | bytes 405512 | tf_op jit(solution)/shard_map/member_6/ppermute | solution.py:63
  37.4 1.3 %collective-permute-done.12.refs_6_ = bf16[16,4224]{1,0:T(8,128)(2,1)S(1)} collective-permute-done((bf16[16,4224]{1,0:T(8,128)(2,1)S(1)}, bf16[16,4224]{1,0:T(8,128)(2,1)S(1)}, u32[]{:S(2)}, u32[]{:S(2)}) %collective-permute-start.12) | collective-permute-done | bytes 135200 | tf_op jit(solution)/shard_map/member_6/ppermute | solution.py:63
  38.7 3.0 %collective-permute-done.13.refs_7_ = bf16[16,4224]{1,0:T(8,128)(2,1)S(1)} collective-permute-done((bf16[16,4224]{1,0:T(8,128)(2,1)S(1)}, bf16[16,4224]{1,0:T(8,128)(2,1)S(1)}, u32[]{:S(2)}, u32[]{:S(2)}) %collective-permute-start.13) | collective-permute-done | bytes 135200 | tf_op jit(solution)/shard_map/member_6/ppermute | solution.py:63
  42.9 1.2 %collective-permute-start.22 = (bf16[16,4224]{1,0:T(8,128)(2,1)S(1)}, bf16[16,4224]{1,0:T(8,128)(2,1)S(1)}, u32[]{:S(2)}, u32[]{:S(2)}) collective-permute-start(bf16[16,4224]{1,0:T(8,128)(2,1)S(1)} %collective-permute-done.4.refs_1_), channel_id=1, source_target_pairs={{0,16},{1,17},{2,18},{3,19},{16,0},{17,1},{18,2},{19,3},{4,20},{5,... | collective-permute-start | bytes 405512 | tf_op jit(solution)/shard_map/member_4/ppermute | solution.py:63
  44.1 1.3 %collective-permute-start.23 = (bf16[16,4224]{1,0:T(8,128)(2,1)S(1)}, bf16[16,4224]{1,0:T(8,128)(2,1)S(1)}, u32[]{:S(2)}, u32[]{:S(2)}) collective-permute-start(bf16[16,4224]{1,0:T(8,128)(2,1)S(1)} %collective-permute-done.4.refs_1_), channel_id=1, source_target_pairs={{0,18},{1,19},{2,16},{3,17},{16,2},{17,3},{18,0},{19,1},{4,22},{5,... | collective-permute-start | bytes 405512 | tf_op jit(solution)/shard_map/member_6/ppermute | solution.py:63
  45.4 8.3 %run_experts.2 = (bf16[128,4096]{1,0:T(8,128)(2,1)S(1)}, bf16[128,4096]{1,0:T(8,128)(2,1)S(1)}, bf16[4096,1536]{1,0:T(8,128)(2,1)S(1)}, bf16[768,4096]{1,0:T(8,128)(2,1)S(1)}) custom-call(s32[1]{0:T(128)} %bitcast.3.expert_ref, bf16[128,4224]{1,0:T(8,128)(2,1)S(1)} %packed.2.own_ref, bf16[128,4224]{1,0:T(8,128)(2,1)S(1)} %collective-permute-done.14.other_ref, ...), custom_call_target="tpu_custom_call" | custom-call | flops 2415919104 | bytes 20971520 | tf_op jit(solution)/shard_map/run_experts/pallas_call | solution.py:431
  54.4 2.0 %collective-permute-done.15.refs_1_ = bf16[128,4096]{1,0:T(8,128)(2,1)S(1)} collective-permute-done((bf16[128,4096]{1,0:T(8,128)(2,1)S(1)}, bf16[128,4096]{1,0:T(8,128)(2,1)S(1)}, u32[]{:S(2)}, u32[]{:S(2)}) %collective-permute-start.15) | collective-permute-done | bytes 1048608 | tf_op jit(solution)/shard_map/member_1/ppermute | solution.py:63
  57.7 1.2 %collective-permute-start.17 = (bf16[32,4096]{1,0:T(8,128)(2,1)S(1)}, bf16[32,4096]{1,0:T(8,128)(2,1)S(1)}, u32[]{:S(2)}, u32[]{:S(2)}) collective-permute-start(bf16[32,4096]{1,0:T(8,128)(2,1)S(1)} %get-tuple-element.65), channel_id=1, source_target_pairs={{0,16},{1,17},{2,18},{3,19},{16,0},{17,1},{18,2},{19,3},{4,20},{5,... | collective-permute-start | bytes 786440 | tf_op jit(solution)/shard_map/member_4/ppermute | solution.py:63
  58.9 5.1 %run_experts.3 = (bf16[128,4096]{1,0:T(8,128)(2,1)S(1)}, bf16[128,4096]{1,0:T(8,128)(2,1)S(1)}) custom-call(s32[1]{0:T(128)} %bitcast.3.expert_ref, bf16[128,4224]{1,0:T(8,128)(2,1)S(1)} %packed.3.own_ref, bf16[128,4224]{1,0:T(8,128)(2,1)S(1)} %collective-permute-done.24.other_ref, bf16[4096,1536]{1,0:T(8,128)(2,1)S(1)} %get-tuple-element.71.refs_0_, ...), custom_call_target="tpu_custom_call" | custom-call | flops 2415919104 | bytes 20971520 | tf_op jit(solution)/shard_map/run_experts/pallas_call | solution.py:431
  65.8 1.6 %collective-permute-start.18 = (bf16[32,4096]{1,0:T(8,128)(2,1)S(1)}, bf16[32,4096]{1,0:T(8,128)(2,1)S(1)}, u32[]{:S(2)}, u32[]{:S(2)}) collective-permute-start(bf16[32,4096]{1,0:T(8,128)(2,1)S(1)} %get-tuple-element.66), channel_id=1, source_target_pairs={{0,18},{1,19},{2,16},{3,17},{16,2},{17,3},{18,0},{19,1},{4,22},{5,... | collective-permute-start | bytes 786440 | tf_op jit(solution)/shard_map/member_6/ppermute | solution.py:63
  70.9 1.4 %collective-permute-start.28 = (bf16[16,4096]{1,0:T(8,128)(2,1)S(1)}, bf16[16,4096]{1,0:T(8,128)(2,1)S(1)}, u32[]{:S(2)}, u32[]{:S(2)}) collective-permute-start(bf16[16,4096]{1,0:T(8,128)(2,1)S(1)} %get-tuple-element.79), channel_id=1, source_target_pairs={{0,18},{1,19},{2,16},{3,17},{16,2},{17,3},{18,0},{19,1},{4,22},{5,... | collective-permute-start | bytes 393224 | tf_op jit(solution)/shard_map/member_6/ppermute | solution.py:63
  72.2 3.6 %collective-permute-done.18.refs_3_ = bf16[32,4096]{1,0:T(8,128)(2,1)S(1)} collective-permute-done((bf16[32,4096]{1,0:T(8,128)(2,1)S(1)}, bf16[32,4096]{1,0:T(8,128)(2,1)S(1)}, u32[]{:S(2)}, u32[]{:S(2)}) %collective-permute-start.18) | collective-permute-done | bytes 262176 | tf_op jit(solution)/shard_map/member_6/ppermute | solution.py:63
  76.7 1.8 %collective-permute-done.26.refs_1_ = bf16[16,4096]{1,0:T(8,128)(2,1)S(1)} collective-permute-done((bf16[16,4096]{1,0:T(8,128)(2,1)S(1)}, bf16[16,4096]{1,0:T(8,128)(2,1)S(1)}, u32[]{:S(2)}, u32[]{:S(2)}) %collective-permute-start.26) | collective-permute-done | bytes 131104 | tf_op jit(solution)/shard_map/member_2/ppermute | solution.py:63
  78.5 2.5 %collective-permute-done.28.refs_3_ = bf16[16,4096]{1,0:T(8,128)(2,1)S(1)} collective-permute-done((bf16[16,4096]{1,0:T(8,128)(2,1)S(1)}, bf16[16,4096]{1,0:T(8,128)(2,1)S(1)}, u32[]{:S(2)}, u32[]{:S(2)}) %collective-permute-start.28) | collective-permute-done | bytes 131104 | tf_op jit(solution)/shard_map/member_6/ppermute | solution.py:63
  83.4 1.3 %collective-permute-done.19.refs_1_ = bf16[16,4096]{1,0:T(8,128)(2,1)S(1)} collective-permute-done((bf16[16,4096]{1,0:T(8,128)(2,1)S(1)}, bf16[16,4096]{1,0:T(8,128)(2,1)S(1)}, u32[]{:S(2)}, u32[]{:S(2)}) %collective-permute-start.19) | collective-permute-done | bytes 131104 | tf_op jit(solution)/shard_map/plane_2/ppermute | solution.py:52
  84.7 1.5 %collective-permute-start.32 = (bf16[16,4096]{1,0:T(8,128)(2,1)S(1)}, bf16[16,4096]{1,0:T(8,128)(2,1)S(1)}, u32[]{:S(2)}, u32[]{:S(2)}) collective-permute-start(bf16[16,4096]{1,0:T(8,128)(2,1)S(1)} %get-tuple-element.83), channel_id=1, source_target_pairs={{0,18},{1,19},{2,16},{3,17},{16,2},{17,3},{18,0},{19,1},{4,22},{5,... | collective-permute-start | bytes 393224 | tf_op jit(solution)/shard_map/member_6/ppermute | solution.py:63
  86.2 2.0 %collective-permute-done.29.refs_3_ = bf16[16,4096]{1,0:T(8,128)(2,1)S(1)} collective-permute-done((bf16[16,4096]{1,0:T(8,128)(2,1)S(1)}, bf16[16,4096]{1,0:T(8,128)(2,1)S(1)}, u32[]{:S(2)}, u32[]{:S(2)}) %collective-permute-start.29) | collective-permute-done | bytes 131104 | tf_op jit(solution)/shard_map/plane_3/ppermute | solution.py:52
  88.3 2.3 %collective-permute-done.32.refs_4_ = bf16[16,4096]{1,0:T(8,128)(2,1)S(1)} collective-permute-done((bf16[16,4096]{1,0:T(8,128)(2,1)S(1)}, bf16[16,4096]{1,0:T(8,128)(2,1)S(1)}, u32[]{:S(2)}, u32[]{:S(2)}) %collective-permute-start.32) | collective-permute-done | bytes 131104 | tf_op jit(solution)/shard_map/member_6/ppermute | solution.py:63
  (59 shorter events, 17.3 us)
Async XLA Ops:
  0.6 4.7 %collective-permute-start = (s32[16]{0:T(128)}, s32[16]{0:T(128)S(1)}, u32[]{:S(2)}, u32[]{:S(2)}) collective-permute-start(s32[16]{0:T(128)} %param.17), channel_id=1, source_target_pairs={{0,16},{16,0},{1,17},{17,1},{2,18},{18,2},{3,19},{19,3},{4,20},{20... | collective-permute-start | bytes 200 | tf_op jit(solution)/shard_map/ppermute | solution.py:68
  7.0 7.2 %collective-permute-start.1 = (bf16[16,16,512]{2,1,0:T(8,128)(2,1)S(1)}, bf16[16,16,512]{2,1,0:T(8,128)(2,1)S(1)}, u32[]{:S(2)}, u32[]{:S(2)}) collective-permute-start(bf16[16,16,512]{2,1,0:T(8,128)(2,1)S(1)} %pick_pages.1), channel_id=1, source_target_pairs={{0,16},{16,0},{1,17},{17,1},{2,18},{18,2},{3,19},{19,3},{4,20},{20... | collective-permute-start | bytes 786440 | tf_op jit(solution)/shard_map/ppermute | solution.py:68
  16.2 7.9 %collective-permute-start.3 = (bf16[16,4224]{1,0:T(8,128)(2,1)S(1)}, bf16[16,4224]{1,0:T(8,128)(2,1)S(1)}, u32[]{:S(2)}, u32[]{:S(2)}) collective-permute-start(bf16[16,4224]{1,0:T(8,128)(2,1)S(1)} %get-tuple-element.69.refs_0_), channel_id=1, source_target_pairs={{0,8},{1,9},{2,10},{3,11},{16,24},{17,25},{18,26},{19,27},{4,12},{... | collective-permute-start | bytes 405512 | tf_op jit(solution)/shard_map/plane_2/ppermute | solution.py:52
  19.0 6.1 %collective-permute-start.2 = (bf16[16,4224]{1,0:T(8,128)(2,1)S(1)}, bf16[16,4224]{1,0:T(8,128)(2,1)S(1)}, u32[]{:S(2)}, u32[]{:S(2)}) collective-permute-start(bf16[16,4224]{1,0:T(8,128)(2,1)S(1)} %get-tuple-element.69.refs_0_), channel_id=1, source_target_pairs={{0,4},{1,5},{2,6},{3,7},{16,20},{17,21},{18,22},{19,23},{4,0},{5,1... | collective-permute-start | bytes 405512 | tf_op jit(solution)/shard_map/plane_1/ppermute | solution.py:52
  20.6 7.4 %collective-permute-start.5 = (bf16[16,4224]{1,0:T(8,128)(2,1)S(1)}, bf16[16,4224]{1,0:T(8,128)(2,1)S(1)}, u32[]{:S(2)}, u32[]{:S(2)}) collective-permute-start(bf16[16,4224]{1,0:T(8,128)(2,1)S(1)} %get-tuple-element.69.refs_0_), channel_id=1, source_target_pairs={{0,2},{1,3},{2,0},{3,1},{16,18},{17,19},{18,16},{19,17},{4,6},{5,7... | collective-permute-start | bytes 405512 | tf_op jit(solution)/shard_map/member_2/ppermute | solution.py:63
  22.1 7.9 %collective-permute-start.8 = (bf16[16,4224]{1,0:T(8,128)(2,1)S(1)}, bf16[16,4224]{1,0:T(8,128)(2,1)S(1)}, u32[]{:S(2)}, u32[]{:S(2)}) collective-permute-start(bf16[16,4224]{1,0:T(8,128)(2,1)S(1)} %get-tuple-element.69.refs_0_), channel_id=1, source_target_pairs={{0,16},{1,17},{2,18},{3,19},{16,0},{17,1},{18,2},{19,3},{4,20},{5,... | collective-permute-start | bytes 405512 | tf_op jit(solution)/shard_map/member_4/ppermute | solution.py:63
  23.6 7.4 %collective-permute-start.11 = (bf16[16,4224]{1,0:T(8,128)(2,1)S(1)}, bf16[16,4224]{1,0:T(8,128)(2,1)S(1)}, u32[]{:S(2)}, u32[]{:S(2)}) collective-permute-start(bf16[16,4224]{1,0:T(8,128)(2,1)S(1)} %get-tuple-element.69.refs_0_), channel_id=1, source_target_pairs={{0,18},{1,19},{2,16},{3,17},{16,2},{17,3},{18,0},{19,1},{4,22},{5,... | collective-permute-start | bytes 405512 | tf_op jit(solution)/shard_map/member_6/ppermute | solution.py:63
  24.1 8.0 %collective-permute-start.4 = (bf16[16,4224]{1,0:T(8,128)(2,1)S(1)}, bf16[16,4224]{1,0:T(8,128)(2,1)S(1)}, u32[]{:S(2)}, u32[]{:S(2)}) collective-permute-start(bf16[16,4224]{1,0:T(8,128)(2,1)S(1)} %collective-permute-done.3.refs_1_), channel_id=1, source_target_pairs={{0,4},{1,5},{2,6},{3,7},{16,20},{17,21},{18,22},{19,23},{4,0},{5,1... | collective-permute-start | bytes 405512 | tf_op jit(solution)/shard_map/plane_1/ppermute | solution.py:52
  28.0 7.8 %collective-permute-start.6 = (bf16[16,4224]{1,0:T(8,128)(2,1)S(1)}, bf16[16,4224]{1,0:T(8,128)(2,1)S(1)}, u32[]{:S(2)}, u32[]{:S(2)}) collective-permute-start(bf16[16,4224]{1,0:T(8,128)(2,1)S(1)} %collective-permute-done.2.refs_0_), channel_id=1, source_target_pairs={{0,2},{1,3},{2,0},{3,1},{16,18},{17,19},{18,16},{19,17},{4,6},{5,7... | collective-permute-start | bytes 405512 | tf_op jit(solution)/shard_map/member_2/ppermute | solution.py:63
  28.8 8.6 %collective-permute-start.7 = (bf16[16,4224]{1,0:T(8,128)(2,1)S(1)}, bf16[16,4224]{1,0:T(8,128)(2,1)S(1)}, u32[]{:S(2)}, u32[]{:S(2)}) collective-permute-start(bf16[16,4224]{1,0:T(8,128)(2,1)S(1)} %collective-permute-done.3.refs_1_), channel_id=1, source_target_pairs={{0,2},{1,3},{2,0},{3,1},{16,18},{17,19},{18,16},{19,17},{4,6},{5,7... | collective-permute-start | bytes 405512 | tf_op jit(solution)/shard_map/member_2/ppermute | solution.py:63
  30.0 7.4 %collective-permute-start.9 = (bf16[16,4224]{1,0:T(8,128)(2,1)S(1)}, bf16[16,4224]{1,0:T(8,128)(2,1)S(1)}, u32[]{:S(2)}, u32[]{:S(2)}) collective-permute-start(bf16[16,4224]{1,0:T(8,128)(2,1)S(1)} %collective-permute-done.2.refs_0_), channel_id=1, source_target_pairs={{0,16},{1,17},{2,18},{3,19},{16,0},{17,1},{18,2},{19,3},{4,20},{5,... | collective-permute-start | bytes 405512 | tf_op jit(solution)/shard_map/member_4/ppermute | solution.py:63
  31.0 6.4 %collective-permute-start.10 = (bf16[16,4224]{1,0:T(8,128)(2,1)S(1)}, bf16[16,4224]{1,0:T(8,128)(2,1)S(1)}, u32[]{:S(2)}, u32[]{:S(2)}) collective-permute-start(bf16[16,4224]{1,0:T(8,128)(2,1)S(1)} %collective-permute-done.3.refs_1_), channel_id=1, source_target_pairs={{0,16},{1,17},{2,18},{3,19},{16,0},{17,1},{18,2},{19,3},{4,20},{5,... | collective-permute-start | bytes 405512 | tf_op jit(solution)/shard_map/member_4/ppermute | solution.py:63
  32.1 6.6 %collective-permute-start.12 = (bf16[16,4224]{1,0:T(8,128)(2,1)S(1)}, bf16[16,4224]{1,0:T(8,128)(2,1)S(1)}, u32[]{:S(2)}, u32[]{:S(2)}) collective-permute-start(bf16[16,4224]{1,0:T(8,128)(2,1)S(1)} %collective-permute-done.2.refs_0_), channel_id=1, source_target_pairs={{0,18},{1,19},{2,16},{3,17},{16,2},{17,3},{18,0},{19,1},{4,22},{5,... | collective-permute-start | bytes 405512 | tf_op jit(solution)/shard_map/member_6/ppermute | solution.py:63
  35.8 5.9 %collective-permute-start.13 = (bf16[16,4224]{1,0:T(8,128)(2,1)S(1)}, bf16[16,4224]{1,0:T(8,128)(2,1)S(1)}, u32[]{:S(2)}, u32[]{:S(2)}) collective-permute-start(bf16[16,4224]{1,0:T(8,128)(2,1)S(1)} %collective-permute-done.3.refs_1_), channel_id=1, source_target_pairs={{0,18},{1,19},{2,16},{3,17},{16,2},{17,3},{18,0},{19,1},{4,22},{5,... | collective-permute-start | bytes 405512 | tf_op jit(solution)/shard_map/member_6/ppermute | solution.py:63
  41.7 3.6 %collective-permute-start.14 = (bf16[128,4224]{1,0:T(8,128)(2,1)S(1)}, bf16[128,4224]{1,0:T(8,128)(2,1)S(1)}, u32[]{:S(2)}, u32[]{:S(2)}) collective-permute-start(bf16[128,4224]{1,0:T(8,128)(2,1)S(1)} %packed.2.own_ref), channel_id=1, source_target_pairs={{0,1},{1,0},{2,3},{3,2},{16,17},{17,16},{18,19},{19,18},{4,5},{5,4... | collective-permute-start | bytes 3244040 | tf_op jit(solution)/shard_map/member_1/ppermute | solution.py:63
  41.8 11.9 %collective-permute-start.21 = (bf16[16,4224]{1,0:T(8,128)(2,1)S(1)}, bf16[16,4224]{1,0:T(8,128)(2,1)S(1)}, u32[]{:S(2)}, u32[]{:S(2)}) collective-permute-start(bf16[16,4224]{1,0:T(8,128)(2,1)S(1)} %collective-permute-done.4.refs_1_), channel_id=1, source_target_pairs={{0,2},{1,3},{2,0},{3,1},{16,18},{17,19},{18,16},{19,17},{4,6},{5,7... | collective-permute-start | bytes 405512 | tf_op jit(solution)/shard_map/member_2/ppermute | solution.py:63
  42.9 10.9 %collective-permute-start.22 = (bf16[16,4224]{1,0:T(8,128)(2,1)S(1)}, bf16[16,4224]{1,0:T(8,128)(2,1)S(1)}, u32[]{:S(2)}, u32[]{:S(2)}) collective-permute-start(bf16[16,4224]{1,0:T(8,128)(2,1)S(1)} %collective-permute-done.4.refs_1_), channel_id=1, source_target_pairs={{0,16},{1,17},{2,18},{3,19},{16,0},{17,1},{18,2},{19,3},{4,20},{5,... | collective-permute-start | bytes 405512 | tf_op jit(solution)/shard_map/member_4/ppermute | solution.py:63
  44.1 9.7 %collective-permute-start.23 = (bf16[16,4224]{1,0:T(8,128)(2,1)S(1)}, bf16[16,4224]{1,0:T(8,128)(2,1)S(1)}, u32[]{:S(2)}, u32[]{:S(2)}) collective-permute-start(bf16[16,4224]{1,0:T(8,128)(2,1)S(1)} %collective-permute-done.4.refs_1_), channel_id=1, source_target_pairs={{0,18},{1,19},{2,16},{3,17},{16,2},{17,3},{18,0},{19,1},{4,22},{5,... | collective-permute-start | bytes 405512 | tf_op jit(solution)/shard_map/member_6/ppermute | solution.py:63
  53.7 2.7 %collective-permute-start.15 = (bf16[128,4096]{1,0:T(8,128)(2,1)S(1)}, bf16[128,4096]{1,0:T(8,128)(2,1)S(1)}, u32[]{:S(2)}, u32[]{:S(2)}) collective-permute-start(bf16[128,4096]{1,0:T(8,128)(2,1)S(1)} %get-tuple-element.62), channel_id=1, source_target_pairs={{0,1},{1,0},{2,3},{3,2},{16,17},{17,16},{18,19},{19,18},{4,5},{5,4... | collective-permute-start | bytes 3145736 | tf_op jit(solution)/shard_map/member_1/ppermute | solution.py:63
  53.9 5.0 %collective-permute-start.24 = (bf16[128,4224]{1,0:T(8,128)(2,1)S(1)}, bf16[128,4224]{1,0:T(8,128)(2,1)S(1)}, u32[]{:S(2)}, u32[]{:S(2)}) collective-permute-start(bf16[128,4224]{1,0:T(8,128)(2,1)S(1)} %packed.3.own_ref), channel_id=1, source_target_pairs={{0,1},{1,0},{2,3},{3,2},{16,17},{17,16},{18,19},{19,18},{4,5},{5,4... | collective-permute-start | bytes 3244040 | tf_op jit(solution)/shard_map/member_1/ppermute | solution.py:63
  56.7 8.4 %collective-permute-start.16 = (bf16[32,4096]{1,0:T(8,128)(2,1)S(1)}, bf16[32,4096]{1,0:T(8,128)(2,1)S(1)}, u32[]{:S(2)}, u32[]{:S(2)}) collective-permute-start(bf16[32,4096]{1,0:T(8,128)(2,1)S(1)} %get-tuple-element.64), channel_id=1, source_target_pairs={{0,2},{1,3},{2,0},{3,1},{16,18},{17,19},{18,16},{19,17},{4,6},{5,7... | collective-permute-start | bytes 786440 | tf_op jit(solution)/shard_map/member_2/ppermute | solution.py:63
  57.7 8.1 %collective-permute-start.17 = (bf16[32,4096]{1,0:T(8,128)(2,1)S(1)}, bf16[32,4096]{1,0:T(8,128)(2,1)S(1)}, u32[]{:S(2)}, u32[]{:S(2)}) collective-permute-start(bf16[32,4096]{1,0:T(8,128)(2,1)S(1)} %get-tuple-element.65), channel_id=1, source_target_pairs={{0,16},{1,17},{2,18},{3,19},{16,0},{17,1},{18,2},{19,3},{4,20},{5,... | collective-permute-start | bytes 786440 | tf_op jit(solution)/shard_map/member_4/ppermute | solution.py:63
  65.8 10.0 %collective-permute-start.18 = (bf16[32,4096]{1,0:T(8,128)(2,1)S(1)}, bf16[32,4096]{1,0:T(8,128)(2,1)S(1)}, u32[]{:S(2)}, u32[]{:S(2)}) collective-permute-start(bf16[32,4096]{1,0:T(8,128)(2,1)S(1)} %get-tuple-element.66), channel_id=1, source_target_pairs={{0,18},{1,19},{2,16},{3,17},{16,2},{17,3},{18,0},{19,1},{4,22},{5,... | collective-permute-start | bytes 786440 | tf_op jit(solution)/shard_map/member_6/ppermute | solution.py:63
  68.7 9.9 %collective-permute-start.26 = (bf16[16,4096]{1,0:T(8,128)(2,1)S(1)}, bf16[16,4096]{1,0:T(8,128)(2,1)S(1)}, u32[]{:S(2)}, u32[]{:S(2)}) collective-permute-start(bf16[16,4096]{1,0:T(8,128)(2,1)S(1)} %get-tuple-element.77), channel_id=1, source_target_pairs={{0,2},{1,3},{2,0},{3,1},{16,18},{17,19},{18,16},{19,17},{4,6},{5,7... | collective-permute-start | bytes 393224 | tf_op jit(solution)/shard_map/member_2/ppermute | solution.py:63
  69.8 8.8 %collective-permute-start.27 = (bf16[16,4096]{1,0:T(8,128)(2,1)S(1)}, bf16[16,4096]{1,0:T(8,128)(2,1)S(1)}, u32[]{:S(2)}, u32[]{:S(2)}) collective-permute-start(bf16[16,4096]{1,0:T(8,128)(2,1)S(1)} %get-tuple-element.78), channel_id=1, source_target_pairs={{0,16},{1,17},{2,18},{3,19},{16,0},{17,1},{18,2},{19,3},{4,20},{5,... | collective-permute-start | bytes 393224 | tf_op jit(solution)/shard_map/member_4/ppermute | solution.py:63
  70.9 10.2 %collective-permute-start.28 = (bf16[16,4096]{1,0:T(8,128)(2,1)S(1)}, bf16[16,4096]{1,0:T(8,128)(2,1)S(1)}, u32[]{:S(2)}, u32[]{:S(2)}) collective-permute-start(bf16[16,4096]{1,0:T(8,128)(2,1)S(1)} %get-tuple-element.79), channel_id=1, source_target_pairs={{0,18},{1,19},{2,16},{3,17},{16,2},{17,3},{18,0},{19,1},{4,22},{5,... | collective-permute-start | bytes 393224 | tf_op jit(solution)/shard_map/member_6/ppermute | solution.py:63
  76.0 8.7 %collective-permute-start.19 = (bf16[16,4096]{1,0:T(8,128)(2,1)S(1)}, bf16[16,4096]{1,0:T(8,128)(2,1)S(1)}, u32[]{:S(2)}, u32[]{:S(2)}) collective-permute-start(bf16[16,4096]{1,0:T(8,128)(2,1)S(1)} %get-tuple-element.67), channel_id=1, source_target_pairs={{0,8},{1,9},{2,10},{3,11},{16,24},{17,25},{18,26},{19,27},{4,12},{... | collective-permute-start | bytes 393224 | tf_op jit(solution)/shard_map/plane_2/ppermute | solution.py:52
  76.3 9.9 %collective-permute-start.20 = (bf16[16,4096]{1,0:T(8,128)(2,1)S(1)}, bf16[16,4096]{1,0:T(8,128)(2,1)S(1)}, u32[]{:S(2)}, u32[]{:S(2)}) collective-permute-start(bf16[16,4096]{1,0:T(8,128)(2,1)S(1)} %get-tuple-element.68), channel_id=1, source_target_pairs={{0,4},{1,5},{2,6},{3,7},{16,20},{17,21},{18,22},{19,23},{4,0},{5,1... | collective-permute-start | bytes 393224 | tf_op jit(solution)/shard_map/plane_1/ppermute | solution.py:52
  81.1 7.1 %collective-permute-start.29 = (bf16[16,4096]{1,0:T(8,128)(2,1)S(1)}, bf16[16,4096]{1,0:T(8,128)(2,1)S(1)}, u32[]{:S(2)}, u32[]{:S(2)}) collective-permute-start(bf16[16,4096]{1,0:T(8,128)(2,1)S(1)} %add_chips.3), channel_id=1, source_target_pairs={{0,12},{1,13},{2,14},{3,15},{16,28},{17,29},{18,30},{19,31},{4,8},... | collective-permute-start | bytes 393224 | tf_op jit(solution)/shard_map/plane_3/ppermute | solution.py:52
  81.2 7.1 %collective-permute-start.30 = (bf16[16,4096]{1,0:T(8,128)(2,1)S(1)}, bf16[16,4096]{1,0:T(8,128)(2,1)S(1)}, u32[]{:S(2)}, u32[]{:S(2)}) collective-permute-start(bf16[16,4096]{1,0:T(8,128)(2,1)S(1)} %get-tuple-element.81), channel_id=1, source_target_pairs={{0,2},{1,3},{2,0},{3,1},{16,18},{17,19},{18,16},{19,17},{4,6},{5,7... | collective-permute-start | bytes 393224 | tf_op jit(solution)/shard_map/member_2/ppermute | solution.py:63
  82.3 6.0 %collective-permute-start.31 = (bf16[16,4096]{1,0:T(8,128)(2,1)S(1)}, bf16[16,4096]{1,0:T(8,128)(2,1)S(1)}, u32[]{:S(2)}, u32[]{:S(2)}) collective-permute-start(bf16[16,4096]{1,0:T(8,128)(2,1)S(1)} %get-tuple-element.82), channel_id=1, source_target_pairs={{0,16},{1,17},{2,18},{3,19},{16,0},{17,1},{18,2},{19,3},{4,20},{5,... | collective-permute-start | bytes 393224 | tf_op jit(solution)/shard_map/member_4/ppermute | solution.py:63
  84.7 6.0 %collective-permute-start.32 = (bf16[16,4096]{1,0:T(8,128)(2,1)S(1)}, bf16[16,4096]{1,0:T(8,128)(2,1)S(1)}, u32[]{:S(2)}, u32[]{:S(2)}) collective-permute-start(bf16[16,4096]{1,0:T(8,128)(2,1)S(1)} %get-tuple-element.83), channel_id=1, source_target_pairs={{0,18},{1,19},{2,16},{3,17},{16,2},{17,3},{18,0},{19,1},{4,22},{5,... | collective-permute-start | bytes 393224 | tf_op jit(solution)/shard_map/member_6/ppermute | solution.py:63
  (7 other events, 46.5 us)

commit v14 on v11

--- a/solution.py
+++ b/solution.py
@@ -635,7 +635,10 @@
     totals = add_up([[part] for part in parts], [count_of_rows] * len(near), "add_chips")
     others = [layout.shifted(total, by) for total, by in list(zip(totals, near))[::-1]]
     for i, by in list(enumerate(far))[:0:-1]:
-        others.append(layout.shifted(total_of(to_owners(far_sums, i)), by))
+        first = total_of(to_owners(far_sums, i))
+        others.append(layout.shifted(first, by))
+    for c in (1, 2, 3):
+        far_sums[c * len(far)] = after(far_sums[c * len(far)], first)
     merged = add_up(
         [[merged]] + [[part] for part in others], [count_of_rows], "add_first", 10**10
     )[0]

time: 89.8 us -> 89.2 us (level)
  starting transfers between devices: 42.9 us -> 41.8 us
    ppermute x25, waiting for transfers between devices: 15.6 us -> 18.4 us  [swapped(): return lax.ppermute(value, AXES, pairs)]
    ppermute x6, waiting for transfers between devices: 4.77 us -> 2.34 us  [shifted(): return lax.ppermute(value, AXES, pairs)]
    ppermute x6, starting transfers between devices: 10.4 us -> 8.94 us  [shifted(): return lax.ppermute(value, AXES, pairs)]
where the time goes in v14:
time: 89.2 us; the launch traced here: 88.8 us
  starting transfers between devices  41.8 us (47%)
  waiting for transfers between devices  22.8 us (26%)
  Pallas kernels  22.6 us (25%)
    ppermute x25, starting transfers between devices, swapped(): return lax.ppermute(value, AXES, pairs)  27.8 us
    ppermute x25, waiting for transfers between devices, swapped(): return lax.ppermute(value, AXES, pairs)  18.4 us
    pallas_call x2, Pallas kernels, run_experts(): pl.pallas_call(kernel, out_shape=(shape, shape) + kept, in_specs=[SMEM, V...  13.4 us
    ppermute x6, starting transfers between devices, shifted(): return lax.ppermute(value, AXES, pairs)  8.94 us
    ppermute x2, starting transfers between devices, from_behind(): lax.ppermute(value, axis, [(i, (i + by) % length) for i in range(length)])  5.09 us
    pallas_call x1, Pallas kernels, own_attention(): pl.pallas_call(kernel, out_shape=(shape, shape, shape, jax.ShapeDtypeStru...  4.74 us
    ppermute x6, waiting for transfers between devices, shifted(): return lax.ppermute(value, AXES, pairs)  2.34 us
    ppermute x2, waiting for transfers between devices, from_behind(): lax.ppermute(value, axis, [(i, (i + by) % length) for i in range(length)])  2.06 us
  transfers between devices with their start and end apart: 33, of which 18 were waited for; matrix products, arithmetic and copies ran while one was open for 0% of the time, Pallas kernels for 21%

profile of v14, /device:TPU:0, one launch (start us, length us, event | category | flops | bytes accessed | tf_op | source)
XLA Modules:
  0.0 88.8 jit_solution(12727197059982991074)
XLA Ops:
  0.6 3.0 %collective-permute-start = (s32[16]{0:T(128)}, s32[16]{0:T(128)S(1)}, u32[]{:S(2)}, u32[]{:S(2)}) collective-permute-start(s32[16]{0:T(128)} %param.17), channel_id=1, source_target_pairs={{0,16},{16,0},{1,17},{17,1},{2,18},{18,2},{3,19},{19,3},{4,20},{20... | collective-permute-start | bytes 200 | tf_op jit(solution)/shard_map/ppermute | solution.py:68
  3.6 1.7 %collective-permute-done.slots_ref = s32[16]{0:T(128)S(1)} collective-permute-done((s32[16]{0:T(128)}, s32[16]{0:T(128)S(1)}, u32[]{:S(2)}, u32[]{:S(2)}) %collective-permute-start) | collective-permute-done | bytes 96 | tf_op jit(solution)/shard_map/ppermute | solution.py:68
  5.3 1.6 %pick_pages.1 = bf16[16,16,512]{2,1,0:T(8,128)(2,1)S(1)} custom-call(s32[16]{0:T(128)S(1)} %collective-permute-done.slots_ref, bf16[128,16,512]{2,1,0:T(8,128)(2,1)} %pages_hbm.1), custom_call_target="tpu_custom_call" | custom-call | bytes 1048576 | tf_op jit(solution)/shard_map/pick_pages/pallas_call | solution.py:84
  7.0 2.1 %collective-permute-start.1 = (bf16[16,16,512]{2,1,0:T(8,128)(2,1)S(1)}, bf16[16,16,512]{2,1,0:T(8,128)(2,1)S(1)}, u32[]{:S(2)}, u32[]{:S(2)}) collective-permute-start(bf16[16,16,512]{2,1,0:T(8,128)(2,1)S(1)} %pick_pages.1), channel_id=1, source_target_pairs={{0,16},{16,0},{1,17},{17,1},{2,18},{18,2},{3,19},{19,3},{4,20},{20... | collective-permute-start | bytes 786440 | tf_op jit(solution)/shard_map/ppermute | solution.py:68
  9.0 4.7 %own_attention.1 = (f32[512,128]{1,0:T(8,128)S(1)}, f32[512,128]{1,0:T(8,128)S(1)}, f32[512,128]{1,0:T(8,128)S(1)}, bf16[512,128]{1,0:T(8,128)(2,1)S(1)}) custom-call(bf16[16,4096]{1,0:T(8,128)(2,1)} %queries_hbm, bf16[16,512]{1,0:T(8,128)(2,1)} %new_hbm.1, bf16[128,16,512]{2,1,0:T(8,128)(2,1)} %pages_hbm.1, s32[16,16]{1,0:T(8,128)} %table_ref.1, s32[16]{0:T(128)} %lengths_ref.1), custom_call_target="tpu_custom_call" | custom-call | flops 1073741824 | bytes 16777216 | tf_op jit(solution)/shard_map/own_attention/pallas_call | solution.py:239
  14.2 1.9 %finish_attention.1 = (bf16[16,4096]{1,0:T(8,128)(2,1)}, bf16[16,4096]{1,0:T(8,128)(2,1)S(1)}, bf16[16,4224]{1,0:T(8,128)(2,1)S(1)}) custom-call(bf16[512,128]{1,0:T(8,128)(2,1)S(1)} %get-tuple-element.47.q_ref, bf16[16,16,512]{2,1,0:T(8,128)(2,1)S(1)} %collective-permute-done.1.fetched_ref, s32[16,16]{1,0:T(8,128)S(1)} %copy-done.2, s32[16]{0:T(128)S(1)} %copy-done.5, ...), custom_call_target="tpu_custom_call" | custom-call | flops 134217728 | bytes 4194304 | tf_op jit(solution)/shard_map/finish_attention/pallas_call | solution.py:538
  16.2 2.8 %collective-permute-start.3 = (bf16[16,4224]{1,0:T(8,128)(2,1)S(1)}, bf16[16,4224]{1,0:T(8,128)(2,1)S(1)}, u32[]{:S(2)}, u32[]{:S(2)}) collective-permute-start(bf16[16,4224]{1,0:T(8,128)(2,1)S(1)} %get-tuple-element.72.refs_0_), channel_id=1, source_target_pairs={{0,8},{1,9},{2,10},{3,11},{16,24},{17,25},{18,26},{19,27},{4,12},{... | collective-permute-start | bytes 405512 | tf_op jit(solution)/shard_map/plane_2/ppermute | solution.py:52
  19.0 2.4 %collective-permute-start.11 = (bf16[16,4224]{1,0:T(8,128)(2,1)S(1)}, bf16[16,4224]{1,0:T(8,128)(2,1)S(1)}, u32[]{:S(2)}, u32[]{:S(2)}) collective-permute-start(bf16[16,4224]{1,0:T(8,128)(2,1)S(1)} %get-tuple-element.72.refs_0_), channel_id=1, source_target_pairs={{0,18},{1,19},{2,16},{3,17},{16,2},{17,3},{18,0},{19,1},{4,22},{5,... | collective-permute-start | bytes 405512 | tf_op jit(solution)/shard_map/member_6/ppermute | solution.py:63
  22.5 1.6 %collective-permute-start.2 = (bf16[16,4224]{1,0:T(8,128)(2,1)S(1)}, bf16[16,4224]{1,0:T(8,128)(2,1)S(1)}, u32[]{:S(2)}, u32[]{:S(2)}) collective-permute-start(bf16[16,4224]{1,0:T(8,128)(2,1)S(1)} %get-tuple-element.72.refs_0_), channel_id=1, source_target_pairs={{0,4},{1,5},{2,6},{3,7},{16,20},{17,21},{18,22},{19,23},{4,0},{5,1... | collective-permute-start | bytes 405512 | tf_op jit(solution)/shard_map/plane_1/ppermute | solution.py:52
  25.0 2.4 %collective-permute-start.13 = (bf16[16,4224]{1,0:T(8,128)(2,1)S(1)}, bf16[16,4224]{1,0:T(8,128)(2,1)S(1)}, u32[]{:S(2)}, u32[]{:S(2)}) collective-permute-start(bf16[16,4224]{1,0:T(8,128)(2,1)S(1)} %collective-permute-done.3.refs_1_), channel_id=1, source_target_pairs={{0,18},{1,19},{2,16},{3,17},{16,2},{17,3},{18,0},{19,1},{4,22},{5,... | collective-permute-start | bytes 405512 | tf_op jit(solution)/shard_map/member_6/ppermute | solution.py:63
  27.8 1.4 %collective-permute-start.10 = (bf16[16,4224]{1,0:T(8,128)(2,1)S(1)}, bf16[16,4224]{1,0:T(8,128)(2,1)S(1)}, u32[]{:S(2)}, u32[]{:S(2)}) collective-permute-start(bf16[16,4224]{1,0:T(8,128)(2,1)S(1)} %collective-permute-done.3.refs_1_), channel_id=1, source_target_pairs={{0,16},{1,17},{2,18},{3,19},{16,0},{17,1},{18,2},{19,3},{4,20},{5,... | collective-permute-start | bytes 405512 | tf_op jit(solution)/shard_map/member_4/ppermute | solution.py:63
  30.2 1.9 %collective-permute-start.12 = (bf16[16,4224]{1,0:T(8,128)(2,1)S(1)}, bf16[16,4224]{1,0:T(8,128)(2,1)S(1)}, u32[]{:S(2)}, u32[]{:S(2)}) collective-permute-start(bf16[16,4224]{1,0:T(8,128)(2,1)S(1)} %collective-permute-done.2.refs_0_), channel_id=1, source_target_pairs={{0,18},{1,19},{2,16},{3,17},{16,2},{17,3},{18,0},{19,1},{4,22},{5,... | collective-permute-start | bytes 405512 | tf_op jit(solution)/shard_map/member_6/ppermute | solution.py:63
  32.7 1.3 %collective-permute-start.6 = (bf16[16,4224]{1,0:T(8,128)(2,1)S(1)}, bf16[16,4224]{1,0:T(8,128)(2,1)S(1)}, u32[]{:S(2)}, u32[]{:S(2)}) collective-permute-start(bf16[16,4224]{1,0:T(8,128)(2,1)S(1)} %collective-permute-done.2.refs_0_), channel_id=1, source_target_pairs={{0,2},{1,3},{2,0},{3,1},{16,18},{17,19},{18,16},{19,17},{4,6},{5,7... | collective-permute-start | bytes 405512 | tf_op jit(solution)/shard_map/member_2/ppermute | solution.py:63
  34.0 1.2 %collective-permute-done.10.refs_5_ = bf16[16,4224]{1,0:T(8,128)(2,1)S(1)} collective-permute-done((bf16[16,4224]{1,0:T(8,128)(2,1)S(1)}, bf16[16,4224]{1,0:T(8,128)(2,1)S(1)}, u32[]{:S(2)}, u32[]{:S(2)}) %collective-permute-start.10) | collective-permute-done | bytes 135200 | tf_op jit(solution)/shard_map/member_4/ppermute | solution.py:63
  35.2 1.7 %collective-permute-done.7.refs_3_ = bf16[16,4224]{1,0:T(8,128)(2,1)S(1)} collective-permute-done((bf16[16,4224]{1,0:T(8,128)(2,1)S(1)}, bf16[16,4224]{1,0:T(8,128)(2,1)S(1)}, u32[]{:S(2)}, u32[]{:S(2)}) %collective-permute-start.7) | collective-permute-done | bytes 135200 | tf_op jit(solution)/shard_map/member_2/ppermute | solution.py:63
  36.9 1.2 %collective-permute-done.9.refs_4_ = bf16[16,4224]{1,0:T(8,128)(2,1)S(1)} collective-permute-done((bf16[16,4224]{1,0:T(8,128)(2,1)S(1)}, bf16[16,4224]{1,0:T(8,128)(2,1)S(1)}, u32[]{:S(2)}, u32[]{:S(2)}) %collective-permute-start.9) | collective-permute-done | bytes 135200 | tf_op jit(solution)/shard_map/member_4/ppermute | solution.py:63
  38.5 1.3 %collective-permute-start.21 = (bf16[16,4224]{1,0:T(8,128)(2,1)S(1)}, bf16[16,4224]{1,0:T(8,128)(2,1)S(1)}, u32[]{:S(2)}, u32[]{:S(2)}) collective-permute-start(bf16[16,4224]{1,0:T(8,128)(2,1)S(1)} %collective-permute-done.4.refs_1_), channel_id=1, source_target_pairs={{0,2},{1,3},{2,0},{3,1},{16,18},{17,19},{18,16},{19,17},{4,6},{5,7... | collective-permute-start | bytes 405512 | tf_op jit(solution)/shard_map/member_2/ppermute | solution.py:63
  39.8 1.4 %collective-permute-start.22 = (bf16[16,4224]{1,0:T(8,128)(2,1)S(1)}, bf16[16,4224]{1,0:T(8,128)(2,1)S(1)}, u32[]{:S(2)}, u32[]{:S(2)}) collective-permute-start(bf16[16,4224]{1,0:T(8,128)(2,1)S(1)} %collective-permute-done.4.refs_1_), channel_id=1, source_target_pairs={{0,16},{1,17},{2,18},{3,19},{16,0},{17,1},{18,2},{19,3},{4,20},{5,... | collective-permute-start | bytes 405512 | tf_op jit(solution)/shard_map/member_4/ppermute | solution.py:63
  42.1 8.3 %run_experts.2 = (bf16[128,4096]{1,0:T(8,128)(2,1)S(1)}, bf16[128,4096]{1,0:T(8,128)(2,1)S(1)}, bf16[4096,1536]{1,0:T(8,128)(2,1)S(1)}, bf16[768,4096]{1,0:T(8,128)(2,1)S(1)}) custom-call(s32[1]{0:T(128)} %bitcast.3.expert_ref, bf16[128,4224]{1,0:T(8,128)(2,1)S(1)} %packed.2.own_ref, bf16[128,4224]{1,0:T(8,128)(2,1)S(1)} %collective-permute-done.14.other_ref, ...), custom_call_target="tpu_custom_call" | custom-call | flops 2415919104 | bytes 20971520 | tf_op jit(solution)/shard_map/run_experts/pallas_call | solution.py:431
  51.1 2.0 %collective-permute-done.15.refs_1_ = bf16[128,4096]{1,0:T(8,128)(2,1)S(1)} collective-permute-done((bf16[128,4096]{1,0:T(8,128)(2,1)S(1)}, bf16[128,4096]{1,0:T(8,128)(2,1)S(1)}, u32[]{:S(2)}, u32[]{:S(2)}) %collective-permute-start.15) | collective-permute-done | bytes 1048608 | tf_op jit(solution)/shard_map/member_1/ppermute | solution.py:63
  53.3 1.3 %collective-permute-start.16 = (bf16[32,4096]{1,0:T(8,128)(2,1)S(1)}, bf16[32,4096]{1,0:T(8,128)(2,1)S(1)}, u32[]{:S(2)}, u32[]{:S(2)}) collective-permute-start(bf16[32,4096]{1,0:T(8,128)(2,1)S(1)} %get-tuple-element.67), channel_id=1, source_target_pairs={{0,2},{1,3},{2,0},{3,1},{16,18},{17,19},{18,16},{19,17},{4,6},{5,7... | collective-permute-start | bytes 786440 | tf_op jit(solution)/shard_map/member_2/ppermute | solution.py:63
  54.6 1.4 %collective-permute-start.17 = (bf16[32,4096]{1,0:T(8,128)(2,1)S(1)}, bf16[32,4096]{1,0:T(8,128)(2,1)S(1)}, u32[]{:S(2)}, u32[]{:S(2)}) collective-permute-start(bf16[32,4096]{1,0:T(8,128)(2,1)S(1)} %get-tuple-element.68), channel_id=1, source_target_pairs={{0,16},{1,17},{2,18},{3,19},{16,0},{17,1},{18,2},{19,3},{4,20},{5,... | collective-permute-start | bytes 786440 | tf_op jit(solution)/shard_map/member_4/ppermute | solution.py:63
  56.0 5.1 %run_experts.3 = (bf16[128,4096]{1,0:T(8,128)(2,1)S(1)}, bf16[128,4096]{1,0:T(8,128)(2,1)S(1)}) custom-call(s32[1]{0:T(128)} %bitcast.3.expert_ref, bf16[128,4224]{1,0:T(8,128)(2,1)S(1)} %packed.3.own_ref, bf16[128,4224]{1,0:T(8,128)(2,1)S(1)} %collective-permute-done.24.other_ref, bf16[4096,1536]{1,0:T(8,128)(2,1)S(1)} %get-tuple-element.74.refs_0_, ...), custom_call_target="tpu_custom_call" | custom-call | flops 2415919104 | bytes 20971520 | tf_op jit(solution)/shard_map/run_experts/pallas_call | solution.py:431
  62.7 1.8 %collective-permute-start.18 = (bf16[32,4096]{1,0:T(8,128)(2,1)S(1)}, bf16[32,4096]{1,0:T(8,128)(2,1)S(1)}, u32[]{:S(2)}, u32[]{:S(2)}) collective-permute-start(bf16[32,4096]{1,0:T(8,128)(2,1)S(1)} %get-tuple-element.69), channel_id=1, source_target_pairs={{0,18},{1,19},{2,16},{3,17},{16,2},{17,3},{18,0},{19,1},{4,22},{5,... | collective-permute-start | bytes 786440 | tf_op jit(solution)/shard_map/member_6/ppermute | solution.py:63
  66.5 1.5 %collective-permute-start.27 = (bf16[16,4096]{1,0:T(8,128)(2,1)S(1)}, bf16[16,4096]{1,0:T(8,128)(2,1)S(1)}, u32[]{:S(2)}, u32[]{:S(2)}) collective-permute-start(bf16[16,4096]{1,0:T(8,128)(2,1)S(1)} %get-tuple-element.81), channel_id=1, source_target_pairs={{0,16},{1,17},{2,18},{3,19},{16,0},{17,1},{18,2},{19,3},{4,20},{5,... | collective-permute-start | bytes 393224 | tf_op jit(solution)/shard_map/member_4/ppermute | solution.py:63
  69.1 3.6 %collective-permute-done.18.refs_3_ = bf16[32,4096]{1,0:T(8,128)(2,1)S(1)} collective-permute-done((bf16[32,4096]{1,0:T(8,128)(2,1)S(1)}, bf16[32,4096]{1,0:T(8,128)(2,1)S(1)}, u32[]{:S(2)}, u32[]{:S(2)}) %collective-permute-start.18) | collective-permute-done | bytes 262176 | tf_op jit(solution)/shard_map/member_6/ppermute | solution.py:63
  72.9 2.1 %collective-permute-start.19 = (bf16[16,4096]{1,0:T(8,128)(2,1)S(1)}, bf16[16,4096]{1,0:T(8,128)(2,1)S(1)}, u32[]{:S(2)}, u32[]{:S(2)}) collective-permute-start(bf16[16,4096]{1,0:T(8,128)(2,1)S(1)} %get-tuple-element.70), channel_id=1, source_target_pairs={{0,8},{1,9},{2,10},{3,11},{16,24},{17,25},{18,26},{19,27},{4,12},{... | collective-permute-start | bytes 393224 | tf_op jit(solution)/shard_map/plane_2/ppermute | solution.py:52
  75.5 2.5 %collective-permute-done.28.refs_3_ = bf16[16,4096]{1,0:T(8,128)(2,1)S(1)} collective-permute-done((bf16[16,4096]{1,0:T(8,128)(2,1)S(1)}, bf16[16,4096]{1,0:T(8,128)(2,1)S(1)}, u32[]{:S(2)}, u32[]{:S(2)}) %collective-permute-start.28) | collective-permute-done | bytes 131104 | tf_op jit(solution)/shard_map/member_6/ppermute | solution.py:63
  78.0 1.5 %collective-permute-start.29 = (bf16[16,4096]{1,0:T(8,128)(2,1)S(1)}, bf16[16,4096]{1,0:T(8,128)(2,1)S(1)}, u32[]{:S(2)}, u32[]{:S(2)}) collective-permute-start(bf16[16,4096]{1,0:T(8,128)(2,1)S(1)} %add_chips.4), channel_id=1, source_target_pairs={{0,12},{1,13},{2,14},{3,15},{16,28},{17,29},{18,30},{19,31},{4,8},... | collective-permute-start | bytes 393224 | tf_op jit(solution)/shard_map/plane_3/ppermute | solution.py:52
  79.5 1.9 %collective-permute-start.32 = (bf16[16,4096]{1,0:T(8,128)(2,1)S(1)}, bf16[16,4096]{1,0:T(8,128)(2,1)S(1)}, u32[]{:S(2)}, u32[]{:S(2)}) collective-permute-start(bf16[16,4096]{1,0:T(8,128)(2,1)S(1)} %get-tuple-element.89), channel_id=1, source_target_pairs={{0,18},{1,19},{2,16},{3,17},{16,2},{17,3},{18,0},{19,1},{4,22},{5,... | collective-permute-start | bytes 393224 | tf_op jit(solution)/shard_map/member_6/ppermute | solution.py:63
  83.0 2.3 %collective-permute-done.29.refs_3_ = bf16[16,4096]{1,0:T(8,128)(2,1)S(1)} collective-permute-done((bf16[16,4096]{1,0:T(8,128)(2,1)S(1)}, bf16[16,4096]{1,0:T(8,128)(2,1)S(1)}, u32[]{:S(2)}, u32[]{:S(2)}) %collective-permute-start.29) | collective-permute-done | bytes 131104 | tf_op jit(solution)/shard_map/plane_3/ppermute | solution.py:52
  85.4 1.3 %collective-permute-done.32.refs_3_ = bf16[16,4096]{1,0:T(8,128)(2,1)S(1)} collective-permute-done((bf16[16,4096]{1,0:T(8,128)(2,1)S(1)}, bf16[16,4096]{1,0:T(8,128)(2,1)S(1)}, u32[]{:S(2)}, u32[]{:S(2)}) %collective-permute-start.32) | collective-permute-done | bytes 131104 | tf_op jit(solution)/shard_map/member_6/ppermute | solution.py:63
  (60 shorter events, 15.8 us)
Async XLA Ops:
  0.6 4.7 %collective-permute-start = (s32[16]{0:T(128)}, s32[16]{0:T(128)S(1)}, u32[]{:S(2)}, u32[]{:S(2)}) collective-permute-start(s32[16]{0:T(128)} %param.17), channel_id=1, source_target_pairs={{0,16},{16,0},{1,17},{17,1},{2,18},{18,2},{3,19},{19,3},{4,20},{20... | collective-permute-start | bytes 200 | tf_op jit(solution)/shard_map/ppermute | solution.py:68
  7.0 7.2 %collective-permute-start.1 = (bf16[16,16,512]{2,1,0:T(8,128)(2,1)S(1)}, bf16[16,16,512]{2,1,0:T(8,128)(2,1)S(1)}, u32[]{:S(2)}, u32[]{:S(2)}) collective-permute-start(bf16[16,16,512]{2,1,0:T(8,128)(2,1)S(1)} %pick_pages.1), channel_id=1, source_target_pairs={{0,16},{16,0},{1,17},{17,1},{2,18},{18,2},{3,19},{19,3},{4,20},{20... | collective-permute-start | bytes 786440 | tf_op jit(solution)/shard_map/ppermute | solution.py:68
  16.2 7.9 %collective-permute-start.3 = (bf16[16,4224]{1,0:T(8,128)(2,1)S(1)}, bf16[16,4224]{1,0:T(8,128)(2,1)S(1)}, u32[]{:S(2)}, u32[]{:S(2)}) collective-permute-start(bf16[16,4224]{1,0:T(8,128)(2,1)S(1)} %get-tuple-element.72.refs_0_), channel_id=1, source_target_pairs={{0,8},{1,9},{2,10},{3,11},{16,24},{17,25},{18,26},{19,27},{4,12},{... | collective-permute-start | bytes 405512 | tf_op jit(solution)/shard_map/plane_2/ppermute | solution.py:52
  19.0 6.0 %collective-permute-start.11 = (bf16[16,4224]{1,0:T(8,128)(2,1)S(1)}, bf16[16,4224]{1,0:T(8,128)(2,1)S(1)}, u32[]{:S(2)}, u32[]{:S(2)}) collective-permute-start(bf16[16,4224]{1,0:T(8,128)(2,1)S(1)} %get-tuple-element.72.refs_0_), channel_id=1, source_target_pairs={{0,18},{1,19},{2,16},{3,17},{16,2},{17,3},{18,0},{19,1},{4,22},{5,... | collective-permute-start | bytes 405512 | tf_op jit(solution)/shard_map/member_6/ppermute | solution.py:63
  21.5 6.4 %collective-permute-start.8 = (bf16[16,4224]{1,0:T(8,128)(2,1)S(1)}, bf16[16,4224]{1,0:T(8,128)(2,1)S(1)}, u32[]{:S(2)}, u32[]{:S(2)}) collective-permute-start(bf16[16,4224]{1,0:T(8,128)(2,1)S(1)} %get-tuple-element.72.refs_0_), channel_id=1, source_target_pairs={{0,16},{1,17},{2,18},{3,19},{16,0},{17,1},{18,2},{19,3},{4,20},{5,... | collective-permute-start | bytes 405512 | tf_op jit(solution)/shard_map/member_4/ppermute | solution.py:63
  22.0 7.2 %collective-permute-start.5 = (bf16[16,4224]{1,0:T(8,128)(2,1)S(1)}, bf16[16,4224]{1,0:T(8,128)(2,1)S(1)}, u32[]{:S(2)}, u32[]{:S(2)}) collective-permute-start(bf16[16,4224]{1,0:T(8,128)(2,1)S(1)} %get-tuple-element.72.refs_0_), channel_id=1, source_target_pairs={{0,2},{1,3},{2,0},{3,1},{16,18},{17,19},{18,16},{19,17},{4,6},{5,7... | collective-permute-start | bytes 405512 | tf_op jit(solution)/shard_map/member_2/ppermute | solution.py:63
  22.5 7.7 %collective-permute-start.2 = (bf16[16,4224]{1,0:T(8,128)(2,1)S(1)}, bf16[16,4224]{1,0:T(8,128)(2,1)S(1)}, u32[]{:S(2)}, u32[]{:S(2)}) collective-permute-start(bf16[16,4224]{1,0:T(8,128)(2,1)S(1)} %get-tuple-element.72.refs_0_), channel_id=1, source_target_pairs={{0,4},{1,5},{2,6},{3,7},{16,20},{17,21},{18,22},{19,23},{4,0},{5,1... | collective-permute-start | bytes 405512 | tf_op jit(solution)/shard_map/plane_1/ppermute | solution.py:52
  24.1 8.0 %collective-permute-start.4 = (bf16[16,4224]{1,0:T(8,128)(2,1)S(1)}, bf16[16,4224]{1,0:T(8,128)(2,1)S(1)}, u32[]{:S(2)}, u32[]{:S(2)}) collective-permute-start(bf16[16,4224]{1,0:T(8,128)(2,1)S(1)} %collective-permute-done.3.refs_1_), channel_id=1, source_target_pairs={{0,4},{1,5},{2,6},{3,7},{16,20},{17,21},{18,22},{19,23},{4,0},{5,1... | collective-permute-start | bytes 405512 | tf_op jit(solution)/shard_map/plane_1/ppermute | solution.py:52
  25.0 7.7 %collective-permute-start.13 = (bf16[16,4224]{1,0:T(8,128)(2,1)S(1)}, bf16[16,4224]{1,0:T(8,128)(2,1)S(1)}, u32[]{:S(2)}, u32[]{:S(2)}) collective-permute-start(bf16[16,4224]{1,0:T(8,128)(2,1)S(1)} %collective-permute-done.3.refs_1_), channel_id=1, source_target_pairs={{0,18},{1,19},{2,16},{3,17},{16,2},{17,3},{18,0},{19,1},{4,22},{5,... | collective-permute-start | bytes 405512 | tf_op jit(solution)/shard_map/member_6/ppermute | solution.py:63
  27.8 7.4 %collective-permute-start.10 = (bf16[16,4224]{1,0:T(8,128)(2,1)S(1)}, bf16[16,4224]{1,0:T(8,128)(2,1)S(1)}, u32[]{:S(2)}, u32[]{:S(2)}) collective-permute-start(bf16[16,4224]{1,0:T(8,128)(2,1)S(1)} %collective-permute-done.3.refs_1_), channel_id=1, source_target_pairs={{0,16},{1,17},{2,18},{3,19},{16,0},{17,1},{18,2},{19,3},{4,20},{5,... | collective-permute-start | bytes 405512 | tf_op jit(solution)/shard_map/member_4/ppermute | solution.py:63
  29.2 7.7 %collective-permute-start.7 = (bf16[16,4224]{1,0:T(8,128)(2,1)S(1)}, bf16[16,4224]{1,0:T(8,128)(2,1)S(1)}, u32[]{:S(2)}, u32[]{:S(2)}) collective-permute-start(bf16[16,4224]{1,0:T(8,128)(2,1)S(1)} %collective-permute-done.3.refs_1_), channel_id=1, source_target_pairs={{0,2},{1,3},{2,0},{3,1},{16,18},{17,19},{18,16},{19,17},{4,6},{5,7... | collective-permute-start | bytes 405512 | tf_op jit(solution)/shard_map/member_2/ppermute | solution.py:63
  30.2 6.7 %collective-permute-start.12 = (bf16[16,4224]{1,0:T(8,128)(2,1)S(1)}, bf16[16,4224]{1,0:T(8,128)(2,1)S(1)}, u32[]{:S(2)}, u32[]{:S(2)}) collective-permute-start(bf16[16,4224]{1,0:T(8,128)(2,1)S(1)} %collective-permute-done.2.refs_0_), channel_id=1, source_target_pairs={{0,18},{1,19},{2,16},{3,17},{16,2},{17,3},{18,0},{19,1},{4,22},{5,... | collective-permute-start | bytes 405512 | tf_op jit(solution)/shard_map/member_6/ppermute | solution.py:63
  32.1 6.0 %collective-permute-start.9 = (bf16[16,4224]{1,0:T(8,128)(2,1)S(1)}, bf16[16,4224]{1,0:T(8,128)(2,1)S(1)}, u32[]{:S(2)}, u32[]{:S(2)}) collective-permute-start(bf16[16,4224]{1,0:T(8,128)(2,1)S(1)} %collective-permute-done.2.refs_0_), channel_id=1, source_target_pairs={{0,16},{1,17},{2,18},{3,19},{16,0},{17,1},{18,2},{19,3},{4,20},{5,... | collective-permute-start | bytes 405512 | tf_op jit(solution)/shard_map/member_4/ppermute | solution.py:63
  32.7 5.7 %collective-permute-start.6 = (bf16[16,4224]{1,0:T(8,128)(2,1)S(1)}, bf16[16,4224]{1,0:T(8,128)(2,1)S(1)}, u32[]{:S(2)}, u32[]{:S(2)}) collective-permute-start(bf16[16,4224]{1,0:T(8,128)(2,1)S(1)} %collective-permute-done.2.refs_0_), channel_id=1, source_target_pairs={{0,2},{1,3},{2,0},{3,1},{16,18},{17,19},{18,16},{19,17},{4,6},{5,7... | collective-permute-start | bytes 405512 | tf_op jit(solution)/shard_map/member_2/ppermute | solution.py:63
  38.4 3.6 %collective-permute-start.14 = (bf16[128,4224]{1,0:T(8,128)(2,1)S(1)}, bf16[128,4224]{1,0:T(8,128)(2,1)S(1)}, u32[]{:S(2)}, u32[]{:S(2)}) collective-permute-start(bf16[128,4224]{1,0:T(8,128)(2,1)S(1)} %packed.2.own_ref), channel_id=1, source_target_pairs={{0,1},{1,0},{2,3},{3,2},{16,17},{17,16},{18,19},{19,18},{4,5},{5,4... | collective-permute-start | bytes 3244040 | tf_op jit(solution)/shard_map/member_1/ppermute | solution.py:63
  38.5 11.9 %collective-permute-start.21 = (bf16[16,4224]{1,0:T(8,128)(2,1)S(1)}, bf16[16,4224]{1,0:T(8,128)(2,1)S(1)}, u32[]{:S(2)}, u32[]{:S(2)}) collective-permute-start(bf16[16,4224]{1,0:T(8,128)(2,1)S(1)} %collective-permute-done.4.refs_1_), channel_id=1, source_target_pairs={{0,2},{1,3},{2,0},{3,1},{16,18},{17,19},{18,16},{19,17},{4,6},{5,7... | collective-permute-start | bytes 405512 | tf_op jit(solution)/shard_map/member_2/ppermute | solution.py:63
  39.8 10.7 %collective-permute-start.22 = (bf16[16,4224]{1,0:T(8,128)(2,1)S(1)}, bf16[16,4224]{1,0:T(8,128)(2,1)S(1)}, u32[]{:S(2)}, u32[]{:S(2)}) collective-permute-start(bf16[16,4224]{1,0:T(8,128)(2,1)S(1)} %collective-permute-done.4.refs_1_), channel_id=1, source_target_pairs={{0,16},{1,17},{2,18},{3,19},{16,0},{17,1},{18,2},{19,3},{4,20},{5,... | collective-permute-start | bytes 405512 | tf_op jit(solution)/shard_map/member_4/ppermute | solution.py:63
  41.2 9.3 %collective-permute-start.23 = (bf16[16,4224]{1,0:T(8,128)(2,1)S(1)}, bf16[16,4224]{1,0:T(8,128)(2,1)S(1)}, u32[]{:S(2)}, u32[]{:S(2)}) collective-permute-start(bf16[16,4224]{1,0:T(8,128)(2,1)S(1)} %collective-permute-done.4.refs_1_), channel_id=1, source_target_pairs={{0,18},{1,19},{2,16},{3,17},{16,2},{17,3},{18,0},{19,1},{4,22},{5,... | collective-permute-start | bytes 405512 | tf_op jit(solution)/shard_map/member_6/ppermute | solution.py:63
  50.4 2.7 %collective-permute-start.15 = (bf16[128,4096]{1,0:T(8,128)(2,1)S(1)}, bf16[128,4096]{1,0:T(8,128)(2,1)S(1)}, u32[]{:S(2)}, u32[]{:S(2)}) collective-permute-start(bf16[128,4096]{1,0:T(8,128)(2,1)S(1)} %get-tuple-element.65), channel_id=1, source_target_pairs={{0,1},{1,0},{2,3},{3,2},{16,17},{17,16},{18,19},{19,18},{4,5},{5,4... | collective-permute-start | bytes 3145736 | tf_op jit(solution)/shard_map/member_1/ppermute | solution.py:63
  50.6 5.5 %collective-permute-start.24 = (bf16[128,4224]{1,0:T(8,128)(2,1)S(1)}, bf16[128,4224]{1,0:T(8,128)(2,1)S(1)}, u32[]{:S(2)}, u32[]{:S(2)}) collective-permute-start(bf16[128,4224]{1,0:T(8,128)(2,1)S(1)} %packed.3.own_ref), channel_id=1, source_target_pairs={{0,1},{1,0},{2,3},{3,2},{16,17},{17,16},{18,19},{19,18},{4,5},{5,4... | collective-permute-start | bytes 3244040 | tf_op jit(solution)/shard_map/member_1/ppermute | solution.py:63
  53.3 8.4 %collective-permute-start.16 = (bf16[32,4096]{1,0:T(8,128)(2,1)S(1)}, bf16[32,4096]{1,0:T(8,128)(2,1)S(1)}, u32[]{:S(2)}, u32[]{:S(2)}) collective-permute-start(bf16[32,4096]{1,0:T(8,128)(2,1)S(1)} %get-tuple-element.67), channel_id=1, source_target_pairs={{0,2},{1,3},{2,0},{3,1},{16,18},{17,19},{18,16},{19,17},{4,6},{5,7... | collective-permute-start | bytes 786440 | tf_op jit(solution)/shard_map/member_2/ppermute | solution.py:63
  54.6 8.1 %collective-permute-start.17 = (bf16[32,4096]{1,0:T(8,128)(2,1)S(1)}, bf16[32,4096]{1,0:T(8,128)(2,1)S(1)}, u32[]{:S(2)}, u32[]{:S(2)}) collective-permute-start(bf16[32,4096]{1,0:T(8,128)(2,1)S(1)} %get-tuple-element.68), channel_id=1, source_target_pairs={{0,16},{1,17},{2,18},{3,19},{16,0},{17,1},{18,2},{19,3},{4,20},{5,... | collective-permute-start | bytes 786440 | tf_op jit(solution)/shard_map/member_4/ppermute | solution.py:63
  62.7 10.0 %collective-permute-start.18 = (bf16[32,4096]{1,0:T(8,128)(2,1)S(1)}, bf16[32,4096]{1,0:T(8,128)(2,1)S(1)}, u32[]{:S(2)}, u32[]{:S(2)}) collective-permute-start(bf16[32,4096]{1,0:T(8,128)(2,1)S(1)} %get-tuple-element.69), channel_id=1, source_target_pairs={{0,18},{1,19},{2,16},{3,17},{16,2},{17,3},{18,0},{19,1},{4,22},{5,... | collective-permute-start | bytes 786440 | tf_op jit(solution)/shard_map/member_6/ppermute | solution.py:63
  65.6 9.9 %collective-permute-start.26 = (bf16[16,4096]{1,0:T(8,128)(2,1)S(1)}, bf16[16,4096]{1,0:T(8,128)(2,1)S(1)}, u32[]{:S(2)}, u32[]{:S(2)}) collective-permute-start(bf16[16,4096]{1,0:T(8,128)(2,1)S(1)} %get-tuple-element.80), channel_id=1, source_target_pairs={{0,2},{1,3},{2,0},{3,1},{16,18},{17,19},{18,16},{19,17},{4,6},{5,7... | collective-permute-start | bytes 393224 | tf_op jit(solution)/shard_map/member_2/ppermute | solution.py:63
  66.5 9.0 %collective-permute-start.27 = (bf16[16,4096]{1,0:T(8,128)(2,1)S(1)}, bf16[16,4096]{1,0:T(8,128)(2,1)S(1)}, u32[]{:S(2)}, u32[]{:S(2)}) collective-permute-start(bf16[16,4096]{1,0:T(8,128)(2,1)S(1)} %get-tuple-element.81), channel_id=1, source_target_pairs={{0,16},{1,17},{2,18},{3,19},{16,0},{17,1},{18,2},{19,3},{4,20},{5,... | collective-permute-start | bytes 393224 | tf_op jit(solution)/shard_map/member_4/ppermute | solution.py:63
  68.0 10.0 %collective-permute-start.28 = (bf16[16,4096]{1,0:T(8,128)(2,1)S(1)}, bf16[16,4096]{1,0:T(8,128)(2,1)S(1)}, u32[]{:S(2)}, u32[]{:S(2)}) collective-permute-start(bf16[16,4096]{1,0:T(8,128)(2,1)S(1)} %get-tuple-element.82), channel_id=1, source_target_pairs={{0,18},{1,19},{2,16},{3,17},{16,2},{17,3},{18,0},{19,1},{4,22},{5,... | collective-permute-start | bytes 393224 | tf_op jit(solution)/shard_map/member_6/ppermute | solution.py:63
  72.9 9.1 %collective-permute-start.19 = (bf16[16,4096]{1,0:T(8,128)(2,1)S(1)}, bf16[16,4096]{1,0:T(8,128)(2,1)S(1)}, u32[]{:S(2)}, u32[]{:S(2)}) collective-permute-start(bf16[16,4096]{1,0:T(8,128)(2,1)S(1)} %get-tuple-element.70), channel_id=1, source_target_pairs={{0,8},{1,9},{2,10},{3,11},{16,24},{17,25},{18,26},{19,27},{4,12},{... | collective-permute-start | bytes 393224 | tf_op jit(solution)/shard_map/plane_2/ppermute | solution.py:52
  75.0 8.1 %collective-permute-start.20 = (bf16[16,4096]{1,0:T(8,128)(2,1)S(1)}, bf16[16,4096]{1,0:T(8,128)(2,1)S(1)}, u32[]{:S(2)}, u32[]{:S(2)}) collective-permute-start(bf16[16,4096]{1,0:T(8,128)(2,1)S(1)} %get-tuple-element.71), channel_id=1, source_target_pairs={{0,4},{1,5},{2,6},{3,7},{16,20},{17,21},{18,22},{19,23},{4,0},{5,1... | collective-permute-start | bytes 393224 | tf_op jit(solution)/shard_map/plane_1/ppermute | solution.py:52
  78.0 7.3 %collective-permute-start.29 = (bf16[16,4096]{1,0:T(8,128)(2,1)S(1)}, bf16[16,4096]{1,0:T(8,128)(2,1)S(1)}, u32[]{:S(2)}, u32[]{:S(2)}) collective-permute-start(bf16[16,4096]{1,0:T(8,128)(2,1)S(1)} %add_chips.4), channel_id=1, source_target_pairs={{0,12},{1,13},{2,14},{3,15},{16,28},{17,29},{18,30},{19,31},{4,8},... | collective-permute-start | bytes 393224 | tf_op jit(solution)/shard_map/plane_3/ppermute | solution.py:52
  79.5 7.2 %collective-permute-start.32 = (bf16[16,4096]{1,0:T(8,128)(2,1)S(1)}, bf16[16,4096]{1,0:T(8,128)(2,1)S(1)}, u32[]{:S(2)}, u32[]{:S(2)}) collective-permute-start(bf16[16,4096]{1,0:T(8,128)(2,1)S(1)} %get-tuple-element.89), channel_id=1, source_target_pairs={{0,18},{1,19},{2,16},{3,17},{16,2},{17,3},{18,0},{19,1},{4,22},{5,... | collective-permute-start | bytes 393224 | tf_op jit(solution)/shard_map/member_6/ppermute | solution.py:63
  81.4 6.2 %collective-permute-start.31 = (bf16[16,4096]{1,0:T(8,128)(2,1)S(1)}, bf16[16,4096]{1,0:T(8,128)(2,1)S(1)}, u32[]{:S(2)}, u32[]{:S(2)}) collective-permute-start(bf16[16,4096]{1,0:T(8,128)(2,1)S(1)} %get-tuple-element.87), channel_id=1, source_target_pairs={{0,16},{1,17},{2,18},{3,19},{16,0},{17,1},{18,2},{19,3},{4,20},{5,... | collective-permute-start | bytes 393224 | tf_op jit(solution)/shard_map/member_4/ppermute | solution.py:63
  82.0 6.1 %collective-permute-start.30 = (bf16[16,4096]{1,0:T(8,128)(2,1)S(1)}, bf16[16,4096]{1,0:T(8,128)(2,1)S(1)}, u32[]{:S(2)}, u32[]{:S(2)}) collective-permute-start(bf16[16,4096]{1,0:T(8,128)(2,1)S(1)} %get-tuple-element.85), channel_id=1, source_target_pairs={{0,2},{1,3},{2,0},{3,1},{16,18},{17,19},{18,16},{19,17},{4,6},{5,7... | collective-permute-start | bytes 393224 | tf_op jit(solution)/shard_map/member_2/ppermute | solution.py:63
  (7 other events, 46.5 us)

commit v15 on v14

--- a/solution.py
+++ b/solution.py
@@ -321,21 +321,27 @@
     out_width = 1024 if rows <= 512 else 512
     out_steps = model_dim // out_width
     strip = 256
+    cuts = 4
 
     def kernel(expert_ref, own_ref, other_ref, *refs):
         copies = {}
         if keep:
             up_hbm, down_hbm, out_ref, over_ref, up_ref, down_ref, tokens_ref, hidden_ref, sems = refs
             for c in range(up_steps):
-                for half in range(2):
-                    columns = pl.ds(half * hidden_dim + c * width, width)
-                    copies["up", c, half] = pltpu.make_async_copy(
-                        up_hbm.at[0, :, columns], up_ref.at[:, columns], sems.at[2 * c + half]
+                for part in range(2 * cuts):
+                    columns = pl.ds(part // cuts * hidden_dim + c * width, width)
+                    lines = pl.ds(part % cuts * (model_dim // cuts), model_dim // cuts)
+                    copies["up", c, part] = pltpu.make_async_copy(
+                        up_hbm.at[0, lines, columns],
+                        up_ref.at[lines, columns],
+                        sems.at[2 * cuts * c + part],
                     )
             for c in range(out_steps):
                 columns = pl.ds(c * out_width, out_width)
                 copies["down", c] = pltpu.make_async_copy(
-                    down_hbm.at[0, :, columns], down_ref.at[:, columns], sems.at[2 * up_steps + c]
+                    down_hbm.at[0, :, columns],
+                    down_ref.at[:, columns],
+                    sems.at[2 * cuts * up_steps + c],
                 )
             for copy in copies.values():
                 copy.start()
@@ -390,8 +396,8 @@
             ).astype(jnp.bfloat16)
 
         for c in range(up_steps):
-            arrive("up", c, 0)
-            arrive("up", c, 1)
+            for part in range(2 * cuts):
+                arrive("up", c, part)
             start = c * width
             tokens = tokens_ref[...]
             gated = jnp.dot(
@@ -424,7 +430,7 @@
             pltpu.VMEM((model_dim, double), jnp.bfloat16),
             pltpu.VMEM((hidden_dim, model_dim), jnp.bfloat16),
         )
-        scratch = [pltpu.SemaphoreType.DMA((2 * up_steps + out_steps,))]
+        scratch = [pltpu.SemaphoreType.DMA((2 * cuts * up_steps + out_steps,))]
         weights = [in_hbm(gate_up), in_hbm(down_proj)]
     else:
         weights = [pltpu.with_memory_space_constraint(value, pltpu.VMEM) for value in weights]

time: 89.2 us -> 90 us (level)
  transfers between devices with their start and end apart: 33 -> 33, of which waited for: 18 -> 18; matrix products, arithmetic and copies ran while one was open for 0% -> 0% of each run, Pallas kernels for 21% -> 22%
where the time goes in v15:
time: 90 us; the launch traced here: 89.7 us
  starting transfers between devices  41.8 us (46%)
  Pallas kernels  23.4 us (26%)
  waiting for transfers between devices  22.8 us (25%)
    ppermute x25, starting transfers between devices, swapped(): return lax.ppermute(value, AXES, pairs)  27.8 us
    ppermute x25, waiting for transfers between devices, swapped(): return lax.ppermute(value, AXES, pairs)  18.4 us
    pallas_call x2, Pallas kernels, run_experts(): pl.pallas_call(kernel, out_shape=(shape, shape) + kept, in_specs=[SMEM, V...  14.2 us
    ppermute x6, starting transfers between devices, shifted(): return lax.ppermute(value, AXES, pairs)  8.93 us
    ppermute x2, starting transfers between devices, from_behind(): lax.ppermute(value, axis, [(i, (i + by) % length) for i in range(length)])  5.09 us
    pallas_call x1, Pallas kernels, own_attention(): pl.pallas_call(kernel, out_shape=(shape, shape, shape, jax.ShapeDtypeStru...  4.74 us
    ppermute x6, waiting for transfers between devices, shifted(): return lax.ppermute(value, AXES, pairs)  2.32 us
    ppermute x2, waiting for transfers between devices, from_behind(): lax.ppermute(value, axis, [(i, (i + by) % length) for i in range(length)])  2.06 us
  transfers between devices with their start and end apart: 33, of which 18 were waited for; matrix products, arithmetic and copies ran while one was open for 0% of the time, Pallas kernels for 22%

profile of v15, /device:TPU:0, one launch (start us, length us, event | category | flops | bytes accessed | tf_op | source)
XLA Modules:
  0.0 89.7 jit_solution(13338784238229426994)
XLA Ops:
  0.6 3.0 %collective-permute-start = (s32[16]{0:T(128)}, s32[16]{0:T(128)S(1)}, u32[]{:S(2)}, u32[]{:S(2)}) collective-permute-start(s32[16]{0:T(128)} %param.17), channel_id=1, source_target_pairs={{0,16},{16,0},{1,17},{17,1},{2,18},{18,2},{3,19},{19,3},{4,20},{20... | collective-permute-start | bytes 200 | tf_op jit(solution)/shard_map/ppermute | solution.py:68
  3.6 1.7 %collective-permute-done.slots_ref = s32[16]{0:T(128)S(1)} collective-permute-done((s32[16]{0:T(128)}, s32[16]{0:T(128)S(1)}, u32[]{:S(2)}, u32[]{:S(2)}) %collective-permute-start) | collective-permute-done | bytes 96 | tf_op jit(solution)/shard_map/ppermute | solution.py:68
  5.3 1.6 %pick_pages.1 = bf16[16,16,512]{2,1,0:T(8,128)(2,1)S(1)} custom-call(s32[16]{0:T(128)S(1)} %collective-permute-done.slots_ref, bf16[128,16,512]{2,1,0:T(8,128)(2,1)} %pages_hbm.1), custom_call_target="tpu_custom_call" | custom-call | bytes 1048576 | tf_op jit(solution)/shard_map/pick_pages/pallas_call | solution.py:84
  7.0 2.1 %collective-permute-start.1 = (bf16[16,16,512]{2,1,0:T(8,128)(2,1)S(1)}, bf16[16,16,512]{2,1,0:T(8,128)(2,1)S(1)}, u32[]{:S(2)}, u32[]{:S(2)}) collective-permute-start(bf16[16,16,512]{2,1,0:T(8,128)(2,1)S(1)} %pick_pages.1), channel_id=1, source_target_pairs={{0,16},{16,0},{1,17},{17,1},{2,18},{18,2},{3,19},{19,3},{4,20},{20... | collective-permute-start | bytes 786440 | tf_op jit(solution)/shard_map/ppermute | solution.py:68
  9.0 4.7 %own_attention.1 = (f32[512,128]{1,0:T(8,128)S(1)}, f32[512,128]{1,0:T(8,128)S(1)}, f32[512,128]{1,0:T(8,128)S(1)}, bf16[512,128]{1,0:T(8,128)(2,1)S(1)}) custom-call(bf16[16,4096]{1,0:T(8,128)(2,1)} %queries_hbm, bf16[16,512]{1,0:T(8,128)(2,1)} %new_hbm.1, bf16[128,16,512]{2,1,0:T(8,128)(2,1)} %pages_hbm.1, s32[16,16]{1,0:T(8,128)} %table_ref.1, s32[16]{0:T(128)} %lengths_ref.1), custom_call_target="tpu_custom_call" | custom-call | flops 1073741824 | bytes 16777216 | tf_op jit(solution)/shard_map/own_attention/pallas_call | solution.py:239
  14.2 1.9 %finish_attention.1 = (bf16[16,4096]{1,0:T(8,128)(2,1)}, bf16[16,4096]{1,0:T(8,128)(2,1)S(1)}, bf16[16,4224]{1,0:T(8,128)(2,1)S(1)}) custom-call(bf16[512,128]{1,0:T(8,128)(2,1)S(1)} %get-tuple-element.47.q_ref, bf16[16,16,512]{2,1,0:T(8,128)(2,1)S(1)} %collective-permute-done.1.fetched_ref, s32[16,16]{1,0:T(8,128)S(1)} %copy-done.2, s32[16]{0:T(128)S(1)} %copy-done.5, ...), custom_call_target="tpu_custom_call" | custom-call | flops 134217728 | bytes 4194304 | tf_op jit(solution)/shard_map/finish_attention/pallas_call | solution.py:544
  16.2 2.8 %collective-permute-start.3 = (bf16[16,4224]{1,0:T(8,128)(2,1)S(1)}, bf16[16,4224]{1,0:T(8,128)(2,1)S(1)}, u32[]{:S(2)}, u32[]{:S(2)}) collective-permute-start(bf16[16,4224]{1,0:T(8,128)(2,1)S(1)} %get-tuple-element.72.refs_0_), channel_id=1, source_target_pairs={{0,8},{1,9},{2,10},{3,11},{16,24},{17,25},{18,26},{19,27},{4,12},{... | collective-permute-start | bytes 405512 | tf_op jit(solution)/shard_map/plane_2/ppermute | solution.py:52
  19.0 2.5 %collective-permute-start.11 = (bf16[16,4224]{1,0:T(8,128)(2,1)S(1)}, bf16[16,4224]{1,0:T(8,128)(2,1)S(1)}, u32[]{:S(2)}, u32[]{:S(2)}) collective-permute-start(bf16[16,4224]{1,0:T(8,128)(2,1)S(1)} %get-tuple-element.72.refs_0_), channel_id=1, source_target_pairs={{0,18},{1,19},{2,16},{3,17},{16,2},{17,3},{18,0},{19,1},{4,22},{5,... | collective-permute-start | bytes 405512 | tf_op jit(solution)/shard_map/member_6/ppermute | solution.py:63
  22.5 1.6 %collective-permute-start.2 = (bf16[16,4224]{1,0:T(8,128)(2,1)S(1)}, bf16[16,4224]{1,0:T(8,128)(2,1)S(1)}, u32[]{:S(2)}, u32[]{:S(2)}) collective-permute-start(bf16[16,4224]{1,0:T(8,128)(2,1)S(1)} %get-tuple-element.72.refs_0_), channel_id=1, source_target_pairs={{0,4},{1,5},{2,6},{3,7},{16,20},{17,21},{18,22},{19,23},{4,0},{5,1... | collective-permute-start | bytes 405512 | tf_op jit(solution)/shard_map/plane_1/ppermute | solution.py:52
  25.0 2.4 %collective-permute-start.13 = (bf16[16,4224]{1,0:T(8,128)(2,1)S(1)}, bf16[16,4224]{1,0:T(8,128)(2,1)S(1)}, u32[]{:S(2)}, u32[]{:S(2)}) collective-permute-start(bf16[16,4224]{1,0:T(8,128)(2,1)S(1)} %collective-permute-done.3.refs_1_), channel_id=1, source_target_pairs={{0,18},{1,19},{2,16},{3,17},{16,2},{17,3},{18,0},{19,1},{4,22},{5,... | collective-permute-start | bytes 405512 | tf_op jit(solution)/shard_map/member_6/ppermute | solution.py:63
  27.8 1.3 %collective-permute-start.10 = (bf16[16,4224]{1,0:T(8,128)(2,1)S(1)}, bf16[16,4224]{1,0:T(8,128)(2,1)S(1)}, u32[]{:S(2)}, u32[]{:S(2)}) collective-permute-start(bf16[16,4224]{1,0:T(8,128)(2,1)S(1)} %collective-permute-done.3.refs_1_), channel_id=1, source_target_pairs={{0,16},{1,17},{2,18},{3,19},{16,0},{17,1},{18,2},{19,3},{4,20},{5,... | collective-permute-start | bytes 405512 | tf_op jit(solution)/shard_map/member_4/ppermute | solution.py:63
  30.2 1.9 %collective-permute-start.12 = (bf16[16,4224]{1,0:T(8,128)(2,1)S(1)}, bf16[16,4224]{1,0:T(8,128)(2,1)S(1)}, u32[]{:S(2)}, u32[]{:S(2)}) collective-permute-start(bf16[16,4224]{1,0:T(8,128)(2,1)S(1)} %collective-permute-done.2.refs_0_), channel_id=1, source_target_pairs={{0,18},{1,19},{2,16},{3,17},{16,2},{17,3},{18,0},{19,1},{4,22},{5,... | collective-permute-start | bytes 405512 | tf_op jit(solution)/shard_map/member_6/ppermute | solution.py:63
  32.7 1.3 %collective-permute-start.6 = (bf16[16,4224]{1,0:T(8,128)(2,1)S(1)}, bf16[16,4224]{1,0:T(8,128)(2,1)S(1)}, u32[]{:S(2)}, u32[]{:S(2)}) collective-permute-start(bf16[16,4224]{1,0:T(8,128)(2,1)S(1)} %collective-permute-done.2.refs_0_), channel_id=1, source_target_pairs={{0,2},{1,3},{2,0},{3,1},{16,18},{17,19},{18,16},{19,17},{4,6},{5,7... | collective-permute-start | bytes 405512 | tf_op jit(solution)/shard_map/member_2/ppermute | solution.py:63
  34.0 1.2 %collective-permute-done.10.refs_5_ = bf16[16,4224]{1,0:T(8,128)(2,1)S(1)} collective-permute-done((bf16[16,4224]{1,0:T(8,128)(2,1)S(1)}, bf16[16,4224]{1,0:T(8,128)(2,1)S(1)}, u32[]{:S(2)}, u32[]{:S(2)}) %collective-permute-start.10) | collective-permute-done | bytes 135200 | tf_op jit(solution)/shard_map/member_4/ppermute | solution.py:63
  35.2 1.7 %collective-permute-done.7.refs_3_ = bf16[16,4224]{1,0:T(8,128)(2,1)S(1)} collective-permute-done((bf16[16,4224]{1,0:T(8,128)(2,1)S(1)}, bf16[16,4224]{1,0:T(8,128)(2,1)S(1)}, u32[]{:S(2)}, u32[]{:S(2)}) %collective-permute-start.7) | collective-permute-done | bytes 135200 | tf_op jit(solution)/shard_map/member_2/ppermute | solution.py:63
  36.9 1.2 %collective-permute-done.9.refs_4_ = bf16[16,4224]{1,0:T(8,128)(2,1)S(1)} collective-permute-done((bf16[16,4224]{1,0:T(8,128)(2,1)S(1)}, bf16[16,4224]{1,0:T(8,128)(2,1)S(1)}, u32[]{:S(2)}, u32[]{:S(2)}) %collective-permute-start.9) | collective-permute-done | bytes 135200 | tf_op jit(solution)/shard_map/member_4/ppermute | solution.py:63
  38.5 1.3 %collective-permute-start.21 = (bf16[16,4224]{1,0:T(8,128)(2,1)S(1)}, bf16[16,4224]{1,0:T(8,128)(2,1)S(1)}, u32[]{:S(2)}, u32[]{:S(2)}) collective-permute-start(bf16[16,4224]{1,0:T(8,128)(2,1)S(1)} %collective-permute-done.4.refs_1_), channel_id=1, source_target_pairs={{0,2},{1,3},{2,0},{3,1},{16,18},{17,19},{18,16},{19,17},{4,6},{5,7... | collective-permute-start | bytes 405512 | tf_op jit(solution)/shard_map/member_2/ppermute | solution.py:63
  39.8 1.4 %collective-permute-start.22 = (bf16[16,4224]{1,0:T(8,128)(2,1)S(1)}, bf16[16,4224]{1,0:T(8,128)(2,1)S(1)}, u32[]{:S(2)}, u32[]{:S(2)}) collective-permute-start(bf16[16,4224]{1,0:T(8,128)(2,1)S(1)} %collective-permute-done.4.refs_1_), channel_id=1, source_target_pairs={{0,16},{1,17},{2,18},{3,19},{16,0},{17,1},{18,2},{19,3},{4,20},{5,... | collective-permute-start | bytes 405512 | tf_op jit(solution)/shard_map/member_4/ppermute | solution.py:63
  42.1 9.1 %run_experts.2 = (bf16[128,4096]{1,0:T(8,128)(2,1)S(1)}, bf16[128,4096]{1,0:T(8,128)(2,1)S(1)}, bf16[4096,1536]{1,0:T(8,128)(2,1)S(1)}, bf16[768,4096]{1,0:T(8,128)(2,1)S(1)}) custom-call(s32[1]{0:T(128)} %bitcast.3.expert_ref, bf16[128,4224]{1,0:T(8,128)(2,1)S(1)} %packed.2.own_ref, bf16[128,4224]{1,0:T(8,128)(2,1)S(1)} %collective-permute-done.14.other_ref, ...), custom_call_target="tpu_custom_call" | custom-call | flops 2415919104 | bytes 20971520 | tf_op jit(solution)/shard_map/run_experts/pallas_call | solution.py:437
  51.9 2.0 %collective-permute-done.15.refs_1_ = bf16[128,4096]{1,0:T(8,128)(2,1)S(1)} collective-permute-done((bf16[128,4096]{1,0:T(8,128)(2,1)S(1)}, bf16[128,4096]{1,0:T(8,128)(2,1)S(1)}, u32[]{:S(2)}, u32[]{:S(2)}) %collective-permute-start.15) | collective-permute-done | bytes 1048608 | tf_op jit(solution)/shard_map/member_1/ppermute | solution.py:63
  54.1 1.3 %collective-permute-start.16 = (bf16[32,4096]{1,0:T(8,128)(2,1)S(1)}, bf16[32,4096]{1,0:T(8,128)(2,1)S(1)}, u32[]{:S(2)}, u32[]{:S(2)}) collective-permute-start(bf16[32,4096]{1,0:T(8,128)(2,1)S(1)} %get-tuple-element.67), channel_id=1, source_target_pairs={{0,2},{1,3},{2,0},{3,1},{16,18},{17,19},{18,16},{19,17},{4,6},{5,7... | collective-permute-start | bytes 786440 | tf_op jit(solution)/shard_map/member_2/ppermute | solution.py:63
  55.4 1.5 %collective-permute-start.17 = (bf16[32,4096]{1,0:T(8,128)(2,1)S(1)}, bf16[32,4096]{1,0:T(8,128)(2,1)S(1)}, u32[]{:S(2)}, u32[]{:S(2)}) collective-permute-start(bf16[32,4096]{1,0:T(8,128)(2,1)S(1)} %get-tuple-element.68), channel_id=1, source_target_pairs={{0,16},{1,17},{2,18},{3,19},{16,0},{17,1},{18,2},{19,3},{4,20},{5,... | collective-permute-start | bytes 786440 | tf_op jit(solution)/shard_map/member_4/ppermute | solution.py:63
  56.9 5.1 %run_experts.3 = (bf16[128,4096]{1,0:T(8,128)(2,1)S(1)}, bf16[128,4096]{1,0:T(8,128)(2,1)S(1)}) custom-call(s32[1]{0:T(128)} %bitcast.3.expert_ref, bf16[128,4224]{1,0:T(8,128)(2,1)S(1)} %packed.3.own_ref, bf16[128,4224]{1,0:T(8,128)(2,1)S(1)} %collective-permute-done.24.other_ref, bf16[4096,1536]{1,0:T(8,128)(2,1)S(1)} %get-tuple-element.74.refs_0_, ...), custom_call_target="tpu_custom_call" | custom-call | flops 2415919104 | bytes 20971520 | tf_op jit(solution)/shard_map/run_experts/pallas_call | solution.py:437
  63.5 1.8 %collective-permute-start.18 = (bf16[32,4096]{1,0:T(8,128)(2,1)S(1)}, bf16[32,4096]{1,0:T(8,128)(2,1)S(1)}, u32[]{:S(2)}, u32[]{:S(2)}) collective-permute-start(bf16[32,4096]{1,0:T(8,128)(2,1)S(1)} %get-tuple-element.69), channel_id=1, source_target_pairs={{0,18},{1,19},{2,16},{3,17},{16,2},{17,3},{18,0},{19,1},{4,22},{5,... | collective-permute-start | bytes 786440 | tf_op jit(solution)/shard_map/member_6/ppermute | solution.py:63
  67.3 1.5 %collective-permute-start.27 = (bf16[16,4096]{1,0:T(8,128)(2,1)S(1)}, bf16[16,4096]{1,0:T(8,128)(2,1)S(1)}, u32[]{:S(2)}, u32[]{:S(2)}) collective-permute-start(bf16[16,4096]{1,0:T(8,128)(2,1)S(1)} %get-tuple-element.81), channel_id=1, source_target_pairs={{0,16},{1,17},{2,18},{3,19},{16,0},{17,1},{18,2},{19,3},{4,20},{5,... | collective-permute-start | bytes 393224 | tf_op jit(solution)/shard_map/member_4/ppermute | solution.py:63
  69.9 3.6 %collective-permute-done.18.refs_3_ = bf16[32,4096]{1,0:T(8,128)(2,1)S(1)} collective-permute-done((bf16[32,4096]{1,0:T(8,128)(2,1)S(1)}, bf16[32,4096]{1,0:T(8,128)(2,1)S(1)}, u32[]{:S(2)}, u32[]{:S(2)}) %collective-permute-start.18) | collective-permute-done | bytes 262176 | tf_op jit(solution)/shard_map/member_6/ppermute | solution.py:63
  73.7 2.1 %collective-permute-start.19 = (bf16[16,4096]{1,0:T(8,128)(2,1)S(1)}, bf16[16,4096]{1,0:T(8,128)(2,1)S(1)}, u32[]{:S(2)}, u32[]{:S(2)}) collective-permute-start(bf16[16,4096]{1,0:T(8,128)(2,1)S(1)} %get-tuple-element.70), channel_id=1, source_target_pairs={{0,8},{1,9},{2,10},{3,11},{16,24},{17,25},{18,26},{19,27},{4,12},{... | collective-permute-start | bytes 393224 | tf_op jit(solution)/shard_map/plane_2/ppermute | solution.py:52
  76.3 2.5 %collective-permute-done.28.refs_3_ = bf16[16,4096]{1,0:T(8,128)(2,1)S(1)} collective-permute-done((bf16[16,4096]{1,0:T(8,128)(2,1)S(1)}, bf16[16,4096]{1,0:T(8,128)(2,1)S(1)}, u32[]{:S(2)}, u32[]{:S(2)}) %collective-permute-start.28) | collective-permute-done | bytes 131104 | tf_op jit(solution)/shard_map/member_6/ppermute | solution.py:63
  78.8 1.5 %collective-permute-start.29 = (bf16[16,4096]{1,0:T(8,128)(2,1)S(1)}, bf16[16,4096]{1,0:T(8,128)(2,1)S(1)}, u32[]{:S(2)}, u32[]{:S(2)}) collective-permute-start(bf16[16,4096]{1,0:T(8,128)(2,1)S(1)} %add_chips.4), channel_id=1, source_target_pairs={{0,12},{1,13},{2,14},{3,15},{16,28},{17,29},{18,30},{19,31},{4,8},... | collective-permute-start | bytes 393224 | tf_op jit(solution)/shard_map/plane_3/ppermute | solution.py:52
  80.3 1.9 %collective-permute-start.32 = (bf16[16,4096]{1,0:T(8,128)(2,1)S(1)}, bf16[16,4096]{1,0:T(8,128)(2,1)S(1)}, u32[]{:S(2)}, u32[]{:S(2)}) collective-permute-start(bf16[16,4096]{1,0:T(8,128)(2,1)S(1)} %get-tuple-element.89), channel_id=1, source_target_pairs={{0,18},{1,19},{2,16},{3,17},{16,2},{17,3},{18,0},{19,1},{4,22},{5,... | collective-permute-start | bytes 393224 | tf_op jit(solution)/shard_map/member_6/ppermute | solution.py:63
  83.8 2.3 %collective-permute-done.29.refs_3_ = bf16[16,4096]{1,0:T(8,128)(2,1)S(1)} collective-permute-done((bf16[16,4096]{1,0:T(8,128)(2,1)S(1)}, bf16[16,4096]{1,0:T(8,128)(2,1)S(1)}, u32[]{:S(2)}, u32[]{:S(2)}) %collective-permute-start.29) | collective-permute-done | bytes 131104 | tf_op jit(solution)/shard_map/plane_3/ppermute | solution.py:52
  86.2 1.3 %collective-permute-done.32.refs_3_ = bf16[16,4096]{1,0:T(8,128)(2,1)S(1)} collective-permute-done((bf16[16,4096]{1,0:T(8,128)(2,1)S(1)}, bf16[16,4096]{1,0:T(8,128)(2,1)S(1)}, u32[]{:S(2)}, u32[]{:S(2)}) %collective-permute-start.32) | collective-permute-done | bytes 131104 | tf_op jit(solution)/shard_map/member_6/ppermute | solution.py:63
  (60 shorter events, 15.7 us)
Async XLA Ops:
  0.6 4.7 %collective-permute-start = (s32[16]{0:T(128)}, s32[16]{0:T(128)S(1)}, u32[]{:S(2)}, u32[]{:S(2)}) collective-permute-start(s32[16]{0:T(128)} %param.17), channel_id=1, source_target_pairs={{0,16},{16,0},{1,17},{17,1},{2,18},{18,2},{3,19},{19,3},{4,20},{20... | collective-permute-start | bytes 200 | tf_op jit(solution)/shard_map/ppermute | solution.py:68
  7.0 7.2 %collective-permute-start.1 = (bf16[16,16,512]{2,1,0:T(8,128)(2,1)S(1)}, bf16[16,16,512]{2,1,0:T(8,128)(2,1)S(1)}, u32[]{:S(2)}, u32[]{:S(2)}) collective-permute-start(bf16[16,16,512]{2,1,0:T(8,128)(2,1)S(1)} %pick_pages.1), channel_id=1, source_target_pairs={{0,16},{16,0},{1,17},{17,1},{2,18},{18,2},{3,19},{19,3},{4,20},{20... | collective-permute-start | bytes 786440 | tf_op jit(solution)/shard_map/ppermute | solution.py:68
  16.2 7.9 %collective-permute-start.3 = (bf16[16,4224]{1,0:T(8,128)(2,1)S(1)}, bf16[16,4224]{1,0:T(8,128)(2,1)S(1)}, u32[]{:S(2)}, u32[]{:S(2)}) collective-permute-start(bf16[16,4224]{1,0:T(8,128)(2,1)S(1)} %get-tuple-element.72.refs_0_), channel_id=1, source_target_pairs={{0,8},{1,9},{2,10},{3,11},{16,24},{17,25},{18,26},{19,27},{4,12},{... | collective-permute-start | bytes 405512 | tf_op jit(solution)/shard_map/plane_2/ppermute | solution.py:52
  19.0 6.0 %collective-permute-start.11 = (bf16[16,4224]{1,0:T(8,128)(2,1)S(1)}, bf16[16,4224]{1,0:T(8,128)(2,1)S(1)}, u32[]{:S(2)}, u32[]{:S(2)}) collective-permute-start(bf16[16,4224]{1,0:T(8,128)(2,1)S(1)} %get-tuple-element.72.refs_0_), channel_id=1, source_target_pairs={{0,18},{1,19},{2,16},{3,17},{16,2},{17,3},{18,0},{19,1},{4,22},{5,... | collective-permute-start | bytes 405512 | tf_op jit(solution)/shard_map/member_6/ppermute | solution.py:63
  21.5 6.4 %collective-permute-start.8 = (bf16[16,4224]{1,0:T(8,128)(2,1)S(1)}, bf16[16,4224]{1,0:T(8,128)(2,1)S(1)}, u32[]{:S(2)}, u32[]{:S(2)}) collective-permute-start(bf16[16,4224]{1,0:T(8,128)(2,1)S(1)} %get-tuple-element.72.refs_0_), channel_id=1, source_target_pairs={{0,16},{1,17},{2,18},{3,19},{16,0},{17,1},{18,2},{19,3},{4,20},{5,... | collective-permute-start | bytes 405512 | tf_op jit(solution)/shard_map/member_4/ppermute | solution.py:63
  22.0 7.2 %collective-permute-start.5 = (bf16[16,4224]{1,0:T(8,128)(2,1)S(1)}, bf16[16,4224]{1,0:T(8,128)(2,1)S(1)}, u32[]{:S(2)}, u32[]{:S(2)}) collective-permute-start(bf16[16,4224]{1,0:T(8,128)(2,1)S(1)} %get-tuple-element.72.refs_0_), channel_id=1, source_target_pairs={{0,2},{1,3},{2,0},{3,1},{16,18},{17,19},{18,16},{19,17},{4,6},{5,7... | collective-permute-start | bytes 405512 | tf_op jit(solution)/shard_map/member_2/ppermute | solution.py:63
  22.5 7.7 %collective-permute-start.2 = (bf16[16,4224]{1,0:T(8,128)(2,1)S(1)}, bf16[16,4224]{1,0:T(8,128)(2,1)S(1)}, u32[]{:S(2)}, u32[]{:S(2)}) collective-permute-start(bf16[16,4224]{1,0:T(8,128)(2,1)S(1)} %get-tuple-element.72.refs_0_), channel_id=1, source_target_pairs={{0,4},{1,5},{2,6},{3,7},{16,20},{17,21},{18,22},{19,23},{4,0},{5,1... | collective-permute-start | bytes 405512 | tf_op jit(solution)/shard_map/plane_1/ppermute | solution.py:52
  24.1 8.0 %collective-permute-start.4 = (bf16[16,4224]{1,0:T(8,128)(2,1)S(1)}, bf16[16,4224]{1,0:T(8,128)(2,1)S(1)}, u32[]{:S(2)}, u32[]{:S(2)}) collective-permute-start(bf16[16,4224]{1,0:T(8,128)(2,1)S(1)} %collective-permute-done.3.refs_1_), channel_id=1, source_target_pairs={{0,4},{1,5},{2,6},{3,7},{16,20},{17,21},{18,22},{19,23},{4,0},{5,1... | collective-permute-start | bytes 405512 | tf_op jit(solution)/shard_map/plane_1/ppermute | solution.py:52
  25.0 7.7 %collective-permute-start.13 = (bf16[16,4224]{1,0:T(8,128)(2,1)S(1)}, bf16[16,4224]{1,0:T(8,128)(2,1)S(1)}, u32[]{:S(2)}, u32[]{:S(2)}) collective-permute-start(bf16[16,4224]{1,0:T(8,128)(2,1)S(1)} %collective-permute-done.3.refs_1_), channel_id=1, source_target_pairs={{0,18},{1,19},{2,16},{3,17},{16,2},{17,3},{18,0},{19,1},{4,22},{5,... | collective-permute-start | bytes 405512 | tf_op jit(solution)/shard_map/member_6/ppermute | solution.py:63
  27.8 7.4 %collective-permute-start.10 = (bf16[16,4224]{1,0:T(8,128)(2,1)S(1)}, bf16[16,4224]{1,0:T(8,128)(2,1)S(1)}, u32[]{:S(2)}, u32[]{:S(2)}) collective-permute-start(bf16[16,4224]{1,0:T(8,128)(2,1)S(1)} %collective-permute-done.3.refs_1_), channel_id=1, source_target_pairs={{0,16},{1,17},{2,18},{3,19},{16,0},{17,1},{18,2},{19,3},{4,20},{5,... | collective-permute-start | bytes 405512 | tf_op jit(solution)/shard_map/member_4/ppermute | solution.py:63
  29.2 7.7 %collective-permute-start.7 = (bf16[16,4224]{1,0:T(8,128)(2,1)S(1)}, bf16[16,4224]{1,0:T(8,128)(2,1)S(1)}, u32[]{:S(2)}, u32[]{:S(2)}) collective-permute-start(bf16[16,4224]{1,0:T(8,128)(2,1)S(1)} %collective-permute-done.3.refs_1_), channel_id=1, source_target_pairs={{0,2},{1,3},{2,0},{3,1},{16,18},{17,19},{18,16},{19,17},{4,6},{5,7... | collective-permute-start | bytes 405512 | tf_op jit(solution)/shard_map/member_2/ppermute | solution.py:63
  30.2 6.7 %collective-permute-start.12 = (bf16[16,4224]{1,0:T(8,128)(2,1)S(1)}, bf16[16,4224]{1,0:T(8,128)(2,1)S(1)}, u32[]{:S(2)}, u32[]{:S(2)}) collective-permute-start(bf16[16,4224]{1,0:T(8,128)(2,1)S(1)} %collective-permute-done.2.refs_0_), channel_id=1, source_target_pairs={{0,18},{1,19},{2,16},{3,17},{16,2},{17,3},{18,0},{19,1},{4,22},{5,... | collective-permute-start | bytes 405512 | tf_op jit(solution)/shard_map/member_6/ppermute | solution.py:63
  32.1 6.0 %collective-permute-start.9 = (bf16[16,4224]{1,0:T(8,128)(2,1)S(1)}, bf16[16,4224]{1,0:T(8,128)(2,1)S(1)}, u32[]{:S(2)}, u32[]{:S(2)}) collective-permute-start(bf16[16,4224]{1,0:T(8,128)(2,1)S(1)} %collective-permute-done.2.refs_0_), channel_id=1, source_target_pairs={{0,16},{1,17},{2,18},{3,19},{16,0},{17,1},{18,2},{19,3},{4,20},{5,... | collective-permute-start | bytes 405512 | tf_op jit(solution)/shard_map/member_4/ppermute | solution.py:63
  32.7 5.7 %collective-permute-start.6 = (bf16[16,4224]{1,0:T(8,128)(2,1)S(1)}, bf16[16,4224]{1,0:T(8,128)(2,1)S(1)}, u32[]{:S(2)}, u32[]{:S(2)}) collective-permute-start(bf16[16,4224]{1,0:T(8,128)(2,1)S(1)} %collective-permute-done.2.refs_0_), channel_id=1, source_target_pairs={{0,2},{1,3},{2,0},{3,1},{16,18},{17,19},{18,16},{19,17},{4,6},{5,7... | collective-permute-start | bytes 405512 | tf_op jit(solution)/shard_map/member_2/ppermute | solution.py:63
  38.4 3.6 %collective-permute-start.14 = (bf16[128,4224]{1,0:T(8,128)(2,1)S(1)}, bf16[128,4224]{1,0:T(8,128)(2,1)S(1)}, u32[]{:S(2)}, u32[]{:S(2)}) collective-permute-start(bf16[128,4224]{1,0:T(8,128)(2,1)S(1)} %packed.2.own_ref), channel_id=1, source_target_pairs={{0,1},{1,0},{2,3},{3,2},{16,17},{17,16},{18,19},{19,18},{4,5},{5,4... | collective-permute-start | bytes 3244040 | tf_op jit(solution)/shard_map/member_1/ppermute | solution.py:63
  38.5 12.7 %collective-permute-start.21 = (bf16[16,4224]{1,0:T(8,128)(2,1)S(1)}, bf16[16,4224]{1,0:T(8,128)(2,1)S(1)}, u32[]{:S(2)}, u32[]{:S(2)}) collective-permute-start(bf16[16,4224]{1,0:T(8,128)(2,1)S(1)} %collective-permute-done.4.refs_1_), channel_id=1, source_target_pairs={{0,2},{1,3},{2,0},{3,1},{16,18},{17,19},{18,16},{19,17},{4,6},{5,7... | collective-permute-start | bytes 405512 | tf_op jit(solution)/shard_map/member_2/ppermute | solution.py:63
  39.8 11.5 %collective-permute-start.22 = (bf16[16,4224]{1,0:T(8,128)(2,1)S(1)}, bf16[16,4224]{1,0:T(8,128)(2,1)S(1)}, u32[]{:S(2)}, u32[]{:S(2)}) collective-permute-start(bf16[16,4224]{1,0:T(8,128)(2,1)S(1)} %collective-permute-done.4.refs_1_), channel_id=1, source_target_pairs={{0,16},{1,17},{2,18},{3,19},{16,0},{17,1},{18,2},{19,3},{4,20},{5,... | collective-permute-start | bytes 405512 | tf_op jit(solution)/shard_map/member_4/ppermute | solution.py:63
  41.2 10.0 %collective-permute-start.23 = (bf16[16,4224]{1,0:T(8,128)(2,1)S(1)}, bf16[16,4224]{1,0:T(8,128)(2,1)S(1)}, u32[]{:S(2)}, u32[]{:S(2)}) collective-permute-start(bf16[16,4224]{1,0:T(8,128)(2,1)S(1)} %collective-permute-done.4.refs_1_), channel_id=1, source_target_pairs={{0,18},{1,19},{2,16},{3,17},{16,2},{17,3},{18,0},{19,1},{4,22},{5,... | collective-permute-start | bytes 405512 | tf_op jit(solution)/shard_map/member_6/ppermute | solution.py:63
  51.2 2.7 %collective-permute-start.15 = (bf16[128,4096]{1,0:T(8,128)(2,1)S(1)}, bf16[128,4096]{1,0:T(8,128)(2,1)S(1)}, u32[]{:S(2)}, u32[]{:S(2)}) collective-permute-start(bf16[128,4096]{1,0:T(8,128)(2,1)S(1)} %get-tuple-element.65), channel_id=1, source_target_pairs={{0,1},{1,0},{2,3},{3,2},{16,17},{17,16},{18,19},{19,18},{4,5},{5,4... | collective-permute-start | bytes 3145736 | tf_op jit(solution)/shard_map/member_1/ppermute | solution.py:63
  51.4 5.5 %collective-permute-start.24 = (bf16[128,4224]{1,0:T(8,128)(2,1)S(1)}, bf16[128,4224]{1,0:T(8,128)(2,1)S(1)}, u32[]{:S(2)}, u32[]{:S(2)}) collective-permute-start(bf16[128,4224]{1,0:T(8,128)(2,1)S(1)} %packed.3.own_ref), channel_id=1, source_target_pairs={{0,1},{1,0},{2,3},{3,2},{16,17},{17,16},{18,19},{19,18},{4,5},{5,4... | collective-permute-start | bytes 3244040 | tf_op jit(solution)/shard_map/member_1/ppermute | solution.py:63
  54.1 8.4 %collective-permute-start.16 = (bf16[32,4096]{1,0:T(8,128)(2,1)S(1)}, bf16[32,4096]{1,0:T(8,128)(2,1)S(1)}, u32[]{:S(2)}, u32[]{:S(2)}) collective-permute-start(bf16[32,4096]{1,0:T(8,128)(2,1)S(1)} %get-tuple-element.67), channel_id=1, source_target_pairs={{0,2},{1,3},{2,0},{3,1},{16,18},{17,19},{18,16},{19,17},{4,6},{5,7... | collective-permute-start | bytes 786440 | tf_op jit(solution)/shard_map/member_2/ppermute | solution.py:63
  55.4 8.1 %collective-permute-start.17 = (bf16[32,4096]{1,0:T(8,128)(2,1)S(1)}, bf16[32,4096]{1,0:T(8,128)(2,1)S(1)}, u32[]{:S(2)}, u32[]{:S(2)}) collective-permute-start(bf16[32,4096]{1,0:T(8,128)(2,1)S(1)} %get-tuple-element.68), channel_id=1, source_target_pairs={{0,16},{1,17},{2,18},{3,19},{16,0},{17,1},{18,2},{19,3},{4,20},{5,... | collective-permute-start | bytes 786440 | tf_op jit(solution)/shard_map/member_4/ppermute | solution.py:63
  63.5 10.0 %collective-permute-start.18 = (bf16[32,4096]{1,0:T(8,128)(2,1)S(1)}, bf16[32,4096]{1,0:T(8,128)(2,1)S(1)}, u32[]{:S(2)}, u32[]{:S(2)}) collective-permute-start(bf16[32,4096]{1,0:T(8,128)(2,1)S(1)} %get-tuple-element.69), channel_id=1, source_target_pairs={{0,18},{1,19},{2,16},{3,17},{16,2},{17,3},{18,0},{19,1},{4,22},{5,... | collective-permute-start | bytes 786440 | tf_op jit(solution)/shard_map/member_6/ppermute | solution.py:63
  66.4 9.9 %collective-permute-start.26 = (bf16[16,4096]{1,0:T(8,128)(2,1)S(1)}, bf16[16,4096]{1,0:T(8,128)(2,1)S(1)}, u32[]{:S(2)}, u32[]{:S(2)}) collective-permute-start(bf16[16,4096]{1,0:T(8,128)(2,1)S(1)} %get-tuple-element.80), channel_id=1, source_target_pairs={{0,2},{1,3},{2,0},{3,1},{16,18},{17,19},{18,16},{19,17},{4,6},{5,7... | collective-permute-start | bytes 393224 | tf_op jit(solution)/shard_map/member_2/ppermute | solution.py:63
  67.3 9.0 %collective-permute-start.27 = (bf16[16,4096]{1,0:T(8,128)(2,1)S(1)}, bf16[16,4096]{1,0:T(8,128)(2,1)S(1)}, u32[]{:S(2)}, u32[]{:S(2)}) collective-permute-start(bf16[16,4096]{1,0:T(8,128)(2,1)S(1)} %get-tuple-element.81), channel_id=1, source_target_pairs={{0,16},{1,17},{2,18},{3,19},{16,0},{17,1},{18,2},{19,3},{4,20},{5,... | collective-permute-start | bytes 393224 | tf_op jit(solution)/shard_map/member_4/ppermute | solution.py:63
  68.8 10.0 %collective-permute-start.28 = (bf16[16,4096]{1,0:T(8,128)(2,1)S(1)}, bf16[16,4096]{1,0:T(8,128)(2,1)S(1)}, u32[]{:S(2)}, u32[]{:S(2)}) collective-permute-start(bf16[16,4096]{1,0:T(8,128)(2,1)S(1)} %get-tuple-element.82), channel_id=1, source_target_pairs={{0,18},{1,19},{2,16},{3,17},{16,2},{17,3},{18,0},{19,1},{4,22},{5,... | collective-permute-start | bytes 393224 | tf_op jit(solution)/shard_map/member_6/ppermute | solution.py:63
  73.7 9.1 %collective-permute-start.19 = (bf16[16,4096]{1,0:T(8,128)(2,1)S(1)}, bf16[16,4096]{1,0:T(8,128)(2,1)S(1)}, u32[]{:S(2)}, u32[]{:S(2)}) collective-permute-start(bf16[16,4096]{1,0:T(8,128)(2,1)S(1)} %get-tuple-element.70), channel_id=1, source_target_pairs={{0,8},{1,9},{2,10},{3,11},{16,24},{17,25},{18,26},{19,27},{4,12},{... | collective-permute-start | bytes 393224 | tf_op jit(solution)/shard_map/plane_2/ppermute | solution.py:52
  75.8 8.1 %collective-permute-start.20 = (bf16[16,4096]{1,0:T(8,128)(2,1)S(1)}, bf16[16,4096]{1,0:T(8,128)(2,1)S(1)}, u32[]{:S(2)}, u32[]{:S(2)}) collective-permute-start(bf16[16,4096]{1,0:T(8,128)(2,1)S(1)} %get-tuple-element.71), channel_id=1, source_target_pairs={{0,4},{1,5},{2,6},{3,7},{16,20},{17,21},{18,22},{19,23},{4,0},{5,1... | collective-permute-start | bytes 393224 | tf_op jit(solution)/shard_map/plane_1/ppermute | solution.py:52
  78.8 7.3 %collective-permute-start.29 = (bf16[16,4096]{1,0:T(8,128)(2,1)S(1)}, bf16[16,4096]{1,0:T(8,128)(2,1)S(1)}, u32[]{:S(2)}, u32[]{:S(2)}) collective-permute-start(bf16[16,4096]{1,0:T(8,128)(2,1)S(1)} %add_chips.4), channel_id=1, source_target_pairs={{0,12},{1,13},{2,14},{3,15},{16,28},{17,29},{18,30},{19,31},{4,8},... | collective-permute-start | bytes 393224 | tf_op jit(solution)/shard_map/plane_3/ppermute | solution.py:52
  80.3 7.2 %collective-permute-start.32 = (bf16[16,4096]{1,0:T(8,128)(2,1)S(1)}, bf16[16,4096]{1,0:T(8,128)(2,1)S(1)}, u32[]{:S(2)}, u32[]{:S(2)}) collective-permute-start(bf16[16,4096]{1,0:T(8,128)(2,1)S(1)} %get-tuple-element.89), channel_id=1, source_target_pairs={{0,18},{1,19},{2,16},{3,17},{16,2},{17,3},{18,0},{19,1},{4,22},{5,... | collective-permute-start | bytes 393224 | tf_op jit(solution)/shard_map/member_6/ppermute | solution.py:63
  82.2 6.2 %collective-permute-start.31 = (bf16[16,4096]{1,0:T(8,128)(2,1)S(1)}, bf16[16,4096]{1,0:T(8,128)(2,1)S(1)}, u32[]{:S(2)}, u32[]{:S(2)}) collective-permute-start(bf16[16,4096]{1,0:T(8,128)(2,1)S(1)} %get-tuple-element.87), channel_id=1, source_target_pairs={{0,16},{1,17},{2,18},{3,19},{16,0},{17,1},{18,2},{19,3},{4,20},{5,... | collective-permute-start | bytes 393224 | tf_op jit(solution)/shard_map/member_4/ppermute | solution.py:63
  82.8 6.1 %collective-permute-start.30 = (bf16[16,4096]{1,0:T(8,128)(2,1)S(1)}, bf16[16,4096]{1,0:T(8,128)(2,1)S(1)}, u32[]{:S(2)}, u32[]{:S(2)}) collective-permute-start(bf16[16,4096]{1,0:T(8,128)(2,1)S(1)} %get-tuple-element.85), channel_id=1, source_target_pairs={{0,2},{1,3},{2,0},{3,1},{16,18},{17,19},{18,16},{19,17},{4,6},{5,7... | collective-permute-start | bytes 393224 | tf_op jit(solution)/shard_map/member_2/ppermute | solution.py:63
  (7 other events, 46.5 us)
